TPU v7x, 32 devices: a whole 2x2x4 slice. The times are simulated.
32 devices in a mesh: tile: 8 (over z, x), sub: 4 (over y, core).
Axes of the slice: x: 2, y: 2, z: 4, core: 2. Of those that a mesh axis runs over, the one named last changes fastest.
Arguments:
- outer_image: bfloat16 [1, 256, 256, 256], P(None, 'tile', 'sub'), may hold values from -6 to 6
- inner_image: bfloat16 [1, 4096, 1024], P(None, 'tile', 'sub'), may hold values from -6 to 6
- text_states: bfloat16 [1, 128, 4096], replicated, may hold values from -6 to 6
- time_steps: int32 [1], replicated, may hold values from 0 to 999
- text_lengths: int32 [1], replicated, may hold values from 32 to 128
- first_gain: float32 [256], replicated, may hold values from 0.1 to 1.9
- first_bias: float32 [256], replicated, may hold values from -3 to 3
- conv_first: bfloat16 [3, 3, 256, 256], replicated, may hold values from -0.125 to 0.125
- time_weight: bfloat16 [256, 256], replicated, may hold values from -0.75 to 0.75
- second_gain: float32 [256], replicated, may hold values from 0.1 to 1.9
- second_bias: float32 [256], replicated, may hold values from -3 to 3
- conv_second: bfloat16 [3, 3, 256, 256], replicated, may hold values from -0.125 to 0.125
- lift_weight: bfloat16 [256, 1024], replicated, may hold values from -1.5 to 1.5
- attn_gain: float32 [1024], P('sub'), may hold values from 0.1 to 1.9
- query_weight: bfloat16 [1024, 1024], P(None, 'sub'), may hold values from -0.1875 to 0.1875
- key_weight: bfloat16 [1024, 1024], P(None, 'sub'), may hold values from -0.1875 to 0.1875
- value_weight: bfloat16 [1024, 1024], P(None, 'sub'), may hold values from -0.1875 to 0.1875
- out_weight: bfloat16 [1024, 1024], P('sub'), may hold values from -1.5 to 1.5
- cross_gain: float32 [1024], P('sub'), may hold values from 0.1 to 1.9
- cross_query: bfloat16 [1024, 1024], P(None, 'sub'), may hold values from -0.1875 to 0.1875
- cross_key: bfloat16 [4096, 1024], P(None, 'sub'), may hold values from -0.09375 to 0.09375
- cross_value: bfloat16 [4096, 1024], P(None, 'sub'), may hold values from -0.09375 to 0.09375
- cross_out: bfloat16 [1024, 1024], P('sub'), may hold values from -0.75 to 0.75
- mlp_gain: float32 [1024], P('sub'), may hold values from 0.1 to 1.9
- up_weight: bfloat16 [1024, 4096], P(None, 'sub'), may hold values from -0.1875 to 0.1875
- down_weight: bfloat16 [4096, 1024], P('sub'), may hold values from -0.1875 to 0.1875
- outer_cotan: bfloat16 [1, 256, 256, 256], P(None, 'tile', 'sub'), may hold values from -6 to 6
- inner_cotan: bfloat16 [1, 4096, 1024], P(None, 'tile', 'sub'), may hold values from -6 to 6
Outputs:
- outer_out: bfloat16 [1, 256, 256, 256], P(None, 'tile', 'sub')
- inner_out: bfloat16 [1, 4096, 1024], P(None, 'tile', 'sub')
- outer_grad: float32 [1, 256, 256, 256], P(None, 'tile', 'sub')
- inner_grad: float32 [1, 4096, 1024], P(None, 'tile', 'sub')
- first_gain_grad: float32 [256], replicated
- first_bias_grad: float32 [256], replicated
- conv_first_grad: float32 [3, 3, 256, 256], replicated
- time_weight_grad: float32 [256, 256], replicated
- second_gain_grad: float32 [256], replicated
- second_bias_grad: float32 [256], replicated
- conv_second_grad: float32 [3, 3, 256, 256], replicated
- lift_weight_grad: float32 [256, 1024], replicated
- attn_gain_grad: float32 [1024], P('sub')
- query_weight_grad: float32 [1024, 1024], P(None, 'sub')
- key_weight_grad: float32 [1024, 1024], P(None, 'sub')
- value_weight_grad: float32 [1024, 1024], P(None, 'sub')
- out_weight_grad: float32 [1024, 1024], P('sub')
- cross_gain_grad: float32 [1024], P('sub')
- cross_query_grad: float32 [1024, 1024], P(None, 'sub')
- cross_key_grad: float32 [4096, 1024], P(None, 'sub')
- cross_value_grad: float32 [4096, 1024], P(None, 'sub')
- cross_out_grad: float32 [1024, 1024], P('sub')
- mlp_gain_grad: float32 [1024], P('sub')
- up_weight_grad: float32 [1024, 4096], P(None, 'sub')
- down_weight_grad: float32 [4096, 1024], P('sub')
All inputs are finite; a program needn't handle non-finite values.
Results may differ from a plain program's by a relative error of at most 0.033.
Values may be sent and summed in bfloat16 or wider, within the bound.
A program may use at most 256 MiB of HBM per device.

v0:
```python
import math

import jax
import jax.numpy as jnp
from jax import lax
from jax.sharding import PartitionSpec as P

C = 256
G = 32
HD = 64
D = 1024
TXT = 128
S = 256
POOL = 4


EPSILON = 1e-05
precise = lax.Precision.HIGHEST


def padded_2(block, sides, width):
    for axis, dim in sides:
        count = lax.axis_size(axis)
        forward = [(i, i + 1) for i in range(count - 1)]
        backward = [(target, source) for source, target in forward]
        low = lax.ppermute(
            lax.slice_in_dim(block, block.shape[dim] - width, None, axis=dim), axis, forward
        )
        high = lax.ppermute(lax.slice_in_dim(block, 0, width, axis=dim), axis, backward)
        block = jnp.concatenate([low, block, high], axis=dim)
    return block


def global_sum(values):
    return lax.psum(values, ("tile", "sub"))


def feature_total(values):
    return lax.psum(values, "sub")


def features_full(values):
    return lax.all_gather(values, "sub", axis=2, tiled=True)


def features_back(values):
    return lax.psum_scatter(
        values.astype(jnp.bfloat16), "sub", scatter_dimension=2, tiled=True
    ).astype(jnp.float32)


def padded_tile(values):
    return padded_2(values, (("tile", 1), ("sub", 2)), 1)


def gather_keys(key_loc, value_loc):
    return (
        lax.all_gather(key_loc, "tile", axis=1, tiled=True),
        lax.all_gather(value_loc, "tile", axis=1, tiled=True),
    )


def time_embed(time_steps):
    half_width = C // 2
    frequency = jnp.exp(
        -math.log(10000.0) * jnp.arange(half_width).astype(jnp.float32) / half_width
    )
    angles = time_steps.astype(jnp.float32)[:, None] * frequency[None, :]
    return jnp.concatenate([jnp.sin(angles), jnp.cos(angles)], axis=1)


def conv_valid(padded, kernel):
    return lax.conv_general_dilated(
        padded,
        kernel,
        (1, 1),
        "VALID",
        dimension_numbers=("NHWC", "HWIO", "NHWC"),
        preferred_element_type=jnp.float32,
    )


def conv_backward(padded_in, grad_out, kernel):
    row_count, col_count = (grad_out.shape[1], grad_out.shape[2])
    grad_pad = padded_tile(grad_out)
    flipped = jnp.transpose(kernel[::-1, ::-1], (0, 1, 3, 2))
    grad_in = conv_valid(grad_pad, flipped)
    tap_grads = []
    for offset_y in range(3):
        for offset_x in range(3):
            window = padded_in[
                :, offset_y : offset_y + row_count, offset_x : offset_x + col_count, :
            ]
            tap_grads.append(
                jnp.einsum("bhwc,bhwd->cd", window, grad_out, preferred_element_type=jnp.float32)
            )
    grad_kernel = jnp.stack(tap_grads).reshape(3, 3, kernel.shape[2], kernel.shape[3])
    return (grad_in, grad_kernel)


def group_stats(values, norm_gain, norm_bias, group_size):
    in_shape = values.shape
    grouped = values.reshape(in_shape[0], in_shape[1], in_shape[2], G, in_shape[3] // G)
    group_sums = global_sum(
        (jnp.sum(grouped, axis=(1, 2, 4)), jnp.sum(grouped * grouped, axis=(1, 2, 4)))
    )
    center = group_sums[0] / group_size
    inv_std = lax.rsqrt(group_sums[1] / group_size - center * center + EPSILON)
    normed = (grouped - center[:, None, None, :, None]) * inv_std[:, None, None, :, None]
    return (normed.reshape(in_shape) * norm_gain + norm_bias, normed, inv_std)


def group_back(grad_out, normed, inv_std, norm_gain, group_size):
    in_shape = grad_out.shape
    scaled = (grad_out * norm_gain).reshape(normed.shape)
    group_sums = global_sum(
        (jnp.sum(scaled, axis=(1, 2, 4)), jnp.sum(scaled * normed, axis=(1, 2, 4)))
    )
    mean_grad = group_sums[0][:, None, None, :, None] / group_size
    mean_cross = group_sums[1][:, None, None, :, None] / group_size
    grad_in = inv_std[:, None, None, :, None] * (scaled - mean_grad - normed * mean_cross)
    grad_gain = jnp.sum(grad_out * normed.reshape(in_shape), axis=(0, 1, 2))
    grad_bias = jnp.sum(grad_out, axis=(0, 1, 2))
    return (grad_in.reshape(in_shape), grad_gain, grad_bias)


def layer_stats(values, norm_gain):
    token_sums = feature_total((jnp.sum(values, axis=2), jnp.sum(values * values, axis=2)))
    center = token_sums[0] / D
    inv_std = lax.rsqrt(token_sums[1] / D - center * center + EPSILON)
    normed = (values - center[..., None]) * inv_std[..., None]
    return (normed * norm_gain, normed, inv_std)


def layer_back(grad_out, normed, inv_std, norm_gain):
    scaled = grad_out * norm_gain
    token_sums = feature_total((jnp.sum(scaled, axis=2), jnp.sum(scaled * normed, axis=2)))
    grad_in = inv_std[..., None] * (
        scaled - token_sums[0][..., None] / D - normed * token_sums[1][..., None] / D
    )
    return (grad_in, jnp.sum(grad_out * normed, axis=(0, 1)))


def silu_grad(values):
    sigma = jax.nn.sigmoid(values)
    return sigma * (1.0 + values * (1.0 - sigma))


def gelu_tanh(values):
    return jax.nn.gelu(values, approximate=True)


def project(values, weight):
    return jnp.einsum("btd,de->bte", values, weight, preferred_element_type=jnp.float32)


def project_back(values, weight):
    return jnp.einsum("bte,de->btd", values, weight, preferred_element_type=jnp.float32)


def weight_grad(inputs, grads):
    return jnp.einsum("btd,bte->de", inputs, grads, preferred_element_type=jnp.float32)


def split_heads(values):
    return values.reshape(values.shape[0], values.shape[1], values.shape[2] // HD, HD)


def attention_scores(query_heads, key_heads, text_mask):
    scores = jnp.einsum(
        "bqhd,bkhd->bhqk", query_heads, key_heads, preferred_element_type=jnp.float32
    ) * HD ** (-0.5)
    if text_mask is not None:
        scores = jnp.where(text_mask[:, None, None, :], scores, -1000000000.0)
    return scores


def attend_forward(query_loc, key_all, value_all, text_mask):
    scores = attention_scores(split_heads(query_loc), split_heads(key_all), text_mask)
    maximum = jnp.max(scores, axis=3, keepdims=True)
    raised = jnp.exp(scores - maximum)
    row_total = jnp.sum(raised, axis=3, keepdims=True)
    weights = (raised / row_total).astype(jnp.bfloat16)
    mixed_rows = jnp.einsum(
        "bhqk,bkhd->bqhd", weights, split_heads(value_all), preferred_element_type=jnp.float32
    )
    return (mixed_rows.reshape(query_loc.shape).astype(jnp.bfloat16), maximum + jnp.log(row_total))


def attend_backward(query_loc, key_all, value_all, log_total, grad_mixed, text_mask):
    query_heads = split_heads(query_loc)
    key_heads = split_heads(key_all)
    value_heads = split_heads(value_all)
    scores = attention_scores(query_heads, key_heads, text_mask)
    weights_f = jnp.exp(scores - log_total)
    weights_low = weights_f.astype(jnp.bfloat16)
    grad_heads = split_heads(grad_mixed)
    grad_value = jnp.einsum(
        "bhqk,bqhd->bkhd", weights_low, grad_heads, preferred_element_type=jnp.float32
    )
    grad_weights = jnp.einsum(
        "bqhd,bkhd->bhqk", grad_heads, value_heads, preferred_element_type=jnp.float32
    )
    grad_scores = (
        weights_f * (grad_weights - jnp.sum(weights_f * grad_weights, axis=3, keepdims=True))
    ).astype(jnp.bfloat16)
    grad_query = jnp.einsum(
        "bhqk,bkhd->bqhd", grad_scores, key_heads, preferred_element_type=jnp.float32
    ) * HD ** (-0.5)
    grad_key = jnp.einsum(
        "bhqk,bqhd->bkhd", grad_scores, query_heads, preferred_element_type=jnp.float32
    ) * HD ** (-0.5)
    return (
        grad_query.reshape(query_loc.shape),
        grad_key.reshape(key_all.shape),
        grad_value.reshape(value_all.shape),
    )


def outer_forward(
    outer_f, first_gain, first_bias, conv_first, time_shift, second_gain, second_bias, conv_second
):
    group_size = S * S * (C // G)
    norm_first, hat_first, std_first = group_stats(outer_f, first_gain, first_bias, group_size)
    padded_first = padded_tile(jax.nn.silu(norm_first).astype(jnp.bfloat16))
    hidden = conv_valid(padded_first, conv_first) + time_shift[:, None, None, :]
    norm_second, hat_second, std_second = group_stats(hidden, second_gain, second_bias, group_size)
    padded_second = padded_tile(jax.nn.silu(norm_second).astype(jnp.bfloat16))
    outer_sum = outer_f + conv_valid(padded_second, conv_second)
    saved_outer = (
        norm_first,
        hat_first,
        std_first,
        padded_first,
        norm_second,
        hat_second,
        std_second,
        padded_second,
    )
    return (outer_sum, saved_outer)


def local(
    outer_image,
    inner_image,
    text_states,
    time_steps,
    text_lengths,
    first_gain,
    first_bias,
    conv_first,
    time_weight,
    second_gain,
    second_bias,
    conv_second,
    lift_weight,
    attn_gain,
    query_weight,
    key_weight,
    value_weight,
    out_weight,
    cross_gain,
    cross_query,
    cross_key,
    cross_value,
    cross_out,
    mlp_gain,
    up_weight,
    down_weight,
    outer_cotan,
    inner_cotan,
):
    group_size = S * S * (C // G)
    outer_f = outer_image.astype(jnp.float32)
    time_act = jax.nn.silu(time_embed(time_steps))
    time_shift = jnp.dot(time_act, time_weight.astype(jnp.float32), precision=precise)
    outer_sum, saved_outer = outer_forward(
        outer_f,
        first_gain,
        first_bias,
        conv_first,
        time_shift,
        second_gain,
        second_bias,
        conv_second,
    )
    batch_count, row_count, col_count = (outer_sum.shape[0], outer_sum.shape[1], outer_sum.shape[2])
    pooled = jnp.mean(
        outer_sum.reshape(batch_count, row_count // POOL, POOL, col_count // POOL, POOL, C),
        axis=(2, 4),
    ).astype(jnp.bfloat16)
    lifted = jnp.einsum(
        "bijc,cd->bijd", pooled, lift_weight, preferred_element_type=jnp.float32
    ).astype(jnp.bfloat16)
    regrouped = lax.all_to_all(lifted, "sub", split_axis=3, concat_axis=2, tiled=True)
    token_count = regrouped.shape[1] * regrouped.shape[2]
    stream_in = inner_image.astype(jnp.float32) + regrouped.reshape(
        batch_count, token_count, regrouped.shape[3]
    ).astype(jnp.float32)
    attn_norm, attn_hat, attn_std = layer_stats(stream_in, attn_gain)
    attn_in = features_full(attn_norm.astype(jnp.bfloat16))
    query_loc = project(attn_in, query_weight).astype(jnp.bfloat16)
    key_loc = project(attn_in, key_weight).astype(jnp.bfloat16)
    value_loc = project(attn_in, value_weight).astype(jnp.bfloat16)
    key_all, value_all = gather_keys(key_loc, value_loc)
    self_mixed, self_lse = attend_forward(query_loc, key_all, value_all, None)
    after_attn = stream_in + features_back(project(self_mixed, out_weight))
    cross_norm, cross_hat, cross_std = layer_stats(after_attn, cross_gain)
    cross_in = features_full(cross_norm.astype(jnp.bfloat16))
    cross_q = project(cross_in, cross_query).astype(jnp.bfloat16)
    cross_k = project(text_states, cross_key).astype(jnp.bfloat16)
    cross_v = project(text_states, cross_value).astype(jnp.bfloat16)
    text_mask = jnp.arange(TXT)[None, :] < text_lengths[:, None]
    cross_mixed, cross_lse = attend_forward(cross_q, cross_k, cross_v, text_mask)
    after_cross = after_attn + features_back(project(cross_mixed, cross_out))
    mlp_norm, mlp_hat, mlp_std = layer_stats(after_cross, mlp_gain)
    mlp_in = features_full(mlp_norm.astype(jnp.bfloat16))
    lifted_up = project(mlp_in, up_weight)
    activated_f, gelu_pull = jax.vjp(gelu_tanh, lifted_up)
    activated = activated_f.astype(jnp.bfloat16)
    inner_sum = after_cross + features_back(project(activated, down_weight))
    grad_top = features_full(inner_cotan)
    grad_down = weight_grad(activated, grad_top)
    grad_act = project_back(grad_top, down_weight)
    grad_lift_up = gelu_pull(grad_act)[0].astype(jnp.bfloat16)
    grad_up = weight_grad(mlp_in, grad_lift_up)
    grad_mid, grad_mlp_gain = layer_back(
        features_back(project_back(grad_lift_up, up_weight)), mlp_hat, mlp_std, mlp_gain
    )
    grad_after_cross = inner_cotan.astype(jnp.float32) + grad_mid
    grad_cross_full = features_full(grad_after_cross.astype(jnp.bfloat16))
    grad_cross_out = weight_grad(cross_mixed, grad_cross_full)
    grad_cross_mixed = project_back(grad_cross_full, cross_out).astype(jnp.bfloat16)
    grad_cq, grad_ck, grad_cv = attend_backward(
        cross_q, cross_k, cross_v, cross_lse, grad_cross_mixed, text_mask
    )
    grad_cq = grad_cq.astype(jnp.bfloat16)
    grad_cross_query = weight_grad(cross_in, grad_cq)
    text_f = text_states.astype(jnp.float32)
    grad_cross_key = jnp.einsum("bsw,bse->we", text_f, grad_ck, precision=precise)
    grad_cross_value = jnp.einsum("bsw,bse->we", text_f, grad_cv, precision=precise)
    grad_cross_in = features_back(project_back(grad_cq, cross_query))
    grad_mid, grad_cross_gain = layer_back(grad_cross_in, cross_hat, cross_std, cross_gain)
    grad_after_attn = grad_after_cross + grad_mid
    grad_attn_full = features_full(grad_after_attn.astype(jnp.bfloat16))
    grad_out = weight_grad(self_mixed, grad_attn_full)
    grad_self_mixed = project_back(grad_attn_full, out_weight).astype(jnp.bfloat16)
    keys_back, values_back = gather_keys(key_loc, value_loc)
    grad_q, grad_k_all, grad_v_all = attend_backward(
        query_loc, keys_back, values_back, self_lse, grad_self_mixed, None
    )
    grad_k, grad_v = (
        lax.psum_scatter(
            grad_k_all.astype(jnp.bfloat16), "tile", scatter_dimension=1, tiled=True
        ).astype(jnp.float32),
        lax.psum_scatter(
            grad_v_all.astype(jnp.bfloat16), "tile", scatter_dimension=1, tiled=True
        ).astype(jnp.float32),
    )
    grad_q = grad_q.astype(jnp.bfloat16)
    grad_k = grad_k.astype(jnp.bfloat16)
    grad_v = grad_v.astype(jnp.bfloat16)
    grad_query = weight_grad(attn_in, grad_q)
    grad_key = weight_grad(attn_in, grad_k)
    grad_value = weight_grad(attn_in, grad_v)
    grad_attn_in = (
        project_back(grad_q, query_weight)
        + project_back(grad_k, key_weight)
        + project_back(grad_v, value_weight)
    )
    grad_mid, grad_attn_gain = layer_back(
        features_back(grad_attn_in), attn_hat, attn_std, attn_gain
    )
    inner_grad = grad_after_attn + grad_mid
    grad_lifted = inner_grad.astype(jnp.bfloat16).reshape(regrouped.shape)
    grad_block = lax.all_to_all(grad_lifted, "sub", split_axis=2, concat_axis=3, tiled=True)
    grad_lift = jnp.einsum("bijc,bijd->cd", pooled, grad_block, preferred_element_type=jnp.float32)
    grad_pooled = jnp.einsum(
        "bijd,cd->bijc", grad_block, lift_weight, preferred_element_type=jnp.float32
    ) / (POOL * POOL)
    spread_shape = (batch_count, row_count // POOL, POOL, col_count // POOL, POOL, C)
    grad_spread = jnp.broadcast_to(grad_pooled[:, :, None, :, None, :], spread_shape).reshape(
        outer_sum.shape
    )
    grad_outer = outer_cotan.astype(jnp.float32) + grad_spread
    unused_sum, saved_back = outer_forward(
        outer_f,
        first_gain,
        first_bias,
        conv_first,
        time_shift,
        second_gain,
        second_bias,
        conv_second,
    )
    (
        norm_first,
        hat_first,
        std_first,
        padded_first,
        norm_second,
        hat_second,
        std_second,
        padded_second,
    ) = saved_back
    grad_act_second, grad_conv_second = conv_backward(
        padded_second, grad_outer.astype(jnp.bfloat16), conv_second
    )
    grad_hidden, grad_second_gain, grad_second_bias = group_back(
        grad_act_second * silu_grad(norm_second), hat_second, std_second, second_gain, group_size
    )
    grad_time = jnp.dot(time_act.T, jnp.sum(grad_hidden, axis=(1, 2)), precision=precise)
    grad_act_first, grad_conv_first = conv_backward(
        padded_first, grad_hidden.astype(jnp.bfloat16), conv_first
    )
    grad_input, grad_first_gain, grad_first_bias = group_back(
        grad_act_first * silu_grad(norm_first), hat_first, std_first, first_gain, group_size
    )
    outer_grad = grad_outer + grad_input
    outer_grads = global_sum(
        (
            grad_first_gain,
            grad_first_bias,
            grad_conv_first,
            grad_time,
            grad_second_gain,
            grad_second_bias,
            grad_conv_second,
            grad_lift,
        )
    )
    inner_grads = (
        lax.psum(grad_attn_gain.astype(jnp.bfloat16), "tile").astype(jnp.float32),
        lax.psum(grad_query.astype(jnp.bfloat16), "tile").astype(jnp.float32),
        lax.psum(grad_key.astype(jnp.bfloat16), "tile").astype(jnp.float32),
        lax.psum(grad_value.astype(jnp.bfloat16), "tile").astype(jnp.float32),
        lax.psum(grad_out.astype(jnp.bfloat16), "tile").astype(jnp.float32),
        lax.psum(grad_cross_gain.astype(jnp.bfloat16), "tile").astype(jnp.float32),
        lax.psum(grad_cross_query.astype(jnp.bfloat16), "tile").astype(jnp.float32),
        lax.psum(grad_cross_key.astype(jnp.bfloat16), "tile").astype(jnp.float32),
        lax.psum(grad_cross_value.astype(jnp.bfloat16), "tile").astype(jnp.float32),
        lax.psum(grad_cross_out.astype(jnp.bfloat16), "tile").astype(jnp.float32),
        lax.psum(grad_mlp_gain.astype(jnp.bfloat16), "tile").astype(jnp.float32),
        lax.psum(grad_up.astype(jnp.bfloat16), "tile").astype(jnp.float32),
        lax.psum(grad_down.astype(jnp.bfloat16), "tile").astype(jnp.float32),
    )
    return (
        outer_sum.astype(jnp.bfloat16),
        inner_sum.astype(jnp.bfloat16),
        outer_grad,
        inner_grad,
        outer_grads[0],
        outer_grads[1],
        outer_grads[2],
        outer_grads[3],
        outer_grads[4],
        outer_grads[5],
        outer_grads[6],
        outer_grads[7],
        inner_grads[0],
        inner_grads[1],
        inner_grads[2],
        inner_grads[3],
        inner_grads[4],
        inner_grads[5],
        inner_grads[6],
        inner_grads[7],
        inner_grads[8],
        inner_grads[9],
        inner_grads[10],
        inner_grads[11],
        inner_grads[12],
    )


def solution(mesh):
    placed = (
        P(None, "tile", "sub", None),
        P(None, "tile", "sub"),
        P(),
        P(),
        P(),
        P(),
        P(),
        P(),
        P(),
        P(),
        P(),
        P(),
        P(),
        P("sub"),
        P(None, "sub"),
        P(None, "sub"),
        P(None, "sub"),
        P("sub", None),
        P("sub"),
        P(None, "sub"),
        P(None, "sub"),
        P(None, "sub"),
        P("sub", None),
        P("sub"),
        P(None, "sub"),
        P("sub", None),
        P(None, "tile", "sub", None),
        P(None, "tile", "sub"),
    )
    return jax.shard_map(
        local,
        mesh=mesh,
        in_specs=placed,
        out_specs=(
            P(None, "tile", "sub", None),
            P(None, "tile", "sub"),
            P(None, "tile", "sub", None),
            P(None, "tile", "sub"),
            P(),
            P(),
            P(),
            P(),
            P(),
            P(),
            P(),
            P(),
            P("sub"),
            P(None, "sub"),
            P(None, "sub"),
            P(None, "sub"),
            P("sub", None),
            P("sub"),
            P(None, "sub"),
            P(None, "sub"),
            P(None, "sub"),
            P("sub", None),
            P("sub"),
            P(None, "sub"),
            P("sub", None),
        ),
        check_vma=False,
    )
```

profile of v0, /device:TPU:0, one launch (start us, length us, event | category | flops | bytes accessed | tf_op | source)
XLA Modules:
  0.0 1366.7 jit_solution(18264607793531903873)
XLA Ops:
  9.4 42.0 %all-reduce.3 = (f32[1,32]{1,0:T(1,128)S(1)}, f32[1,32]{1,0:T(1,128)S(1)}) all-reduce(f32[1,32]{1,0:T(1,128)S(1)} %bitcast.574, f32[1,32]{1,0:T(1,128)S(1)} %bitcast.575), channel_id=1, replica_groups=mesh['tile'=8,'sub'=4] {'tile','sub'}, use_global_device_ids=true, to_apply=%region_5.6 | all-reduce | flops 64 | bytes 512 | tf_op jit(solution)/shard_map/psum | solution.py:35
  55.1 4.8 collective-permute-start
  69.2 4.6 select_reduce_fusion.6
  74.3 43.5 %all-reduce.2 = (f32[1,32]{1,0:T(1,128)S(1)}, f32[1,32]{1,0:T(1,128)S(1)}) all-reduce(f32[1,32]{1,0:T(1,128)S(1)} %bitcast.572, f32[1,32]{1,0:T(1,128)S(1)} %bitcast.576), channel_id=1, replica_groups=mesh['tile'=8,'sub'=4] {'tile','sub'}, use_global_device_ids=true, to_apply=%region_11.12 | all-reduce | flops 64 | bytes 512 | tf_op jit(solution)/shard_map/psum | solution.py:35
  122.3 4.8 collective-permute-start.4
  155.9 11.1 all_to_all.24
  172.3 5.8 all-reduce.10
  179.6 19.1 %all-gather.11.cloned.1.call-done = bf16[1,512,1024]{2,1,0:T(8,128)(2,1)} async-done(((bf16[1,512,256]{2,1,0:T(8,128)(2,1)}), bf16[1,512,1024]{2,1,0:T(8,128)(2,1)}) %all-gather.11.cloned.1.call-update) | async-done | bytes 1048592 | tf_op jit(solution)/shard_map/all_gather | solution.py:43
  205.5 45.2 %all-gather.25.cloned.1.call-done = bf16[4096,256]{1,0:T(8,128)(2,1)} async-done(((bf16[512,256]{1,0:T(8,128)(2,1)}), bf16[4096,256]{1,0:T(8,128)(2,1)}) %all-gather.25.cloned.1.call-update) | async-done | bytes 2097168 | tf_op jit(solution)/shard_map/all_gather | solution.py:58
  254.8 14.9 %multiply_reduce_fusion.1 = (f32[4,512]{1,0:T(4,128)S(1)}, f32[4,512,4096]{2,1,0:T(8,128)}) fusion(bf16[512,4,64]{0,2,1:T(8,128)(2,1)S(1)} %bitcast.511, bf16[4096,4,64]{0,2,1:T(8,128)(2,1)} %bitcast.485), kind=kOutput, calls=%fused_computation.6 | convolution fusion | flops 1090516992 | bytes 35921920 | tf_op jit(solution)/shard_map/bqhd,bkhd->bhqk/dot_general | solution.py:170
  269.7 14.3 %fusion = f32[4,512]{1,0:T(4,128)S(1)} fusion(f32[4,512,4096]{2,1,0:T(8,128)} %get-tuple-element.215, f32[4,512]{1,0:T(4,128)S(1)} %get-tuple-element.214), kind=kLoop, calls=%fused_computation.5 | loop fusion | flops 25163776 | bytes 33570816 | tf_op jit(solution)/shard_map/reduce_sum | solution.py:182
  283.9 17.3 %all-gather.23.cloned.1.call-done = bf16[4096,256]{1,0:T(8,128)(2,1)} async-done(((bf16[512,256]{1,0:T(8,128)(2,1)}), bf16[4096,256]{1,0:T(8,128)(2,1)}) %all-gather.23.cloned.1.call-update) | async-done | bytes 2097168 | tf_op jit(solution)/shard_map/all_gather | solution.py:59
  305.3 14.7 %fusion.81 = bf16[4,64,512]{2,1,0:T(8,128)(2,1)S(1)} fusion(bf16[4096,4,64]{0,2,1:T(8,128)(2,1)} %bitcast.496, f32[4,512,4096]{2,1,0:T(8,128)} %get-tuple-element.215, f32[4,512]{1,0:T(4,128)S(1)} %fusion, f32[4,512]{1,0:T(4,128)S(1)} %get-tuple-element.214), kind=kOutput, calls=%fused_computation.145 | convolution fusion | flops 1107427328 | bytes 35930112 | tf_op jit(solution)/shard_map/bhqk,bkhd->bqhd/dot_general | solution.py:184
  322.2 23.5 %reduce-scatter.9.cloned.1.call-done = bf16[1,512,256]{2,1,0:T(8,128)(2,1)} async-done(((bf16[1,512,1024]{2,1,0:T(8,128)(2,1)}), bf16[1,512,256]{2,1,0:T(8,128)(2,1)}) %reduce-scatter.9.cloned.1.call-update) | async-done | bytes 262160 | tf_op jit(solution)/shard_map/reduce_scatter | solution.py:47
  347.7 5.7 all-reduce.9
  362.5 11.5 all-gather.13.cloned.1.call-done
  379.0 25.0 %reduce-scatter.11.cloned.1.call-done = bf16[1,512,256]{2,1,0:T(8,128)(2,1)} async-done(((bf16[1,512,1024]{2,1,0:T(8,128)(2,1)}), bf16[1,512,256]{2,1,0:T(8,128)(2,1)}) %reduce-scatter.11.cloned.1.call-update) | async-done | bytes 262160 | tf_op jit(solution)/shard_map/reduce_scatter | solution.py:47
  405.9 6.3 all-reduce.8
  415.9 17.1 %all-gather.15.cloned.1.call-done = bf16[1,512,1024]{2,1,0:T(8,128)(2,1)} async-done(((bf16[1,512,256]{2,1,0:T(8,128)(2,1)}), bf16[1,512,1024]{2,1,0:T(8,128)(2,1)}) %all-gather.15.cloned.1.call-update) | async-done | bytes 1048592 | tf_op jit(solution)/shard_map/all_gather | solution.py:43
  436.8 14.6 %all-gather.17.cloned.1.call-done = bf16[1,512,1024]{2,1,0:T(8,128)(2,1)} async-done(((bf16[1,512,256]{2,1,0:T(8,128)(2,1)}), bf16[1,512,1024]{2,1,0:T(8,128)(2,1)}) %all-gather.17.cloned.1.call-update) | async-done | bytes 1048592 | tf_op jit(solution)/shard_map/all_gather | solution.py:43
  451.5 4.9 fusion.23
  459.7 4.7 fusion.74
  464.5 20.2 %reduce-scatter.15.cloned.1.call-done = bf16[1,512,256]{2,1,0:T(8,128)(2,1)} async-done(((bf16[1,512,1024]{2,1,0:T(8,128)(2,1)}), bf16[1,512,256]{2,1,0:T(8,128)(2,1)}) %reduce-scatter.15.cloned.1.call-update) | async-done | bytes 262160 | tf_op jit(solution)/shard_map/reduce_scatter | solution.py:47
  486.5 5.7 all-reduce.7
  492.2 20.5 %reduce-scatter.13.cloned.1.call-done = bf16[1,512,256]{2,1,0:T(8,128)(2,1)} async-done(((bf16[1,512,1024]{2,1,0:T(8,128)(2,1)}), bf16[1,512,256]{2,1,0:T(8,128)(2,1)}) %reduce-scatter.13.cloned.1.call-update) | async-done | bytes 262160 | tf_op jit(solution)/shard_map/reduce_scatter | solution.py:47
  515.2 16.9 %all-gather.19.cloned.1.call-done = bf16[1,512,1024]{2,1,0:T(8,128)(2,1)} async-done(((bf16[1,512,256]{2,1,0:T(8,128)(2,1)}), bf16[1,512,1024]{2,1,0:T(8,128)(2,1)}) %all-gather.19.cloned.1.call-update) | async-done | bytes 1048592 | tf_op jit(solution)/shard_map/all_gather | solution.py:43
  536.8 25.0 %reduce-scatter.17.cloned.1.call-done = bf16[1,512,256]{2,1,0:T(8,128)(2,1)} async-done(((bf16[1,512,1024]{2,1,0:T(8,128)(2,1)}), bf16[1,512,256]{2,1,0:T(8,128)(2,1)}) %reduce-scatter.17.cloned.1.call-update) | async-done | bytes 262160 | tf_op jit(solution)/shard_map/reduce_scatter | solution.py:47
  563.1 5.8 all-reduce.6
  571.4 17.8 %all-gather.21.cloned.1.call-done = bf16[1,512,1024]{2,1,0:T(8,128)(2,1)} async-done(((bf16[1,512,256]{2,1,0:T(8,128)(2,1)}), bf16[1,512,1024]{2,1,0:T(8,128)(2,1)}) %all-gather.21.cloned.1.call-update) | async-done | bytes 1048592 | tf_op jit(solution)/shard_map/all_gather | solution.py:43
  591.0 22.3 %multiply_reduce_fusion = (f32[4,512]{1,0:T(4,128)S(1)}, f32[4,512,4096]{2,1,0:T(8,128)}) fusion(f32[4,512,4096]{2,1,0:T(8,128)} %get-tuple-element.215, f32[4,512]{1,0:T(4,128)S(1)} %log_add_fusion, bf16[512,4,64]{0,2,1:T(8,128)(2,1)S(1)} %bitcast.518, bf16[4096,4,64]{0,2,1:T(8,128)(2,1)S(1)} %bitcast.497), kind=kOutput, calls=%fused_computation.1 | convolution fusion | flops 1107294208 | bytes 69484544 | tf_op jit(solution)/shard_map/bqhd,bkhd->bhqk/dot_general | solution.py:201
  613.3 27.5 %multiply_convert_fusion = bf16[4,512,4096]{2,1,0:T(8,128)(2,1)} fusion(f32[4,512,4096]{2,1,0:T(8,128)} %get-tuple-element.221, f32[4,512,4096]{2,1,0:T(8,128)} %get-tuple-element.215, f32[4,512]{1,0:T(4,128)S(1)} %get-tuple-element.220, f32[4,512]{1,0:T(4,128)S(1)} %log_add_fusion), kind=kLoop, calls=%fused_computation | loop fusion | flops 41943040 | bytes 83902464 | tf_op jit(solution)/shard_map/convert_element_type | solution.py:206
  640.9 10.1 fusion.7
  651.9 15.4 %fusion.8 = bf16[4,64,4096]{2,1,0:T(8,128)(2,1)} fusion(bf16[512,4,64]{0,2,1:T(8,128)(2,1)S(1)} %bitcast.519, f32[4,512,4096]{2,1,0:T(8,128)} %get-tuple-element.215, f32[4,512]{1,0:T(4,128)S(1)} %log_add_fusion), kind=kOutput, calls=%fused_computation.16 | convolution fusion | flops 1099956224 | bytes 35921920 | tf_op jit(solution)/shard_map/bhqk,bqhd->bkhd/dot_general | solution.py:198
  677.2 11.2 fusion.80
  688.9 30.5 %reduce-scatter.19.cloned.1.call-done = bf16[1,512,256]{1,2,0:T(8,128)(2,1)} async-done(((bf16[1,4096,256]{1,2,0:T(8,128)(2,1)}), bf16[1,512,256]{1,2,0:T(8,128)(2,1)}) %reduce-scatter.19.cloned.1.call-update) | async-done | bytes 262160 | tf_op jit(solution)/shard_map/reduce_scatter | solution.py:353
  722.1 68.8 %reduce-scatter.21.cloned.1.call-done = bf16[1,512,256]{1,2,0:T(8,128)(2,1)} async-done(((bf16[1,4096,256]{1,2,0:T(8,128)(2,1)}), bf16[1,512,256]{1,2,0:T(8,128)(2,1)}) %reduce-scatter.21.cloned.1.call-update) | async-done | bytes 262160 | tf_op jit(solution)/shard_map/reduce_scatter | solution.py:356
  812.6 5.6 reduce-scatter.23.cloned.1.call-done
  819.6 5.8 all-reduce.5
  846.8 4.8 collective-permute-start.8
  866.0 5.4 select_reduce_fusion.3
  871.7 45.8 %all-reduce.1 = (f32[1,32]{1,0:T(1,128)S(1)}, f32[1,32]{1,0:T(1,128)S(1)}) all-reduce(f32[1,32]{1,0:T(1,128)S(1)} %bitcast.573, f32[1,32]{1,0:T(1,128)S(1)} %bitcast.577), channel_id=1, replica_groups=mesh['tile'=8,'sub'=4] {'tile','sub'}, use_global_device_ids=true, to_apply=%region_56.57 | all-reduce | flops 64 | bytes 512 | tf_op jit(solution)/shard_map/psum | solution.py:35
  939.5 4.8 collective-permute-start.12
  950.3 23.2 %all-reduce.11 = (bf16[256]{0:T(256)(128)(2,1)S(1)}, bf16[256]{0:T(256)(128)(2,1)S(1)}, bf16[256]{0:T(256)(128)(2,1)S(1)}) all-reduce(bf16[256]{0:T(256)(128)(2,1)S(1)} %get-tuple-element.117, bf16[256]{0:T(256)(128)(2,1)S(1)} %get-tuple-element.115, bf16[256]{0:T(256)(128)(2,1)S(1)} %copy-done.127), channel_id=1, replica_groups=mesh['tile'=8,'sub'=4] {'tile'}, use_global_device_ids=true, to_apply=%region_77.78 | all-reduce | flops 768 | bytes 3072 | tf_op jit(solution)/shard_map/psum | solution.py:433
  986.6 39.9 %all-reduce = (f32[1,32]{1,0:T(1,128)S(1)}, f32[1,32]{1,0:T(1,128)S(1)}, f32[256]{0:T(256)}, f32[256]{0:T(256)}, f32[256]{0:T(256)}, /*index=5*/f32[256]{0:T(256)}) all-reduce(f32[1,32]{1,0:T(1,128)S(1)} %bitcast.570, f32[1,32]{1,0:T(1,128)S(1)} %bitcast.571, ...), channel_id=1, replica_groups=mesh['tile'=8,'sub'=4] {'tile','sub'}, use_global_device_ids=true, to_apply=%region_62.63 | all-reduce | flops 1088 | bytes 8704 | tf_op jit(solution)/shard_map/psum | solution.py:35
  1026.8 4.4 fusion.43
  1031.2 161.2 %all-reduce.18.cloned.1.call-done = (bf16[4096,256]{0,1:T(8,128)(2,1)}, bf16[4096,256]{0,1:T(8,128)(2,1)}, bf16[1024,256]{1,0:T(8,128)(2,1)}, bf16[1024,256]{1,0...) async-done(((bf16[4096,256]{0,1:T(8,128)(2,1)}, ...) | async-done | bytes 11534352 | tf_op jit(solution)/shard_map/psum | solution.py:440
  1199.9 4.4 copy.141
  1215.1 137.6 %all-reduce.16.cloned.1.call-done = (f32[3,3,256,256]{3,2,1,0:T(8,128)}, f32[256,256]{1,0:T(8,128)}, f32[3,3,256,256]{3,2,1,0:T(8,128)}, f32[256,1024]{1,0:T(8,128)}) async-done(((f32[3,3,256,256]{3,2,1,0:T(8,128)}, f32[256,256]{1,0:T(8,128)}, f32[3,3,256,256]{3,2,1,0:T(8,128)}, f32[256,1024]{1,0:T(8,128)}), (f32[3,3,256,256]{3,2,1,0:T(8,128)}, f32[256,256]{1,0:T(8,128)}, f32[3,3,256,256]{3,2,1,0:T(8,128)}, ...) | async-done | bytes 6029328 | tf_op jit(solution)/shard_map/psum | solution.py:35
  (548 shorter events, 252.8 us)
Async XLA Ops:
  7.2 425.9 %copy-start = (bf16[1024,1024]{1,0:T(8,128)(2,1)S(1)}, bf16[1024,1024]{1,0:T(8,128)(2,1)}, u32[]{:S(2)}) copy-start(bf16[1024,1024]{1,0:T(8,128)(2,1)} %param.52) | copy-start | bytes 6291460
  7.2 58.6 %copy-start.87 = (bf16[256,256]{1,0:T(8,128)(2,1)S(1)}, bf16[256,256]{1,0:T(8,128)(2,1)}, u32[]{:S(2)}) copy-start(bf16[256,256]{1,0:T(8,128)(2,1)} %param.36) | copy-start | bytes 393220
  7.2 191.4 %all-gather.11.cloned.1.call-start = ((), (), s32[]{:S(2)}) async-start(), calls=%async_computation.10 | async-start | bytes 1310720 | tf_op jit(solution)/shard_map/all_gather | solution.py:43
  53.8 6.8 collective-permute-start.1
  55.1 6.4 collective-permute-start
  61.5 4.5 collective-permute-start.3
  62.8 3.9 collective-permute-start.2
  66.0 52.2 %copy-start.112 = (f32[1,256]{1,0:T(1,128)}, f32[1,256]{1,0:T(1,128)S(1)}, u32[]{:S(2)}) copy-start(f32[1,256]{1,0:T(1,128)S(1)} %fusion.246) | copy-start | bytes 3076
  69.2 49.0 %copy-start.122 = (f32[256]{0:T(256)S(1)}, f32[256]{0:T(256)}, u32[]{:S(2)}) copy-start(f32[256]{0:T(256)} %param.37) | copy-start | bytes 3076
  69.2 49.0 %copy-start.125 = (f32[256]{0:T(256)S(1)}, f32[256]{0:T(256)}, u32[]{:S(2)}) copy-start(f32[256]{0:T(256)} %param.38) | copy-start | bytes 3076
  121.0 7.2 collective-permute-start.5
  122.3 6.4 collective-permute-start.4
  128.8 4.6 collective-permute-start.7
  130.1 3.9 collective-permute-start.6
  179.5 71.2 %all-gather.25.cloned.1.call-start = ((), (), s32[]{:S(2)}) async-start(), calls=%async_computation.25 | async-start | bytes 2359296 | tf_op jit(solution)/shard_map/all_gather | solution.py:58
  201.3 100.0 %all-gather.23.cloned.1.call-start = ((), (), s32[]{:S(2)}) async-start(), calls=%async_computation.24 | async-start | bytes 2359296 | tf_op jit(solution)/shard_map/all_gather | solution.py:59
  203.9 141.8 %reduce-scatter.9.cloned.1.call-start = ((), (), s32[]{:S(2)}) async-start(), calls=%async_computation.11 | async-start | bytes 1310720 | tf_op jit(solution)/shard_map/reduce_scatter | solution.py:47
  269.7 35.6 %copy-start.88 = (f32[4,512]{1,0:T(4,128)}, f32[4,512]{1,0:T(4,128)S(1)}, u32[]{:S(2)}) copy-start(f32[4,512]{1,0:T(4,128)S(1)} %get-tuple-element.214) | copy-start | bytes 24580
  322.1 51.9 %all-gather.13.cloned.1.call-start = ((), (), s32[]{:S(2)}) async-start(), calls=%async_computation.12 | async-start | bytes 1310720 | tf_op jit(solution)/shard_map/all_gather | solution.py:43
  356.0 48.0 %reduce-scatter.11.cloned.1.call-start = ((), (), s32[]{:S(2)}) async-start(), calls=%async_computation.13 | async-start | bytes 1310720 | tf_op jit(solution)/shard_map/reduce_scatter | solution.py:47
  379.0 54.1 %all-gather.15.cloned.1.call-start = ((), (), s32[]{:S(2)}) async-start(), calls=%async_computation.14 | async-start | bytes 1310720 | tf_op jit(solution)/shard_map/all_gather | solution.py:43
  414.9 36.5 %all-gather.17.cloned.1.call-start = ((), (), s32[]{:S(2)}) async-start(), calls=%async_computation.16 | async-start | bytes 1310720 | tf_op jit(solution)/shard_map/all_gather | solution.py:43
  415.7 69.0 %reduce-scatter.15.cloned.1.call-start = ((), (), s32[]{:S(2)}) async-start(), calls=%async_computation.17 | async-start | bytes 1310720 | tf_op jit(solution)/shard_map/reduce_scatter | solution.py:47
  459.6 53.1 %copy-start.54 = (bf16[1,512,256]{2,1,0:T(8,128)(2,1)S(1)}, bf16[1,512,256]{2,1,0:T(8,128)(2,1)}, u32[]{:S(2)}) copy-start(bf16[1,512,256]{2,1,0:T(8,128)(2,1)} %param.55) | copy-start | bytes 786436
  459.7 53.1 %reduce-scatter.13.cloned.1.call-start = ((), (), s32[]{:S(2)}) async-start(), calls=%async_computation.15 | async-start | bytes 1310720 | tf_op jit(solution)/shard_map/reduce_scatter | solution.py:47
  464.4 50.8 %copy-start.91 = (f32[4,512]{1,0:T(4,128)S(1)}, f32[4,512]{1,0:T(4,128)}, u32[]{:S(2)}) copy-start(f32[4,512]{1,0:T(4,128)} %copy-done.90) | copy-start | bytes 24580
  464.4 67.7 %copy-start.60 = (bf16[256,1024]{1,0:T(8,128)(2,1)S(1)}, bf16[256,1024]{1,0:T(8,128)(2,1)}, u32[]{:S(2)}) copy-start(bf16[256,1024]{1,0:T(8,128)(2,1)} %param.50) | copy-start | bytes 1572868
  464.4 67.7 %all-gather.19.cloned.1.call-start = ((), (), s32[]{:S(2)}) async-start(), calls=%async_computation.18 | async-start | bytes 1310720 | tf_op jit(solution)/shard_map/all_gather | solution.py:43
  515.1 46.7 %reduce-scatter.17.cloned.1.call-start = ((), (), s32[]{:S(2)}) async-start(), calls=%async_computation.19 | async-start | bytes 1310720 | tf_op jit(solution)/shard_map/reduce_scatter | solution.py:47
  536.7 34.7 %copy-start.101 = (f32[4,512]{1,0:T(4,128)S(1)}, f32[4,512]{1,0:T(4,128)}, u32[]{:S(2)}) copy-start(f32[4,512]{1,0:T(4,128)} %copy-done.100) | copy-start | bytes 24580
  536.7 52.5 %all-gather.21.cloned.1.call-start = ((), (), s32[]{:S(2)}) async-start(), calls=%async_computation.20 | async-start | bytes 1310720 | tf_op jit(solution)/shard_map/all_gather | solution.py:43
  571.1 148.2 %reduce-scatter.19.cloned.1.call-start = ((), (), s32[]{:S(2)}) async-start(), calls=%async_computation.21 | async-start | bytes 2359296 | tf_op jit(solution)/shard_map/reduce_scatter | solution.py:353
  651.0 139.8 %reduce-scatter.21.cloned.1.call-start = ((), (), s32[]{:S(2)}) async-start(), calls=%async_computation.22 | async-start | bytes 2359296 | tf_op jit(solution)/shard_map/reduce_scatter | solution.py:356
  667.4 150.8 %reduce-scatter.23.cloned.1.call-start = ((), (), s32[]{:S(2)}) async-start(), calls=%async_computation.23 | async-start | bytes 1310720 | tf_op jit(solution)/shard_map/reduce_scatter | solution.py:47
  722.1 72.3 %copy-start.21 = (bf16[4,512,128]{1,2,0:T(8,128)(2,1)S(1)}, bf16[4,512,128]{1,2,0:T(8,128)(2,1)}, u32[]{:S(2)}) copy-start(bf16[4,512,128]{1,2,0:T(8,128)(2,1)} %copy-done.20) | copy-start | bytes 1572868
  722.1 72.3 %copy-start.30 = (bf16[512,256]{0,1:T(8,128)(2,1)S(1)}, bf16[512,256]{0,1:T(8,128)(2,1)}, u32[]{:S(2)}) copy-start(bf16[512,256]{0,1:T(8,128)(2,1)} %copy-done.29) | copy-start | bytes 786436
  794.2 398.2 %all-reduce.18.cloned.1.call-start = ((), (), s32[]{:S(2)}) async-start(), calls=%async_computation.27 | async-start | bytes 23068672 | tf_op jit(solution)/shard_map/psum | solution.py:440
  828.3 9.4 all-to-all-start.1
  831.7 520.9 %all-reduce.16.cloned.1.call-start = ((), (), s32[]{:S(2)}) async-start(), calls=%async_computation.26 | async-start | bytes 12058624 | tf_op jit(solution)/shard_map/psum | solution.py:35
  845.5 11.6 collective-permute-start.9
  846.8 10.3 collective-permute-start.8
  857.2 5.6 collective-permute-start.11
  858.5 4.3 collective-permute-start.10
  938.0 6.9 collective-permute-start.13
  939.5 6.4 collective-permute-start.12
  945.9 29.3 %collective-permute-start.15 = (bf16[1,34,1,256]{3,2,1,0:T(2,128)(2,1)S(1)}, bf16[1,34,1,256]{3,2,1,0:T(2,128)(2,1)S(1)}, u32[]{:S(2)}, u32[]{:S(2)}) collective-permute-start(bf16[1,34,1,256]{3,2,1,0:T(2,128)(2,1)S(1)} %get-tuple-element.191), channel_id=1, source_target_pairs={{1,0},{2,1},{3,2},{5,4},{6,5},{7,6},{9,8},{10,9},{11,10},{13,12},{... | collective-permute-start | bytes 52232 | tf_op jit(solution)/shard_map/ppermute | solution.py:29
  947.2 28.0 %collective-permute-start.14 = (bf16[1,34,1,256]{3,2,1,0:T(2,128)(2,1)S(1)}, bf16[1,34,1,256]{3,2,1,0:T(2,128)(2,1)S(1)}, u32[]{:S(2)}, u32[]{:S(2)}) collective-permute-start(bf16[1,34,1,256]{3,2,1,0:T(2,128)(2,1)S(1)} %get-tuple-element.190), channel_id=1, source_target_pairs={{0,1},{1,2},{2,3},{4,5},{5,6},{6,7},{8,9},{9,10},{10,11},{12,13},{... | collective-permute-start | bytes 52232 | tf_op jit(solution)/shard_map/ppermute | solution.py:26
  982.9 43.9 %copy-start.27 = (bf16[1,32,64,256]{3,2,1,0:T(8,128)(2,1)S(1)}, bf16[1,32,64,256]{3,2,1,0:T(8,128)(2,1)}, u32[]{:S(2)}) copy-start(bf16[1,32,64,256]{3,2,1,0:T(8,128)(2,1)} %param.54) | copy-start | bytes 3145732
  (123 other events, 943.2 us)
Sparse Core Ops, SparseCore 0:
  179.6 18.9 all-gather.10
  201.4 49.2 all-gather.24
  253.4 47.7 all-gather.22
  322.3 23.4 reduce-scatter.8
  356.1 17.8 all-gather.12
  379.1 24.8 reduce-scatter.10
  415.1 17.9 all-gather.14
  434.6 16.8 all-gather.16
  459.7 24.8 reduce-scatter.14
  487.8 24.8 reduce-scatter.12
  515.2 16.8 all-gather.18
  536.8 24.8 reduce-scatter.16
  571.2 17.9 all-gather.20
  651.1 68.1 reduce-scatter.18
  723.7 67.1 reduce-scatter.20
  794.3 23.8 reduce-scatter.22
  825.4 366.9 all-reduce.17
  1199.6 153.0 all-reduce.15
where the time goes:
time: 1380 us; the launch traced here: 1370 us
  waiting for transfers between devices  686 us (50%)
  blocking collectives  241 us (17%)
  matrix products  192 us (14%)
  other arithmetic  115 us (8%)
  local copies, waits for them, and re-layouts  68.2 us (5%)
  starting transfers between devices  47.5 us (3%)
  between operations  18 us (1%)
    psum x4, blocking collectives, global_sum(): return lax.psum(values, ('tile', 'sub'))  171 us
    psum x1, waiting for transfers between devices, local(): lax.psum(grad_cross_key.astype(jnp.bfloat16), 'tile').astype(jnp.float32)  161 us
    psum x1, waiting for transfers between devices, global_sum(): return lax.psum(values, ('tile', 'sub'))  138 us
    reduce_scatter x6, waiting for transfers between devices, features_back(): lax.psum_scatter(values.astype(jnp.bfloat16), 'sub', scatter_dimension=2,...  120 us
    all_gather x6, waiting for transfers between devices, features_full(): return lax.all_gather(values, 'sub', axis=2, tiled=True)  97.1 us
    reduce_scatter x1, waiting for transfers between devices, local(): lax.psum_scatter(grad_v_all.astype(jnp.bfloat16), 'tile', scatter_dimensi...  68.8 us
    all_gather x1, waiting for transfers between devices, gather_keys(): lax.all_gather(key_loc, 'tile', axis=1, tiled=True)  45.2 us
    unnamed x286, local copies, waits for them, and re-layouts  38.6 us
  transfers between devices with their start and end apart: 35, of which 24 were waited for; matrix products, arithmetic and copies ran while one was open for 14% of the time, Pallas kernels for 0%

commit v1 on v0

v1 whole, which is shorter than its diff:
```python
import functools
import math

import jax
import jax.numpy as jnp
from jax import lax
from jax.experimental import pallas as pl
from jax.experimental.pallas import tpu as pltpu
from jax.sharding import PartitionSpec as P

G = 32
HD = 64
POOL = 4
EPSILON = 1e-05
MESH = pl.DeviceIdType.MESH
precise = lax.Precision.HIGHEST
f32 = jnp.float32
bf16 = jnp.bfloat16


def params(cid=None, vmem=56):
    if cid is None:
        return pltpu.CompilerParams(vmem_limit_bytes=vmem << 20)
    return pltpu.CompilerParams(
        collective_id=cid, has_side_effects=True, vmem_limit_bytes=vmem << 20
    )


def in_vmem():
    return pl.BlockSpec(memory_space=pltpu.VMEM)


def anywhere():
    return pl.BlockSpec(memory_space=pl.ANY)


def dma(*shape):
    return pltpu.SemaphoreType.DMA(shape)


def remote(src, dst, send_sem, recv_sem, where):
    return pltpu.make_async_remote_copy(
        src_ref=src,
        dst_ref=dst,
        send_sem=send_sem,
        recv_sem=recv_sem,
        device_id=where,
        device_id_type=MESH,
    )


def arrived(dst, send_sem, recv_sem, me):
    remote(dst, dst, send_sem, recv_sem, me).wait_recv()


def greet(peers):
    barrier = pltpu.get_barrier_semaphore()
    for peer in peers:
        pl.semaphore_signal(barrier, inc=1, device_id=peer, device_id_type=MESH)
    pl.semaphore_wait(barrier, len(peers))


def total_kernel(nt, ns, x_ref, o_ref, first, second, ss1, rs1, ss2, rs2):
    t, s = lax.axis_index("tile"), lax.axis_index("sub")
    near = [lax.rem(s + k, ns) for k in range(1, ns)]
    far = [lax.rem(t + k, nt) for k in range(1, nt)]
    first[s] = x_ref[...]
    greet([(t, p) for p in near] + [(p, s) for p in far])
    copies = []
    for k, p in enumerate(near):
        copies.append(remote(first.at[s], first.at[s], ss1.at[k], rs1.at[s], (t, p)))
        copies[-1].start()
    for k, p in enumerate(near):
        arrived(first.at[p], ss1.at[k], rs1.at[p], (t, s))
    total = first[0]
    for k in range(1, ns):
        total = total + first[k]
    second[t] = total
    for k, p in enumerate(far):
        copies.append(remote(second.at[t], second.at[t], ss2.at[k], rs2.at[t], (p, s)))
        copies[-1].start()
    for k, p in enumerate(far):
        arrived(second.at[p], ss2.at[k], rs2.at[p], (t, s))
    total = second[0]
    for k in range(1, nt):
        total = total + second[k]
    o_ref[...] = total
    for copy in copies:
        copy.wait_send()


def total_all(values, cid):
    nt, ns = lax.axis_size("tile"), lax.axis_size("sub")
    flat = values.reshape(-1, 128)
    out = pl.pallas_call(
        functools.partial(total_kernel, nt, ns),
        out_shape=jax.ShapeDtypeStruct(flat.shape, f32),
        in_specs=[in_vmem()],
        out_specs=in_vmem(),
        scratch_shapes=[
            pltpu.VMEM((ns,) + flat.shape, f32),
            pltpu.VMEM((nt,) + flat.shape, f32),
            dma(ns),
            dma(ns),
            dma(nt),
            dma(nt),
        ],
        compiler_params=params(cid),
        name="total_all",
    )(flat)
    return out.reshape(values.shape)


def chunks_of(rows):
    return max(1, min(4, rows // 16))


def gather_kernel(ns, count, x_ref, o_ref, s1, r1, s2, r2, own):
    far = ns // 2
    t, s = lax.axis_index("tile"), lax.axis_index("sub")
    r, c = s // 2, lax.rem(s, 2)
    me, twin = (t, s), (t, r * 2 + 1 - c)
    size = x_ref.shape[0] // count
    greet([twin] + [(t, lax.rem(r + k, far) * 2 + c) for k in range(1, far)])
    local = pltpu.make_async_copy(x_ref, o_ref.at[s], own)
    local.start()
    copies = []

    def send(src, dst, send_sem, recv_sem, where):
        copies.append(remote(src, dst, send_sem, recv_sem, where))
        copies[-1].start()

    for j in range(count):
        part = pl.ds(j * size, size)
        for k in range(1, far):
            peer = (t, lax.rem(r + k, far) * 2 + c)
            send(x_ref.at[part], o_ref.at[s, part], s1.at[k, j], r1.at[k, j], peer)
    for j in range(count):
        part = pl.ds(j * size, size)
        send(x_ref.at[part], o_ref.at[s, part], s2.at[0, j], r2.at[0, j], twin)
    for j in range(count):
        part = pl.ds(j * size, size)
        for k in range(1, far):
            block = o_ref.at[lax.rem(r + far - k, far) * 2 + c, part]
            arrived(block, s1.at[k, j], r1.at[k, j], me)
            send(block, block, s2.at[k, j], r2.at[k, j], twin)
    for j in range(count):
        part = pl.ds(j * size, size)
        for k in range(far):
            block = o_ref.at[lax.rem(r + far - k, far) * 2 + 1 - c, part]
            arrived(block, s2.at[k, j], r2.at[k, j], me)
    for copy in copies:
        copy.wait_send()
    local.wait()


def gather_sub(x, cid):
    ns = lax.axis_size("sub")
    far, count = ns // 2, chunks_of(x.shape[0])
    return pl.pallas_call(
        functools.partial(gather_kernel, ns, count),
        out_shape=jax.ShapeDtypeStruct((ns,) + x.shape, x.dtype),
        in_specs=[anywhere()],
        out_specs=anywhere(),
        scratch_shapes=[dma(far, count) for _ in range(4)] + [pltpu.SemaphoreType.DMA],
        compiler_params=params(cid),
        name="gather_sub",
    )(x)


def scatter_kernel(ns, count, x_ref, o_ref, got, stage, last, s1, r1, s2, r2):
    far = ns // 2
    t, s = lax.axis_index("tile"), lax.axis_index("sub")
    r, c = s // 2, lax.rem(s, 2)
    me, twin = (t, s), (t, r * 2 + 1 - c)
    size = x_ref.shape[1] // count
    greet([twin] + [(t, lax.rem(r + k, far) * 2 + c) for k in range(1, far)])
    copies = []

    def send(src, dst, send_sem, recv_sem, where):
        copies.append(remote(src, dst, send_sem, recv_sem, where))
        copies[-1].start()

    for k in list(range(1, far)) + [0]:
        for j in range(count):
            part = pl.ds(j * size, size)
            block = x_ref.at[lax.rem(r + k, far) * 2 + 1 - c, part]
            send(block, got.at[k, part], s1.at[k, j], r1.at[k, j], twin)
    for j in range(count):
        part = pl.ds(j * size, size)
        for k in range(1, far):
            p = lax.rem(r + k, far) * 2 + c
            arrived(got.at[k, part], s1.at[k, j], r1.at[k, j], me)
            stage[k, part] = (x_ref[p, part].astype(f32) + got[k, part].astype(f32)).astype(bf16)
            send(stage.at[k, part], last.at[k, part], s2.at[k, j], r2.at[k, j], (t, p))
    for j in range(count):
        part = pl.ds(j * size, size)
        arrived(got.at[0, part], s1.at[0, j], r1.at[0, j], me)
        total = x_ref[s, part].astype(f32) + got[0, part].astype(f32)
        for k in range(1, far):
            arrived(last.at[k, part], s2.at[k, j], r2.at[k, j], me)
            total = total + last[k, part].astype(f32)
        o_ref[part] = total
    for copy in copies:
        copy.wait_send()


def scatter_sub(x, cid):
    ns = lax.axis_size("sub")
    x = x.astype(bf16).reshape(ns, x.shape[0] // ns, x.shape[1])
    block = x.shape[1:]
    far, count = ns // 2, chunks_of(block[0])
    return pl.pallas_call(
        functools.partial(scatter_kernel, ns, count),
        out_shape=jax.ShapeDtypeStruct(block, f32),
        in_specs=[in_vmem()],
        out_specs=in_vmem(),
        scratch_shapes=[pltpu.VMEM((far,) + block, bf16) for _ in range(3)]
        + [dma(far, count) for _ in range(4)],
        compiler_params=params(cid),
        name="scatter_sub",
    )(x)


def deal(nt, u):
    t, s = lax.axis_index("tile"), lax.axis_index("sub")
    nb = nt // u
    a, b = t // nb, lax.rem(t, nb)
    a_peer = lambda k: (lax.rem(a + k, u) * nb + b, s)
    b_peer = lambda k: (a * nb + lax.rem(b + k, nb), s)
    peers = [a_peer(k) for k in range(1, u)] + [b_peer(k) for k in range(1, nb)]
    return t, s, nb, a, b, a_peer, b_peer, peers


def rows_of(ref, i, size):
    return ref.at[:, pl.ds(pl.multiple_of(i * size, size), size), :]


def lanes_of(ref, i, size):
    return ref.at[:, :, pl.ds(pl.multiple_of(i * size, size), size)]


def qkv_out_kernel(nt, u, q_ref, kv_ref, qo, kvo, qs, qr, ks, kr, fs, fr, own):
    t, s, nb, a, b, a_peer, b_peer, peers = deal(nt, u)
    me = (t, s)
    greet(peers)
    local = [
        pltpu.make_async_copy(rows_of(q_ref, a, HD), qo.at[a], own.at[0]),
        pltpu.make_async_copy(lanes_of(kv_ref, a, 2 * HD), kvo.at[t], own.at[1]),
    ]
    for copy in local:
        copy.start()
    copies = []

    def send(src, dst, send_sem, recv_sem, where):
        copies.append(remote(src, dst, send_sem, recv_sem, where))
        copies[-1].start()

    for k in range(1, u):
        block = lanes_of(kv_ref, lax.rem(a + k, u), 2 * HD)
        send(block, kvo.at[t], ks.at[k], kr.at[k], a_peer(k))
    for m in range(1, nb):
        send(lanes_of(kv_ref, a, 2 * HD), kvo.at[t], fs.at[0, m], fr.at[0, m], b_peer(m))
    for k in range(1, u):
        block = rows_of(q_ref, lax.rem(a + k, u), HD)
        send(block, qo.at[a], qs.at[k], qr.at[k], a_peer(k))
    for k in range(1, u):
        block = kvo.at[lax.rem(a + u - k, u) * nb + b]
        arrived(block, ks.at[k], kr.at[k], me)
        for m in range(1, nb):
            send(block, block, fs.at[k, m], fr.at[k, m], b_peer(m))
    for k in range(1, u):
        arrived(qo.at[lax.rem(a + u - k, u)], qs.at[k], qr.at[k], me)
    for k in range(u):
        for m in range(1, nb):
            block = kvo.at[lax.rem(a + u - k, u) * nb + lax.rem(b + nb - m, nb)]
            arrived(block, fs.at[k, m], fr.at[k, m], me)
    for copy in copies:
        copy.wait_send()
    for copy in local:
        copy.wait()


def qkv_out(q, kv, cid):
    nt = lax.axis_size("tile")
    batch, width, length = q.shape
    u = width // HD
    nb = nt // u
    return pl.pallas_call(
        functools.partial(qkv_out_kernel, nt, u),
        out_shape=(
            jax.ShapeDtypeStruct((u, batch, HD, length), bf16),
            jax.ShapeDtypeStruct((nt, batch, length, 2 * HD), bf16),
        ),
        in_specs=[anywhere()] * 2,
        out_specs=(anywhere(), anywhere()),
        scratch_shapes=[dma(u), dma(u), dma(u), dma(u), dma(u, nb), dma(u, nb), dma(2)],
        compiler_params=params(cid),
        name="qkv_out",
    )(q, kv)


def swap_kernel(nt, u, home, x_ref, o_ref, ss, rs, own):
    t, s, nb, a, b, a_peer, b_peer, peers = deal(nt, u)
    greet([a_peer(k) for k in range(1, u)])
    taken = lambda i: x_ref.at[i] if home else rows_of(x_ref, i, HD)
    placed = lambda i: rows_of(o_ref, i, HD) if home else o_ref.at[i]
    local = pltpu.make_async_copy(taken(a), placed(a), own)
    local.start()
    copies = []
    for k in range(1, u):
        copies.append(
            remote(taken(lax.rem(a + k, u)), placed(a), ss.at[k], rs.at[k], a_peer(k))
        )
        copies[-1].start()
    for k in range(1, u):
        arrived(placed(lax.rem(a + u - k, u)), ss.at[k], rs.at[k], (t, s))
    for copy in copies:
        copy.wait_send()
    local.wait()


def swap_heads(x, home, cid):
    nt = lax.axis_size("tile")
    if home:
        u, batch, _, length = x.shape
        shape = (batch, u * HD, length)
    else:
        batch, width, length = x.shape
        u = width // HD
        shape = (u, batch, HD, length)
    if u == 1:
        return x.reshape(shape)
    return pl.pallas_call(
        functools.partial(swap_kernel, nt, u, home),
        out_shape=jax.ShapeDtypeStruct(shape, bf16),
        in_specs=[anywhere()],
        out_specs=anywhere(),
        scratch_shapes=[dma(u), dma(u), pltpu.SemaphoreType.DMA],
        compiler_params=params(cid),
        name="swap_heads",
    )(x)


def dqkv_home_kernel(nt, u, dq_ref, dkv_ref, qo, kvo, got, stage, qs, qr, fs, fr, ks, kr, own):
    t, s, nb, a, b, a_peer, b_peer, peers = deal(nt, u)
    me = (t, s)
    greet(peers)
    copies = []

    def send(src, dst, send_sem, recv_sem, where):
        copies.append(remote(src, dst, send_sem, recv_sem, where))
        copies[-1].start()

    order = list(range(1, u)) + [0]
    for k in order:
        for m in range(1, nb):
            block = dkv_ref.at[lax.rem(a + k, u) * nb + lax.rem(b + m, nb)]
            send(block, got.at[m, k], fs.at[k, m], fr.at[k, m], b_peer(m))
    for k in range(1, u):
        send(dq_ref.at[lax.rem(a + k, u)], rows_of(qo, a, HD), qs.at[k], qr.at[k], a_peer(k))
    local = [pltpu.make_async_copy(dq_ref.at[a], rows_of(qo, a, HD), own.at[0])]
    local[0].start()
    for k in order:
        total = dkv_ref[lax.rem(a + k, u) * nb + b].astype(f32)
        for m in range(1, nb):
            arrived(got.at[m, k], fs.at[k, m], fr.at[k, m], me)
            total = total + got[m, k].astype(f32)
        stage[k] = total.astype(bf16)
        if k:
            send(stage.at[k], lanes_of(kvo, a, 2 * HD), ks.at[k], kr.at[k], a_peer(k))
        else:
            local.append(pltpu.make_async_copy(stage.at[0], lanes_of(kvo, a, 2 * HD), own.at[1]))
            local[1].start()
    for k in range(1, u):
        i = lax.rem(a + u - k, u)
        arrived(rows_of(qo, i, HD), qs.at[k], qr.at[k], me)
        arrived(lanes_of(kvo, i, 2 * HD), ks.at[k], kr.at[k], me)
    for copy in copies:
        copy.wait_send()
    for copy in local:
        copy.wait()


def dqkv_home(dq, dkv, cid):
    nt = lax.axis_size("tile")
    u, batch, _, length = dq.shape
    nb = nt // u
    block = (batch, length, 2 * HD)
    return pl.pallas_call(
        functools.partial(dqkv_home_kernel, nt, u),
        out_shape=(
            jax.ShapeDtypeStruct((batch, u * HD, length), bf16),
            jax.ShapeDtypeStruct((batch, length, u * 2 * HD), bf16),
        ),
        in_specs=[in_vmem()] * 2,
        out_specs=(anywhere(), anywhere()),
        scratch_shapes=[
            pltpu.VMEM((nb, u) + block, bf16),
            pltpu.VMEM((u,) + block, bf16),
            dma(u),
            dma(u),
            dma(u, nb),
            dma(u, nb),
            dma(u),
            dma(u),
            dma(2),
        ],
        compiler_params=params(cid),
        name="dqkv_home",
    )(dq, dkv)


def dot(left, right):
    return jnp.dot(left, right, preferred_element_type=f32)


def flash_kernel(q_ref, kv_ref, o_ref, of_ref, lse_ref, vt):
    count, length = kv_ref.shape[0], kv_ref.shape[2]

    @pl.when(pl.program_id(1) == 0)
    def _():
        for j in range(count):
            vt[j] = kv_ref[j, 0].T[HD:]

    q = q_ref[0, 0] * 0.125
    padded = jnp.concatenate([q, jnp.zeros_like(q)], axis=0)
    top = jnp.full((1, q.shape[1]), -jnp.inf, f32)
    total = jnp.zeros((1, q.shape[1]), f32)
    mixed = jnp.zeros(q.shape, f32)
    for j in range(count):
        scores = dot(kv_ref[j, 0], padded)
        new = jnp.maximum(top, jnp.max(scores, axis=0, keepdims=True))
        raised = jnp.exp(scores - new)
        scale = jnp.exp(top - new)
        total = total * scale + jnp.sum(raised, axis=0, keepdims=True)
        mixed = mixed * scale + dot(vt[j], raised.astype(bf16))
        top = new
    mixed = mixed / total
    o_ref[0, 0] = mixed.astype(bf16)
    of_ref[0, 0] = mixed
    lse_ref[0, 0] = top + jnp.log(total)


def flash(q, kv):
    u, batch, _, length = q.shape
    nt = kv.shape[0]
    rows = pl.BlockSpec((1, 1, HD, length), lambda b, i: (i, b, 0, 0))
    return pl.pallas_call(
        flash_kernel,
        grid=(batch, u),
        out_shape=(
            jax.ShapeDtypeStruct(q.shape, bf16),
            jax.ShapeDtypeStruct(q.shape, f32),
            jax.ShapeDtypeStruct((u, batch, 1, length), f32),
        ),
        in_specs=[rows, pl.BlockSpec((nt, 1, length, 2 * HD), lambda b, i: (0, b, 0, 0))],
        out_specs=(rows, rows, pl.BlockSpec((1, 1, 1, length), lambda b, i: (i, b, 0, 0))),
        scratch_shapes=[pltpu.VMEM((nt, HD, length), bf16)],
        compiler_params=params(),
        name="flash",
    )(q, kv)


def flash_back_kernel(q_ref, d_ref, of_ref, lse_ref, kv_ref, dq_ref, dkv_ref, qd, rows, delta, acc):
    u, length = q_ref.shape[0], q_ref.shape[3]
    j = pl.program_id(1)

    @pl.when(j == 0)
    def _():
        for i in range(u):
            q, d = q_ref[i, 0], d_ref[i, 0]
            zero = jnp.zeros_like(q)
            qd[i, 0] = jnp.concatenate([q * 0.125, zero], axis=0)
            qd[i, 1] = jnp.concatenate([zero, d], axis=0)
            rows[i, 0] = qd[i, 0].T
            rows[i, 1] = qd[i, 1].T
            delta[i] = jnp.sum(d.astype(f32) * of_ref[i, 0], axis=0, keepdims=True)
            acc[i] = jnp.zeros_like(acc[i])

    kv = kv_ref[0, 0]
    kt = kv.T[:HD]
    total = jnp.zeros(kv.shape, f32)
    for i in range(u):
        probs = jnp.exp(dot(kv, qd[i, 0]) - lse_ref[i, 0])
        slope = dot(kv, qd[i, 1])
        grads = (probs * (slope - delta[i])).astype(bf16)
        total = total + dot(probs.astype(bf16), rows[i, 1]) + dot(grads, rows[i, 0])
        acc[i] += dot(kt, grads)
    dkv_ref[0, 0] = total.astype(bf16)

    @pl.when(j == pl.num_programs(1) - 1)
    def _():
        for i in range(u):
            dq_ref[i, 0] = (acc[i] * 0.125).astype(bf16)


def flash_back(q, d, of, lse, kv):
    u, batch, _, length = q.shape
    nt = kv.shape[0]
    whole = pl.BlockSpec((u, 1, HD, length), lambda b, j: (0, b, 0, 0))
    part = pl.BlockSpec((1, 1, length, 2 * HD), lambda b, j: (j, b, 0, 0))
    return pl.pallas_call(
        flash_back_kernel,
        grid=(batch, nt),
        out_shape=(jax.ShapeDtypeStruct(q.shape, bf16), jax.ShapeDtypeStruct(kv.shape, bf16)),
        in_specs=[
            whole,
            whole,
            whole,
            pl.BlockSpec((u, 1, 1, length), lambda b, j: (0, b, 0, 0)),
            part,
        ],
        out_specs=(whole, part),
        scratch_shapes=[
            pltpu.VMEM((u, 2, 2 * HD, length), bf16),
            pltpu.VMEM((u, 2, length, 2 * HD), bf16),
            pltpu.VMEM((u, 1, length), f32),
            pltpu.VMEM((u, HD, length), f32),
        ],
        compiler_params=params(),
        name="flash_back",
    )(q, d, of, lse, kv)


def bordered(block, width):
    for axis, dim in (("tile", 1), ("sub", 2)):
        count = lax.axis_size(axis)
        forward = [(i, i + 1) for i in range(count - 1)]
        backward = [(target, source) for source, target in forward]
        low = lax.ppermute(
            lax.slice_in_dim(block, block.shape[dim] - width, None, axis=dim), axis, forward
        )
        high = lax.ppermute(lax.slice_in_dim(block, 0, width, axis=dim), axis, backward)
        block = jnp.concatenate([low, block, high], axis=dim)
    return block


def inside(shape, width):
    rows, cols = shape[1] - 2 * width, shape[2] - 2 * width
    y = lax.axis_index("tile") * rows - width + jnp.arange(shape[1])
    x = lax.axis_index("sub") * cols - width + jnp.arange(shape[2])
    good_y = (y >= 0) & (y < rows * lax.axis_size("tile"))
    good_x = (x >= 0) & (x < cols * lax.axis_size("sub"))
    return (good_y[:, None] & good_x[None, :])[None, :, :, None]


def trim(values, width):
    return values[:, width:-width, width:-width]


def time_embed(time_steps, channels):
    half_width = channels // 2
    frequency = jnp.exp(
        -math.log(10000.0) * jnp.arange(half_width).astype(f32) / half_width
    )
    angles = time_steps.astype(f32)[:, None] * frequency[None, :]
    return jnp.concatenate([jnp.sin(angles), jnp.cos(angles)], axis=1)


def conv_valid(padded, kernel):
    return lax.conv_general_dilated(
        padded,
        kernel,
        (1, 1),
        "VALID",
        dimension_numbers=("NHWC", "HWIO", "NHWC"),
        preferred_element_type=f32,
    )


def conv_transposed(padded, kernel):
    return conv_valid(padded, jnp.transpose(kernel[::-1, ::-1], (0, 1, 3, 2)))


def conv_kernel_grad(padded_in, grad_out):
    rows, cols = grad_out.shape[1], grad_out.shape[2]
    taps = []
    for y in range(3):
        for x in range(3):
            window = padded_in[:, y : y + rows, x : x + cols, :]
            taps.append(
                jnp.einsum("bhwc,bhwd->cd", window, grad_out, preferred_element_type=f32)
            )
    return jnp.stack(taps).reshape(3, 3, padded_in.shape[3], grad_out.shape[3])


def by_group(values):
    channels = values.shape[-1]
    grouped = values.reshape(values.shape[:-1] + (G, channels // G))
    return jnp.repeat(jnp.sum(grouped, axis=-1), channels // G, axis=-1)


def pixel_sums(first, second):
    return jnp.stack([jnp.sum(first, axis=(1, 2)), jnp.sum(second, axis=(1, 2))], axis=1)


def group_stats(sums, group_size):
    center = by_group(sums[:, 0]) / group_size
    inv_std = lax.rsqrt(by_group(sums[:, 1]) / group_size - center * center + EPSILON)
    return center[:, None, None, :], inv_std[:, None, None, :]


def layer_stats(values, gain):
    width = values.shape[1]
    center = jnp.sum(values, axis=1, keepdims=True) / width
    moved = values - center
    inv_std = lax.rsqrt(jnp.sum(moved * moved, axis=1, keepdims=True) / width + EPSILON)
    normed = moved * inv_std
    return (normed * gain).astype(bf16), normed, inv_std


def layer_back(grad_out, normed, inv_std, gain):
    width = normed.shape[1]
    scaled = grad_out * gain
    mean_grad = jnp.sum(scaled, axis=1, keepdims=True) / width
    mean_cross = jnp.sum(scaled * normed, axis=1, keepdims=True) / width
    grad_in = inv_std * (scaled - mean_grad - normed * mean_cross)
    return grad_in, jnp.sum(grad_out * normed, axis=0)


def silu_grad(values):
    sigma = jax.nn.sigmoid(values)
    return sigma * (1.0 + values * (1.0 - sigma))


def gelu_tanh(values):
    return jax.nn.gelu(values, approximate=True)


def weight_grad(inputs, grads):
    return lax.dot_general(inputs, grads, (((0,), (0,)), ((), ())), preferred_element_type=f32)


def dot_t(left, right):
    return lax.dot_general(left, right, (((1,), (1,)), ((), ())), preferred_element_type=f32)


def cross_scores(queries, keys, text_mask):
    scores = jnp.einsum("sbqhd,bkhd->sbhqk", queries, keys, preferred_element_type=f32)
    return jnp.where(text_mask[None, :, None, None, :], scores * HD ** (-0.5), -1000000000.0)


def local(
    outer_image,
    inner_image,
    text_states,
    time_steps,
    text_lengths,
    first_gain,
    first_bias,
    conv_first,
    time_weight,
    second_gain,
    second_bias,
    conv_second,
    lift_weight,
    attn_gain,
    query_weight,
    key_weight,
    value_weight,
    out_weight,
    cross_gain,
    cross_query,
    cross_key,
    cross_value,
    cross_out,
    mlp_gain,
    up_weight,
    down_weight,
    outer_cotan,
    inner_cotan,
):
    nt, ns = lax.axis_size("tile"), lax.axis_size("sub")
    s = lax.axis_index("sub")
    batch, rows, cols, channels = outer_image.shape
    lr, lc = rows // POOL, cols // POOL
    width = inner_image.shape[2] * ns
    features = inner_image.shape[2]
    heads = features // HD
    own = batch * lr * lc
    length = ns * lr * lc
    pixels = rows * cols * nt * ns
    group_size = pixels * (channels // G)

    image_ext = bordered(outer_image, 2)
    cotan_ext = bordered(outer_cotan, 2)

    def whole_tokens(values):
        full = lax.all_gather(values, "sub", axis=2, tiled=True)
        full = full.reshape(batch, lr, ns, lc, width)
        mine = lax.dynamic_index_in_dim(full, s, 2, keepdims=False).reshape(own, width)
        return full, mine

    _, inner_own = whole_tokens(inner_image)
    cotan_full, cotan_own = whole_tokens(inner_cotan)
    cotan_full = jnp.transpose(cotan_full, (2, 0, 1, 3, 4)).reshape(ns * own, width)
    gains = lax.all_gather(
        jnp.stack([attn_gain, cross_gain, mlp_gain]), "sub", axis=1, tiled=True
    )

    time_act = jax.nn.silu(time_embed(time_steps, channels))
    time_shift = jnp.dot(time_act, time_weight.astype(f32), precision=precise)
    outer_f = outer_image.astype(f32)
    center1, std1 = group_stats(
        total_all(pixel_sums(outer_f, outer_f * outer_f), 0), group_size
    )
    hat1 = lambda v: (v.astype(f32) - center1) * std1
    norm1 = lambda v: hat1(v) * first_gain + first_bias
    act1 = jnp.where(
        inside(image_ext.shape, 2), jax.nn.silu(norm1(image_ext)), 0.0
    ).astype(bf16)
    hidden = conv_valid(act1, conv_first) + time_shift[:, None, None, :]
    middle = trim(hidden, 1)
    sums2 = total_all(pixel_sums(middle, middle * middle), 1)
    center2, std2 = group_stats(sums2, group_size)
    hat2 = lambda v: (v - center2) * std2
    norm2 = lambda v: hat2(v) * second_gain + second_bias
    act2 = jnp.where(inside(hidden.shape, 1), jax.nn.silu(norm2(hidden)), 0.0).astype(bf16)
    outer_sum = outer_f + conv_valid(act2, conv_second)
    pooled = jnp.mean(
        outer_sum.reshape(batch, lr, POOL, lc, POOL, channels), axis=(2, 4)
    ).astype(bf16)
    pooled = pooled.reshape(own, channels)

    stream_in = inner_own.astype(f32) + dot(pooled, lift_weight).astype(bf16).astype(f32)
    attn_low, attn_hat, attn_std = layer_stats(stream_in, gains[0])
    attn_in = gather_sub(attn_low, 2).reshape(ns * own, width)

    def per_sample(values, tokens_last):
        if tokens_last:
            values = values.reshape(-1, ns, batch, lr * lc)
            return jnp.transpose(values, (2, 0, 1, 3)).reshape(batch, -1, length)
        values = values.reshape(ns, batch, lr * lc, -1)
        return jnp.transpose(values, (1, 0, 2, 3)).reshape(batch, length, -1)

    def all_samples(values, tokens_last):
        if tokens_last:
            values = values.reshape(batch, -1, ns, lr * lc)
            return jnp.transpose(values, (1, 2, 0, 3)).reshape(-1, ns * own)
        values = values.reshape(batch, ns, lr * lc, -1)
        return jnp.transpose(values, (1, 0, 2, 3)).reshape(ns * own, -1)

    pair = lambda k, v: jnp.concatenate(
        [k.reshape(-1, heads, HD), v.reshape(-1, heads, HD)], axis=2
    ).reshape(-1, heads * 2 * HD)
    kv_weight = pair(key_weight, value_weight)
    query_t = lax.dot_general(
        query_weight, attn_in, (((0,), (1,)), ((), ())), preferred_element_type=f32
    ).astype(bf16)
    kv = dot(attn_in, kv_weight).astype(bf16)
    head_q, head_kv = qkv_out(per_sample(query_t, True), per_sample(kv, False), 3)
    head_mixed, head_mixed_f, head_lse = flash(head_q, head_kv)
    mixed_t = all_samples(swap_heads(head_mixed, True, 4), True)
    after_attn = stream_in + scatter_sub(weight_grad(mixed_t, out_weight), 5)

    cross_low, cross_hat, cross_std = layer_stats(after_attn, gains[1])
    cross_in = gather_sub(cross_low, 6).reshape(ns * own, width)
    text_split = lambda w: jnp.einsum(
        "bsw,we->bse", text_states, w, preferred_element_type=f32
    ).astype(bf16).reshape(batch, -1, heads, HD)
    cross_k, cross_v = text_split(cross_key), text_split(cross_value)
    text_mask = jnp.arange(text_states.shape[1])[None, :] < text_lengths[:, None]
    split = lambda v: v.reshape(ns, batch, lr * lc, heads, HD)
    cross_q = split(dot(cross_in, cross_query).astype(bf16))
    scores = cross_scores(cross_q, cross_k, text_mask)
    cross_probs = jax.nn.softmax(scores, axis=-1)
    cross_probs_low = cross_probs.astype(bf16)
    cross_mixed = (
        jnp.einsum("sbhqk,bkhd->sbqhd", cross_probs_low, cross_v, preferred_element_type=f32)
        .astype(bf16)
        .reshape(ns * own, features)
    )
    after_cross = after_attn + scatter_sub(dot(cross_mixed, cross_out), 7)

    mlp_low, mlp_hat, mlp_std = layer_stats(after_cross, gains[2])
    mlp_in = gather_sub(mlp_low, 8).reshape(ns * own, width)
    lifted_up = dot(mlp_in, up_weight)
    activated_f, gelu_pull = jax.vjp(gelu_tanh, lifted_up)
    activated = activated_f.astype(bf16)

    grad_act = dot_t(cotan_full, down_weight)
    grad_lift_up = gelu_pull(grad_act)[0].astype(bf16)
    grad_mid, grad_mlp_gain = layer_back(
        scatter_sub(dot_t(grad_lift_up, up_weight), 9), mlp_hat, mlp_std, gains[2]
    )
    grad_after_cross = cotan_own.astype(f32) + grad_mid
    grad_cross_full = gather_sub(grad_after_cross.astype(bf16), 10).reshape(ns * own, width)
    grad_cross_mixed = split(dot_t(grad_cross_full, cross_out).astype(bf16))
    grad_cv = jnp.einsum(
        "sbhqk,sbqhd->bkhd", cross_probs_low, grad_cross_mixed, preferred_element_type=f32
    )
    grad_probs = jnp.einsum(
        "sbqhd,bkhd->sbhqk", grad_cross_mixed, cross_v, preferred_element_type=f32
    )
    grad_scores = (
        cross_probs
        * (grad_probs - jnp.sum(cross_probs * grad_probs, axis=-1, keepdims=True))
    ).astype(bf16)
    grad_cq = (
        jnp.einsum("sbhqk,bkhd->sbqhd", grad_scores, cross_k, preferred_element_type=f32)
        * HD ** (-0.5)
    ).astype(bf16).reshape(ns * own, features)
    grad_ck = jnp.einsum(
        "sbhqk,sbqhd->bkhd", grad_scores, cross_q, preferred_element_type=f32
    ) * HD ** (-0.5)
    grad_mid, grad_cross_gain = layer_back(
        scatter_sub(dot_t(grad_cq, cross_query), 11), cross_hat, cross_std, gains[1]
    )
    grad_after_attn = grad_after_cross + grad_mid
    grad_attn_full = gather_sub(grad_after_attn.astype(bf16), 12).reshape(ns * own, width)
    grad_mixed_t = dot_t(out_weight, grad_attn_full).astype(bf16)
    head_d = swap_heads(per_sample(grad_mixed_t, True), False, 13)
    head_dq, head_dkv = flash_back(head_q, head_d, head_mixed_f, head_lse, head_kv)
    grad_q_t, grad_kv = dqkv_home(head_dq, head_dkv, 14)
    grad_q_t, grad_kv = all_samples(grad_q_t, True), all_samples(grad_kv, False)
    grad_attn_in = weight_grad(grad_q_t, query_weight.T) + dot_t(grad_kv, kv_weight)
    grad_mid, grad_attn_gain = layer_back(
        scatter_sub(grad_attn_in, 15), attn_hat, attn_std, gains[0]
    )
    inner_grad = grad_after_attn + grad_mid
    grad_lifted = inner_grad.astype(bf16)

    grad_lift = weight_grad(pooled, grad_lifted)
    grad_pooled = dot_t(grad_lifted, lift_weight) / (POOL * POOL)
    pooled_ext = bordered(grad_pooled.reshape(batch, lr, lc, channels), 1)
    spread = jnp.repeat(jnp.repeat(pooled_ext, POOL, axis=1), POOL, axis=2)
    grad_outer = cotan_ext.astype(f32) + trim(spread, POOL - 2)
    grad_conv2 = jnp.where(inside(grad_outer.shape, 2), grad_outer, 0.0).astype(bf16)
    slope2 = conv_transposed(grad_conv2, conv_second) * silu_grad(norm2(hidden))
    back2 = total_all(pixel_sums(trim(slope2, 1), trim(slope2 * hat2(hidden), 1)), 16)

    def group_means(back, gain):
        spread_out = lambda v: (by_group(v * gain) / group_size)[:, None, None, :]
        return spread_out(back[:, 0]), spread_out(back[:, 1])

    mean_grad2, mean_cross2 = group_means(back2, second_gain)
    grad_hidden = std2 * (slope2 * second_gain - mean_grad2 - hat2(hidden) * mean_cross2)
    grad_conv1 = jnp.where(inside(grad_hidden.shape, 1), grad_hidden, 0.0).astype(bf16)
    flat = lambda v: v[:, 0, 0, :]
    hat2_sum = flat(std2) * (sums2[:, 0] - pixels * flat(center2))
    hidden_sum = flat(std2) * (
        second_gain * back2[:, 0] - pixels * flat(mean_grad2) - flat(mean_cross2) * hat2_sum
    )
    grad_time = jnp.dot(time_act.T, hidden_sum, precision=precise)
    slope1 = conv_transposed(grad_conv1, conv_first) * silu_grad(norm1(outer_image))
    back1 = total_all(pixel_sums(slope1, slope1 * hat1(outer_image)), 17)
    mean_grad1, mean_cross1 = group_means(back1, first_gain)
    outer_grad = trim(grad_outer, 2) + std1 * (
        slope1 * first_gain - mean_grad1 - hat1(outer_image) * mean_cross1
    )

    down = dot(activated, down_weight).astype(bf16)
    inner_sum = after_cross + lax.psum_scatter(
        down, "sub", scatter_dimension=0, tiled=True
    ).astype(f32)

    def by_feature(values):
        full = lax.all_gather(values.astype(bf16), "sub", axis=0)
        mine = lax.dynamic_slice_in_dim(full, s * features, features, axis=2)
        mine = mine.reshape(ns, batch, lr, lc, features)
        return jnp.transpose(mine, (1, 2, 0, 3, 4)).reshape(batch, length, features)

    inner_out = by_feature(inner_sum)
    inner_grad = by_feature(inner_grad).astype(f32)

    over_tile = lambda *values: tuple(
        v.astype(f32) for v in lax.psum(tuple(v.astype(bf16) for v in values), "tile")
    )
    grad_down = weight_grad(activated, cotan_full)
    grad_up = weight_grad(mlp_in, grad_lift_up)
    grad_down, grad_up = over_tile(grad_down, grad_up)
    grad_cq_w = weight_grad(cross_in, grad_cq)
    grad_co_w = weight_grad(cross_mixed, grad_cross_full)
    grad_ck, grad_cv = lax.psum((grad_ck, grad_cv), "tile")

    def text_grad(grads):
        grads = grads.reshape(batch, -1, features)
        high = grads.astype(bf16)
        rest = (grads - high.astype(f32)).astype(bf16)
        both = jnp.concatenate([high, rest], axis=1)
        text = jnp.concatenate([text_states, text_states], axis=1)
        return jnp.einsum("bsw,bse->we", text, both, preferred_element_type=f32)

    grad_ck_w, grad_cv_w = text_grad(grad_ck), text_grad(grad_cv)
    grad_o_w = lax.dot_general(
        mixed_t, grad_attn_full, (((1,), (0,)), ((), ())), preferred_element_type=f32
    )
    grad_q_w = lax.dot_general(
        attn_in, grad_q_t, (((0,), (1,)), ((), ())), preferred_element_type=f32
    )
    grad_kv_w = weight_grad(attn_in, grad_kv)
    grad_cq_w, grad_co_w, grad_o_w, grad_q_w, grad_kv_w = over_tile(
        grad_cq_w, grad_co_w, grad_o_w, grad_q_w, grad_kv_w
    )
    grad_kv_w = grad_kv_w.reshape(width, heads, 2, HD)
    grad_k_w = grad_kv_w[:, :, 0].reshape(width, features)
    grad_v_w = grad_kv_w[:, :, 1].reshape(width, features)

    grad_conv_second = conv_kernel_grad(act2, trim(grad_conv2, 2))
    grad_conv_first = conv_kernel_grad(trim(act1, 1), trim(grad_conv1, 1))
    grad_gains = jnp.stack([grad_attn_gain, grad_cross_gain, grad_mlp_gain])
    everywhere = lax.psum(
        tuple(
            v.astype(bf16) for v in (grad_conv_first, grad_conv_second, grad_lift, grad_gains)
        ),
        ("tile", "sub"),
    )
    grad_conv_first, grad_conv_second, grad_lift, grad_gains = (
        v.astype(f32) for v in everywhere
    )
    grad_gains = lax.dynamic_slice_in_dim(grad_gains, s * features, features, axis=1)
    back1, back2 = jnp.sum(back1, axis=0), jnp.sum(back2, axis=0)
    return (
        outer_sum.astype(bf16),
        inner_out,
        outer_grad,
        inner_grad,
        back1[1],
        back1[0],
        grad_conv_first,
        grad_time,
        back2[1],
        back2[0],
        grad_conv_second,
        grad_lift,
        grad_gains[0],
        grad_q_w,
        grad_k_w,
        grad_v_w,
        grad_o_w,
        grad_gains[1],
        grad_cq_w,
        grad_ck_w,
        grad_cv_w,
        grad_co_w,
        grad_gains[2],
        grad_up,
        grad_down,
    )


def solution(mesh):
    pixels = P(None, "tile", "sub", None)
    tokens = P(None, "tile", "sub")
    columns, rows, vector = P(None, "sub"), P("sub", None), P("sub")
    return jax.shard_map(
        local,
        mesh=mesh,
        in_specs=(pixels, tokens)
        + (P(),) * 11
        + (vector, columns, columns, columns, rows)
        + (vector, columns, columns, columns, rows)
        + (vector, columns, rows)
        + (pixels, tokens),
        out_specs=(pixels, tokens, pixels, tokens)
        + (P(),) * 8
        + (vector, columns, columns, columns, rows)
        + (vector, columns, columns, columns, rows)
        + (vector, columns, rows),
        check_vma=False,
    )
```

time: 1380 us -> 1010 us (0.73)
  waiting for transfers between devices: 686 us -> 317 us
  Pallas kernels: 0 us -> 267 us
  blocking collectives: 241 us -> 44 us
  matrix products: 192 us -> 134 us
  local copies, waits for them, and re-layouts: 68.2 us -> 97.8 us
  other arithmetic: 115 us -> 90.6 us
    pallas_call x0 -> x20, Pallas kernels: none -> 267 us  [the longest x5 59.1 us: scatter_sub(): pl.pallas_call(functools.partial(scatter_kernel, ns, count), out_shape=ja...]
    reduce_scatter x8 -> x1, waiting for transfers between devices: 219 us -> 0.01 us  [local(): lax.psum_scatter(down, 'sub', scatter_dimension=0, tiled=True).astype(f32)]
    psum x11 -> x1, blocking collectives: 230 us -> 38.8 us  [local(): lax.psum(tuple((v.astype(bf16) for v in (grad_conv_first, grad_conv_secon...]
    all_gather x8 -> x4, waiting for transfers between devices: 160 us -> 29.6 us  [the longest x2 29.5 us: by_feature(): full = lax.all_gather(values.astype(bf16), 'sub', axis=0)]
    dot_general x62 -> x53, matrix products: 175 us -> 69 us  [the longest x8 13.7 us: weight_grad(): lax.dot_general(inputs, grads, (((0,), (0,)), ((), ())), preferred_elemen...]
    conv_general_dilated x4, matrix products: 16.4 us -> 64.8 us  [conv_valid(): lax.conv_general_dilated(padded, kernel, (1, 1), 'VALID', dimension_numbe...]
    slice x2 -> x14, local copies, waits for them, and re-layouts: 0.01 us -> 34.7 us  [the longest x1 26.7 us: conv_kernel_grad(): window = padded_in[:, y:y + rows, x:x + cols, :]]
    psum x2 -> x3, waiting for transfers between devices: 299 us -> 285 us  [the longest x1 251 us: local(): lax.psum(tuple((v.astype(bf16) for v in values)), 'tile')]
  transfers between devices with their start and end apart: 35 -> 20, of which waited for: 24 -> 5; matrix products, arithmetic and copies ran while one was open for 14% -> 29% of each run, Pallas kernels for 0% -> 27%
where the time goes in v1:
time: 1010 us; the launch traced here: 1000 us
  waiting for transfers between devices  317 us (31%)
  Pallas kernels  267 us (26%)
  matrix products  134 us (13%)
  local copies, waits for them, and re-layouts  97.8 us (10%)
  other arithmetic  90.6 us (9%)
  blocking collectives  44 us (4%)
  starting transfers between devices  33.8 us (3%)
  between operations  17.8 us (2%)
    psum x1, waiting for transfers between devices, local(): lax.psum(tuple((v.astype(bf16) for v in values)), 'tile')  251 us
    conv_general_dilated x4, matrix products, conv_valid(): lax.conv_general_dilated(padded, kernel, (1, 1), 'VALID', dimension_numbe...  64.8 us
    pallas_call x5, Pallas kernels, scatter_sub(): pl.pallas_call(functools.partial(scatter_kernel, ns, count), out_shape=ja...  59.1 us
    pallas_call x5, Pallas kernels, gather_sub(): pl.pallas_call(functools.partial(gather_kernel, ns, count), out_shape=jax...  52.2 us
    pallas_call x4, Pallas kernels, total_all(): pl.pallas_call(functools.partial(total_kernel, nt, ns), out_shape=jax.Sha...  50.7 us
    psum x1, blocking collectives, local(): lax.psum(tuple((v.astype(bf16) for v in (grad_conv_first, grad_conv_secon...  38.8 us
    psum x1, waiting for transfers between devices, local(): lax.psum(tuple((v.astype(bf16) for v in (grad_conv_first, grad_conv_secon...  34.5 us
    all_gather x2, waiting for transfers between devices, by_feature(): full = lax.all_gather(values.astype(bf16), 'sub', axis=0)  29.5 us
  transfers between devices with their start and end apart: 20, of which 5 were waited for; matrix products, arithmetic and copies ran while one was open for 29% of the time, Pallas kernels for 27%

profile of v1, /device:TPU:0, one launch (start us, length us, event | category | flops | bytes accessed | tf_op | source)
XLA Modules:
  0.0 1002.0 jit_solution(15996607061132635932)
XLA Ops:
  9.6 5.5 collective-permute-start
  17.9 4.5 collective-permute-start.4
  27.0 13.7 %total_all.4 = f32[4,128]{1,0:T(4,128)} custom-call(f32[4,128]{1,0:T(4,128)} %reshape.1051.x_ref), custom_call_target="tpu_custom_call" | custom-call | tf_op jit(solution)/shard_map/total_all/pallas_call | solution.py:95
  45.6 5.2 all_gather.22
  71.8 3.0 collective-permute-start.2
  77.0 5.1 collective-permute-start.6
  83.9 14.2 %convolution_add_fusion = f32[1,34,66,256]{3,0,2,1:T(1,128)S(1)} fusion(bf16[3,3,256,256]{3,2,1,0:T(8,128)(2,1)S(1)} %copy-done.123, bf16[1,36,68,256]{3,2,1,0:T(8,128)(2,1)S(1)} %select_convert_fusion.1, f32[256]{0:T(256)S(1)} %bitcast.627), kind=kOutput, calls=%fused_computation.12 | convolution fusion | flops 2647704576 | bytes 4731904 | tf_op jit(solution)/shard_map/conv_general_dilated | solution.py:562
  99.5 2.8 slice_reduce_fusion.1
  102.9 10.7 %total_all.5 = f32[4,128]{1,0:T(4,128)} custom-call(f32[4,128]{1,0:T(4,128)} %reshape.1053.x_ref), custom_call_target="tpu_custom_call" | custom-call | tf_op jit(solution)/shard_map/total_all/pallas_call | solution.py:95
  116.2 9.4 fusion.2
  125.7 14.2 %fusion.182 = f32[1,32,64,256]{3,0,2,1:T(1,128)S(1)} fusion(bf16[1,34,66,256]{3,0,2,1:T(2,128)(2,1)S(1)} %get-tuple-element.193, bf16[3,3,256,256]{3,2,1,0:T(8,128)(2,1)S(1)} %copy-done.121), kind=kOutput, calls=%fused_computation.351 | convolution fusion | flops 2415919104 | bytes 4425728 | tf_op jit(solution)/shard_map/conv_general_dilated | solution.py:562
  142.0 2.8 reshape.1056
  151.9 10.3 %gather_sub.5 = bf16[4,128,1024]{2,1,0:T(8,128)(2,1)} custom-call(bf16[128,1024]{1,0:T(8,128)(2,1)} %multiply_convert_fusion.4.x_ref), custom_call_target="tpu_custom_call" | custom-call | tf_op jit(solution)/shard_map/gather_sub/pallas_call | solution.py:160
  167.4 20.7 %qkv_out.1 = (bf16[4,1,64,512]{3,2,1,0:T(8,128)(2,1)}, bf16[8,1,512,128]{3,2,1,0:T(8,128)(2,1)}) custom-call(bf16[1,256,512]{2,1,0:T(8,128)(2,1)} %fusion.41.q_ref, bf16[1,512,512]{2,1,0:T(8,128)(2,1)} %fusion.35.kv_ref), custom_call_target="tpu_custom_call" | custom-call | tf_op jit(solution)/shard_map/qkv_out/pallas_call | solution.py:289
  188.1 18.1 %flash.1 = (bf16[4,1,64,512]{3,2,1,0:T(8,128)(2,1)}, f32[4,1,64,512]{3,2,1,0:T(8,128)}, f32[4,1,1,512]{3,2,1,0:T(1,128)}) custom-call(bf16[4,1,64,512]{3,2,1,0:T(8,128)(2,1)} %get-tuple-element.34.q_ref, bf16[8,1,512,128]{3,2,1,0:T(8,128)(2,1)} %get-tuple-element.35.kv_ref), custom_call_target="tpu_custom_call" | custom-call | tf_op jit(solution)/shard_map/flash/pallas_call | solution.py:449
  206.2 11.1 %swap_heads.2 = bf16[1,256,512]{2,1,0:T(8,128)(2,1)} custom-call(bf16[4,1,64,512]{3,2,1,0:T(8,128)(2,1)} %get-tuple-element.36.x_ref), custom_call_target="tpu_custom_call" | custom-call | tf_op jit(solution)/shard_map/swap_heads/pallas_call | solution.py:334
  219.7 11.2 %scatter_sub.5 = f32[128,1024]{1,0:T(8,128)} custom-call(bf16[4,128,1024]{2,1,0:T(8,128)(2,1)} %bitcast.556), custom_call_target="tpu_custom_call" | custom-call | tf_op jit(solution)/shard_map/scatter_sub/pallas_call | solution.py:213
  233.3 10.7 %gather_sub.6 = bf16[4,128,1024]{2,1,0:T(8,128)(2,1)} custom-call(bf16[128,1024]{1,0:T(8,128)(2,1)} %multiply_convert_fusion.3.x_ref), custom_call_target="tpu_custom_call" | custom-call | tf_op jit(solution)/shard_map/gather_sub/pallas_call | solution.py:160
  252.8 11.8 %scatter_sub.6 = f32[128,1024]{1,0:T(8,128)} custom-call(bf16[4,128,1024]{2,1,0:T(8,128)(2,1)} %bitcast.557), custom_call_target="tpu_custom_call" | custom-call | tf_op jit(solution)/shard_map/scatter_sub/pallas_call | solution.py:213
  267.6 10.5 %gather_sub.7 = bf16[4,128,1024]{2,1,0:T(8,128)(2,1)} custom-call(bf16[128,1024]{1,0:T(8,128)(2,1)} %multiply_convert_fusion.2.x_ref), custom_call_target="tpu_custom_call" | custom-call | tf_op jit(solution)/shard_map/gather_sub/pallas_call | solution.py:160
  279.5 3.4 fusion.10
  286.7 26.7 %fusion.167 = (bf16[1,32,64,256]{3,0,2,1:T(2,128)(2,1)}, bf16[1,32,64,256]{3,0,2,1:T(2,128)(2,1)}, bf16[1,32,64,256]{3,0,2,1:T(2,128)(2,1)}, bf16[1,32,64,256]{3...) fusion(bf16[1,34,66,256]{3,0,2,1:T(2,128)(2,1)} %copy-done.2), kind=kLoop, calls=%fused_computation.336 | loop fusion | bytes 18874368 | tf_op jit(solution)/shard_map/slice | solution.py:581
  315.7 12.1 %scatter_sub.7 = f32[128,1024]{1,0:T(8,128)} custom-call(bf16[4,128,1024]{2,1,0:T(8,128)(2,1)} %bitcast.584), custom_call_target="tpu_custom_call" | custom-call | tf_op jit(solution)/shard_map/scatter_sub/pallas_call | solution.py:213
  332.8 10.3 %gather_sub.8 = bf16[4,128,1024]{2,1,0:T(8,128)(2,1)} custom-call(bf16[128,1024]{1,0:T(8,128)(2,1)} %get-tuple-element.185.x_ref), custom_call_target="tpu_custom_call" | custom-call | tf_op jit(solution)/shard_map/gather_sub/pallas_call | solution.py:160
  352.7 12.1 %scatter_sub.8 = f32[128,1024]{1,0:T(8,128)} custom-call(bf16[4,128,1024]{2,1,0:T(8,128)(2,1)} %bitcast.558), custom_call_target="tpu_custom_call" | custom-call | tf_op jit(solution)/shard_map/scatter_sub/pallas_call | solution.py:213
  368.2 10.4 %gather_sub.9 = bf16[4,128,1024]{2,1,0:T(8,128)(2,1)} custom-call(bf16[128,1024]{1,0:T(8,128)(2,1)} %get-tuple-element.183.x_ref), custom_call_target="tpu_custom_call" | custom-call | tf_op jit(solution)/shard_map/gather_sub/pallas_call | solution.py:160
  381.1 9.3 swap_heads.3.d_ref
  390.4 25.4 %flash_back.1 = (bf16[4,1,64,512]{3,2,1,0:T(8,128)(2,1)}, bf16[8,1,512,128]{3,2,1,0:T(8,128)(2,1)}) custom-call(bf16[4,1,64,512]{3,2,1,0:T(8,128)(2,1)} %get-tuple-element.34.q_ref, bf16[4,1,64,512]{3,2,1,0:T(8,128)(2,1)} %swap_heads.3.d_ref, f32[4,1,64,512]{3,2,1,0:T(8,128)} %get-tuple-element.37.of_ref, f32[4,1,1,512]{3,2,1,0:T(1,128)} %get-tuple-element.38.lse_ref, ...), custom_call_target="tpu_custom_call" | custom-call | tf_op jit(solution)/shard_map/flash_back/pallas_call | solution.py:503
  415.8 20.8 %dqkv_home.1 = (bf16[1,256,512]{2,1,0:T(8,128)(2,1)}, bf16[1,512,512]{2,1,0:T(8,128)(2,1)}) custom-call(bf16[4,1,64,512]{3,2,1,0:T(8,128)(2,1)} %get-tuple-element.39.dq_ref, bf16[8,1,512,128]{3,2,1,0:T(8,128)(2,1)} %get-tuple-element.40.dkv_ref), custom_call_target="tpu_custom_call" | custom-call | tf_op jit(solution)/shard_map/dqkv_home/pallas_call | solution.py:390
  439.8 11.9 %scatter_sub.9 = f32[128,1024]{1,0:T(8,128)} custom-call(bf16[4,128,1024]{2,1,0:T(8,128)(2,1)} %bitcast.563), custom_call_target="tpu_custom_call" | custom-call | tf_op jit(solution)/shard_map/scatter_sub/pallas_call | solution.py:213
  456.1 4.5 collective-permute-start.8
  463.4 3.0 collective-permute-start.10
  469.9 4.9 broadcast_in_dim.85
  474.8 3.8 select_convert_fusion
  479.3 20.7 %convolution_multiply_fusion = f32[1,34,66,256]{3,0,2,1:T(1,128)S(1)} fusion(bf16[3,3,256,256]{3,2,1,0:T(8,128)(2,1)S(1)} %copy-done.122, bf16[1,36,68,256]{3,2,1,0:T(8,128)(2,1)S(1)} %get-tuple-element.181, f32[1,34,66,256]{3,0,2,1:T(1,128)S(1)} %copy-done.27, f32[256]{0:T(256)S(1)} %copy-done.114, f32[1,34,66,256]{3,0,2,1:T(1,128)S(1)} %copy-done.5, ...), kind=kOutput, calls=%fused_computation.6 | convolution fusion | flops 2651151360 | bytes 9328640 | tf_op jit(solution)/shard_map/conv_general_dilated | solution.py:562
  500.0 4.4 slice_reduce_fusion
  505.1 14.7 %total_all.6 = f32[4,128]{1,0:T(4,128)} custom-call(f32[4,128]{1,0:T(4,128)} %reshape.1084.x_ref), custom_call_target="tpu_custom_call" | custom-call | tf_op jit(solution)/shard_map/total_all/pallas_call | solution.py:95
  521.3 10.9 %fusion.3 = bf16[1,34,66,256]{3,0,2,1:T(2,128)(2,1)S(1)} fusion(pred[34,66]{1,0:T(8,128)(4,1)S(1)} %copy-done.77, f32[1,34,66,256]{3,0,2,1:T(1,128)} %get-tuple-element.195, f32[1,34,66,256]{3,0,2,1:T(1,128)} %copy-done.14, f32[256]{0:T(256)S(1)} %div.165, f32[256]{0:T(256)S(1)} %div.163, f32[256]{0:T(256)S(1)} %copy-done.92, f32[256]{0:T(256)S(1)} %copy-done.85), kind=kLoop, calls=%fused_computation.16 | loop fusion | flops 4021248 | bytes 5750980 | tf_op jit(solution)/shard_map/convert_element_type | solution.py:839
  560.1 2.8 convolution_convert_fusion
  564.9 38.8 %psum.94 = bf16[3,1024]{1,0:T(4,128)(2,1)S(1)} all-reduce(bf16[3,1024]{1,0:T(4,128)(2,1)S(1)} %pad_maximum_fusion.4), channel_id=1, replica_groups=mesh['tile'=8,'sub'=4] {'tile','sub'}, use_global_device_ids=true, to_apply=%region_39.40 | all-reduce | flops 3072 | bytes 12288 | tf_op jit(solution)/shard_map/psum | solution.py:903
  611.6 15.6 %fusion.183 = f32[1,32,64,256]{3,0,2,1:T(1,128)S(1)} fusion(bf16[1,34,66,256]{3,0,2,1:T(2,128)(2,1)} %copy-done.13, bf16[3,3,256,256]{3,2,1,0:T(8,128)(2,1)S(1)} %copy-done.124), kind=kOutput, calls=%fused_computation.352 | convolution fusion | flops 2415919104 | bytes 4425728 | tf_op jit(solution)/shard_map/conv_general_dilated | solution.py:562
  630.4 11.7 %total_all.7 = f32[4,128]{1,0:T(4,128)} custom-call(f32[4,128]{1,0:T(4,128)} %reshape.1088.x_ref), custom_call_target="tpu_custom_call" | custom-call | tf_op jit(solution)/shard_map/total_all/pallas_call | solution.py:95
  646.4 4.6 fusion.28
  657.5 34.5 %all-reduce.9.cloned.1.call-done = (bf16[3,3,256,256]{3,2,1,0:T(8,128)(2,1)}, bf16[3,3,256,256]{3,2,1,0:T(8,128)(2,1)}, bf16[256,1024]{1,0:T(8,128)(2,1)}) async-done(((bf16[3,3,256,256]{3,2,1,0:T(8,128)(2,1)}, bf16[3,3,256,256]{3,2,1,0:T(8,128)(2,1)}, bf16[256,1024]{1,0:T(8,128)(2,1)}), (bf16[3,3,256,256]{3,2,1,0:T(8,128)(2,1)}, bf16[3,3,256,256]{3,2,1,0:T(8,128)(2,1)}, ...) | async-done | bytes 2883600 | tf_op jit(solution)/shard_map/psum | solution.py:903
  692.1 3.0 convert_element_type.407
  697.8 12.3 %all-gather.11.cloned.1.call-done = bf16[512,1024]{1,0:T(8,128)(2,1)} async-done(((bf16[128,1024]{1,0:T(8,128)(2,1)}), bf16[512,1024]{1,0:T(8,128)(2,1)}) %all-gather.11.cloned.1.call-update) | async-done | bytes 1048592 | tf_op jit(solution)/shard_map/all_gather | solution.py:859
  711.8 17.2 %all-gather.13.cloned.1.call-done = bf16[512,1024]{1,0:T(8,128)(2,1)} async-done(((bf16[128,1024]{1,0:T(8,128)(2,1)}), bf16[512,1024]{1,0:T(8,128)(2,1)}) %all-gather.13.cloned.1.call-update) | async-done | bytes 1048592 | tf_op jit(solution)/shard_map/all_gather | solution.py:859
  730.8 250.9 %all-reduce.11.cloned.1.call-done = (bf16[1024,4,2,64]{0,3,1,2:T(8,128)(2,1)}, bf16[1024,256]{1,0:T(8,128)(2,1)}, bf16[256,1024]{1,0:T(8,128)(2,1)}, bf16[1024,2...) async-done(((bf16[1024,4,2,64]{0,3,1,2:T(8,128)(2,1)}, bf16[1024,256]{1,0:T(8,128)(2,1)}, ...) | async-done | bytes 7340048 | tf_op jit(solution)/shard_map/psum | solution.py:868
  (515 shorter events, 187.8 us)
Async XLA Ops:
  7.2 272.2 %copy-start = (bf16[1024,1024]{1,0:T(8,128)(2,1)S(1)}, bf16[1024,1024]{1,0:T(8,128)(2,1)}, u32[]{:S(2)}) copy-start(bf16[1024,1024]{1,0:T(8,128)(2,1)} %param.52) | copy-start | bytes 6291460
  7.2 38.4 %copy-start.116 = (f32[256]{0:T(256)S(1)}, f32[256]{0:T(256)}, u32[]{:S(2)}) copy-start(f32[256]{0:T(256)} %param.51) | copy-start | bytes 3076
  7.2 38.3 %copy-start.117 = (f32[256]{0:T(256)S(1)}, f32[256]{0:T(256)}, u32[]{:S(2)}) copy-start(f32[256]{0:T(256)} %param.46) | copy-start | bytes 3076
  7.2 38.3 %copy-start.118 = (f32[256]{0:T(256)S(1)}, f32[256]{0:T(256)}, u32[]{:S(2)}) copy-start(f32[256]{0:T(256)} %param.41) | copy-start | bytes 3076
  7.2 140.0 %all-gather.9.cloned.1.call-start = ((), (), s32[]{:S(2)}) async-start(), calls=%async_computation.3 | async-start | bytes 1310720 | tf_op jit(solution)/shard_map/all_gather | solution.py:690
  8.0 47.5 %copy-start.6 = (bf16[1,128,4096]{2,1,0:T(8,128)(2,1)S(1)}, bf16[1,128,4096]{2,1,0:T(8,128)(2,1)}, u32[]{:S(2)}) copy-start(bf16[1,128,4096]{2,1,0:T(8,128)(2,1)} %param.30) | copy-start | bytes 3145732
  8.0 141.5 %all-gather.7.cloned.1.call-start = ((), (), s32[]{:S(2)}) async-start(), calls=%async_computation.1 | async-start | bytes 1310720 | tf_op jit(solution)/shard_map/all_gather | solution.py:690
  9.6 58.9 %collective-permute-start = (bf16[1,2,64,256]{3,2,1,0:T(8,128)(2,1)}, bf16[1,2,64,256]{3,2,1,0:T(8,128)(2,1)}, u32[]{:S(2)}, u32[]{:S(2)}) collective-permute-start(bf16[1,2,64,256]{3,2,1,0:T(8,128)(2,1)} %get-tuple-element.214), channel_id=1, source_target_pairs={{0,4},{4,8},{8,12},{12,16},{16,20},{20,24},{24,28},{1,5},{5,9},{9,... | collective-permute-start | bytes 196616 | tf_op jit(solution)/shard_map/ppermute | solution.py:531
  15.1 54.5 %collective-permute-start.1 = (bf16[1,2,64,256]{3,2,1,0:T(8,128)(2,1)}, bf16[1,2,64,256]{3,2,1,0:T(8,128)(2,1)}, u32[]{:S(2)}, u32[]{:S(2)}) collective-permute-start(bf16[1,2,64,256]{3,2,1,0:T(8,128)(2,1)} %get-tuple-element.213), channel_id=1, source_target_pairs={{4,0},{8,4},{12,8},{16,12},{20,16},{24,20},{28,24},{5,1},{9,5},{13... | collective-permute-start | bytes 196616 | tf_op jit(solution)/shard_map/ppermute | solution.py:534
  17.9 56.9 %collective-permute-start.4 = (bf16[1,2,64,256]{3,2,1,0:T(8,128)(2,1)}, bf16[1,2,64,256]{3,2,1,0:T(8,128)(2,1)S(1)}, u32[]{:S(2)}, u32[]{:S(2)}) collective-permute-start(bf16[1,2,64,256]{3,2,1,0:T(8,128)(2,1)} %get-tuple-element.212), channel_id=1, source_target_pairs={{0,4},{4,8},{8,12},{12,16},{16,20},{20,24},{24,28},{1,5},{5,9},{9,... | collective-permute-start | bytes 196616 | tf_op jit(solution)/shard_map/ppermute | solution.py:531
  22.5 52.5 %collective-permute-start.5 = (bf16[1,2,64,256]{3,2,1,0:T(8,128)(2,1)}, bf16[1,2,64,256]{3,2,1,0:T(8,128)(2,1)S(1)}, u32[]{:S(2)}, u32[]{:S(2)}) collective-permute-start(bf16[1,2,64,256]{3,2,1,0:T(8,128)(2,1)} %get-tuple-element.211), channel_id=1, source_target_pairs={{4,0},{8,4},{12,8},{16,12},{20,16},{24,20},{28,24},{5,1},{9,5},{13... | collective-permute-start | bytes 196616 | tf_op jit(solution)/shard_map/ppermute | solution.py:534
  23.8 306.9 %reduce-scatter.2.cloned.1.call-start = ((), (), s32[]{:S(2)}) async-start(), calls=%async_computation.2 | async-start | bytes 1310720 | tf_op jit(solution)/shard_map/reduce_scatter | solution.py:854
  62.2 54.0 %copy-start.76 = (pred[34,66]{1,0:T(8,128)(4,1)}, pred[34,66]{1,0:T(8,128)(4,1)S(1)}, u32[]{:S(2)}) copy-start(pred[34,66]{1,0:T(8,128)(4,1)S(1)} %broadcast_and_fusion.1) | copy-start | bytes 6736
  64.2 17.9 %copy-start.78 = (pred[36,68]{1,0:T(8,128)(4,1)}, pred[36,68]{1,0:T(8,128)(4,1)S(1)}, u32[]{:S(2)}) copy-start(pred[36,68]{1,0:T(8,128)(4,1)S(1)} %broadcast_and_fusion) | copy-start | bytes 7348
  70.5 11.7 %collective-permute-start.3 = (bf16[1,36,2,256]{3,2,1,0:T(2,128)(2,1)S(1)}, bf16[1,36,2,256]{3,2,1,0:T(2,128)(2,1)S(1)}, u32[]{:S(2)}, u32[]{:S(2)}) collective-permute-start(bf16[1,36,2,256]{3,2,1,0:T(2,128)(2,1)S(1)} %get-tuple-element.208), channel_id=1, source_target_pairs={{1,0},{2,1},{3,2},{5,4},{6,5},{7,6},{9,8},{10,9},{11,10},{13,12},{... | collective-permute-start | bytes 110600 | tf_op jit(solution)/shard_map/ppermute | solution.py:534
  71.8 10.4 %collective-permute-start.2 = (bf16[1,36,2,256]{3,2,1,0:T(2,128)(2,1)S(1)}, bf16[1,36,2,256]{3,2,1,0:T(2,128)(2,1)S(1)}, u32[]{:S(2)}, u32[]{:S(2)}) collective-permute-start(bf16[1,36,2,256]{3,2,1,0:T(2,128)(2,1)S(1)} %get-tuple-element.207), channel_id=1, source_target_pairs={{0,1},{1,2},{2,3},{4,5},{5,6},{6,7},{8,9},{9,10},{10,11},{12,13},{... | collective-permute-start | bytes 110600 | tf_op jit(solution)/shard_map/ppermute | solution.py:531
  75.7 399.1 %collective-permute-start.7 = (bf16[1,36,2,256]{3,2,1,0:T(2,128)(2,1)}, bf16[1,36,2,256]{3,2,1,0:T(2,128)(2,1)}, u32[]{:S(2)}, u32[]{:S(2)}) collective-permute-start(bf16[1,36,2,256]{3,2,1,0:T(2,128)(2,1)} %get-tuple-element.206), channel_id=1, source_target_pairs={{1,0},{2,1},{3,2},{5,4},{6,5},{7,6},{9,8},{10,9},{11,10},{13,12},{... | collective-permute-start | bytes 110600 | tf_op jit(solution)/shard_map/ppermute | solution.py:534
  77.0 397.8 %collective-permute-start.6 = (bf16[1,36,2,256]{3,2,1,0:T(2,128)(2,1)}, bf16[1,36,2,256]{3,2,1,0:T(2,128)(2,1)}, u32[]{:S(2)}, u32[]{:S(2)}) collective-permute-start(bf16[1,36,2,256]{3,2,1,0:T(2,128)(2,1)} %get-tuple-element.205), channel_id=1, source_target_pairs={{0,1},{1,2},{2,3},{4,5},{5,6},{6,7},{8,9},{9,10},{10,11},{12,13},{... | collective-permute-start | bytes 110600 | tf_op jit(solution)/shard_map/ppermute | solution.py:531
  99.5 16.7 %copy-start.91 = (f32[256]{0:T(256)S(1)}, f32[256]{0:T(256)}, u32[]{:S(2)}) copy-start(f32[256]{0:T(256)} %param.37) | copy-start | bytes 3076
  99.5 16.7 %copy-start.113 = (f32[256]{0:T(256)S(1)}, f32[256]{0:T(256)}, u32[]{:S(2)}) copy-start(f32[256]{0:T(256)} %param.38) | copy-start | bytes 3076
  151.1 16.3 %copy-start.102 = (f32[128]{0:T(128)}, f32[128]{0:T(128)S(1)}, u32[]{:S(2)}) copy-start(f32[128]{0:T(128)S(1)} %add_rsqrt_fusion.4) | copy-start | bytes 1540
  167.4 49.9 %copy-start.62 = (bf16[256,1024]{1,0:T(8,128)(2,1)S(1)}, bf16[256,1024]{1,0:T(8,128)(2,1)}, u32[]{:S(2)}) copy-start(bf16[256,1024]{1,0:T(8,128)(2,1)} %param.45) | copy-start | bytes 1572868
  286.6 364.3 %all-reduce.7.cloned.1.call-start = ((), (), s32[]{:S(2)}) async-start(), calls=%async_computation.6 | async-start | bytes 524288 | tf_op jit(solution)/shard_map/psum | solution.py:875
  286.6 26.7 %copy-start.125 = (bf16[512,1024]{1,0:T(8,128)(2,1)S(1)}, bf16[512,1024]{1,0:T(8,128)(2,1)}, u32[]{:S(2)}) copy-start(bf16[512,1024]{1,0:T(8,128)(2,1)} %get-tuple-element.243) | copy-start | bytes 3145732
  350.9 15.2 %copy-start.54 = (bf16[4,1,128,4,64]{2,0,4,3,1:T(4,128)(2,1)}, bf16[4,1,128,4,64]{2,0,4,3,1:T(4,128)(2,1)S(1)}, u32[]{:S(2)}) copy-start(bf16[4,1,128,4,64]{2,0,4,3,1:T(4,128)(2,1)S(1)} %copy.164) | copy-start | bytes 786436
  381.1 55.5 %copy-start.42 = (bf16[1024,256]{1,0:T(8,128)(2,1)S(1)}, bf16[1024,256]{1,0:T(8,128)(2,1)}, u32[]{:S(2)}) copy-start(bf16[1024,256]{1,0:T(8,128)(2,1)} %param.42) | copy-start | bytes 1572868
  415.8 22.3 %copy-start.23 = (bf16[1024,4,128]{0,2,1:T(8,128)(2,1)S(1)}, bf16[1024,4,128]{0,2,1:T(8,128)(2,1)}, u32[]{:S(2)}) copy-start(bf16[1024,4,128]{0,2,1:T(8,128)(2,1)} %pad_maximum_fusion) | copy-start | bytes 3145732
  454.8 6.8 collective-permute-start.9
  456.1 6.0 collective-permute-start.8
  462.1 5.5 collective-permute-start.11
  463.4 4.2 collective-permute-start.10
  467.5 224.5 %all-reduce.9.cloned.1.call-start = ((), (), s32[]{:S(2)}) async-start(), calls=%async_computation.7 | async-start | bytes 5767168 | tf_op jit(solution)/shard_map/psum | solution.py:903
  500.0 21.3 %copy-start.77 = (pred[34,66]{1,0:T(8,128)(4,1)S(1)}, pred[34,66]{1,0:T(8,128)(4,1)}, u32[]{:S(2)}) copy-start(pred[34,66]{1,0:T(8,128)(4,1)} %copy-done.76) | copy-start | bytes 6736
  500.0 21.3 %copy-start.85 = (f32[256]{0:T(256)S(1)}, f32[256]{0:T(256)}, u32[]{:S(2)}) copy-start(f32[256]{0:T(256)} %copy-done.84) | copy-start | bytes 3076
  555.9 154.2 %all-gather.11.cloned.1.call-start = ((), (), s32[]{:S(2)}) async-start(), calls=%async_computation.4 | async-start | bytes 1310720 | tf_op jit(solution)/shard_map/all_gather | solution.py:859
  556.5 172.5 %all-gather.13.cloned.1.call-start = ((), (), s32[]{:S(2)}) async-start(), calls=%async_computation.5 | async-start | bytes 1310720 | tf_op jit(solution)/shard_map/all_gather | solution.py:859
  562.9 418.8 %all-reduce.11.cloned.1.call-start = ((), (), s32[]{:S(2)}) async-start(), calls=%async_computation.8 | async-start | bytes 14680064 | tf_op jit(solution)/shard_map/psum | solution.py:868
  563.7 42.9 %copy-start.19 = (bf16[4,128,1024]{2,1,0:T(8,128)(2,1)S(1)}, bf16[4,128,1024]{2,1,0:T(8,128)(2,1)}, u32[]{:S(2)}) copy-start(bf16[4,128,1024]{2,1,0:T(8,128)(2,1)} %gather_sub.9) | copy-start | bytes 3145732
  563.7 42.8 %copy-start.24 = (bf16[1,256,512]{2,1,0:T(8,128)(2,1)S(1)}, bf16[1,256,512]{2,1,0:T(8,128)(2,1)}, u32[]{:S(2)}) copy-start(bf16[1,256,512]{2,1,0:T(8,128)(2,1)} %swap_heads.2) | copy-start | bytes 786436
  564.8 43.0 %copy-start.51 = (bf16[4,128,1024]{2,1,0:T(8,128)(2,1)S(1)}, bf16[4,128,1024]{2,1,0:T(8,128)(2,1)}, u32[]{:S(2)}) copy-start(bf16[4,128,1024]{2,1,0:T(8,128)(2,1)} %gather_sub.6) | copy-start | bytes 3145732
  611.6 15.6 %copy-start.4 = (bf16[1,32,64,256]{3,2,1,0:T(8,128)(2,1)S(1)}, bf16[1,32,64,256]{3,2,1,0:T(8,128)(2,1)}, u32[]{:S(2)}) copy-start(bf16[1,32,64,256]{3,2,1,0:T(8,128)(2,1)} %param.28) | copy-start | bytes 3145732
  611.6 15.6 %copy-start.83 = (f32[256]{0:T(256)S(1)}, f32[256]{0:T(256)}, u32[]{:S(2)}) copy-start(f32[256]{0:T(256)} %div.132) | copy-start | bytes 3076
  611.6 15.7 %copy-start.87 = (f32[256]{0:T(256)S(1)}, f32[256]{0:T(256)}, u32[]{:S(2)}) copy-start(f32[256]{0:T(256)} %param.33) | copy-start | bytes 3076
  611.6 15.7 %copy-start.89 = (f32[256]{0:T(256)S(1)}, f32[256]{0:T(256)}, u32[]{:S(2)}) copy-start(f32[256]{0:T(256)} %add_rsqrt_fusion.1) | copy-start | bytes 3076
  611.6 15.7 %copy-start.112 = (f32[256]{0:T(256)S(1)}, f32[256]{0:T(256)}, u32[]{:S(2)}) copy-start(f32[256]{0:T(256)} %param.34) | copy-start | bytes 3076
  627.3 17.7 %copy-start.90 = (f32[4,128]{1,0:T(4,128)S(1)}, f32[4,128]{1,0:T(4,128)}, u32[]{:S(2)}) copy-start(f32[4,128]{1,0:T(4,128)} %total_all.6) | copy-start | bytes 6148
  627.3 18.2 %copy-start.108 = (f32[1,1,256]{2,1,0:T(1,128)S(1)}, f32[1,1,256]{2,1,0:T(1,128)}, u32[]{:S(2)}) copy-start(f32[1,1,256]{2,1,0:T(1,128)} %get-tuple-element.226) | copy-start | bytes 3076
  627.3 18.2 %copy-start.94 = (f32[256]{0:T(256)S(1)}, f32[256]{0:T(256)}, u32[]{:S(2)}) copy-start(f32[256]{0:T(256)} %copy-done.93) | copy-start | bytes 3076
  (101 other events, 631.0 us)
Sparse Core Ops, SparseCore 0:
  9.6 19.5 all-gather.8
  30.8 16.8 all-gather.6
  286.7 25.6 reduce-scatter.1
  467.7 72.5 all-reduce.6
  556.0 135.9 all-reduce.8
  694.0 16.0 all-gather.10
  712.3 16.7 all-gather.12
  735.6 246.0 all-reduce.10

commit v2 on v1

--- a/solution.py
+++ b/solution.py
@@ -26,6 +26,9 @@
     )
 
 
+SHORT = pl.CostEstimate(flops=1, transcendentals=0, bytes_accessed=1)
+
+
 def in_vmem():
     return pl.BlockSpec(memory_space=pltpu.VMEM)
 
@@ -60,55 +63,12 @@
     pl.semaphore_wait(barrier, len(peers))
 
 
-def total_kernel(nt, ns, x_ref, o_ref, first, second, ss1, rs1, ss2, rs2):
-    t, s = lax.axis_index("tile"), lax.axis_index("sub")
-    near = [lax.rem(s + k, ns) for k in range(1, ns)]
-    far = [lax.rem(t + k, nt) for k in range(1, nt)]
-    first[s] = x_ref[...]
-    greet([(t, p) for p in near] + [(p, s) for p in far])
-    copies = []
-    for k, p in enumerate(near):
-        copies.append(remote(first.at[s], first.at[s], ss1.at[k], rs1.at[s], (t, p)))
-        copies[-1].start()
-    for k, p in enumerate(near):
-        arrived(first.at[p], ss1.at[k], rs1.at[p], (t, s))
-    total = first[0]
-    for k in range(1, ns):
-        total = total + first[k]
-    second[t] = total
-    for k, p in enumerate(far):
-        copies.append(remote(second.at[t], second.at[t], ss2.at[k], rs2.at[t], (p, s)))
-        copies[-1].start()
-    for k, p in enumerate(far):
-        arrived(second.at[p], ss2.at[k], rs2.at[p], (t, s))
-    total = second[0]
-    for k in range(1, nt):
-        total = total + second[k]
-    o_ref[...] = total
-    for copy in copies:
-        copy.wait_send()
-
-
-def total_all(values, cid):
-    nt, ns = lax.axis_size("tile"), lax.axis_size("sub")
-    flat = values.reshape(-1, 128)
-    out = pl.pallas_call(
-        functools.partial(total_kernel, nt, ns),
-        out_shape=jax.ShapeDtypeStruct(flat.shape, f32),
-        in_specs=[in_vmem()],
-        out_specs=in_vmem(),
-        scratch_shapes=[
-            pltpu.VMEM((ns,) + flat.shape, f32),
-            pltpu.VMEM((nt,) + flat.shape, f32),
-            dma(ns),
-            dma(ns),
-            dma(nt),
-            dma(nt),
-        ],
-        compiler_params=params(cid),
-        name="total_all",
-    )(flat)
-    return out.reshape(values.shape)
+def dot(left, right):
+    return jnp.dot(left, right, preferred_element_type=f32)
+
+
+def round_up(rows, step):
+    return (rows + step - 1) // step * step
 
 
 def chunks_of(rows):
@@ -163,60 +123,107 @@
         in_specs=[anywhere()],
         out_specs=anywhere(),
         scratch_shapes=[dma(far, count) for _ in range(4)] + [pltpu.SemaphoreType.DMA],
+        cost_estimate=SHORT,
         compiler_params=params(cid),
         name="gather_sub",
     )(x)
 
 
-def scatter_kernel(ns, count, x_ref, o_ref, got, stage, last, s1, r1, s2, r2):
-    far = ns // 2
-    t, s = lax.axis_index("tile"), lax.axis_index("sub")
-    r, c = s // 2, lax.rem(s, 2)
-    me, twin = (t, s), (t, r * 2 + 1 - c)
-    size = x_ref.shape[1] // count
-    greet([twin] + [(t, lax.rem(r + k, far) * 2 + c) for k in range(1, far)])
-    copies = []
-
-    def send(src, dst, send_sem, recv_sem, where):
-        copies.append(remote(src, dst, send_sem, recv_sem, where))
-        copies[-1].start()
-
-    for k in list(range(1, far)) + [0]:
-        for j in range(count):
-            part = pl.ds(j * size, size)
-            block = x_ref.at[lax.rem(r + k, far) * 2 + 1 - c, part]
-            send(block, got.at[k, part], s1.at[k, j], r1.at[k, j], twin)
-    for j in range(count):
-        part = pl.ds(j * size, size)
-        for k in range(1, far):
-            p = lax.rem(r + k, far) * 2 + c
-            arrived(got.at[k, part], s1.at[k, j], r1.at[k, j], me)
-            stage[k, part] = (x_ref[p, part].astype(f32) + got[k, part].astype(f32)).astype(bf16)
-            send(stage.at[k, part], last.at[k, part], s2.at[k, j], r2.at[k, j], (t, p))
-    for j in range(count):
-        part = pl.ds(j * size, size)
-        arrived(got.at[0, part], s1.at[0, j], r1.at[0, j], me)
-        total = x_ref[s, part].astype(f32) + got[0, part].astype(f32)
-        for k in range(1, far):
-            arrived(last.at[k, part], s2.at[k, j], r2.at[k, j], me)
-            total = total + last[k, part].astype(f32)
-        o_ref[part] = total
-    for copy in copies:
-        copy.wait_send()
+class Copies:
+    def __init__(self):
+        self.started = []
+
+    def send(self, src, dst, send_sem, recv_sem, where, when=None):
+        copy = remote(src, dst, send_sem, recv_sem, where)
+        if when is None:
+            copy.start()
+        else:
+            pl.when(when)(copy.start)
+        self.started.append((when, copy))
+
+    def finish(self):
+        for when, copy in self.started:
+            if when is None:
+                copy.wait_send()
+            else:
+                pl.when(when)(copy.wait_send)
+
+
+class SubScatter:
+    def __init__(self, ns, copies, x, got, stage, last, sems):
+        t, s = lax.axis_index("tile"), lax.axis_index("sub")
+        self.far, self.copies, self.x, self.s, self.t = ns // 2, copies, x, s, t
+        self.got, self.stage, self.last = got, stage, last
+        self.r, self.c = s // 2, lax.rem(s, 2)
+        self.me, self.twin = (t, s), (t, self.r * 2 + 1 - self.c)
+        self.count = chunks_of(x.shape[1])
+        self.size = x.shape[1] // self.count
+        self.s1, self.r1, self.s2, self.r2 = sems
+
+    @staticmethod
+    def scratch(ns, rows, width):
+        far, count = ns // 2, chunks_of(rows)
+        blocks = [pltpu.VMEM((far, rows, width), bf16) for _ in range(3)]
+        return blocks + [dma(far, count) for _ in range(4)]
+
+    def peers(self):
+        return [self.twin] + [self.peer(k) for k in range(1, self.far)]
+
+    def peer(self, k):
+        return (self.t, lax.rem(self.r + k, self.far) * 2 + self.c)
+
+    def part(self, j):
+        return pl.ds(j * self.size, self.size)
+
+    def start(self):
+        for k in list(range(1, self.far)) + [0]:
+            for j in range(self.count):
+                block = self.x.at[lax.rem(self.r + k, self.far) * 2 + 1 - self.c, self.part(j)]
+                got = self.got.at[k, self.part(j)]
+                self.copies.send(block, got, self.s1.at[k, j], self.r1.at[k, j], self.twin)
+
+    def cross(self):
+        for j in range(self.count):
+            part = self.part(j)
+            for k in range(1, self.far):
+                arrived(self.got.at[k, part], self.s1.at[k, j], self.r1.at[k, j], self.me)
+                own = self.x[self.peer(k)[1], part].astype(f32)
+                self.stage[k, part] = (own + self.got[k, part].astype(f32)).astype(bf16)
+                src, dst = self.stage.at[k, part], self.last.at[k, part]
+                self.copies.send(src, dst, self.s2.at[k, j], self.r2.at[k, j], self.peer(k))
+
+    def end(self, out):
+        for j in range(self.count):
+            part = self.part(j)
+            arrived(self.got.at[0, part], self.s1.at[0, j], self.r1.at[0, j], self.me)
+            total = self.x[self.s, part].astype(f32) + self.got[0, part].astype(f32)
+            for k in range(1, self.far):
+                arrived(self.last.at[k, part], self.s2.at[k, j], self.r2.at[k, j], self.me)
+                total = total + self.last[k, part].astype(f32)
+            out[part] = total
+
+
+def scatter_kernel(ns, x_ref, o_ref, got, stage, last, *sems):
+    copies = Copies()
+    scatter = SubScatter(ns, copies, x_ref, got, stage, last, sems)
+    greet(scatter.peers())
+    scatter.start()
+    scatter.cross()
+    scatter.end(o_ref)
+    copies.finish()
 
 
 def scatter_sub(x, cid):
     ns = lax.axis_size("sub")
     x = x.astype(bf16).reshape(ns, x.shape[0] // ns, x.shape[1])
     block = x.shape[1:]
-    far, count = ns // 2, chunks_of(block[0])
     return pl.pallas_call(
-        functools.partial(scatter_kernel, ns, count),
+        functools.partial(scatter_kernel, ns),
         out_shape=jax.ShapeDtypeStruct(block, f32),
         in_specs=[in_vmem()],
         out_specs=in_vmem(),
-        scratch_shapes=[pltpu.VMEM((far,) + block, bf16) for _ in range(3)]
-        + [dma(far, count) for _ in range(4)],
+        scratch_shapes=SubScatter.scratch(ns, *block),
+        cost_estimate=SHORT,
         compiler_params=params(cid),
         name="scatter_sub",
     )(x)
@@ -295,6 +302,7 @@
         in_specs=[anywhere()] * 2,
         out_specs=(anywhere(), anywhere()),
         scratch_shapes=[dma(u), dma(u), dma(u), dma(u), dma(u, nb), dma(u, nb), dma(2)],
+        cost_estimate=SHORT,
         compiler_params=params(cid),
         name="qkv_out",
     )(q, kv)
@@ -337,30 +345,40 @@
         in_specs=[anywhere()],
         out_specs=anywhere(),
         scratch_shapes=[dma(u), dma(u), pltpu.SemaphoreType.DMA],
+        cost_estimate=SHORT,
         compiler_params=params(cid),
         name="swap_heads",
     )(x)
 
 
-def dqkv_home_kernel(nt, u, dq_ref, dkv_ref, qo, kvo, got, stage, qs, qr, fs, fr, ks, kr, own):
+def dqkv_home_kernel(
+    nt, ns, u, dq_ref, dkv_ref, beside_ref, mixed_t, grad_attn, cross_mixed, grad_cross, cross_in,
+    grad_cq, qo, kvo, beside_out, wide, cq_out, got, stage, qs, qr, fs, fr, ks, kr, own, *scratch
+):
     t, s, nb, a, b, a_peer, b_peer, peers = deal(nt, u)
     me = (t, s)
-    greet(peers)
-    copies = []
-
-    def send(src, dst, send_sem, recv_sem, where):
-        copies.append(remote(src, dst, send_sem, recv_sem, where))
-        copies[-1].start()
-
+    copies = Copies()
+    beside = SubScatter(ns, copies, beside_ref, *scratch[:3], scratch[3:])
+    greet(peers + beside.peers())
     order = list(range(1, u)) + [0]
     for k in order:
         for m in range(1, nb):
             block = dkv_ref.at[lax.rem(a + k, u) * nb + lax.rem(b + m, nb)]
-            send(block, got.at[m, k], fs.at[k, m], fr.at[k, m], b_peer(m))
+            copies.send(block, got.at[m, k], fs.at[k, m], fr.at[k, m], b_peer(m))
+    beside.start()
     for k in range(1, u):
-        send(dq_ref.at[lax.rem(a + k, u)], rows_of(qo, a, HD), qs.at[k], qr.at[k], a_peer(k))
+        block = dq_ref.at[lax.rem(a + k, u)]
+        copies.send(block, rows_of(qo, a, HD), qs.at[k], qr.at[k], a_peer(k))
     local = [pltpu.make_async_copy(dq_ref.at[a], rows_of(qo, a, HD), own.at[0])]
     local[0].start()
+    features = mixed_t.shape[0]
+    wide[pl.ds(0, features), :] = dot(mixed_t[...], grad_attn[...]).astype(bf16)
+    beside.cross()
+    turned = cross_mixed[...].T
+    wide[pl.ds(features, features), :] = dot(turned, grad_cross[...]).astype(bf16)
+    if 2 * features < wide.shape[0]:
+        spare = wide.shape[0] - 2 * features
+        wide[pl.ds(2 * features, spare), :] = jnp.zeros((spare, wide.shape[1]), bf16)
     for k in order:
         total = dkv_ref[lax.rem(a + k, u) * nb + b].astype(f32)
         for m in range(1, nb):
@@ -368,33 +386,38 @@
             total = total + got[m, k].astype(f32)
         stage[k] = total.astype(bf16)
         if k:
-            send(stage.at[k], lanes_of(kvo, a, 2 * HD), ks.at[k], kr.at[k], a_peer(k))
+            copies.send(stage.at[k], lanes_of(kvo, a, 2 * HD), ks.at[k], kr.at[k], a_peer(k))
         else:
             local.append(pltpu.make_async_copy(stage.at[0], lanes_of(kvo, a, 2 * HD), own.at[1]))
             local[1].start()
+    beside.end(beside_out)
+    cq_out[...] = dot(cross_in[...].T, grad_cq[...]).astype(bf16)
     for k in range(1, u):
         i = lax.rem(a + u - k, u)
         arrived(rows_of(qo, i, HD), qs.at[k], qr.at[k], me)
         arrived(lanes_of(kvo, i, 2 * HD), ks.at[k], kr.at[k], me)
-    for copy in copies:
-        copy.wait_send()
+    copies.finish()
     for copy in local:
         copy.wait()
 
 
-def dqkv_home(dq, dkv, cid):
-    nt = lax.axis_size("tile")
+def dqkv_home(dq, dkv, beside, mixed_t, grad_attn, cross_mixed, grad_cross, cross_in, grad_cq, cid):
+    nt, ns = lax.axis_size("tile"), lax.axis_size("sub")
     u, batch, _, length = dq.shape
     nb = nt // u
     block = (batch, length, 2 * HD)
+    beside = beside.reshape(ns, -1, beside.shape[1])
     return pl.pallas_call(
-        functools.partial(dqkv_home_kernel, nt, u),
+        functools.partial(dqkv_home_kernel, nt, ns, u),
         out_shape=(
             jax.ShapeDtypeStruct((batch, u * HD, length), bf16),
             jax.ShapeDtypeStruct((batch, length, u * 2 * HD), bf16),
+            jax.ShapeDtypeStruct(beside.shape[1:], f32),
+            jax.ShapeDtypeStruct((round_up(2 * u * HD, 16 * nt), grad_attn.shape[1]), bf16),
+            jax.ShapeDtypeStruct((cross_in.shape[1], u * HD), bf16),
         ),
-        in_specs=[in_vmem()] * 2,
-        out_specs=(anywhere(), anywhere()),
+        in_specs=[in_vmem()] * 9,
+        out_specs=(anywhere(), anywhere()) + (in_vmem(),) * 3,
         scratch_shapes=[
             pltpu.VMEM((nb, u) + block, bf16),
             pltpu.VMEM((u,) + block, bf16),
@@ -405,14 +428,12 @@
             dma(u),
             dma(u),
             dma(2),
-        ],
+        ]
+        + SubScatter.scratch(ns, *beside.shape[1:]),
+        cost_estimate=SHORT,
         compiler_params=params(cid),
         name="dqkv_home",
-    )(dq, dkv)
-
-
-def dot(left, right):
-    return jnp.dot(left, right, preferred_element_type=f32)
+    )(dq, dkv, beside, mixed_t, grad_attn, cross_mixed, grad_cross, cross_in, grad_cq)
 
 
 def flash_kernel(q_ref, kv_ref, o_ref, of_ref, lse_ref, vt):
@@ -457,6 +478,7 @@
         in_specs=[rows, pl.BlockSpec((nt, 1, length, 2 * HD), lambda b, i: (0, b, 0, 0))],
         out_specs=(rows, rows, pl.BlockSpec((1, 1, 1, length), lambda b, i: (i, b, 0, 0))),
         scratch_shapes=[pltpu.VMEM((nt, HD, length), bf16)],
+        cost_estimate=SHORT,
         compiler_params=params(),
         name="flash",
     )(q, kv)
@@ -518,35 +540,946 @@
             pltpu.VMEM((u, 1, length), f32),
             pltpu.VMEM((u, HD, length), f32),
         ],
+        cost_estimate=SHORT,
         compiler_params=params(),
         name="flash_back",
     )(q, d, of, lse, kv)
 
 
-def bordered(block, width):
-    for axis, dim in (("tile", 1), ("sub", 2)):
-        count = lax.axis_size(axis)
-        forward = [(i, i + 1) for i in range(count - 1)]
-        backward = [(target, source) for source, target in forward]
-        low = lax.ppermute(
-            lax.slice_in_dim(block, block.shape[dim] - width, None, axis=dim), axis, forward
+class TileSum:
+    PARTS = 4
+
+    def __init__(self, nt, copies, x, out, got1, stage, got2, sems):
+        t, s = lax.axis_index("tile"), lax.axis_index("sub")
+        self.na, self.copies, self.x, self.out = nt // 2, copies, x, out
+        self.got1, self.stage, self.got2 = got1, stage, got2
+        self.a, self.b, self.s = t // 2, lax.rem(t, 2), s
+        self.me, self.pair = (t, s), (self.a * 2 + 1 - self.b, s)
+        self.half = x.shape[0] // 2
+        self.piece = self.half // 2 // self.PARTS
+        (self.s1, self.r1, self.s2, self.r2, self.s3, self.r3, self.s4, self.r4) = sems
+
+    @staticmethod
+    def scratch(nt, rows, width):
+        return [pltpu.VMEM((rows // 2, width), bf16) for _ in range(3)] + [
+            dma(2, TileSum.PARTS) for _ in range(8)
+        ]
+
+    def rows(self, b, e, j):
+        start = b * self.half + (j * 2 + e) * self.piece
+        return pl.ds(pl.multiple_of(start, 16), self.piece)
+
+    def along(self, e):
+        up, down = (self.a * 2 + 2 + self.b, self.s), (self.a * 2 - 2 + self.b, self.s)
+        return (down, up, self.a) if e else (up, down, self.na - 1 - self.a)
+
+    def start(self):
+        for j in range(self.PARTS):
+            for e in range(2):
+                src, dst = self.x.at[self.rows(1 - self.b, e, j)], self.got1.at[self.rows(0, e, j)]
+                self.copies.send(src, dst, self.s1.at[e, j], self.r1.at[e, j], self.pair)
+
+    def steps(self):
+        return range(self.PARTS + self.na - 1)
+
+    def step_of(self, way, step, action):
+        j = step - way
+        pl.when((j >= 0) & (j < self.PARTS))(lambda: action(jnp.clip(j, 0, self.PARTS - 1)))
+
+    def add(self, steps):
+        for step in steps:
+            for e in range(2):
+                self.step_of(self.along(e)[2], step, functools.partial(self.add_one, e))
+
+    def add_one(self, e, j):
+        _, after, way = self.along(e)
+        here, mine = self.rows(0, e, j), self.rows(self.b, e, j)
+        arrived(self.got1.at[here], self.s1.at[e, j], self.r1.at[e, j], self.me)
+        both = self.x[mine].astype(f32) + self.got1[here].astype(f32)
+
+        @pl.when(way == 0)
+        def _():
+            self.stage[here] = both.astype(bf16)
+
+        @pl.when(way > 0)
+        def _():
+            arrived(self.got2.at[here], self.s2.at[e, j], self.r2.at[e, j], self.me)
+            self.stage[here] = (both + self.got2[here].astype(f32)).astype(bf16)
+
+        @pl.when(way < self.na - 1)
+        def _():
+            src, dst = self.stage.at[here], self.got2.at[here]
+            remote(src, dst, self.s2.at[e, j], self.r2.at[e, j], after).start()
+
+        @pl.when(way == self.na - 1)
+        def _():
+            self.out[mine] = self.stage[here]
+
+    def share(self, steps):
+        for step in steps:
+            for e in range(2):
+                way = self.na - 1 - self.along(e)[2]
+                self.step_of(way, step, functools.partial(self.share_one, e))
+
+    def share_one(self, e, j):
+        before, _, way = self.along(e)
+        block = self.out.at[self.rows(self.b, e, j)]
+
+        @pl.when(way < self.na - 1)
+        def _():
+            arrived(block, self.s3.at[e, j], self.r3.at[e, j], self.me)
+
+        @pl.when(way > 0)
+        def _():
+            remote(block, block, self.s3.at[e, j], self.r3.at[e, j], before).start()
+
+        remote(block, block, self.s4.at[e, j], self.r4.at[e, j], self.pair).start()
+
+    def end(self):
+        for j in range(self.PARTS):
+            for e in range(2):
+                block = self.out.at[self.rows(1 - self.b, e, j)]
+                arrived(block, self.s4.at[e, j], self.r4.at[e, j], self.me)
+        for j in range(self.PARTS):
+            for e in range(2):
+                before, after, way = self.along(e)
+                block = self.out.at[self.rows(self.b, e, j)]
+                stage = self.stage.at[self.rows(0, e, j)]
+                sent = remote(stage, stage, self.s2.at[e, j], self.r2.at[e, j], after)
+                pl.when(way < self.na - 1)(sent.wait_send)
+                sent = remote(block, block, self.s3.at[e, j], self.r3.at[e, j], before)
+                pl.when(way > 0)(sent.wait_send)
+                remote(block, block, self.s4.at[e, j], self.r4.at[e, j], self.pair).wait_send()
+
+
+class FullSum:
+    def __init__(self, nt, ns, copies, x, out, got1, stage, got2, mine, got3, sems):
+        t, s = lax.axis_index("tile"), lax.axis_index("sub")
+        self.nt, self.far, self.copies, self.x, self.out = nt, ns // 2, copies, x, out
+        self.got1, self.stage, self.got2, self.mine, self.got3 = got1, stage, got2, mine, got3
+        self.t, self.s, self.r, self.c = t, s, s // 2, lax.rem(s, 2)
+        self.me, self.twin = (t, s), (t, self.r * 2 + 1 - self.c)
+        self.part = x.shape[0] // ns
+        self.piece = self.part // nt
+        (self.s1, self.r1, self.s2, self.r2, self.s3, self.r3) = sems[:6]
+        (self.s4, self.r4, self.s5, self.r5, self.s6, self.r6) = sems[6:]
+
+    @staticmethod
+    def scratch(nt, ns, rows, width):
+        far, part = ns // 2, rows // ns
+        return (
+            [pltpu.VMEM((far, part, width), bf16) for _ in range(3)]
+            + [pltpu.VMEM((part, width), bf16), pltpu.VMEM((nt, part // nt, width), bf16)]
+            + [dma(far) for _ in range(4)]
+            + [dma(nt) for _ in range(4)]
+            + [dma(far) for _ in range(4)]
         )
-        high = lax.ppermute(lax.slice_in_dim(block, 0, width, axis=dim), axis, backward)
-        block = jnp.concatenate([low, block, high], axis=dim)
-    return block
-
-
-def inside(shape, width):
-    rows, cols = shape[1] - 2 * width, shape[2] - 2 * width
-    y = lax.axis_index("tile") * rows - width + jnp.arange(shape[1])
-    x = lax.axis_index("sub") * cols - width + jnp.arange(shape[2])
-    good_y = (y >= 0) & (y < rows * lax.axis_size("tile"))
-    good_x = (x >= 0) & (x < cols * lax.axis_size("sub"))
-    return (good_y[:, None] & good_x[None, :])[None, :, :, None]
-
-
-def trim(values, width):
-    return values[:, width:-width, width:-width]
+
+    def rows(self, r, c):
+        return pl.ds(pl.multiple_of((c * self.far + r) * self.part, 16), self.part)
+
+    def slot(self, t):
+        return pl.ds(pl.multiple_of(t * self.piece, 16), self.piece)
+
+    def other(self, k):
+        return lax.rem(self.r + k, self.far)
+
+    def tile(self, k):
+        return lax.rem(self.t + k, self.nt)
+
+    def start(self):
+        for k in list(range(1, self.far)) + [0]:
+            src = self.x.at[self.rows(self.other(k), 1 - self.c)]
+            self.copies.send(src, self.got1.at[k], self.s1.at[k], self.r1.at[k], self.twin)
+
+    def cross(self):
+        for k in range(1, self.far):
+            arrived(self.got1.at[k], self.s1.at[k], self.r1.at[k], self.me)
+            own = self.x[self.rows(self.other(k), self.c)].astype(f32)
+            self.stage[k] = (own + self.got1[k].astype(f32)).astype(bf16)
+            peer = (self.t, self.other(k) * 2 + self.c)
+            self.copies.send(self.stage.at[k], self.got2.at[k], self.s2.at[k], self.r2.at[k], peer)
+
+    def spread(self):
+        arrived(self.got1.at[0], self.s1.at[0], self.r1.at[0], self.me)
+        total = self.x[self.rows(self.r, self.c)].astype(f32) + self.got1[0].astype(f32)
+        for k in range(1, self.far):
+            arrived(self.got2.at[k], self.s2.at[k], self.r2.at[k], self.me)
+            total = total + self.got2[k].astype(f32)
+        self.mine[...] = total.astype(bf16)
+        for k in range(1, self.nt):
+            p = self.tile(k)
+            src = self.mine.at[self.slot(p)]
+            self.copies.send(src, self.got3.at[k], self.s3.at[k], self.r3.at[k], (p, self.s))
+
+    def place(self, t, r, c):
+        start = (c * self.far + r) * self.part + t * self.piece
+        return pl.ds(pl.multiple_of(start, 16), self.piece)
+
+    def settle(self):
+        total = self.mine[self.slot(self.t)].astype(f32)
+        for k in range(1, self.nt):
+            arrived(self.got3.at[k], self.s3.at[k], self.r3.at[k], self.me)
+            total = total + self.got3[k].astype(f32)
+        here = self.place(self.t, self.r, self.c)
+        self.out[here] = total.astype(bf16)
+        block = self.out.at[here]
+        for k in range(1, self.nt):
+            self.copies.send(block, block, self.s4.at[k], self.r4.at[k], (self.tile(k), self.s))
+
+    def share(self):
+        for k in range(1, self.nt):
+            block = self.out.at[self.place(self.tile(self.nt - k), self.r, self.c)]
+            arrived(block, self.s4.at[k], self.r4.at[k], self.me)
+        block = self.out.at[self.rows(self.r, self.c)]
+        for k in range(1, self.far):
+            peer = (self.t, self.other(k) * 2 + self.c)
+            self.copies.send(block, block, self.s5.at[k], self.r5.at[k], peer)
+        self.copies.send(block, block, self.s6.at[0], self.r6.at[0], self.twin)
+
+    def relay(self):
+        for k in range(1, self.far):
+            block = self.out.at[self.rows(self.other(self.far - k), self.c)]
+            arrived(block, self.s5.at[k], self.r5.at[k], self.me)
+            self.copies.send(block, block, self.s6.at[k], self.r6.at[k], self.twin)
+
+    def end(self):
+        for k in range(self.far):
+            block = self.out.at[self.rows(self.other(self.far - k), 1 - self.c)]
+            arrived(block, self.s6.at[k], self.r6.at[k], self.me)
+
+
+AROUND = [(-1, 0), (1, 0), (0, -1), (0, 1), (-1, -1), (-1, 1), (1, -1), (1, 1)]
+DIAGONAL = AROUND[4:]
+
+
+def present(nt, ns, t, s, dt, ds):
+    y, x = t + dt, s + ds
+    return (y >= 0) & (y < nt) & (x >= 0) & (x < ns)
+
+
+def greet_all(nt, ns):
+    t, s = lax.axis_index("tile"), lax.axis_index("sub")
+    barrier = pltpu.get_barrier_semaphore()
+    for k in range(1, ns):
+        peer = (t, lax.rem(s + k, ns))
+        pl.semaphore_signal(barrier, inc=1, device_id=peer, device_id_type=MESH)
+    for k in range(1, nt):
+        peer = (lax.rem(t + k, nt), s)
+        pl.semaphore_signal(barrier, inc=1, device_id=peer, device_id_type=MESH)
+    count = ns + nt - 2
+    for dt, ds in DIAGONAL:
+        there = present(nt, ns, t, s, dt, ds)
+        count = count + jnp.where(there, 1, 0)
+
+        @pl.when(there)
+        def _():
+            pl.semaphore_signal(
+                barrier, inc=1, device_id=(t + dt, s + ds), device_id_type=MESH
+            )
+
+    pl.semaphore_wait(barrier, count)
+
+
+def border_copies(nt, ns, src, top, bottom, left, right, ss, rs):
+    t, s = lax.axis_index("tile"), lax.axis_index("sub")
+    rows, cols = src.shape[0], src.shape[1]
+    high, low = pl.ds(0, 2), pl.ds(rows - 2, 2)
+    first, last = pl.ds(0, 16), pl.ds(cols - 16, 16)
+    inner, before, after = pl.ds(2, rows), pl.ds(0, 2), pl.ds(rows + 2, 2)
+    pairs = [
+        (src.at[high], bottom),
+        (src.at[low], top),
+        (src.at[:, first], right.at[inner]),
+        (src.at[:, last], left.at[inner]),
+        (src.at[high, first], right.at[after]),
+        (src.at[high, last], left.at[after]),
+        (src.at[low, first], right.at[before]),
+        (src.at[low, last], left.at[before]),
+    ]
+    copies = []
+    for i, (dt, ds) in enumerate(AROUND):
+        out = present(nt, ns, t, s, dt, ds)
+        back = present(nt, ns, t, s, -dt, -ds)
+        copies.append((out, back, remote(*pairs[i], ss.at[i], rs.at[i], (t + dt, s + ds))))
+    return copies
+
+
+def begin(copies):
+    for out, _, copy in copies:
+        pl.when(out)(copy.start)
+
+
+def finish(copies):
+    for out, back, copy in copies:
+        pl.when(back)(copy.wait_recv)
+        pl.when(out)(copy.wait_send)
+
+
+def sum_near(nt, ns, value, first, ss, rs):
+    t, s = lax.axis_index("tile"), lax.axis_index("sub")
+    first[s] = value
+    copies = []
+    for k in range(1, ns):
+        peer = (t, lax.rem(s + k, ns))
+        copies.append(remote(first.at[s], first.at[s], ss.at[k], rs.at[s], peer))
+        copies[-1].start()
+    return copies
+
+
+def sum_far(nt, ns, first, second, ss1, rs1, ss2, rs2):
+    t, s = lax.axis_index("tile"), lax.axis_index("sub")
+    for k in range(1, ns):
+        p = lax.rem(s + k, ns)
+        arrived(first.at[p], ss1.at[k], rs1.at[p], (t, s))
+    total = first[0]
+    for k in range(1, ns):
+        total = total + first[k]
+    second[t] = total
+    copies = []
+    for k in range(1, nt):
+        peer = (lax.rem(t + k, nt), s)
+        copies.append(remote(second.at[t], second.at[t], ss2.at[k], rs2.at[t], peer))
+        copies[-1].start()
+    return copies
+
+
+def sum_end(nt, second, ss2, rs2):
+    t, s = lax.axis_index("tile"), lax.axis_index("sub")
+    for k in range(1, nt):
+        p = lax.rem(t + k, nt)
+        arrived(second.at[p], ss2.at[k], rs2.at[p], (t, s))
+    total = second[0]
+    for k in range(1, nt):
+        total = total + second[k]
+    return total
+
+
+def sum_scratch(nt, ns, channels, rows=2):
+    return [
+        pltpu.VMEM((ns, rows, channels), f32),
+        pltpu.VMEM((nt, rows, channels), f32),
+        dma(ns),
+        dma(ns),
+        dma(nt),
+        dma(nt),
+    ]
+
+
+def in_groups(values):
+    count, channels = values.shape
+    per = channels // G
+    row = lax.broadcasted_iota(jnp.int32, (channels, channels), 0) // per
+    col = lax.broadcasted_iota(jnp.int32, (channels, channels), 1) // per
+    same = jnp.where(row == col, 1.0, 0.0).astype(bf16)
+    parts, rest = [], values
+    for _ in range(3):
+        parts.append(rest.astype(bf16))
+        rest = rest - parts[-1].astype(f32)
+    out = [dot(part, same) for part in parts]
+    return out[0] + out[1] + out[2]
+
+
+def fold(values):
+    return jnp.sum(values.reshape(-1, 8, values.shape[-1]), axis=0)
+
+
+def row_sums(count, channels, pair):
+    def step(i, carry):
+        first, second = pair(i)
+        return carry[0] + fold(first), carry[1] + fold(second)
+
+    zero = jnp.zeros((8, channels), f32)
+    first, second = lax.fori_loop(0, count, step, (zero, zero), unroll=2)
+    return jnp.concatenate(
+        [jnp.sum(first, axis=0, keepdims=True), jnp.sum(second, axis=0, keepdims=True)], axis=0
+    )
+
+
+def sigmoid(values):
+    return 1.0 / (1.0 + jnp.exp(-values))
+
+
+def silu_slope(values):
+    sigma = sigmoid(values)
+    return sigma * (1.0 + values * (1.0 - sigma))
+
+
+def block_of(total, step, limit):
+    return max(n for n in range(step, limit + 1, step) if total % n == 0)
+
+
+def put_left_to_right(flat, triple):
+    total, channels = triple.shape[0], flat.shape[1]
+    size = block_of(total, 16, 256)
+    for start in range(0, total, size):
+        for j in range(3):
+            piece = flat[pl.ds(8 + start + j - 1, size), :]
+            triple[pl.ds(start, size), pl.ds(j * channels, channels)] = piece.astype(bf16)
+
+
+def conv_rows(triple, weight, start, size, pitch, multiply=dot):
+    taps = [triple[pl.ds(start + i * pitch, size), :] for i in range(3)]
+    return multiply(jnp.concatenate(taps, axis=1), weight)
+
+
+def dot_t(left, right):
+    return lax.dot_general(left, right, (((1,), (1,)), ((), ())), preferred_element_type=f32)
+
+
+def turned_taps(weight):
+    return jnp.concatenate([weight[8 - k] for k in range(9)], axis=1)
+
+
+def list_length(rows, pitch):
+    return 16 + rows * pitch + 16
+
+
+def fill(flat, rows, cols, row_ok, left_ok, right_ok, body, ending, opening):
+    pitch = cols + 16
+    channels = flat.shape[1]
+    place = lax.broadcasted_iota(jnp.int32, (16, channels), 0)
+    flat[pl.ds(0, 8), :] = jnp.zeros((8, channels), f32)
+    end = 8 + 16 + rows * pitch
+    flat[pl.ds(end, 24), :] = jnp.zeros((24, channels), f32)
+
+    def places(right_good, left_good):
+        good = jnp.where(place < 8, jnp.where(right_good, 1, 0), jnp.where(left_good, 1, 0))
+        return good > 0
+
+    flat[pl.ds(8, 16), :] = jnp.where(
+        places(False, left_ok & row_ok(0)), opening(), 0.0
+    )
+
+    def step(i, carry):
+        start = pl.multiple_of(24 + i * pitch, 8)
+        value = body(i)
+        good = jnp.full(value.shape, jnp.where(row_ok(i), 1, 0), jnp.int32)
+        flat[pl.ds(start, cols), :] = jnp.where(good > 0, value, 0.0)
+        good = places(right_ok & row_ok(i), left_ok & row_ok(i + 1))
+        flat[pl.ds(start + cols, 16), :] = jnp.where(good, ending(i), 0.0)
+        return carry
+
+    lax.fori_loop(0, rows, step, 0)
+
+
+def sides(left, right, i):
+    place = lax.broadcasted_iota(jnp.int32, right.shape[1:], 0)
+    return jnp.where(place < 8, right[i].astype(f32), left[i + 1].astype(f32))
+
+
+def clear(*refs):
+    for ref in refs:
+        ref[...] = jnp.zeros_like(ref)
+
+
+def outer_forward_kernel(
+    nt, ns, img, w1, w2, vec, gains, out, pooled, act1_out, act2_out, hidden, stats, gains_out,
+    body, left, right, flat, act1, act2, rowsum, border_ss, border_rs, keep, gain_ss, gain_rs, *sums
+):
+    rows, cols, channels = img.shape
+    pitch = cols + 16
+    t, s = lax.axis_index("tile"), lax.axis_index("sub")
+    sums1, sums2 = sums[:6], sums[6:]
+    count = float(nt * ns * rows * cols * (channels // G))
+    clear(body, left, right)
+    greet_all(nt, ns)
+    top, bottom = body.at[pl.ds(0, 2)], body.at[pl.ds(rows + 2, 2)]
+    border = border_copies(nt, ns, img, top, bottom, left, right, border_ss, border_rs)
+    begin(border)
+    pixel = lambda i: img[i].astype(f32)
+    local1 = row_sums(rows, channels, lambda i: (pixel(i), pixel(i) * pixel(i)))
+    copies = sum_near(nt, ns, local1, sums1[0], sums1[2], sums1[3])
+    copies += sum_far(nt, ns, sums1[0], sums1[1], *sums1[2:])
+    gains_out[s] = gains[...]
+    for k in range(1, ns):
+        block, peer = gains_out.at[s], (t, lax.rem(s + k, ns))
+        copies.append(remote(block, block, gain_ss.at[k], gain_rs.at[s], peer))
+        copies[-1].start()
+
+    def inner(i, carry):
+        body[i + 2] = img[i]
+        return carry
+
+    lax.fori_loop(0, rows, inner, 0)
+    total1 = sum_end(nt, sums1[1], sums1[4], sums1[5])
+
+    def moments(total):
+        grouped = in_groups(total) / count
+        center = grouped[0:1]
+        return center, lax.rsqrt(grouped[1:2] - center * center + EPSILON)
+
+    center1, std1 = moments(total1)
+    scale1 = std1 * vec[0:1]
+    shift1 = vec[1:2] - center1 * scale1
+    finish(border)
+
+    def first_act(values):
+        normed = values.astype(f32) * scale1 + shift1
+        return normed * sigmoid(normed)
+
+    ok = lambda lift: (
+        lambda i: (t * rows + i - lift >= 0) & (t * rows + i - lift < nt * rows)
+    )
+    fill(
+        flat, rows + 4, cols, ok(2), s > 0, s < ns - 1,
+        lambda i: first_act(body[i]),
+        lambda i: first_act(sides(left, right, i)),
+        lambda: first_act(left[0]),
+    )
+    put_left_to_right(flat, act1)
+    saved = [pltpu.make_async_copy(act1, act1_out, keep.at[0])]
+    saved[0].start()
+    length = list_length(rows + 2, pitch)
+    size = block_of(length, 16, 700)
+    for start in range(0, length, size):
+        hidden[pl.ds(start, size), :] = conv_rows(act1, w1[...], start, size, pitch) + vec[4:5]
+
+    def hidden_row(i):
+        return hidden[pl.ds(pl.multiple_of(16 + (i + 1) * pitch, 16), cols), :]
+
+    local2 = row_sums(rows, channels, lambda i: (hidden_row(i), hidden_row(i) * hidden_row(i)))
+    copies += sum_near(nt, ns, local2, sums2[0], sums2[2], sums2[3])
+    copies += sum_far(nt, ns, sums2[0], sums2[1], *sums2[2:])
+    total2 = sum_end(nt, sums2[1], sums2[4], sums2[5])
+    center2, std2 = moments(total2)
+    scale2 = std2 * vec[2:3]
+    shift2 = vec[3:4] - center2 * scale2
+    stats[...] = jnp.concatenate(
+        [center1, std1, center2, std2, total2, jnp.zeros_like(total2)], axis=0
+    )
+
+    def second_act(start, amount):
+        normed = hidden[pl.ds(start, amount), :] * scale2 + shift2
+        return normed * sigmoid(normed)
+
+    at = lambda i: pl.multiple_of(16 + i * pitch, 16)
+    fill(
+        flat, rows + 2, cols, ok(1), s > 0, s < ns - 1,
+        lambda i: second_act(at(i), cols),
+        lambda i: second_act(at(i) + cols, 16),
+        lambda: second_act(0, 16),
+    )
+    put_left_to_right(flat, act2)
+    saved.append(pltpu.make_async_copy(act2, act2_out, keep.at[1]))
+    saved[1].start()
+    lc = cols // POOL
+    for start in range(0, rows, 2 * POOL):
+        grown = conv_rows(act2, w2[...], 16 + start * pitch, 2 * POOL * pitch, pitch)
+        grown = grown.reshape(2 * POOL, pitch, channels)[:, :cols]
+        grown = grown + img[pl.ds(start, 2 * POOL)].astype(f32)
+        out[pl.ds(start, 2 * POOL)] = grown.astype(bf16)
+        for half in range(2):
+            added = jnp.sum(grown[half * POOL : (half + 1) * POOL], axis=0)
+            means = []
+            for n in range(channels // 128):
+                rowsum[n] = added[:, n * 128 : (n + 1) * 128]
+                mean = rowsum[n, pl.ds(0, lc, stride=POOL), :]
+                for k in range(1, POOL):
+                    mean = mean + rowsum[n, pl.ds(k, lc, stride=POOL), :]
+                means.append(mean * (1.0 / (POOL * POOL)))
+            pooled[start // POOL + half] = jnp.concatenate(means, axis=1)
+    for k in range(1, ns):
+        p = lax.rem(s + k, ns)
+        arrived(gains_out.at[p], gain_ss.at[k], gain_rs.at[p], (t, s))
+    for copy in copies:
+        copy.wait_send()
+    for copy in saved:
+        copy.wait()
+
+
+def outer_forward(img, w1, w2, vec, gains, cid):
+    nt, ns = lax.axis_size("tile"), lax.axis_size("sub")
+    rows, cols, channels = img.shape
+    pitch = cols + 16
+    long1, long2 = list_length(rows + 4, pitch), list_length(rows + 2, pitch)
+    shape = jax.ShapeDtypeStruct
+    return pl.pallas_call(
+        functools.partial(outer_forward_kernel, nt, ns),
+        out_shape=(
+            shape(img.shape, bf16),
+            shape((rows // POOL, cols // POOL, channels), f32),
+            shape((long1, 3 * channels), bf16),
+            shape((long2, 3 * channels), bf16),
+            shape((long2, channels), f32),
+            shape((8, channels), f32),
+            shape((ns,) + gains.shape, f32),
+        ),
+        in_specs=[in_vmem()] * 5,
+        out_specs=(in_vmem(),) * 2 + (anywhere(),) * 2 + (in_vmem(),) * 3,
+        scratch_shapes=[
+            pltpu.VMEM((rows + 4, cols, channels), bf16),
+            pltpu.VMEM((rows + 5, 16, channels), bf16),
+            pltpu.VMEM((rows + 5, 16, channels), bf16),
+            pltpu.VMEM((long1 + 16, channels), f32),
+            pltpu.VMEM((long1, 3 * channels), bf16),
+            pltpu.VMEM((long2, 3 * channels), bf16),
+            pltpu.VMEM((channels // 128, cols, 128), f32),
+            dma(8),
+            dma(8),
+            dma(2),
+            dma(ns),
+            dma(ns),
+        ]
+        + sum_scratch(nt, ns, channels) * 2,
+        cost_estimate=SHORT,
+        compiler_params=params(cid),
+        name="outer_forward",
+    )(img, w1, w2, vec, gains)
+
+
+def kernel_grads(triple, grads_t, start, size, pitch, out, between=()):
+    for i in range(3):
+        rows = triple[pl.ds(start + i * pitch, size), :]
+        taps = dot(grads_t[...], rows).T.astype(bf16)
+        out[pl.ds(i * taps.shape[0], taps.shape[0]), :] = taps
+        for action in between[i : i + 1]:
+            action()
+
+
+def outer_backward_kernel(
+    nt, ns, cot, img, w2, w1, vec, stats, hidden, wide, tokens, gains, pooled, lifted, lift_weight,
+    attn_in, grad_q_t, grad_kv, grad_cq_w, grad_ck, grad_cv, act1_in, act2_in, outer_grad, tall_out, wide_out, tokens_out, sum2_out, sum1_out, back_out,
+    spread, grad2, body, left, right, flat, act1, act2, triple, inner_t, slope, own2, own1, tall,
+    border_ss, border_rs, keep, token_ss, token_rs, *scratch
+):
+    rows, cols, channels = img.shape
+    pitch = cols + 16
+    lr, lc = rows // POOL, cols // POOL
+    t, s = lax.axis_index("tile"), lax.axis_index("sub")
+    sums2, sums1, scratch = scratch[:6], scratch[6:12], scratch[12:]
+    copies = Copies()
+    weights = []
+    for x, out in ((wide, wide_out), (tall, tall_out)):
+        weights.append(TileSum(nt, copies, x, out, *scratch[:3], scratch[3:11]))
+        scratch = scratch[11:]
+    second = FullSum(nt, ns, copies, own2, sum2_out, *scratch[:5], scratch[5:17])
+    scratch = scratch[17:]
+    first = FullSum(nt, ns, copies, own1, sum1_out, *scratch[:5], scratch[5:17])
+    count = float(nt * ns * rows * cols * (channels // G))
+    held = [
+        pltpu.make_async_copy(act2_in, act2, keep.at[0]),
+        pltpu.make_async_copy(act1_in, act1, keep.at[1]),
+    ]
+    for copy in held:
+        copy.start()
+    clear(body, left, right)
+    greet_all(nt, ns)
+    weights[0].start()
+    width = lifted.shape[1]
+    shrunk = dot_t(lifted[...], lift_weight[...]) * (1.0 / (POOL * POOL))
+
+    def widen(i):
+        for n in range(channels // 128):
+            part = shrunk[i * lc : (i + 1) * lc, n * 128 : (n + 1) * 128]
+            for k in range(POOL):
+                spread[i, n, pl.ds(k, lc, stride=POOL), :] = part
+
+    for i in range(lr):
+        widen(i)
+
+    def outer(i):
+        parts = [spread[i // POOL, n] for n in range(channels // 128)]
+        return cot[i].astype(f32) + jnp.concatenate(parts, axis=1)
+
+    def round_outer(i, carry):
+        value = outer(i).astype(bf16)
+        grad2[i] = value
+        body[i + 2] = value
+        return carry
+
+    lax.fori_loop(0, rows, round_outer, 0)
+    top, bottom = body.at[pl.ds(0, 2)], body.at[pl.ds(rows + 2, 2)]
+    border = border_copies(nt, ns, grad2, top, bottom, left, right, border_ss, border_rs)
+    begin(border)
+    tokens_out[s] = tokens[s]
+    for k in range(1, ns):
+        p = lax.rem(s + k, ns)
+        copies.send(tokens.at[p], tokens_out.at[s], token_ss.at[k], token_rs.at[k], (t, p))
+    features = grad_q_t.shape[0]
+    heads = features // HD
+    attn_t = attn_in[...].T
+    tall[pl.ds(0, width), :] = dot_t(attn_t, grad_q_t[...]).astype(bf16)
+    both = dot(attn_t, grad_kv[...])
+    for n in range(2):
+        lanes = [both[:, (2 * h + n) * HD : (2 * h + n + 1) * HD] for h in range(heads)]
+        part = jnp.concatenate(lanes, axis=1) if heads > 1 else lanes[0]
+        tall[pl.ds((1 + n) * width, width), :] = part.astype(bf16)
+    used = 3 * width
+    for ref in (grad_cq_w, grad_ck, grad_cv):
+        tall[pl.ds(used, ref.shape[0]), :] = ref[...]
+        used += ref.shape[0]
+    if used < tall.shape[0]:
+        tall[pl.ds(used, tall.shape[0] - used), :] = jnp.zeros(
+            (tall.shape[0] - used, features), bf16
+        )
+    weights[1].start()
+    total = rows * pitch
+
+    def turned(row):
+        for start in range(0, rows, 8):
+            block = [row(start + k) for k in range(8)]
+            gap = jnp.zeros((16, channels), bf16)
+            piece = jnp.concatenate([p for b in block for p in (b, gap)], axis=0)
+            inner_t[:, pl.ds(start * pitch, 8 * pitch)] = piece.T
+
+    def pad_below(ref, used):
+        if used < ref.shape[0]:
+            ref[pl.ds(used, ref.shape[0] - used), :] = jnp.zeros(
+                (ref.shape[0] - used, channels), bf16
+            )
+
+    taps = 9 * channels
+    turned(lambda i: grad2[i])
+    held[0].wait()
+    kernel_grads(act2, inner_t, 16, total, pitch, own2)
+    lift_grad = dot(pooled[...].T, lifted[...]).astype(bf16)
+    for n in range(width // channels):
+        own2[pl.ds(taps + n * channels, channels), :] = lift_grad[
+            :, n * channels : (n + 1) * channels
+        ]
+    pad_below(own2, taps + width)
+    second.start()
+    finish(border)
+    ok = lambda lift_by: (
+        lambda i: (t * rows + i - lift_by >= 0) & (t * rows + i - lift_by < nt * rows)
+    )
+    fill(
+        flat, rows + 4, cols, ok(2), s > 0, s < ns - 1,
+        lambda i: body[i].astype(f32),
+        lambda i: sides(left, right, i),
+        lambda: left[0].astype(f32),
+    )
+    put_left_to_right(flat, triple)
+    second.cross()
+    center1, std1, center2, std2 = (stats[k : k + 1] for k in range(4))
+    gain1, bias1, gain2, bias2 = (vec[k : k + 1] for k in range(4))
+    length = list_length(rows + 2, pitch)
+    size = block_of(length, 16, 700)
+    w2t = turned_taps(w2)
+    for start in range(0, length, size):
+        hat = (hidden[pl.ds(start, size), :] - center2) * std2
+        slope[pl.ds(start, size), :] = conv_rows(
+            triple, w2t, start, size, pitch, dot_t
+        ) * silu_slope(hat * gain2 + bias2)
+        if start == size:
+            weights[0].add([0])
+    weights[0].add([1])
+
+    at = lambda i: pl.multiple_of(16 + i * pitch, 16)
+
+    def pair2(i):
+        place = pl.ds(at(i + 1), cols)
+        value = slope[place, :]
+        return value, value * ((hidden[place, :] - center2) * std2)
+
+    local2 = jnp.concatenate([row_sums(rows, channels, pair2), gains[...]], axis=0)
+    plain = sum_near(nt, ns, local2, sums2[0], sums2[2], sums2[3])
+    plain += sum_far(nt, ns, sums2[0], sums2[1], *sums2[2:])
+    second.spread()
+    steps = weights[0].steps()
+    weights[0].add(steps[2:5])
+    back2 = sum_end(nt, sums2[1], sums2[4], sums2[5])
+    back2, gains_total = back2[:2], back2[2:]
+    means2 = in_groups(back2 * gain2) / count
+
+    def grad_hidden(start, amount):
+        hat = (hidden[pl.ds(start, amount), :] - center2) * std2
+        value = slope[pl.ds(start, amount), :] * gain2 - means2[0:1] - hat * means2[1:2]
+        return std2 * value
+
+    fill(
+        flat, rows + 2, cols, ok(1), s > 0, s < ns - 1,
+        lambda i: grad_hidden(at(i), cols),
+        lambda i: grad_hidden(at(i) + cols, 16),
+        lambda: grad_hidden(0, 16),
+    )
+    weights[0].add(steps[5:6])
+    turned(lambda i: flat[pl.ds(24 + (i + 1) * pitch, cols), :].astype(bf16))
+    held[1].wait()
+    between = [
+        lambda: weights[0].add(steps[6:]),
+        lambda: weights[1].add([0]),
+        lambda: weights[1].add([1]),
+    ]
+    kernel_grads(act1, inner_t, 16 + pitch, total, pitch, own1, between)
+    pad_below(own1, taps)
+    first.start()
+    second.settle()
+    put_left_to_right(flat, triple.at[pl.ds(0, length)])
+    first.cross()
+    hat1 = lambda i: (img[i].astype(f32) - center1) * std1
+    step = 2 * POOL
+    w1t = turned_taps(w1)
+    for start in range(0, rows, step):
+        value = conv_rows(triple, w1t, 16 + start * pitch, step * pitch, pitch, dot_t)
+        value = value.reshape(step, pitch, channels)[:, :cols]
+        hat = (img[pl.ds(start, step)].astype(f32) - center1) * std1
+        outer_grad[pl.ds(start, step)] = value * silu_slope(hat * gain1 + bias1)
+        if start == step:
+            weights[1].add([2])
+            weights[0].share([0])
+    weights[1].add([3])
+    weights[0].share([1])
+    local1 = row_sums(rows, channels, lambda i: (outer_grad[i], outer_grad[i] * hat1(i)))
+    plain += sum_near(nt, ns, local1, sums1[0], sums1[2], sums1[3])
+    first.spread()
+    plain += sum_far(nt, ns, sums1[0], sums1[1], *sums1[2:])
+    weights[1].add([4])
+    weights[0].share([2])
+    back1 = sum_end(nt, sums1[1], sums1[4], sums1[5])
+    means1 = in_groups(back1 * gain1) / count
+    weights[1].add([5])
+    weights[0].share([3])
+
+    def last(i, carry):
+        value = outer_grad[i] * gain1 - means1[0:1] - hat1(i) * means1[1:2]
+        outer_grad[i] = outer(i) + std1 * value
+        return carry
+
+    lax.fori_loop(0, rows, last, 0)
+    back_out[...] = jnp.concatenate(
+        [back1, back2, means2, jnp.zeros_like(means2), gains_total], axis=0
+    )
+    for step in steps[6:]:
+        weights[1].add([step])
+    weights[1].share([0])
+    first.settle()
+    second.share()
+    for i, step in enumerate(steps[4:]):
+        weights[0].share([step])
+        weights[1].share([1 + i])
+    first.share()
+    second.relay()
+    weights[1].share(steps[1 + len(steps[4:]) :])
+    for k in range(1, ns):
+        block = tokens_out.at[lax.rem(s + ns - k, ns)]
+        arrived(block, token_ss.at[k], token_rs.at[k], (t, s))
+    first.relay()
+    second.end()
+    for each in weights:
+        each.end()
+    first.end()
+    copies.finish()
+    for copy in plain:
+        copy.wait_send()
+
+
+def outer_backward(
+    cot, img, w2, w1, vec, stats, hidden, wide, tokens, gains, pooled, lifted, lift_weight,
+    attn_in, grad_q_t, grad_kv, grad_cq_w, grad_ck, grad_cv, act1, act2, cid
+):
+    nt, ns = lax.axis_size("tile"), lax.axis_size("sub")
+    rows, cols, channels = img.shape
+    pitch = cols + 16
+    long1, long2 = list_length(rows + 4, pitch), list_length(rows + 2, pitch)
+    shape = jax.ShapeDtypeStruct
+    step = 16 * nt * ns
+    width, features = attn_in.shape[1], grad_q_t.shape[0]
+    rows2 = round_up(9 * channels + width, step)
+    tall = (round_up(4 * width + 2 * grad_ck.shape[0], 16 * nt), features)
+    rows1 = round_up(9 * channels, step)
+    return pl.pallas_call(
+        functools.partial(outer_backward_kernel, nt, ns),
+        out_shape=(
+            shape(img.shape, f32),
+            shape(tall, bf16),
+            shape(wide.shape, bf16),
+            shape(tokens.shape, bf16),
+            shape((rows2, channels), bf16),
+            shape((rows1, channels), bf16),
+            shape((8 + gains.shape[0], channels), f32),
+        ),
+        in_specs=[in_vmem()] * 19 + [anywhere()] * 2,
+        out_specs=(in_vmem(),) * 7,
+        scratch_shapes=[
+            pltpu.VMEM((rows // POOL, channels // 128, cols, 128), f32),
+            pltpu.VMEM((rows, cols, channels), bf16),
+            pltpu.VMEM((rows + 4, cols, channels), bf16),
+            pltpu.VMEM((rows + 5, 16, channels), bf16),
+            pltpu.VMEM((rows + 5, 16, channels), bf16),
+            pltpu.VMEM((long1 + 16, channels), f32),
+            pltpu.VMEM((long1, 3 * channels), bf16),
+            pltpu.VMEM((long2, 3 * channels), bf16),
+            pltpu.VMEM((long1, 3 * channels), bf16),
+            pltpu.VMEM((channels, rows * pitch), bf16),
+            pltpu.VMEM((long2, channels), f32),
+            pltpu.VMEM((rows2, channels), bf16),
+            pltpu.VMEM((rows1, channels), bf16),
+            pltpu.VMEM(tall, bf16),
+            dma(8),
+            dma(8),
+            dma(2),
+            dma(ns),
+            dma(ns),
+        ]
+        + sum_scratch(nt, ns, channels, 2 + gains.shape[0])
+        + sum_scratch(nt, ns, channels)
+        + TileSum.scratch(nt, *wide.shape)
+        + TileSum.scratch(nt, *tall)
+        + FullSum.scratch(nt, ns, rows2, channels)
+        + FullSum.scratch(nt, ns, rows1, channels),
+        cost_estimate=SHORT,
+        compiler_params=params(cid, 62),
+        name="outer_backward",
+    )(
+        cot, img, w2, w1, vec, stats, hidden, wide, tokens, gains, pooled, lifted, lift_weight,
+        attn_in, grad_q_t, grad_kv, grad_cq_w, grad_ck, grad_cv, act1, act2,
+    )
+
+
+def finish_kernel(text, up, down, *refs):
+    q, k, v, cq, ck, cv, o, co, second, first = refs[:10]
+    lift, refs = refs[10:-13], refs[-13:]
+    for src, dst in zip((q, k, v, cq, o, co, second, first, up, down), refs[:10]):
+        dst[...] = src[...].astype(f32)
+    turned = text[...].T
+    refs[10][...] = dot(turned, ck[...])
+    refs[11][...] = dot(turned, cv[...])
+    refs[12][...] = jnp.concatenate([part[...].astype(f32) for part in lift], axis=1)
+
+
+def finish_grads(text, up, down, tall, wide, second, first, taps, text_rows):
+    features, width = tall.shape[1], wide.shape[1]
+    channels = first.shape[1]
+    steps = features // 16
+    row = lambda size, lanes, skip=0: pl.BlockSpec((size, lanes), lambda i: (skip + i, 0))
+    size = width // steps
+    tall_specs = [row(size, features, n * steps) for n in range(4)]
+    start = 4 * width // text_rows
+    tall_specs += [
+        pl.BlockSpec((text_rows, features), lambda i, n=n: (start + n, 0)) for n in range(2)
+    ]
+    wide_specs = [row(16, width, n * steps) for n in range(2)]
+    size = taps // steps
+    lift_size = channels // steps
+    lift_specs = [
+        row(lift_size, channels, taps // lift_size + n * steps) for n in range(width // channels)
+    ]
+    full = text.shape[1]
+    up_specs = [row(w.shape[0] // steps, w.shape[1]) for w in (up, down)]
+    in_specs = [pl.BlockSpec((text.shape[0], full // steps), lambda i: (0, i))] + up_specs
+    in_specs += tall_specs + wide_specs + [row(size, channels)] * 2 + lift_specs
+    shape = lambda *dims: jax.ShapeDtypeStruct(dims, f32)
+    return pl.pallas_call(
+        finish_kernel,
+        grid=(steps,),
+        out_shape=(shape(width, features),) * 4
+        + (shape(features, width),) * 2
+        + (shape(taps, channels),) * 2
+        + (shape(*up.shape), shape(*down.shape))
+        + (shape(full, features), shape(full, features), shape(channels, width)),
+        in_specs=in_specs,
+        out_specs=[row(width // steps, features)] * 4
+        + [row(16, width)] * 2
+        + [row(size, channels)] * 2
+        + up_specs
+        + [row(full // steps, features)] * 2
+        + [row(lift_size, width)],
+        cost_estimate=SHORT,
+        compiler_params=params(),
+        name="finish_grads",
+    )(text, up, down, *[tall] * 6, *[wide] * 2, second, first, *[second] * len(lift_specs))
 
 
 def time_embed(time_steps, channels):
@@ -556,49 +1489,6 @@
     )
     angles = time_steps.astype(f32)[:, None] * frequency[None, :]
     return jnp.concatenate([jnp.sin(angles), jnp.cos(angles)], axis=1)
-
-
-def conv_valid(padded, kernel):
-    return lax.conv_general_dilated(
-        padded,
-        kernel,
-        (1, 1),
-        "VALID",
-        dimension_numbers=("NHWC", "HWIO", "NHWC"),
-        preferred_element_type=f32,
-    )
-
-
-def conv_transposed(padded, kernel):
-    return conv_valid(padded, jnp.transpose(kernel[::-1, ::-1], (0, 1, 3, 2)))
-
-
-def conv_kernel_grad(padded_in, grad_out):
-    rows, cols = grad_out.shape[1], grad_out.shape[2]
-    taps = []
-    for y in range(3):
-        for x in range(3):
-            window = padded_in[:, y : y + rows, x : x + cols, :]
-            taps.append(
-                jnp.einsum("bhwc,bhwd->cd", window, grad_out, preferred_element_type=f32)
-            )
-    return jnp.stack(taps).reshape(3, 3, padded_in.shape[3], grad_out.shape[3])
-
-
-def by_group(values):
-    channels = values.shape[-1]
-    grouped = values.reshape(values.shape[:-1] + (G, channels // G))
-    return jnp.repeat(jnp.sum(grouped, axis=-1), channels // G, axis=-1)
-
-
-def pixel_sums(first, second):
-    return jnp.stack([jnp.sum(first, axis=(1, 2)), jnp.sum(second, axis=(1, 2))], axis=1)
-
-
-def group_stats(sums, group_size):
-    center = by_group(sums[:, 0]) / group_size
-    inv_std = lax.rsqrt(by_group(sums[:, 1]) / group_size - center * center + EPSILON)
-    return center[:, None, None, :], inv_std[:, None, None, :]
 
 
 def layer_stats(values, gain):
@@ -619,21 +1509,12 @@
     return grad_in, jnp.sum(grad_out * normed, axis=0)
 
 
-def silu_grad(values):
-    sigma = jax.nn.sigmoid(values)
-    return sigma * (1.0 + values * (1.0 - sigma))
-
-
 def gelu_tanh(values):
     return jax.nn.gelu(values, approximate=True)
 
 
 def weight_grad(inputs, grads):
     return lax.dot_general(inputs, grads, (((0,), (0,)), ((), ())), preferred_element_type=f32)
-
-
-def dot_t(left, right):
-    return lax.dot_general(left, right, (((1,), (1,)), ((), ())), preferred_element_type=f32)
 
 
 def cross_scores(queries, keys, text_mask):
@@ -681,10 +1562,7 @@
     own = batch * lr * lc
     length = ns * lr * lc
     pixels = rows * cols * nt * ns
-    group_size = pixels * (channels // G)
-
-    image_ext = bordered(outer_image, 2)
-    cotan_ext = bordered(outer_cotan, 2)
+
 
     def whole_tokens(values):
         full = lax.all_gather(values, "sub", axis=2, tiled=True)
@@ -695,33 +1573,29 @@
     _, inner_own = whole_tokens(inner_image)
     cotan_full, cotan_own = whole_tokens(inner_cotan)
     cotan_full = jnp.transpose(cotan_full, (2, 0, 1, 3, 4)).reshape(ns * own, width)
-    gains = lax.all_gather(
-        jnp.stack([attn_gain, cross_gain, mlp_gain]), "sub", axis=1, tiled=True
-    )
+    own_gains = jnp.stack([attn_gain, cross_gain, mlp_gain])
 
     time_act = jax.nn.silu(time_embed(time_steps, channels))
     time_shift = jnp.dot(time_act, time_weight.astype(f32), precision=precise)
-    outer_f = outer_image.astype(f32)
-    center1, std1 = group_stats(
-        total_all(pixel_sums(outer_f, outer_f * outer_f), 0), group_size
-    )
-    hat1 = lambda v: (v.astype(f32) - center1) * std1
-    norm1 = lambda v: hat1(v) * first_gain + first_bias
-    act1 = jnp.where(
-        inside(image_ext.shape, 2), jax.nn.silu(norm1(image_ext)), 0.0
-    ).astype(bf16)
-    hidden = conv_valid(act1, conv_first) + time_shift[:, None, None, :]
-    middle = trim(hidden, 1)
-    sums2 = total_all(pixel_sums(middle, middle * middle), 1)
-    center2, std2 = group_stats(sums2, group_size)
-    hat2 = lambda v: (v - center2) * std2
-    norm2 = lambda v: hat2(v) * second_gain + second_bias
-    act2 = jnp.where(inside(hidden.shape, 1), jax.nn.silu(norm2(hidden)), 0.0).astype(bf16)
-    outer_sum = outer_f + conv_valid(act2, conv_second)
-    pooled = jnp.mean(
-        outer_sum.reshape(batch, lr, POOL, lc, POOL, channels), axis=(2, 4)
-    ).astype(bf16)
-    pooled = pooled.reshape(own, channels)
+    vectors = jnp.zeros((batch, 8, channels), f32)
+    for i, vector in enumerate([first_gain, first_bias, second_gain, second_bias]):
+        vectors = vectors.at[:, i].set(vector)
+    vectors = vectors.at[:, 4].set(time_shift)
+    as_rows = lambda w: w.reshape(9 * channels, channels)
+    forward = [
+        outer_forward(
+            outer_image[b],
+            as_rows(conv_first),
+            as_rows(conv_second),
+            vectors[b],
+            own_gains,
+            20 + b,
+        )
+        for b in range(batch)
+    ]
+    outer_out = jnp.stack([f[0] for f in forward])
+    gains = jnp.transpose(forward[0][6], (1, 0, 2)).reshape(3, width)
+    pooled = jnp.stack([f[1] for f in forward]).astype(bf16).reshape(own, channels)
 
     stream_in = inner_own.astype(f32) + dot(pooled, lift_weight).astype(bf16).astype(f32)
     attn_low, attn_hat, attn_std = layer_stats(stream_in, gains[0])
@@ -781,8 +1655,15 @@
 
     grad_act = dot_t(cotan_full, down_weight)
     grad_lift_up = gelu_pull(grad_act)[0].astype(bf16)
+    grad_mlp_in = dot_t(grad_lift_up, up_weight).astype(bf16)
+    grad_down = weight_grad(activated, cotan_full).astype(bf16)
+    grad_up = weight_grad(mlp_in, grad_lift_up).astype(bf16)
+    grad_mlp_in, grad_down, grad_up = lax.optimization_barrier(
+        (grad_mlp_in, grad_down, grad_up)
+    )
+    grad_down, grad_up = lax.psum((grad_down, grad_up), "tile")
     grad_mid, grad_mlp_gain = layer_back(
-        scatter_sub(dot_t(grad_lift_up, up_weight), 9), mlp_hat, mlp_std, gains[2]
+        scatter_sub(grad_mlp_in, 9), mlp_hat, mlp_std, gains[2]
     )
     grad_after_cross = cotan_own.astype(f32) + grad_mid
     grad_cross_full = gather_sub(grad_after_cross.astype(bf16), 10).reshape(ns * own, width)
@@ -812,7 +1693,19 @@
     grad_mixed_t = dot_t(out_weight, grad_attn_full).astype(bf16)
     head_d = swap_heads(per_sample(grad_mixed_t, True), False, 13)
     head_dq, head_dkv = flash_back(head_q, head_d, head_mixed_f, head_lse, head_kv)
-    grad_q_t, grad_kv = dqkv_home(head_dq, head_dkv, 14)
+    down = dot(activated, down_weight).astype(bf16)
+    grad_q_t, grad_kv, down_own, wide, grad_cq_w = dqkv_home(
+        head_dq,
+        head_dkv,
+        down,
+        mixed_t,
+        grad_attn_full,
+        cross_mixed,
+        grad_cross_full,
+        cross_in,
+        grad_cq,
+        14,
+    )
     grad_q_t, grad_kv = all_samples(grad_q_t, True), all_samples(grad_kv, False)
     grad_attn_in = weight_grad(grad_q_t, query_weight.T) + dot_t(grad_kv, kv_weight)
     grad_mid, grad_attn_gain = layer_back(
@@ -821,107 +1714,91 @@
     inner_grad = grad_after_attn + grad_mid
     grad_lifted = inner_grad.astype(bf16)
 
-    grad_lift = weight_grad(pooled, grad_lifted)
-    grad_pooled = dot_t(grad_lifted, lift_weight) / (POOL * POOL)
-    pooled_ext = bordered(grad_pooled.reshape(batch, lr, lc, channels), 1)
-    spread = jnp.repeat(jnp.repeat(pooled_ext, POOL, axis=1), POOL, axis=2)
-    grad_outer = cotan_ext.astype(f32) + trim(spread, POOL - 2)
-    grad_conv2 = jnp.where(inside(grad_outer.shape, 2), grad_outer, 0.0).astype(bf16)
-    slope2 = conv_transposed(grad_conv2, conv_second) * silu_grad(norm2(hidden))
-    back2 = total_all(pixel_sums(trim(slope2, 1), trim(slope2 * hat2(hidden), 1)), 16)
-
-    def group_means(back, gain):
-        spread_out = lambda v: (by_group(v * gain) / group_size)[:, None, None, :]
-        return spread_out(back[:, 0]), spread_out(back[:, 1])
-
-    mean_grad2, mean_cross2 = group_means(back2, second_gain)
-    grad_hidden = std2 * (slope2 * second_gain - mean_grad2 - hat2(hidden) * mean_cross2)
-    grad_conv1 = jnp.where(inside(grad_hidden.shape, 1), grad_hidden, 0.0).astype(bf16)
-    flat = lambda v: v[:, 0, 0, :]
-    hat2_sum = flat(std2) * (sums2[:, 0] - pixels * flat(center2))
-    hidden_sum = flat(std2) * (
-        second_gain * back2[:, 0] - pixels * flat(mean_grad2) - flat(mean_cross2) * hat2_sum
+    text_rows = grad_ck.shape[0] * grad_ck.shape[1]
+    grad_ck, grad_cv = (v.reshape(text_rows, features).astype(bf16) for v in (grad_ck, grad_cv))
+    inner_sum = after_cross + down_own
+    tokens = jnp.stack([inner_sum.astype(bf16), grad_lifted])
+    tokens = tokens.reshape(2, own, ns, features).transpose(2, 0, 1, 3)
+    gain_rows = jnp.stack([grad_attn_gain, grad_cross_gain, grad_mlp_gain]).reshape(-1, channels)
+    by_tap = lambda w: w.reshape(9, channels, channels)
+    backward = []
+    for b in range(batch):
+        once = (lambda v: v) if b == 0 else jnp.zeros_like
+        sample = lambda v: v.reshape(batch, lr * lc, -1)[b]
+        backward.append(
+            outer_backward(
+                outer_cotan[b],
+                outer_image[b],
+                by_tap(conv_second),
+                by_tap(conv_first),
+                vectors[b],
+                forward[b][5],
+                forward[b][4],
+                once(wide),
+                once(tokens),
+                once(gain_rows),
+                sample(pooled),
+                sample(grad_lifted),
+                lift_weight,
+                attn_in,
+                once(grad_q_t),
+                once(grad_kv),
+                once(grad_cq_w),
+                once(grad_ck),
+                once(grad_cv),
+                forward[b][2],
+                forward[b][3],
+                20 + batch + b,
+            )
+        )
+    outer_grad = jnp.stack([f[0] for f in backward])
+    tall, wide, tokens = backward[0][1:4]
+    tokens = tokens.reshape(ns, 2, batch, lr, lc, features).transpose(1, 2, 3, 0, 4, 5)
+    inner_out, inner_grad = tokens.reshape(2, batch, length, features)
+    inner_grad = inner_grad.astype(f32)
+    if batch > 1:
+        sum2, sum1 = (
+            sum(f[k].astype(f32) for f in backward).astype(bf16) for k in (4, 5)
+        )
+    else:
+        sum2, sum1 = backward[0][4:6]
+    ends = finish_grads(
+        text_states.reshape(text_rows, -1),
+        grad_up,
+        grad_down,
+        tall,
+        wide,
+        sum2,
+        sum1,
+        9 * channels,
+        text_rows,
+    )
+    grad_q_w, grad_k_w, grad_v_w, grad_cq_w, grad_o_w, grad_co_w = ends[:6]
+    grad_conv_second, grad_conv_first = (v.reshape(conv_first.shape) for v in ends[6:8])
+    grad_up, grad_down = ends[8:10]
+    grad_ck_w, grad_cv_w, grad_lift = ends[10:]
+    stats = jnp.stack([f[5] for f in forward])
+    back = jnp.stack([f[6] for f in backward])
+    grad_gains = back[0, 8:].reshape(3, width)
+    center2, std2, hidden_total = stats[:, 2], stats[:, 3], stats[:, 4]
+    hat2_total = std2 * (hidden_total - pixels * center2)
+    hidden_sum = std2 * (
+        second_gain * back[:, 2] - pixels * back[:, 4] - back[:, 5] * hat2_total
     )
     grad_time = jnp.dot(time_act.T, hidden_sum, precision=precise)
-    slope1 = conv_transposed(grad_conv1, conv_first) * silu_grad(norm1(outer_image))
-    back1 = total_all(pixel_sums(slope1, slope1 * hat1(outer_image)), 17)
-    mean_grad1, mean_cross1 = group_means(back1, first_gain)
-    outer_grad = trim(grad_outer, 2) + std1 * (
-        slope1 * first_gain - mean_grad1 - hat1(outer_image) * mean_cross1
-    )
-
-    down = dot(activated, down_weight).astype(bf16)
-    inner_sum = after_cross + lax.psum_scatter(
-        down, "sub", scatter_dimension=0, tiled=True
-    ).astype(f32)
-
-    def by_feature(values):
-        full = lax.all_gather(values.astype(bf16), "sub", axis=0)
-        mine = lax.dynamic_slice_in_dim(full, s * features, features, axis=2)
-        mine = mine.reshape(ns, batch, lr, lc, features)
-        return jnp.transpose(mine, (1, 2, 0, 3, 4)).reshape(batch, length, features)
-
-    inner_out = by_feature(inner_sum)
-    inner_grad = by_feature(inner_grad).astype(f32)
-
-    over_tile = lambda *values: tuple(
-        v.astype(f32) for v in lax.psum(tuple(v.astype(bf16) for v in values), "tile")
-    )
-    grad_down = weight_grad(activated, cotan_full)
-    grad_up = weight_grad(mlp_in, grad_lift_up)
-    grad_down, grad_up = over_tile(grad_down, grad_up)
-    grad_cq_w = weight_grad(cross_in, grad_cq)
-    grad_co_w = weight_grad(cross_mixed, grad_cross_full)
-    grad_ck, grad_cv = lax.psum((grad_ck, grad_cv), "tile")
-
-    def text_grad(grads):
-        grads = grads.reshape(batch, -1, features)
-        high = grads.astype(bf16)
-        rest = (grads - high.astype(f32)).astype(bf16)
-        both = jnp.concatenate([high, rest], axis=1)
-        text = jnp.concatenate([text_states, text_states], axis=1)
-        return jnp.einsum("bsw,bse->we", text, both, preferred_element_type=f32)
-
-    grad_ck_w, grad_cv_w = text_grad(grad_ck), text_grad(grad_cv)
-    grad_o_w = lax.dot_general(
-        mixed_t, grad_attn_full, (((1,), (0,)), ((), ())), preferred_element_type=f32
-    )
-    grad_q_w = lax.dot_general(
-        attn_in, grad_q_t, (((0,), (1,)), ((), ())), preferred_element_type=f32
-    )
-    grad_kv_w = weight_grad(attn_in, grad_kv)
-    grad_cq_w, grad_co_w, grad_o_w, grad_q_w, grad_kv_w = over_tile(
-        grad_cq_w, grad_co_w, grad_o_w, grad_q_w, grad_kv_w
-    )
-    grad_kv_w = grad_kv_w.reshape(width, heads, 2, HD)
-    grad_k_w = grad_kv_w[:, :, 0].reshape(width, features)
-    grad_v_w = grad_kv_w[:, :, 1].reshape(width, features)
-
-    grad_conv_second = conv_kernel_grad(act2, trim(grad_conv2, 2))
-    grad_conv_first = conv_kernel_grad(trim(act1, 1), trim(grad_conv1, 1))
-    grad_gains = jnp.stack([grad_attn_gain, grad_cross_gain, grad_mlp_gain])
-    everywhere = lax.psum(
-        tuple(
-            v.astype(bf16) for v in (grad_conv_first, grad_conv_second, grad_lift, grad_gains)
-        ),
-        ("tile", "sub"),
-    )
-    grad_conv_first, grad_conv_second, grad_lift, grad_gains = (
-        v.astype(f32) for v in everywhere
-    )
+    back = jnp.sum(back, axis=0)
     grad_gains = lax.dynamic_slice_in_dim(grad_gains, s * features, features, axis=1)
-    back1, back2 = jnp.sum(back1, axis=0), jnp.sum(back2, axis=0)
     return (
-        outer_sum.astype(bf16),
+        outer_out,
         inner_out,
         outer_grad,
         inner_grad,
-        back1[1],
-        back1[0],
+        back[1],
+        back[0],
         grad_conv_first,
         grad_time,
-        back2[1],
-        back2[0],
+        back[3],
+        back[2],
         grad_conv_second,
         grad_lift,
         grad_gains[0],

time: 1010 us -> 610 us (0.60)
  waiting for transfers between devices: 317 us -> 1.43 us
  Pallas kernels: 267 us -> 483 us
  matrix products: 134 us -> 43.6 us
  local copies, waits for them, and re-layouts: 97.8 us -> 23.4 us
  other arithmetic: 90.6 us -> 31.8 us
  blocking collectives: 44 us -> 0 us
  starting transfers between devices: 33.8 us -> 0.11 us
    psum x3 -> x1, waiting for transfers between devices: 285 us -> 0.01 us  [local(): grad_down, grad_up = lax.psum((grad_down, grad_up), 'tile')]
    pallas_call x10 -> x9, Pallas kernels: 131 us -> 345 us  [the longest x1 190 us: outer_backward(): pl.pallas_call(functools.partial(outer_backward_kernel, nt, ns), out_shap...]
    conv_general_dilated x4 -> x0, matrix products: 64.8 us -> none  [conv_valid(): lax.conv_general_dilated(padded, kernel, (1, 1), 'VALID', dimension_numbe...]
    convert_element_type x18 -> x3, other arithmetic: 44.9 us -> 2.09 us  [the longest x1 1.12 us: local(): inner_grad = inner_grad.astype(f32)]
    psum x1 -> x0, blocking collectives: 38.8 us -> none  [local(): lax.psum(tuple((v.astype(bf16) for v in (grad_conv_first, grad_conv_secon...]
    ppermute x12 -> x0, starting transfers between devices: 33.5 us -> none  [the longest x6 25.7 us: bordered(): lax.ppermute(lax.slice_in_dim(block, block.shape[dim] - width, None, axis...]
    slice x12 -> x2, local copies, waits for them, and re-layouts: 33.6 us -> 0.58 us  [the longest x1 0.57 us: local(): back[2]]
    all_gather x2 -> x0, waiting for transfers between devices: 29.5 us -> none  [by_feature(): full = lax.all_gather(values.astype(bf16), 'sub', axis=0)]
  transfers between devices with their start and end apart: 20 -> 3, of which waited for: 5 -> 0; matrix products, arithmetic and copies ran while one was open for 29% -> 5% of each run, Pallas kernels for 27% -> 51%
where the time goes in v2:
time: 610 us; the launch traced here: 600 us
  Pallas kernels  483 us (79%)
  matrix products  43.6 us (7%)
  other arithmetic  31.8 us (5%)
  local copies, waits for them, and re-layouts  23.4 us (4%)
  between operations  16.5 us (3%)
    pallas_call x1, Pallas kernels, outer_backward(): pl.pallas_call(functools.partial(outer_backward_kernel, nt, ns), out_shap...  190 us
    pallas_call x5, Pallas kernels, scatter_sub(): pl.pallas_call(functools.partial(scatter_kernel, ns), out_shape=jax.Shape...  58.9 us
    pallas_call x5, Pallas kernels, gather_sub(): pl.pallas_call(functools.partial(gather_kernel, ns, count), out_shape=jax...  52.9 us
    pallas_call x1, Pallas kernels, outer_forward(): pl.pallas_call(functools.partial(outer_forward_kernel, nt, ns), out_shape...  41.5 us
    pallas_call x1, Pallas kernels, dqkv_home(): pl.pallas_call(functools.partial(dqkv_home_kernel, nt, ns, u), out_shape=...  36.4 us
    pallas_call x1, Pallas kernels, flash_back(): pl.pallas_call(flash_back_kernel, grid=(batch, nt), out_shape=(jax.ShapeD...  25.3 us
    pallas_call x1, Pallas kernels, qkv_out(): pl.pallas_call(functools.partial(qkv_out_kernel, nt, u), out_shape=(jax.S...  21.8 us
    pallas_call x2, Pallas kernels, swap_heads(): pl.pallas_call(functools.partial(swap_kernel, nt, u, home), out_shape=jax...  20 us
  transfers between devices with their start and end apart: 3, of which 0 were waited for; matrix products, arithmetic and copies ran while one was open for 5% of the time, Pallas kernels for 51%

profile of v2, /device:TPU:0, one launch (start us, length us, event | category | flops | bytes accessed | tf_op | source)
XLA Modules:
  0.0 600.3 jit_solution(8144640441265005407)
XLA Ops:
  13.4 1.3 pad_maximum_fusion.2.gains
  14.7 41.5 %outer_forward.1 = (bf16[32,64,256]{2,1,0:T(8,128)(2,1)}, f32[8,16,256]{2,1,0:T(8,128)}, bf16[2912,768]{1,0:T(8,128)(2,1)}, bf16[2752,768]{1,0:T(8,128)(2,1)}, f...) custom-call(bf16[32,64,256]{2,1,0:T(8,128)(2,1)} %bitcast.231, bf16[2304,256]{1,0:T(8,128)(2,1)} %bitcast.224, ...), custom_call_target="tpu_custom_call" | custom-call | flops 1 | bytes 1 | tf_op jit(solution)/shard_map/outer_forward/pallas_call | solution.py:1097
  58.5 2.0 convolution_convert_fusion.14
  61.3 2.0 convolution_convert_fusion.15
  65.2 1.4 fusion.28
  66.7 1.8 constant_dynamic-slice_fusion.1
  69.9 10.8 %gather_sub.5 = bf16[4,128,1024]{2,1,0:T(8,128)(2,1)} custom-call(bf16[128,1024]{1,0:T(8,128)(2,1)} %multiply_convert_fusion.4.x_ref), custom_call_target="tpu_custom_call" | custom-call | flops 1 | bytes 1 | tf_op jit(solution)/shard_map/gather_sub/pallas_call | solution.py:120
  80.7 2.8 fusion.10.kv_ref
  84.8 21.8 %qkv_out.1 = (bf16[4,1,64,512]{3,2,1,0:T(8,128)(2,1)}, bf16[8,1,512,128]{3,2,1,0:T(8,128)(2,1)}) custom-call(bf16[1,256,512]{2,1,0:T(8,128)(2,1)} %fusion.16.q_ref, bf16[1,512,512]{2,1,0:T(8,128)(2,1)} %fusion.10.kv_ref), custom_call_target="tpu_custom_call" | custom-call | flops 1 | bytes 1 | tf_op jit(solution)/shard_map/qkv_out/pallas_call | solution.py:296
  106.6 18.2 %flash.1 = (bf16[4,1,64,512]{3,2,1,0:T(8,128)(2,1)}, f32[4,1,64,512]{3,2,1,0:T(8,128)}, f32[4,1,1,512]{3,2,1,0:T(1,128)}) custom-call(bf16[4,1,64,512]{3,2,1,0:T(8,128)(2,1)} %get-tuple-element.132.q_ref, bf16[8,1,512,128]{3,2,1,0:T(8,128)(2,1)} %get-tuple-element.133.kv_ref), custom_call_target="tpu_custom_call" | custom-call | flops 1 | bytes 1 | tf_op jit(solution)/shard_map/flash/pallas_call | solution.py:470
  124.8 10.5 %swap_heads.2 = bf16[1,256,512]{2,1,0:T(8,128)(2,1)} custom-call(bf16[4,1,64,512]{3,2,1,0:T(8,128)(2,1)} %get-tuple-element.134.x_ref), custom_call_target="tpu_custom_call" | custom-call | flops 1 | bytes 1 | tf_op jit(solution)/shard_map/swap_heads/pallas_call | solution.py:342
  135.4 2.4 convolution_convert_fusion.6
  137.7 11.0 %scatter_sub.5 = f32[128,1024]{1,0:T(8,128)} custom-call(bf16[4,128,1024]{2,1,0:T(8,128)(2,1)} %bitcast.229), custom_call_target="tpu_custom_call" | custom-call | flops 1 | bytes 1 | tf_op jit(solution)/shard_map/scatter_sub/pallas_call | solution.py:220
  148.8 1.2 fusion.42
  151.1 10.9 %gather_sub.6 = bf16[4,128,1024]{2,1,0:T(8,128)(2,1)} custom-call(bf16[128,1024]{1,0:T(8,128)(2,1)} %multiply_convert_fusion.3.x_ref), custom_call_target="tpu_custom_call" | custom-call | flops 1 | bytes 1 | tf_op jit(solution)/shard_map/gather_sub/pallas_call | solution.py:120
  162.1 1.7 convolution_convert_fusion.11
  166.3 1.4 convolution_convert_fusion.5
  167.7 11.7 %scatter_sub.6 = f32[128,1024]{1,0:T(8,128)} custom-call(bf16[4,128,1024]{2,1,0:T(8,128)(2,1)} %bitcast.230), custom_call_target="tpu_custom_call" | custom-call | flops 1 | bytes 1 | tf_op jit(solution)/shard_map/scatter_sub/pallas_call | solution.py:220
  181.7 10.5 %gather_sub.7 = bf16[4,128,1024]{2,1,0:T(8,128)(2,1)} custom-call(bf16[128,1024]{1,0:T(8,128)(2,1)} %multiply_convert_fusion.2.x_ref), custom_call_target="tpu_custom_call" | custom-call | flops 1 | bytes 1 | tf_op jit(solution)/shard_map/gather_sub/pallas_call | solution.py:120
  192.2 1.3 copy.114
  193.5 1.3 fusion.50
  195.4 2.4 fusion.6
  197.9 2.6 convolution_convert_fusion
  200.5 2.3 convolution_convert_fusion.4
  202.7 2.8 convolution_convert_fusion.1
  205.5 12.0 %scatter_sub.7 = f32[128,1024]{1,0:T(8,128)} custom-call(bf16[4,128,1024]{2,1,0:T(8,128)(2,1)} %bitcast.257), custom_call_target="tpu_custom_call" | custom-call | flops 1 | bytes 1 | tf_op jit(solution)/shard_map/scatter_sub/pallas_call | solution.py:220
  217.5 1.3 multiply_reduce_fusion.1
  218.9 12.2 %fusion.40 = (bf16[128,1024]{1,0:T(8,128)(2,1)}, f32[128,1024]{1,0:T(8,128)}) fusion(f32[128]{0:T(128)S(1)} %broadcast_multiply_fusion.5, f32[128,1024]{1,0:T(8,128)S(1)} %get-tuple-element.185, f32[128]{0:T(128)S(1)} %broadcast_multiply_fusion.7, f32[128]{0:T(128)S(1)} %broadcast_multiply_fusion.6, f32[128,1024]{1,0:T(8,128)} %scatter_sub.7, ...), kind=kLoop, calls=%fused_computation.119 | loop fusion | flops 1310720 | bytes 2103296 | tf_op jit(solution)/shard_map/convert_element_type | solution.py:1669
  231.1 10.3 %gather_sub.8 = bf16[4,128,1024]{2,1,0:T(8,128)(2,1)} custom-call(bf16[128,1024]{1,0:T(8,128)(2,1)} %get-tuple-element.182.x_ref), custom_call_target="tpu_custom_call" | custom-call | flops 1 | bytes 1 | tf_op jit(solution)/shard_map/gather_sub/pallas_call | solution.py:120
  241.4 2.4 convolution_convert_fusion.9
  243.8 1.2 reshape.605
  246.1 1.4 multiply_reduce_fusion
  248.5 1.5 convolution_convert_fusion.3
  250.7 12.1 %scatter_sub.8 = f32[128,1024]{1,0:T(8,128)} custom-call(bf16[4,128,1024]{2,1,0:T(8,128)(2,1)} %bitcast.228), custom_call_target="tpu_custom_call" | custom-call | flops 1 | bytes 1 | tf_op jit(solution)/shard_map/scatter_sub/pallas_call | solution.py:220
  262.8 1.3 multiply_reduce_fusion.2
  264.2 2.2 fusion.39
  266.4 10.4 %gather_sub.9 = bf16[4,128,1024]{2,1,0:T(8,128)(2,1)} custom-call(bf16[128,1024]{1,0:T(8,128)(2,1)} %get-tuple-element.180.x_ref), custom_call_target="tpu_custom_call" | custom-call | flops 1 | bytes 1 | tf_op jit(solution)/shard_map/gather_sub/pallas_call | solution.py:120
  276.8 2.4 fusion.17.x_ref
  279.2 9.5 %swap_heads.3.d_ref = bf16[4,1,64,512]{3,2,1,0:T(8,128)(2,1)} custom-call(bf16[1,256,512]{2,1,0:T(8,128)(2,1)} %fusion.17.x_ref), custom_call_target="tpu_custom_call" | custom-call | flops 1 | bytes 1 | tf_op jit(solution)/shard_map/swap_heads/pallas_call | solution.py:342
  290.5 25.3 %flash_back.1 = (bf16[4,1,64,512]{3,2,1,0:T(8,128)(2,1)}, bf16[8,1,512,128]{3,2,1,0:T(8,128)(2,1)}) custom-call(bf16[4,1,64,512]{3,2,1,0:T(8,128)(2,1)} %get-tuple-element.132.q_ref, bf16[4,1,64,512]{3,2,1,0:T(8,128)(2,1)} %swap_heads.3.d_ref, f32[4,1,64,512]{3,2,1,0:T(8,128)} %get-tuple-element.136.of_ref, f32[4,1,1,512]{3,2,1,0:T(1,128)} %get-tuple-element.137.lse_ref, ...), custom_call_target="tpu_custom_call" | custom-call | flops 1 | bytes 1 | tf_op jit(solution)/shard_map/flash_back/pallas_call | solution.py:525
  315.8 4.0 convolution_convert_fusion.2
  319.9 36.4 %dqkv_home.1 = (bf16[1,256,512]{2,1,0:T(8,128)(2,1)}, bf16[1,512,512]{2,1,0:T(8,128)(2,1)}, f32[128,1024]{1,0:T(8,128)}, bf16[512,1024]{1,0:T(8,128)(2,1)}, bf16[1024,256]{1,0:T(8,128)(2,1)}) custom-call(bf16[4,1,64,512]{3,2,1,0:T(8,128)(2,1)} %get-tuple-element.138.dq_ref, bf16[8,1,512,128]{3,2,1,0:T(8,128)(2,1)} %get-tuple-element.139.dkv_ref, ...), custom_call_target="tpu_custom_call" | custom-call | flops 1 | bytes 1 | tf_op jit(solution)/shard_map/dqkv_home/pallas_call | solution.py:410
  356.3 1.5 fusion.32
  357.9 1.7 add_convert_fusion
  359.6 12.1 %scatter_sub.9 = f32[128,1024]{1,0:T(8,128)} custom-call(bf16[4,128,1024]{2,1,0:T(8,128)(2,1)} %bitcast.241), custom_call_target="tpu_custom_call" | custom-call | flops 1 | bytes 1 | tf_op jit(solution)/shard_map/scatter_sub/pallas_call | solution.py:220
  376.5 189.6 %outer_backward.1 = (f32[32,64,256]{2,1,0:T(8,128)}, bf16[4352,256]{1,0:T(8,128)(2,1)}, bf16[512,1024]{1,0:T(8,128)(2,1)}, bf16[4,2,128,256]{3,2,1,0:T(8,128)(2,...) custom-call(bf16[32,64,256]{2,1,0:T(8,128)(2,1)} %bitcast.254, ...), custom_call_target="tpu_custom_call" | custom-call | flops 1 | bytes 1 | tf_op jit(solution)/shard_map/outer_backward/pallas_call | solution.py:1382
  571.5 18.5 %finish_grads.1 = (f32[1024,256]{1,0:T(8,128)}, f32[1024,256]{1,0:T(8,128)}, f32[1024,256]{1,0:T(8,128)}, f32[1024,256]{1,0:T(8,128)}, f32[256,1024]{1,0:T(8,128...) custom-call(bf16[128,4096]{1,0:T(8,128)(2,1)} %bitcast.223, ...), custom_call_target="tpu_custom_call" | custom-call | flops 1 | bytes 1 | tf_op jit(solution)/shard_map/finish_grads/pallas_call | solution.py:1464
  592.0 1.3 copy.166
  (181 shorter events, 35.1 us)
Async XLA Ops:
  7.2 159.1 %copy-start = (bf16[256,1024]{1,0:T(8,128)(2,1)S(1)}, bf16[256,1024]{1,0:T(8,128)(2,1)}, u32[]{:S(2)}) copy-start(bf16[256,1024]{1,0:T(8,128)(2,1)} %param.60) | copy-start | bytes 1572868
  7.2 59.5 %all-gather.5.cloned.1.call-start = ((), (), s32[]{:S(2)}) async-start(), calls=%async_computation.1 | async-start | bytes 1310720 | tf_op jit(solution)/shard_map/all_gather | solution.py:1568
  8.0 49.3 %copy-start.26 = (bf16[1024,256]{1,0:T(8,128)(2,1)S(1)}, bf16[1024,256]{1,0:T(8,128)(2,1)}, u32[]{:S(2)}) copy-start(bf16[1024,256]{1,0:T(8,128)(2,1)} %param.53) | copy-start | bytes 1572868
  8.0 58.7 %all-gather.3.cloned.1.call-start = ((), (), s32[]{:S(2)}) async-start(), calls=%async_computation | async-start | bytes 1310720 | tf_op jit(solution)/shard_map/all_gather | solution.py:1568
  8.7 562.8 %all-reduce.4.cloned.1.call-start = ((), (), s32[]{:S(2)}) async-start(), calls=%async_computation.2 | async-start | bytes 8388608 | tf_op jit(solution)/shard_map/psum | solution.py:1664
  10.2 4.6 copy-start.34
  13.4 1.3 copy-start.30
  14.7 42.7 %copy-start.27 = (bf16[1024,256]{1,0:T(8,128)(2,1)S(1)}, bf16[1024,256]{1,0:T(8,128)(2,1)}, u32[]{:S(2)}) copy-start(bf16[1024,256]{1,0:T(8,128)(2,1)} %param.54) | copy-start | bytes 1572868
  14.7 43.7 %copy-start.3 = (bf16[1,128,4096]{2,1,0:T(8,128)(2,1)S(1)}, bf16[1,128,4096]{2,1,0:T(8,128)(2,1)}, u32[]{:S(2)}) copy-start(bf16[1,128,4096]{2,1,0:T(8,128)(2,1)} %param.40) | copy-start | bytes 3145732
  57.2 11.3 %copy-start.21 = (bf16[8,16,256]{2,1,0:T(8,128)(2,1)}, bf16[8,16,256]{2,1,0:T(8,128)(2,1)S(1)}, u32[]{:S(2)}) copy-start(bf16[8,16,256]{2,1,0:T(8,128)(2,1)S(1)} %convert_element_type.175) | copy-start | bytes 196612
  61.3 5.4 copy-start.36
  63.3 5.2 copy-start.10
  65.2 15.5 %copy-start.5 = (bf16[1024,4,128]{0,2,1:T(8,128)(2,1)}, bf16[1024,4,128]{0,2,1:T(8,128)(2,1)S(1)}, u32[]{:S(2)}) copy-start(bf16[1024,4,128]{0,2,1:T(8,128)(2,1)S(1)} %pad_maximum_fusion) | copy-start | bytes 3145732
  68.8 14.8 %copy-start.37 = (f32[128]{0:T(128)}, f32[128]{0:T(128)S(1)}, u32[]{:S(2)}) copy-start(f32[128]{0:T(128)S(1)} %broadcast_multiply_fusion.9) | copy-start | bytes 1540
  69.1 14.5 %copy-start.39 = (f32[128]{0:T(128)}, f32[128]{0:T(128)S(1)}, u32[]{:S(2)}) copy-start(f32[128]{0:T(128)S(1)} %add_rsqrt_fusion.2) | copy-start | bytes 1540
  69.9 13.7 %copy-start.13 = (bf16[1024,256]{1,0:T(8,128)(2,1)S(1)}, bf16[1024,256]{1,0:T(8,128)(2,1)}, u32[]{:S(2)}) copy-start(bf16[1024,256]{1,0:T(8,128)(2,1)} %param.52) | copy-start | bytes 1572868
  80.7 2.9 copy-start.2
  83.6 51.7 %copy-start.24 = (bf16[256,1024]{1,0:T(8,128)(2,1)S(1)}, bf16[256,1024]{1,0:T(8,128)(2,1)}, u32[]{:S(2)}) copy-start(bf16[256,1024]{1,0:T(8,128)(2,1)} %param.55) | copy-start | bytes 1572868
  148.8 13.3 %copy-start.22 = (bf16[1024,256]{1,0:T(8,128)(2,1)S(1)}, bf16[1024,256]{1,0:T(8,128)(2,1)}, u32[]{:S(2)}) copy-start(bf16[1024,256]{1,0:T(8,128)(2,1)} %param.57) | copy-start | bytes 1572868
  164.9 82.6 %copy-start.31 = (f32[4,4,128]{2,0,1:T(4,128)}, f32[4,4,128]{2,0,1:T(4,128)S(1)}, u32[]{:S(2)}) copy-start(f32[4,4,128]{2,0,1:T(4,128)S(1)} %fusion.22) | copy-start | bytes 24580
  166.3 1.5 copy-start.8
  181.7 11.8 %copy-start.45 = (bf16[1024,1024]{1,0:T(8,128)(2,1)S(1)}, bf16[1024,1024]{1,0:T(8,128)(2,1)}, u32[]{:S(2)}) copy-start(bf16[1024,1024]{1,0:T(8,128)(2,1)} %param.63) | copy-start | bytes 6291460
  193.5 1.9 copy-start.44
  197.8 4.9 copy-start.47
  205.5 13.3 %copy-start.19 = (bf16[1,8,1,16,1024]{4,3,2,1,0:T(8,128)(2,1)S(1)}, bf16[1,8,1,16,1024]{4,3,2,1,0:T(8,128)(2,1)}, u32[]{:S(2)}) copy-start(bf16[1,8,1,16,1024]{4,3,2,1,0:T(8,128)(2,1)} %get-tuple-element.215) | copy-start | bytes 786436
  248.5 15.7 %copy-start.15 = (f32[128,1024]{1,0:T(8,128)S(1)}, f32[128,1024]{1,0:T(8,128)}, u32[]{:S(2)}) copy-start(f32[128,1024]{1,0:T(8,128)} %get-tuple-element.183) | copy-start | bytes 1572868
  264.1 12.7 %copy-start.25 = (bf16[256,1024]{1,0:T(8,128)(2,1)S(1)}, bf16[256,1024]{1,0:T(8,128)(2,1)}, u32[]{:S(2)}) copy-start(bf16[256,1024]{1,0:T(8,128)(2,1)} %param.55) | copy-start | bytes 1572868
  266.4 12.8 %copy-start.9 = (bf16[4,1,128,4,64]{2,0,4,3,1:T(4,128)(2,1)S(1)}, bf16[4,1,128,4,64]{2,0,4,3,1:T(4,128)(2,1)}, u32[]{:S(2)}) copy-start(bf16[4,1,128,4,64]{2,0,4,3,1:T(4,128)(2,1)} %copy-done.8) | copy-start | bytes 786436
  266.4 22.4 %copy-start.20 = (bf16[32,8,4,128]{3,1,2,0:T(8,128)(2,1)S(1)}, bf16[32,8,4,128]{3,1,2,0:T(8,128)(2,1)}, u32[]{:S(2)}) copy-start(bf16[32,8,4,128]{3,1,2,0:T(8,128)(2,1)} %copy.153) | copy-start | bytes 786436
  290.5 25.4 %copy-start.46 = (bf16[1024,1024]{1,0:T(8,128)(2,1)S(1)}, bf16[1024,1024]{1,0:T(8,128)(2,1)}, u32[]{:S(2)}) copy-start(bf16[1024,1024]{1,0:T(8,128)(2,1)} %param.63) | copy-start | bytes 6291460
  319.9 36.5 %copy-start.14 = (bf16[1024,256]{1,0:T(8,128)(2,1)S(1)}, bf16[1024,256]{1,0:T(8,128)(2,1)}, u32[]{:S(2)}) copy-start(bf16[1024,256]{1,0:T(8,128)(2,1)} %param.52) | copy-start | bytes 1572868
  356.3 1.6 copy-start.6
  356.3 1.6 copy-start.11
  357.9 13.8 %copy-start.29 = (bf16[4,128,4,64]{1,3,0,2:T(8,128)(2,1)S(1)}, bf16[4,128,4,64]{1,3,0,2:T(8,128)(2,1)}, u32[]{:S(2)}) copy-start(bf16[4,128,4,64]{1,3,0,2:T(8,128)(2,1)} %copy.116) | copy-start | bytes 786436
  357.9 13.8 %copy-start.32 = (f32[4,4,128]{2,0,1:T(4,128)S(1)}, f32[4,4,128]{2,0,1:T(4,128)}, u32[]{:S(2)}) copy-start(f32[4,4,128]{2,0,1:T(4,128)} %copy-done.31) | copy-start | bytes 24580
  371.8 2.2 copy-start.4
  371.8 2.2 copy-start.38
  371.8 2.2 copy-start.40
  372.1 2.7 copy-start.28
  372.9 2.3 copy-start.16
  566.1 2.7 copy-start.33
  566.1 4.0 copy-start.41
  566.1 4.0 copy-start.42
  566.2 4.0 copy-start.43
  566.2 4.5 copy-start.35
  571.5 18.5 %copy-start.18 = (bf16[32,64,256]{2,1,0:T(8,128)(2,1)S(1)}, bf16[32,64,256]{2,1,0:T(8,128)(2,1)}, u32[]{:S(2)}) copy-start(bf16[32,64,256]{2,1,0:T(8,128)(2,1)} %get-tuple-element.127) | copy-start | bytes 3145732
  590.0 2.0 copy-start.12
  590.0 3.3 copy-start.1
  (3 other events, 3.4 us)
Sparse Core Ops, SparseCore 0:
  9.6 20.7 all-gather.4
  31.9 18.7 all-gather.2
  290.6 198.5 all-reduce.3

commit v3 on v2

--- a/solution.py
+++ b/solution.py
@@ -67,66 +67,21 @@
     return jnp.dot(left, right, preferred_element_type=f32)
 
 
+def dot_t(left, right):
+    return lax.dot_general(left, right, (((1,), (1,)), ((), ())), preferred_element_type=f32)
+
+
+def clear(*refs):
+    for ref in refs:
+        ref[...] = jnp.zeros_like(ref)
+
+
 def round_up(rows, step):
     return (rows + step - 1) // step * step
 
 
 def chunks_of(rows):
     return max(1, min(4, rows // 16))
-
-
-def gather_kernel(ns, count, x_ref, o_ref, s1, r1, s2, r2, own):
-    far = ns // 2
-    t, s = lax.axis_index("tile"), lax.axis_index("sub")
-    r, c = s // 2, lax.rem(s, 2)
-    me, twin = (t, s), (t, r * 2 + 1 - c)
-    size = x_ref.shape[0] // count
-    greet([twin] + [(t, lax.rem(r + k, far) * 2 + c) for k in range(1, far)])
-    local = pltpu.make_async_copy(x_ref, o_ref.at[s], own)
-    local.start()
-    copies = []
-
-    def send(src, dst, send_sem, recv_sem, where):
-        copies.append(remote(src, dst, send_sem, recv_sem, where))
-        copies[-1].start()
-
-    for j in range(count):
-        part = pl.ds(j * size, size)
-        for k in range(1, far):
-            peer = (t, lax.rem(r + k, far) * 2 + c)
-            send(x_ref.at[part], o_ref.at[s, part], s1.at[k, j], r1.at[k, j], peer)
-    for j in range(count):
-        part = pl.ds(j * size, size)
-        send(x_ref.at[part], o_ref.at[s, part], s2.at[0, j], r2.at[0, j], twin)
-    for j in range(count):
-        part = pl.ds(j * size, size)
-        for k in range(1, far):
-            block = o_ref.at[lax.rem(r + far - k, far) * 2 + c, part]
-            arrived(block, s1.at[k, j], r1.at[k, j], me)
-            send(block, block, s2.at[k, j], r2.at[k, j], twin)
-    for j in range(count):
-        part = pl.ds(j * size, size)
-        for k in range(far):
-            block = o_ref.at[lax.rem(r + far - k, far) * 2 + 1 - c, part]
-            arrived(block, s2.at[k, j], r2.at[k, j], me)
-    for copy in copies:
-        copy.wait_send()
-    local.wait()
-
-
-def gather_sub(x, cid):
-    ns = lax.axis_size("sub")
-    far, count = ns // 2, chunks_of(x.shape[0])
-    return pl.pallas_call(
-        functools.partial(gather_kernel, ns, count),
-        out_shape=jax.ShapeDtypeStruct((ns,) + x.shape, x.dtype),
-        in_specs=[anywhere()],
-        out_specs=anywhere(),
-        scratch_shapes=[dma(far, count) for _ in range(4)] + [pltpu.SemaphoreType.DMA],
-        cost_estimate=SHORT,
-        compiler_params=params(cid),
-        name="gather_sub",
-    )(x)
 
 
 class Copies:
@@ -175,12 +130,31 @@
     def part(self, j):
         return pl.ds(j * self.size, self.size)
 
+    def over(self, k):
+        return lax.rem(self.r + k, self.far) * 2 + 1 - self.c
+
+    def start_one(self, k):
+        for j in range(self.count):
+            block, got = self.x.at[self.over(k), self.part(j)], self.got.at[k, self.part(j)]
+            self.copies.send(block, got, self.s1.at[k, j], self.r1.at[k, j], self.twin)
+
     def start(self):
         for k in list(range(1, self.far)) + [0]:
-            for j in range(self.count):
-                block = self.x.at[lax.rem(self.r + k, self.far) * 2 + 1 - self.c, self.part(j)]
-                got = self.got.at[k, self.part(j)]
-                self.copies.send(block, got, self.s1.at[k, j], self.r1.at[k, j], self.twin)
+            self.start_one(k)
+
+    def run(self, make, out, meanwhile=None, then=None):
+        for k in range(1, self.far):
+            make(self.over(k))
+            self.start_one(k)
+        for k in range(1, self.far):
+            make(self.peer(k)[1])
+        make(self.over(0))
+        self.start_one(0)
+        self.cross()
+        make(self.s)
+        if meanwhile is not None:
+            meanwhile()
+        self.end(out, then)
 
     def cross(self):
         for j in range(self.count):
@@ -192,7 +166,7 @@
                 src, dst = self.stage.at[k, part], self.last.at[k, part]
                 self.copies.send(src, dst, self.s2.at[k, j], self.r2.at[k, j], self.peer(k))
 
-    def end(self, out):
+    def end(self, out, then=None):
         for j in range(self.count):
             part = self.part(j)
             arrived(self.got.at[0, part], self.s1.at[0, j], self.r1.at[0, j], self.me)
@@ -201,32 +175,303 @@
                 arrived(self.last.at[k, part], self.s2.at[k, j], self.r2.at[k, j], self.me)
                 total = total + self.last[k, part].astype(f32)
             out[part] = total
-
-
-def scatter_kernel(ns, x_ref, o_ref, got, stage, last, *sems):
+            if then is not None:
+                then(j, part)
+
+
+class SubGather:
+    def __init__(self, ns, copies, out, sems):
+        t, s = lax.axis_index("tile"), lax.axis_index("sub")
+        self.far, self.copies, self.out, self.t, self.s = ns // 2, copies, out, t, s
+        self.r, self.c = s // 2, lax.rem(s, 2)
+        self.me, self.twin = (t, s), (t, self.r * 2 + 1 - self.c)
+        self.count = chunks_of(out.shape[1])
+        self.size = out.shape[1] // self.count
+        self.s1, self.r1, self.s2, self.r2 = sems
+
+    @staticmethod
+    def scratch(ns, rows):
+        return [dma(ns // 2, chunks_of(rows)) for _ in range(4)]
+
+    def block(self, r, c, j):
+        return self.out.at[lax.rem(r, self.far) * 2 + c, pl.ds(j * self.size, self.size)]
+
+    def start(self):
+        for j in range(self.count):
+            self.start_one(j)
+
+    def start_one(self, j):
+        block = self.block(self.r, self.c, j)
+        for k in range(1, self.far):
+            peer = (self.t, lax.rem(self.r + k, self.far) * 2 + self.c)
+            self.copies.send(block, block, self.s1.at[k, j], self.r1.at[k, j], peer)
+        self.copies.send(block, block, self.s2.at[0, j], self.r2.at[0, j], self.twin)
+
+    def relay(self):
+        for j in range(self.count):
+            for k in range(1, self.far):
+                block = self.block(self.r + self.far - k, self.c, j)
+                arrived(block, self.s1.at[k, j], self.r1.at[k, j], self.me)
+                self.copies.send(block, block, self.s2.at[k, j], self.r2.at[k, j], self.twin)
+
+    def end(self):
+        for j in range(self.count):
+            for k in range(self.far):
+                block = self.block(self.r + self.far - k, 1 - self.c, j)
+                arrived(block, self.s2.at[k, j], self.r2.at[k, j], self.me)
+
+
+def sub_peers(ns):
+    t, s = lax.axis_index("tile"), lax.axis_index("sub")
+    far, r, c = ns // 2, s // 2, lax.rem(s, 2)
+    return [(t, r * 2 + 1 - c)] + [(t, lax.rem(r + k, far) * 2 + c) for k in range(1, far)]
+
+
+def layer_hat(values):
+    width = values.shape[1]
+    center = jnp.sum(values, axis=1, keepdims=True) / width
+    moved = values - center
+    inv_std = lax.rsqrt(jnp.sum(moved * moved, axis=1, keepdims=True) / width + EPSILON)
+    return moved * inv_std, inv_std
+
+
+def layer_back(grad_out, values, gain):
+    width = values.shape[1]
+    hat, inv_std = layer_hat(values)
+    scaled = grad_out * gain
+    mean_grad = jnp.sum(scaled, axis=1, keepdims=True) / width
+    mean_cross = jnp.sum(scaled * hat, axis=1, keepdims=True) / width
+    grad_in = inv_std * (scaled - mean_grad - hat * mean_cross)
+    return grad_in, jnp.sum(grad_out * hat, axis=0, keepdims=True)
+
+
+def enter_kernel(ns, inner, pooled, lift, gain, stream, gathered, *sems):
     copies = Copies()
-    scatter = SubScatter(ns, copies, x_ref, got, stage, last, sems)
-    greet(scatter.peers())
-    scatter.start()
-    scatter.cross()
-    scatter.end(o_ref)
+    gather = SubGather(ns, copies, gathered, sems)
+    value = inner[...].astype(f32) + dot(pooled[...], lift[...]).astype(bf16).astype(f32)
+    stream[...] = value
+    gathered[gather.s] = (layer_hat(value)[0] * gain[...]).astype(bf16)
+    greet(sub_peers(ns))
+    gather.start()
+    gather.relay()
+    gather.end()
     copies.finish()
 
 
-def scatter_sub(x, cid):
+def attn_out_kernel(ns, mixed_t, weight, before, gain, after, gathered, turned, *scratch):
+    copies = Copies()
+    own = before.shape[0]
+    scatter = SubScatter(ns, copies, *scratch[:4], scratch[4:8])
+    gather = SubGather(ns, copies, gathered, scratch[8:])
+    turned[...] = mixed_t[...].T
+
+    def make(p):
+        rows = turned[pl.ds(pl.multiple_of(p * own, 16), own), :]
+        scatter.x[p] = dot(rows, weight[...]).astype(bf16)
+
+    greet(sub_peers(ns))
+
+    def normalize(j, part):
+        value = before[part, :] + after[part, :]
+        after[part, :] = value
+        gathered[gather.s, part] = (layer_hat(value)[0] * gain[...]).astype(bf16)
+        gather.start_one(j)
+
+    scatter.run(make, after, None, normalize)
+    gather.relay()
+    gather.end()
+    copies.finish()
+
+
+def head_of(values, h):
+    return values[:, h * HD : (h + 1) * HD]
+
+
+def head_probs(queries, keys, mask, h):
+    scores = dot_t(head_of(queries, h), head_of(keys, h)) * HD ** (-0.5)
+    scores = jnp.where(mask > 0.5, scores, -1000000000.0)
+    raised = jnp.exp(scores - jnp.max(scores, axis=1, keepdims=True))
+    return raised / jnp.sum(raised, axis=1, keepdims=True)
+
+
+def side_by_side(parts):
+    return jnp.concatenate(parts, axis=1) if len(parts) > 1 else parts[0]
+
+
+def cross_kernel(
+    ns, cross_in, wq, ck, cv, mask, wo, before, gain, after, gathered, queries, mixed, *scratch
+):
+    copies = Copies()
+    scatter = SubScatter(ns, copies, *scratch[:4], scratch[4:8])
+    gather = SubGather(ns, copies, gathered, scratch[8:])
+    heads = wq.shape[1] // HD
+
+    def make(p):
+        q = dot(cross_in[p], wq[...]).astype(bf16)
+        queries[p] = q
+        keys, values, masked = ck[...], cv[...], mask[...]
+        parts = [
+            dot(head_probs(q, keys, masked, h).astype(bf16), head_of(values, h))
+            for h in range(heads)
+        ]
+        mixed[p] = side_by_side(parts).astype(bf16)
+        scatter.x[p] = dot(mixed[p], wo[...]).astype(bf16)
+
+    greet(sub_peers(ns))
+
+    def normalize(j, part):
+        value = before[part, :] + after[part, :]
+        after[part, :] = value
+        gathered[gather.s, part] = (layer_hat(value)[0] * gain[...]).astype(bf16)
+        gather.start_one(j)
+
+    scatter.run(make, after, None, normalize)
+    gather.relay()
+    gather.end()
+    copies.finish()
+
+
+def mlp_kernel(
+    ns, mlp_in, cotan, w_up, w_down, before, gain,
+    grad, gathered, gain_grad, down, up_grad, down_grad, activated, grad_up, *scratch
+):
+    copies = Copies()
+    scatter = SubScatter(ns, copies, *scratch[:4], scratch[4:8])
+    gather = SubGather(ns, copies, gathered, scratch[8:])
+    own = before.shape[0]
+    rate = math.sqrt(2.0 / math.pi)
+
+    def make(p):
+        up = dot(mlp_in[p], w_up[...])
+        square = up * up
+        bent = jnp.tanh(rate * (up + 0.044715 * up * square))
+        rows = pl.ds(pl.multiple_of(p * own, 16), own)
+        activated[rows, :] = (0.5 * up * (1.0 + bent)).astype(bf16)
+        slope = 0.5 * (1.0 + bent) + 0.5 * up * (1.0 - bent * bent) * (
+            rate * (1.0 + 3.0 * 0.044715 * square)
+        )
+        turned = (slope * dot_t(cotan[p], w_down[...])).astype(bf16)
+        grad_up[rows, :] = turned
+        scatter.x[p] = dot_t(turned, w_up[...]).astype(bf16)
+
+    greet(sub_peers(ns))
+    whole = lambda ref: ref[...].reshape(ns * own, ref.shape[2])
+
+    def meanwhile():
+        up_grad[...] = dot(whole(mlp_in).T, grad_up[...]).astype(bf16)
+
+    gain_grad[...] = jnp.zeros_like(gain_grad)
+
+    def normalize(j, part):
+        back, gains = layer_back(grad[part, :], before[part, :], gain[...])
+        gain_grad[...] += gains
+        value = cotan[gather.s, part].astype(f32) + back
+        grad[part, :] = value
+        gathered[gather.s, part] = value.astype(bf16)
+        gather.start_one(j)
+
+    scatter.run(make, grad, meanwhile, normalize)
+    down_grad[...] = dot(activated[...].T, whole(cotan)).astype(bf16)
+    gather.relay()
+    down[...] = dot(activated[...], w_down[...]).astype(bf16)
+    gather.end()
+    copies.finish()
+
+
+def cross_back_kernel(
+    ns, incoming, wo, queries, ck, cv, mask, wq, before, gain, residual, cross_in, mixed,
+    grad, gathered, gain_grad, dk_out, dv_out, weights, dk, dv, dq, *scratch
+):
+    copies = Copies()
+    scatter = SubScatter(ns, copies, *scratch[:4], scratch[4:8])
+    gather = SubGather(ns, copies, gathered, scratch[8:])
+    heads = wq.shape[1] // HD
+    own = before.shape[0]
+    clear(dk, dv)
+
+    def make(p):
+        grad_mixed = dot_t(incoming[p], wo[...]).astype(bf16)
+        q, keys, values, masked = queries[p], ck[...], cv[...], mask[...]
+        parts_q, parts_k, parts_v = [], [], []
+        for h in range(heads):
+            probs = head_probs(q, keys, masked, h)
+            slope = dot_t(head_of(grad_mixed, h), head_of(values, h))
+            lean = probs * (slope - jnp.sum(probs * slope, axis=1, keepdims=True))
+            lean = lean.astype(bf16)
+            parts_q.append(dot(lean, head_of(keys, h)))
+            parts_k.append(dot(lean.T, head_of(q, h)))
+            parts_v.append(dot(probs.astype(bf16).T, head_of(grad_mixed, h)))
+        part = (side_by_side(parts_q) * HD ** (-0.5)).astype(bf16)
+        dq[pl.ds(pl.multiple_of(p * own, 16), own), :] = part
+        dk[...] += side_by_side(parts_k)
+        dv[...] += side_by_side(parts_v)
+        scatter.x[p] = dot_t(part, wq[...]).astype(bf16)
+
+    greet(sub_peers(ns))
+    whole = lambda ref: ref[...].reshape(ns * own, ref.shape[2])
+
+    def meanwhile():
+        weights[0] = dot(whole(mixed).T, whole(incoming)).astype(bf16)
+        dk_out[...] = (dk[...] * HD ** (-0.5)).astype(bf16)
+        dv_out[...] = dv[...].astype(bf16)
+
+    gain_grad[...] = jnp.zeros_like(gain_grad)
+
+    def normalize(j, part):
+        back, gains = layer_back(grad[part, :], before[part, :], gain[...])
+        gain_grad[...] += gains
+        value = residual[part, :] + back
+        grad[part, :] = value
+        gathered[gather.s, part] = value.astype(bf16)
+        gather.start_one(j)
+
+    scatter.run(make, grad, meanwhile, normalize)
+    weights[1] = dot(dq[...].T, whole(cross_in)).astype(bf16)
+    gather.relay()
+    gather.end()
+    copies.finish()
+
+
+def attn_back_kernel(
+    ns, dq_t, dkv, wq, wkv, before, gain, residual, out, gain_grad, turned, *scratch
+):
+    copies = Copies()
+    scatter = SubScatter(ns, copies, *scratch[1:5], scratch[5:9])
+    total = scratch[0]
+    own = before.shape[0]
+    turned[...] = dq_t[...].T
+
+    def make(p):
+        rows = pl.ds(pl.multiple_of(p * own, 16), own)
+        value = dot_t(turned[rows, :], wq[...]) + dot_t(dkv[rows, :], wkv[...])
+        scatter.x[p] = value.astype(bf16)
+
+    greet(sub_peers(ns))
+    scatter.run(make, total)
+    back, gains = layer_back(total[...], before[...], gain[...])
+    gain_grad[...] = gains
+    out[...] = (residual[...] + back).astype(bf16)
+    copies.finish()
+
+
+def chain_call(kernel, name, cid, outs, args, extra, scatter, gather=True):
     ns = lax.axis_size("sub")
-    x = x.astype(bf16).reshape(ns, x.shape[0] // ns, x.shape[1])
-    block = x.shape[1:]
+    own, width = outs[0][0]
+    scratch = list(extra)
+    if scatter:
+        scratch += [pltpu.VMEM((ns, own, width), bf16)] + SubScatter.scratch(ns, own, width)
+    if gather:
+        scratch += SubGather.scratch(ns, own)
     return pl.pallas_call(
-        functools.partial(scatter_kernel, ns),
-        out_shape=jax.ShapeDtypeStruct(block, f32),
-        in_specs=[in_vmem()],
-        out_specs=in_vmem(),
-        scratch_shapes=SubScatter.scratch(ns, *block),
+        functools.partial(kernel, ns),
+        out_shape=tuple(jax.ShapeDtypeStruct(*out) for out in outs),
+        in_specs=[in_vmem()] * len(args),
+        out_specs=(in_vmem(),) * len(outs),
+        scratch_shapes=scratch,
         cost_estimate=SHORT,
         compiler_params=params(cid),
-        name="scatter_sub",
-    )(x)
+        name=name,
+    )(*args)
 
 
 def deal(nt, u):
@@ -245,67 +490,6 @@
 
 def lanes_of(ref, i, size):
     return ref.at[:, :, pl.ds(pl.multiple_of(i * size, size), size)]
-
-
-def qkv_out_kernel(nt, u, q_ref, kv_ref, qo, kvo, qs, qr, ks, kr, fs, fr, own):
-    t, s, nb, a, b, a_peer, b_peer, peers = deal(nt, u)
-    me = (t, s)
-    greet(peers)
-    local = [
-        pltpu.make_async_copy(rows_of(q_ref, a, HD), qo.at[a], own.at[0]),
-        pltpu.make_async_copy(lanes_of(kv_ref, a, 2 * HD), kvo.at[t], own.at[1]),
-    ]
-    for copy in local:
-        copy.start()
-    copies = []
-
-    def send(src, dst, send_sem, recv_sem, where):
-        copies.append(remote(src, dst, send_sem, recv_sem, where))
-        copies[-1].start()
-
-    for k in range(1, u):
-        block = lanes_of(kv_ref, lax.rem(a + k, u), 2 * HD)
-        send(block, kvo.at[t], ks.at[k], kr.at[k], a_peer(k))
-    for m in range(1, nb):
-        send(lanes_of(kv_ref, a, 2 * HD), kvo.at[t], fs.at[0, m], fr.at[0, m], b_peer(m))
-    for k in range(1, u):
-        block = rows_of(q_ref, lax.rem(a + k, u), HD)
-        send(block, qo.at[a], qs.at[k], qr.at[k], a_peer(k))
-    for k in range(1, u):
-        block = kvo.at[lax.rem(a + u - k, u) * nb + b]
-        arrived(block, ks.at[k], kr.at[k], me)
-        for m in range(1, nb):
-            send(block, block, fs.at[k, m], fr.at[k, m], b_peer(m))
-    for k in range(1, u):
-        arrived(qo.at[lax.rem(a + u - k, u)], qs.at[k], qr.at[k], me)
-    for k in range(u):
-        for m in range(1, nb):
-            block = kvo.at[lax.rem(a + u - k, u) * nb + lax.rem(b + nb - m, nb)]
-            arrived(block, fs.at[k, m], fr.at[k, m], me)
-    for copy in copies:
-        copy.wait_send()
-    for copy in local:
-        copy.wait()
-
-
-def qkv_out(q, kv, cid):
-    nt = lax.axis_size("tile")
-    batch, width, length = q.shape
-    u = width // HD
-    nb = nt // u
-    return pl.pallas_call(
-        functools.partial(qkv_out_kernel, nt, u),
-        out_shape=(
-            jax.ShapeDtypeStruct((u, batch, HD, length), bf16),
-            jax.ShapeDtypeStruct((nt, batch, length, 2 * HD), bf16),
-        ),
-        in_specs=[anywhere()] * 2,
-        out_specs=(anywhere(), anywhere()),
-        scratch_shapes=[dma(u), dma(u), dma(u), dma(u), dma(u, nb), dma(u, nb), dma(2)],
-        cost_estimate=SHORT,
-        compiler_params=params(cid),
-        name="qkv_out",
-    )(q, kv)
 
 
 def swap_kernel(nt, u, home, x_ref, o_ref, ss, rs, own):
@@ -352,8 +536,7 @@
 
 
 def dqkv_home_kernel(
-    nt, ns, u, dq_ref, dkv_ref, beside_ref, mixed_t, grad_attn, cross_mixed, grad_cross, cross_in,
-    grad_cq, qo, kvo, beside_out, wide, cq_out, got, stage, qs, qr, fs, fr, ks, kr, own, *scratch
+    nt, ns, u, dq_ref, dkv_ref, beside_ref, qo, kvo, beside_out, got, stage, qs, qr, fs, fr, ks, kr, own, *scratch
 ):
     t, s, nb, a, b, a_peer, b_peer, peers = deal(nt, u)
     me = (t, s)
@@ -371,14 +554,7 @@
         copies.send(block, rows_of(qo, a, HD), qs.at[k], qr.at[k], a_peer(k))
     local = [pltpu.make_async_copy(dq_ref.at[a], rows_of(qo, a, HD), own.at[0])]
     local[0].start()
-    features = mixed_t.shape[0]
-    wide[pl.ds(0, features), :] = dot(mixed_t[...], grad_attn[...]).astype(bf16)
     beside.cross()
-    turned = cross_mixed[...].T
-    wide[pl.ds(features, features), :] = dot(turned, grad_cross[...]).astype(bf16)
-    if 2 * features < wide.shape[0]:
-        spare = wide.shape[0] - 2 * features
-        wide[pl.ds(2 * features, spare), :] = jnp.zeros((spare, wide.shape[1]), bf16)
     for k in order:
         total = dkv_ref[lax.rem(a + k, u) * nb + b].astype(f32)
         for m in range(1, nb):
@@ -391,7 +567,6 @@
             local.append(pltpu.make_async_copy(stage.at[0], lanes_of(kvo, a, 2 * HD), own.at[1]))
             local[1].start()
     beside.end(beside_out)
-    cq_out[...] = dot(cross_in[...].T, grad_cq[...]).astype(bf16)
     for k in range(1, u):
         i = lax.rem(a + u - k, u)
         arrived(rows_of(qo, i, HD), qs.at[k], qr.at[k], me)
@@ -401,7 +576,7 @@
         copy.wait()
 
 
-def dqkv_home(dq, dkv, beside, mixed_t, grad_attn, cross_mixed, grad_cross, cross_in, grad_cq, cid):
+def dqkv_home(dq, dkv, beside, cid):
     nt, ns = lax.axis_size("tile"), lax.axis_size("sub")
     u, batch, _, length = dq.shape
     nb = nt // u
@@ -413,11 +588,9 @@
             jax.ShapeDtypeStruct((batch, u * HD, length), bf16),
             jax.ShapeDtypeStruct((batch, length, u * 2 * HD), bf16),
             jax.ShapeDtypeStruct(beside.shape[1:], f32),
-            jax.ShapeDtypeStruct((round_up(2 * u * HD, 16 * nt), grad_attn.shape[1]), bf16),
-            jax.ShapeDtypeStruct((cross_in.shape[1], u * HD), bf16),
         ),
-        in_specs=[in_vmem()] * 9,
-        out_specs=(anywhere(), anywhere()) + (in_vmem(),) * 3,
+        in_specs=[in_vmem()] * 3,
+        out_specs=(anywhere(), anywhere(), in_vmem()),
         scratch_shapes=[
             pltpu.VMEM((nb, u) + block, bf16),
             pltpu.VMEM((u,) + block, bf16),
@@ -433,60 +606,282 @@
         cost_estimate=SHORT,
         compiler_params=params(cid),
         name="dqkv_home",
-    )(dq, dkv, beside, mixed_t, grad_attn, cross_mixed, grad_cross, cross_in, grad_cq)
-
-
-def flash_kernel(q_ref, kv_ref, o_ref, of_ref, lse_ref, vt):
-    count, length = kv_ref.shape[0], kv_ref.shape[2]
-
-    @pl.when(pl.program_id(1) == 0)
-    def _():
-        for j in range(count):
-            vt[j] = kv_ref[j, 0].T[HD:]
-
-    q = q_ref[0, 0] * 0.125
-    padded = jnp.concatenate([q, jnp.zeros_like(q)], axis=0)
-    top = jnp.full((1, q.shape[1]), -jnp.inf, f32)
-    total = jnp.zeros((1, q.shape[1]), f32)
-    mixed = jnp.zeros(q.shape, f32)
-    for j in range(count):
-        scores = dot(kv_ref[j, 0], padded)
-        new = jnp.maximum(top, jnp.max(scores, axis=0, keepdims=True))
+    )(dq, dkv, beside)
+
+
+class TileSum:
+    PARTS = 4
+
+    def __init__(self, nt, x, out, buffers, add_sems, share_sems):
+        t, s = lax.axis_index("tile"), lax.axis_index("sub")
+        self.na, self.x, self.out = nt // 2, x, out
+        self.a, self.b, self.s = t // 2, lax.rem(t, 2), s
+        self.me, self.pair = (t, s), (self.a * 2 + 1 - self.b, s)
+        self.half = out.shape[0] // 2
+        self.piece = self.half // 2 // self.PARTS
+        if add_sems:
+            self.got1, self.stage, self.got2 = buffers
+            self.s1, self.r1, self.s2, self.r2 = add_sems
+        if share_sems:
+            self.s3, self.r3, self.s4, self.r4 = share_sems
+
+    @staticmethod
+    def buffers(rows, width):
+        return [pltpu.VMEM((rows // 2, width), bf16) for _ in range(3)]
+
+    @staticmethod
+    def sems():
+        return [dma(2, TileSum.PARTS) for _ in range(4)]
+
+    def rows(self, b, e, j):
+        start = b * self.half + (j * 2 + e) * self.piece
+        return pl.ds(pl.multiple_of(start, 16), self.piece)
+
+    def along(self, e):
+        up, down = (self.a * 2 + 2 + self.b, self.s), (self.a * 2 - 2 + self.b, self.s)
+        return (down, up, self.a) if e else (up, down, self.na - 1 - self.a)
+
+    def start(self):
+        for j in range(self.PARTS):
+            for e in range(2):
+                self.to_pair(e, j).start()
+
+    def to_pair(self, e, j):
+        src, dst = self.x.at[self.rows(1 - self.b, e, j)], self.got1.at[self.rows(0, e, j)]
+        return remote(src, dst, self.s1.at[e, j], self.r1.at[e, j], self.pair)
+
+    def steps(self):
+        return range(self.PARTS + self.na - 1)
+
+    def step_of(self, way, step, action):
+        j = step - way
+        pl.when((j >= 0) & (j < self.PARTS))(lambda: action(jnp.clip(j, 0, self.PARTS - 1)))
+
+    def add(self, steps):
+        for step in steps:
+            for e in range(2):
+                self.step_of(self.along(e)[2], step, functools.partial(self.add_one, e))
+
+    def add_one(self, e, j):
+        _, after, way = self.along(e)
+        here, mine = self.rows(0, e, j), self.rows(self.b, e, j)
+        arrived(self.got1.at[here], self.s1.at[e, j], self.r1.at[e, j], self.me)
+        both = self.x[mine].astype(f32) + self.got1[here].astype(f32)
+
+        @pl.when(way == 0)
+        def _():
+            self.stage[here] = both.astype(bf16)
+
+        @pl.when(way > 0)
+        def _():
+            arrived(self.got2.at[here], self.s2.at[e, j], self.r2.at[e, j], self.me)
+            self.stage[here] = (both + self.got2[here].astype(f32)).astype(bf16)
+
+        @pl.when(way < self.na - 1)
+        def _():
+            src, dst = self.stage.at[here], self.got2.at[here]
+            remote(src, dst, self.s2.at[e, j], self.r2.at[e, j], after).start()
+
+        @pl.when(way == self.na - 1)
+        def _():
+            self.out[mine] = self.stage[here]
+
+    def share(self, steps):
+        for step in steps:
+            for e in range(2):
+                way = self.na - 1 - self.along(e)[2]
+                self.step_of(way, step, functools.partial(self.share_one, e))
+
+    def share_one(self, e, j):
+        before, _, way = self.along(e)
+        block = self.out.at[self.rows(self.b, e, j)]
+
+        @pl.when(way < self.na - 1)
+        def _():
+            arrived(block, self.s3.at[e, j], self.r3.at[e, j], self.me)
+
+        @pl.when(way > 0)
+        def _():
+            remote(block, block, self.s3.at[e, j], self.r3.at[e, j], before).start()
+
+        remote(block, block, self.s4.at[e, j], self.r4.at[e, j], self.pair).start()
+
+    def end_add(self):
+        for j in range(self.PARTS):
+            for e in range(2):
+                _, after, way = self.along(e)
+                self.to_pair(e, j).wait_send()
+                stage = self.stage.at[self.rows(0, e, j)]
+                sent = remote(stage, stage, self.s2.at[e, j], self.r2.at[e, j], after)
+                pl.when(way < self.na - 1)(sent.wait_send)
+
+    def end_share(self):
+        for j in range(self.PARTS):
+            for e in range(2):
+                block = self.out.at[self.rows(1 - self.b, e, j)]
+                arrived(block, self.s4.at[e, j], self.r4.at[e, j], self.me)
+        for j in range(self.PARTS):
+            for e in range(2):
+                before, _, way = self.along(e)
+                block = self.out.at[self.rows(self.b, e, j)]
+                sent = remote(block, block, self.s3.at[e, j], self.r3.at[e, j], before)
+                pl.when(way > 0)(sent.wait_send)
+                remote(block, block, self.s4.at[e, j], self.r4.at[e, j], self.pair).wait_send()
+
+
+def self_attention_kernel(
+    nt, u, q_ref, kv_ref, home, qo, kvo, mixed_out, lse, top, total, mixed, low,
+    qs, qr, ks, kr, fs, fr, hs, hr, own
+):
+    t, s, nb, a, b, a_peer, b_peer, peers = deal(nt, u)
+    me = (t, s)
+    batch, length = q_ref.shape[0], q_ref.shape[2]
+    copies = Copies()
+    qo[a] = q_ref[:, pl.ds(pl.multiple_of(a * HD, HD), HD), :]
+    local = [pltpu.make_async_copy(lanes_of(kv_ref, a, 2 * HD), kvo.at[t], own.at[0])]
+    local[0].start()
+    greet(peers)
+    for k in range(1, u):
+        block = rows_of(q_ref, lax.rem(a + k, u), HD)
+        copies.send(block, qo.at[a], qs.at[k], qr.at[k], a_peer(k))
+    for k in range(1, u):
+        block = lanes_of(kv_ref, lax.rem(a + k, u), 2 * HD)
+        copies.send(block, kvo.at[t], ks.at[k], kr.at[k], a_peer(k))
+    for m in range(1, nb):
+        block = lanes_of(kv_ref, a, 2 * HD)
+        copies.send(block, kvo.at[t], fs.at[0, m], fr.at[0, m], b_peer(m))
+    clear(total, mixed)
+    top[...] = jnp.full(top.shape, -jnp.inf, f32)
+
+    def take(tile, i, n):
+        q = qo[i, n] * 0.125
+        padded = jnp.concatenate([q, jnp.zeros_like(q)], axis=0)
+        keys = kvo[tile, n]
+        scores = dot(keys, padded)
+        new = jnp.maximum(top[i, n], jnp.max(scores, axis=0, keepdims=True))
         raised = jnp.exp(scores - new)
-        scale = jnp.exp(top - new)
-        total = total * scale + jnp.sum(raised, axis=0, keepdims=True)
-        mixed = mixed * scale + dot(vt[j], raised.astype(bf16))
-        top = new
-    mixed = mixed / total
-    o_ref[0, 0] = mixed.astype(bf16)
-    of_ref[0, 0] = mixed
-    lse_ref[0, 0] = top + jnp.log(total)
-
-
-def flash(q, kv):
-    u, batch, _, length = q.shape
-    nt = kv.shape[0]
-    rows = pl.BlockSpec((1, 1, HD, length), lambda b, i: (i, b, 0, 0))
+        scale = jnp.exp(top[i, n] - new)
+        added = dot(keys.T[HD:], raised.astype(bf16))
+        return (
+            new,
+            total[i, n] * scale + jnp.sum(raised, axis=0, keepdims=True),
+            mixed[i, n] * scale + added,
+        )
+
+    def take_all(tile):
+        for n in range(batch):
+            for i in range(u):
+                top[i, n], total[i, n], mixed[i, n] = take(tile, i, n)
+
+    def tile_of(k, m):
+        return lax.rem(a + u - k, u) * nb + lax.rem(b + nb - m, nb)
+
+    for k in range(1, u):
+        arrived(qo.at[lax.rem(a + u - k, u)], qs.at[k], qr.at[k], me)
+    local[0].wait()
+    order = [(0, 0)] + [(k, 0) for k in range(1, u)]
+    order += [(k, m) for k in range(u) for m in range(1, nb)]
+    for k, m in order[:-1]:
+        tile = tile_of(k, m)
+        if m:
+            arrived(kvo.at[tile], fs.at[k, m], fr.at[k, m], me)
+        elif k:
+            arrived(kvo.at[tile], ks.at[k], kr.at[k], me)
+            for n in range(1, nb):
+                block = kvo.at[tile]
+                copies.send(block, block, fs.at[k, n], fr.at[k, n], b_peer(n))
+        take_all(tile)
+    k, m = order[-1]
+    tile = tile_of(k, m)
+    if m:
+        arrived(kvo.at[tile], fs.at[k, m], fr.at[k, m], me)
+    elif k:
+        arrived(kvo.at[tile], ks.at[k], kr.at[k], me)
+    for k in list(range(1, u)) + [0]:
+        i = lax.rem(a + k, u)
+        for n in range(batch):
+            peak, weight, value = take(tile, i, n)
+            value = value / weight
+            mixed_out[i, n] = value
+            low[i, n] = value.astype(bf16)
+            lse[i, n] = peak + jnp.log(weight)
+        if k:
+            copies.send(low.at[i], rows_of(home, a, HD), hs.at[k], hr.at[k], a_peer(k))
+        else:
+            local.append(pltpu.make_async_copy(low.at[i], rows_of(home, a, HD), own.at[1]))
+            local[1].start()
+    for k in range(1, u):
+        arrived(rows_of(home, lax.rem(a + u - k, u), HD), hs.at[k], hr.at[k], me)
+    local[1].wait()
+    copies.finish()
+
+
+def self_attention(q, kv, cid):
+    nt = lax.axis_size("tile")
+    batch, width, length = q.shape
+    u = width // HD
+    nb = nt // u
+    shape = jax.ShapeDtypeStruct
+    dealt = (u, batch, HD, length)
     return pl.pallas_call(
-        flash_kernel,
-        grid=(batch, u),
+        functools.partial(self_attention_kernel, nt, u),
         out_shape=(
-            jax.ShapeDtypeStruct(q.shape, bf16),
-            jax.ShapeDtypeStruct(q.shape, f32),
-            jax.ShapeDtypeStruct((u, batch, 1, length), f32),
+            shape(q.shape, bf16),
+            shape(dealt, bf16),
+            shape((nt, batch, length, 2 * HD), bf16),
+            shape(dealt, f32),
+            shape((u, batch, 1, length), f32),
         ),
-        in_specs=[rows, pl.BlockSpec((nt, 1, length, 2 * HD), lambda b, i: (0, b, 0, 0))],
-        out_specs=(rows, rows, pl.BlockSpec((1, 1, 1, length), lambda b, i: (i, b, 0, 0))),
-        scratch_shapes=[pltpu.VMEM((nt, HD, length), bf16)],
+        in_specs=[in_vmem()] * 2,
+        out_specs=(in_vmem(),) * 5,
+        scratch_shapes=[
+            pltpu.VMEM((u, batch, 1, length), f32),
+            pltpu.VMEM((u, batch, 1, length), f32),
+            pltpu.VMEM(dealt, f32),
+            pltpu.VMEM(dealt, bf16),
+        ]
+        + [dma(u) for _ in range(4)]
+        + [dma(u, nb) for _ in range(2)]
+        + [dma(u) for _ in range(2)]
+        + [dma(2)],
         cost_estimate=SHORT,
-        compiler_params=params(),
-        name="flash",
+        compiler_params=params(cid),
+        name="self_attention",
     )(q, kv)
 
 
-def flash_back_kernel(q_ref, d_ref, of_ref, lse_ref, kv_ref, dq_ref, dkv_ref, qd, rows, delta, acc):
+def flash_back_kernel(
+    nt, q_ref, d_ref, of_ref, lse_ref, kv_ref, mixed_t, grad_attn, early_ref, dq_ref, dkv_ref, early,
+    qd, rows, delta, acc, mine, *scratch
+):
     u, length = q_ref.shape[0], q_ref.shape[3]
     j = pl.program_id(1)
+    last_j = pl.num_programs(1) - 1
+    at = lambda step: (pl.program_id(0) == 0) & (j == step)
+    sums = TileSum(nt, mine, early, scratch[:3], scratch[3:], None)
+    steps = list(sums.steps())
+
+    @pl.when(at(0))
+    def _():
+        features = mixed_t.shape[0]
+        mine[pl.ds(0, features), :] = dot(mixed_t[...], grad_attn[...]).astype(bf16)
+        mine[pl.ds(features, 2 * features), :] = early_ref[...]
+        spare = mine.shape[0] - 3 * features
+        if spare:
+            mine[pl.ds(3 * features, spare), :] = jnp.zeros((spare, mine.shape[1]), bf16)
+        clear(early)
+        a, b, s = sums.a, sums.b, sums.s
+        barrier = pltpu.get_barrier_semaphore()
+        up, down = a + 1 < nt // 2, a > 0
+        for there, peer in ((up, (a + 1) * 2 + b), (down, (a - 1) * 2 + b)):
+
+            @pl.when(there)
+            def _():
+                pl.semaphore_signal(barrier, inc=1, device_id=(peer, s), device_id_type=MESH)
+
+        pl.semaphore_signal(barrier, inc=1, device_id=sums.pair, device_id_type=MESH)
+        pl.semaphore_wait(barrier, 1 + jnp.where(up, 1, 0) + jnp.where(down, 1, 0))
+        sums.start()
 
     @pl.when(j == 0)
     def _():
@@ -511,145 +906,64 @@
         acc[i] += dot(kt, grads)
     dkv_ref[0, 0] = total.astype(bf16)
 
-    @pl.when(j == pl.num_programs(1) - 1)
+    for before in range(3, 0, -1):
+
+        @pl.when(at(last_j - before))
+        def _():
+            sums.add(steps[2 * (3 - before) : 2 * (4 - before)])
+
+    @pl.when(at(last_j))
+    def _():
+        sums.add(steps[6:])
+        sums.end_add()
+
+    @pl.when(j == last_j)
     def _():
         for i in range(u):
             dq_ref[i, 0] = (acc[i] * 0.125).astype(bf16)
 
 
-def flash_back(q, d, of, lse, kv):
+def flash_back(q, d, of, lse, kv, mixed_t, grad_attn, early, cid):
     u, batch, _, length = q.shape
     nt = kv.shape[0]
     whole = pl.BlockSpec((u, 1, HD, length), lambda b, j: (0, b, 0, 0))
     part = pl.BlockSpec((1, 1, length, 2 * HD), lambda b, j: (j, b, 0, 0))
+    sums = (round_up(3 * u * HD, 16 * nt), grad_attn.shape[1])
     return pl.pallas_call(
-        flash_back_kernel,
+        functools.partial(flash_back_kernel, nt),
         grid=(batch, nt),
-        out_shape=(jax.ShapeDtypeStruct(q.shape, bf16), jax.ShapeDtypeStruct(kv.shape, bf16)),
+        out_shape=(
+            jax.ShapeDtypeStruct(q.shape, bf16),
+            jax.ShapeDtypeStruct(kv.shape, bf16),
+            jax.ShapeDtypeStruct(sums, bf16),
+        ),
         in_specs=[
             whole,
             whole,
             whole,
             pl.BlockSpec((u, 1, 1, length), lambda b, j: (0, b, 0, 0)),
             part,
-        ],
-        out_specs=(whole, part),
+        ]
+        + [in_vmem()] * 3,
+        out_specs=(whole, part, in_vmem()),
         scratch_shapes=[
             pltpu.VMEM((u, 2, 2 * HD, length), bf16),
             pltpu.VMEM((u, 2, length, 2 * HD), bf16),
             pltpu.VMEM((u, 1, length), f32),
             pltpu.VMEM((u, HD, length), f32),
-        ],
+            pltpu.VMEM(sums, bf16),
+        ]
+        + TileSum.buffers(*sums)
+        + TileSum.sems(),
         cost_estimate=SHORT,
-        compiler_params=params(),
+        compiler_params=params(cid),
         name="flash_back",
-    )(q, d, of, lse, kv)
-
-
-class TileSum:
-    PARTS = 4
-
-    def __init__(self, nt, copies, x, out, got1, stage, got2, sems):
-        t, s = lax.axis_index("tile"), lax.axis_index("sub")
-        self.na, self.copies, self.x, self.out = nt // 2, copies, x, out
-        self.got1, self.stage, self.got2 = got1, stage, got2
-        self.a, self.b, self.s = t // 2, lax.rem(t, 2), s
-        self.me, self.pair = (t, s), (self.a * 2 + 1 - self.b, s)
-        self.half = x.shape[0] // 2
-        self.piece = self.half // 2 // self.PARTS
-        (self.s1, self.r1, self.s2, self.r2, self.s3, self.r3, self.s4, self.r4) = sems
-
-    @staticmethod
-    def scratch(nt, rows, width):
-        return [pltpu.VMEM((rows // 2, width), bf16) for _ in range(3)] + [
-            dma(2, TileSum.PARTS) for _ in range(8)
-        ]
-
-    def rows(self, b, e, j):
-        start = b * self.half + (j * 2 + e) * self.piece
-        return pl.ds(pl.multiple_of(start, 16), self.piece)
-
-    def along(self, e):
-        up, down = (self.a * 2 + 2 + self.b, self.s), (self.a * 2 - 2 + self.b, self.s)
-        return (down, up, self.a) if e else (up, down, self.na - 1 - self.a)
-
-    def start(self):
-        for j in range(self.PARTS):
-            for e in range(2):
-                src, dst = self.x.at[self.rows(1 - self.b, e, j)], self.got1.at[self.rows(0, e, j)]
-                self.copies.send(src, dst, self.s1.at[e, j], self.r1.at[e, j], self.pair)
-
-    def steps(self):
-        return range(self.PARTS + self.na - 1)
-
-    def step_of(self, way, step, action):
-        j = step - way
-        pl.when((j >= 0) & (j < self.PARTS))(lambda: action(jnp.clip(j, 0, self.PARTS - 1)))
-
-    def add(self, steps):
-        for step in steps:
-            for e in range(2):
-                self.step_of(self.along(e)[2], step, functools.partial(self.add_one, e))
-
-    def add_one(self, e, j):
-        _, after, way = self.along(e)
-        here, mine = self.rows(0, e, j), self.rows(self.b, e, j)
-        arrived(self.got1.at[here], self.s1.at[e, j], self.r1.at[e, j], self.me)
-        both = self.x[mine].astype(f32) + self.got1[here].astype(f32)
-
-        @pl.when(way == 0)
-        def _():
-            self.stage[here] = both.astype(bf16)
-
-        @pl.when(way > 0)
-        def _():
-            arrived(self.got2.at[here], self.s2.at[e, j], self.r2.at[e, j], self.me)
-            self.stage[here] = (both + self.got2[here].astype(f32)).astype(bf16)
-
-        @pl.when(way < self.na - 1)
-        def _():
-            src, dst = self.stage.at[here], self.got2.at[here]
-            remote(src, dst, self.s2.at[e, j], self.r2.at[e, j], after).start()
-
-        @pl.when(way == self.na - 1)
-        def _():
-            self.out[mine] = self.stage[here]
-
-    def share(self, steps):
-        for step in steps:
-            for e in range(2):
-                way = self.na - 1 - self.along(e)[2]
-                self.step_of(way, step, functools.partial(self.share_one, e))
-
-    def share_one(self, e, j):
-        before, _, way = self.along(e)
-        block = self.out.at[self.rows(self.b, e, j)]
-
-        @pl.when(way < self.na - 1)
-        def _():
-            arrived(block, self.s3.at[e, j], self.r3.at[e, j], self.me)
-
-        @pl.when(way > 0)
-        def _():
-            remote(block, block, self.s3.at[e, j], self.r3.at[e, j], before).start()
-
-        remote(block, block, self.s4.at[e, j], self.r4.at[e, j], self.pair).start()
-
-    def end(self):
-        for j in range(self.PARTS):
-            for e in range(2):
-                block = self.out.at[self.rows(1 - self.b, e, j)]
-                arrived(block, self.s4.at[e, j], self.r4.at[e, j], self.me)
-        for j in range(self.PARTS):
-            for e in range(2):
-                before, after, way = self.along(e)
-                block = self.out.at[self.rows(self.b, e, j)]
-                stage = self.stage.at[self.rows(0, e, j)]
-                sent = remote(stage, stage, self.s2.at[e, j], self.r2.at[e, j], after)
-                pl.when(way < self.na - 1)(sent.wait_send)
-                sent = remote(block, block, self.s3.at[e, j], self.r3.at[e, j], before)
-                pl.when(way > 0)(sent.wait_send)
-                remote(block, block, self.s4.at[e, j], self.r4.at[e, j], self.pair).wait_send()
+    )(q, d, of, lse, kv, mixed_t, grad_attn, early)
+
+
+class Nothing:
+    def __getattr__(self, name):
+        return lambda *args: None
 
 
 class FullSum:
@@ -923,10 +1237,6 @@
     return multiply(jnp.concatenate(taps, axis=1), weight)
 
 
-def dot_t(left, right):
-    return lax.dot_general(left, right, (((1,), (1,)), ((), ())), preferred_element_type=f32)
-
-
 def turned_taps(weight):
     return jnp.concatenate([weight[8 - k] for k in range(9)], axis=1)
 
@@ -966,11 +1276,6 @@
 def sides(left, right, i):
     place = lax.broadcasted_iota(jnp.int32, right.shape[1:], 0)
     return jnp.where(place < 8, right[i].astype(f32), left[i + 1].astype(f32))
-
-
-def clear(*refs):
-    for ref in refs:
-        ref[...] = jnp.zeros_like(ref)
 
 
 def outer_forward_kernel(
@@ -1078,7 +1383,8 @@
                 for k in range(1, POOL):
                     mean = mean + rowsum[n, pl.ds(k, lc, stride=POOL), :]
                 means.append(mean * (1.0 / (POOL * POOL)))
-            pooled[start // POOL + half] = jnp.concatenate(means, axis=1)
+            place = pl.ds((start // POOL + half) * lc, lc)
+            pooled[place, :] = jnp.concatenate(means, axis=1).astype(bf16)
     for k in range(1, ns):
         p = lax.rem(s + k, ns)
         arrived(gains_out.at[p], gain_ss.at[k], gain_rs.at[p], (t, s))
@@ -1098,7 +1404,7 @@
         functools.partial(outer_forward_kernel, nt, ns),
         out_shape=(
             shape(img.shape, bf16),
-            shape((rows // POOL, cols // POOL, channels), f32),
+            shape((rows // POOL * (cols // POOL), channels), bf16),
             shape((long1, 3 * channels), bf16),
             shape((long2, 3 * channels), bf16),
             shape((long2, channels), f32),
@@ -1138,8 +1444,8 @@
 
 
 def outer_backward_kernel(
-    nt, ns, cot, img, w2, w1, vec, stats, hidden, wide, tokens, gains, pooled, lifted, lift_weight,
-    attn_in, grad_q_t, grad_kv, grad_cq_w, grad_ck, grad_cv, act1_in, act2_in, outer_grad, tall_out, wide_out, tokens_out, sum2_out, sum1_out, back_out,
+    nt, ns, cut, cot, img, w2, w1, vec, stats, hidden, wide, tokens, gains, pooled, lifted, lift_weight,
+    attn_in, grad_q_t, grad_kv, grad_ck, grad_cv, act1_in, act2_in, outer_grad, tall_out, wide_out, tokens_out, sum2_out, sum1_out, back_out,
     spread, grad2, body, left, right, flat, act1, act2, triple, inner_t, slope, own2, own1, tall,
     border_ss, border_rs, keep, token_ss, token_rs, *scratch
 ):
@@ -1149,13 +1455,22 @@
     t, s = lax.axis_index("tile"), lax.axis_index("sub")
     sums2, sums1, scratch = scratch[:6], scratch[6:12], scratch[12:]
     copies = Copies()
-    weights = []
-    for x, out in ((wide, wide_out), (tall, tall_out)):
-        weights.append(TileSum(nt, copies, x, out, *scratch[:3], scratch[3:11]))
-        scratch = scratch[11:]
+    early = TileSum(nt, None, wide_out, None, None, scratch[:4])
+    late = TileSum(nt, tall, tall_out, scratch[4:7], scratch[7:11], scratch[11:15])
+    scratch = scratch[15:]
+    wide_out[...] = wide[...]
     second = FullSum(nt, ns, copies, own2, sum2_out, *scratch[:5], scratch[5:17])
     scratch = scratch[17:]
-    first = FullSum(nt, ns, copies, own1, sum1_out, *scratch[:5], scratch[5:17])
+    first, rest = Nothing(), []
+    for skip, rows_of_sum in ((0, cut), (cut, own1.shape[0] - cut)):
+        if rows_of_sum:
+            part = pl.ds(skip, rows_of_sum)
+            views = own1.at[part], sum1_out.at[part]
+            rest.append(FullSum(nt, ns, copies, *views, *scratch[:5], scratch[5:17]))
+            scratch = scratch[17:]
+    if len(rest) > 1:
+        first = rest[0]
+    rest = rest[-1]
     count = float(nt * ns * rows * cols * (channels // G))
     held = [
         pltpu.make_async_copy(act2_in, act2, keep.at[0]),
@@ -1165,7 +1480,6 @@
         copy.start()
     clear(body, left, right)
     greet_all(nt, ns)
-    weights[0].start()
     width = lifted.shape[1]
     shrunk = dot_t(lifted[...], lift_weight[...]) * (1.0 / (POOL * POOL))
 
@@ -1206,14 +1520,16 @@
         part = jnp.concatenate(lanes, axis=1) if heads > 1 else lanes[0]
         tall[pl.ds((1 + n) * width, width), :] = part.astype(bf16)
     used = 3 * width
-    for ref in (grad_cq_w, grad_ck, grad_cv):
+    for ref in (grad_ck, grad_cv):
         tall[pl.ds(used, ref.shape[0]), :] = ref[...]
         used += ref.shape[0]
     if used < tall.shape[0]:
         tall[pl.ds(used, tall.shape[0] - used), :] = jnp.zeros(
             (tall.shape[0] - used, features), bf16
         )
-    weights[1].start()
+    late.start()
+    steps = list(early.steps())
+    early.share(steps[:1])
     total = rows * pitch
 
     def turned(row):
@@ -1232,7 +1548,8 @@
     taps = 9 * channels
     turned(lambda i: grad2[i])
     held[0].wait()
-    kernel_grads(act2, inner_t, 16, total, pitch, own2)
+    between = [lambda k=k: early.share(steps[k : k + 1]) for k in (1, 2, 3)]
+    kernel_grads(act2, inner_t, 16, total, pitch, own2, between)
     lift_grad = dot(pooled[...].T, lifted[...]).astype(bf16)
     for n in range(width // channels):
         own2[pl.ds(taps + n * channels, channels), :] = lift_grad[
@@ -1240,6 +1557,7 @@
         ]
     pad_below(own2, taps + width)
     second.start()
+    early.share(steps[4:5])
     finish(border)
     ok = lambda lift_by: (
         lambda i: (t * rows + i - lift_by >= 0) & (t * rows + i - lift_by < nt * rows)
@@ -1263,8 +1581,8 @@
             triple, w2t, start, size, pitch, dot_t
         ) * silu_slope(hat * gain2 + bias2)
         if start == size:
-            weights[0].add([0])
-    weights[0].add([1])
+            early.share(steps[5:6])
+    early.share(steps[6:])
 
     at = lambda i: pl.multiple_of(16 + i * pitch, 16)
 
@@ -1277,8 +1595,7 @@
     plain = sum_near(nt, ns, local2, sums2[0], sums2[2], sums2[3])
     plain += sum_far(nt, ns, sums2[0], sums2[1], *sums2[2:])
     second.spread()
-    steps = weights[0].steps()
-    weights[0].add(steps[2:5])
+    late.add(steps[:2])
     back2 = sum_end(nt, sums2[1], sums2[4], sums2[5])
     back2, gains_total = back2[:2], back2[2:]
     means2 = in_groups(back2 * gain2) / count
@@ -1294,20 +1611,17 @@
         lambda i: grad_hidden(at(i) + cols, 16),
         lambda: grad_hidden(0, 16),
     )
-    weights[0].add(steps[5:6])
+    late.add(steps[2:3])
     turned(lambda i: flat[pl.ds(24 + (i + 1) * pitch, cols), :].astype(bf16))
     held[1].wait()
-    between = [
-        lambda: weights[0].add(steps[6:]),
-        lambda: weights[1].add([0]),
-        lambda: weights[1].add([1]),
-    ]
+    between = [lambda: late.add(steps[3:4]), lambda: first.start(), lambda: late.add(steps[4:5])]
     kernel_grads(act1, inner_t, 16 + pitch, total, pitch, own1, between)
     pad_below(own1, taps)
-    first.start()
+    rest.start()
     second.settle()
+    first.cross()
     put_left_to_right(flat, triple.at[pl.ds(0, length)])
-    first.cross()
+    rest.cross()
     hat1 = lambda i: (img[i].astype(f32) - center1) * std1
     step = 2 * POOL
     w1t = turned_taps(w1)
@@ -1317,20 +1631,20 @@
         hat = (img[pl.ds(start, step)].astype(f32) - center1) * std1
         outer_grad[pl.ds(start, step)] = value * silu_slope(hat * gain1 + bias1)
         if start == step:
-            weights[1].add([2])
-            weights[0].share([0])
-    weights[1].add([3])
-    weights[0].share([1])
+            late.add(steps[5:6])
+    first.spread()
+    late.add(steps[6:])
+    late.share(steps[:1])
     local1 = row_sums(rows, channels, lambda i: (outer_grad[i], outer_grad[i] * hat1(i)))
     plain += sum_near(nt, ns, local1, sums1[0], sums1[2], sums1[3])
-    first.spread()
+    rest.spread()
     plain += sum_far(nt, ns, sums1[0], sums1[1], *sums1[2:])
-    weights[1].add([4])
-    weights[0].share([2])
+    late.share(steps[1:3])
+    second.share()
     back1 = sum_end(nt, sums1[1], sums1[4], sums1[5])
     means1 = in_groups(back1 * gain1) / count
-    weights[1].add([5])
-    weights[0].share([3])
+    first.settle()
+    late.share(steps[3:4])
 
     def last(i, carry):
         value = outer_grad[i] * gain1 - means1[0:1] - hat1(i) * means1[1:2]
@@ -1341,25 +1655,23 @@
     back_out[...] = jnp.concatenate(
         [back1, back2, means2, jnp.zeros_like(means2), gains_total], axis=0
     )
-    for step in steps[6:]:
-        weights[1].add([step])
-    weights[1].share([0])
-    first.settle()
-    second.share()
-    for i, step in enumerate(steps[4:]):
-        weights[0].share([step])
-        weights[1].share([1 + i])
+    rest.settle()
+    late.share(steps[4:5])
     first.share()
+    late.share(steps[5:])
     second.relay()
-    weights[1].share(steps[1 + len(steps[4:]) :])
+    rest.share()
+    first.relay()
     for k in range(1, ns):
         block = tokens_out.at[lax.rem(s + ns - k, ns)]
         arrived(block, token_ss.at[k], token_rs.at[k], (t, s))
-    first.relay()
+    rest.relay()
+    early.end_share()
     second.end()
-    for each in weights:
-        each.end()
     first.end()
+    late.end_add()
+    late.end_share()
+    rest.end()
     copies.finish()
     for copy in plain:
         copy.wait_send()
@@ -1367,7 +1679,7 @@
 
 def outer_backward(
     cot, img, w2, w1, vec, stats, hidden, wide, tokens, gains, pooled, lifted, lift_weight,
-    attn_in, grad_q_t, grad_kv, grad_cq_w, grad_ck, grad_cv, act1, act2, cid
+    attn_in, grad_q_t, grad_kv, grad_ck, grad_cv, act1, act2, cid
 ):
     nt, ns = lax.axis_size("tile"), lax.axis_size("sub")
     rows, cols, channels = img.shape
@@ -1377,10 +1689,11 @@
     step = 16 * nt * ns
     width, features = attn_in.shape[1], grad_q_t.shape[0]
     rows2 = round_up(9 * channels + width, step)
-    tall = (round_up(4 * width + 2 * grad_ck.shape[0], 16 * nt), features)
+    tall = (round_up(3 * width + 2 * grad_ck.shape[0], 16 * nt), features)
+    cut = 6 * channels // step * step
     rows1 = round_up(9 * channels, step)
     return pl.pallas_call(
-        functools.partial(outer_backward_kernel, nt, ns),
+        functools.partial(outer_backward_kernel, nt, ns, cut),
         out_shape=(
             shape(img.shape, f32),
             shape(tall, bf16),
@@ -1390,7 +1703,7 @@
             shape((rows1, channels), bf16),
             shape((8 + gains.shape[0], channels), f32),
         ),
-        in_specs=[in_vmem()] * 19 + [anywhere()] * 2,
+        in_specs=[in_vmem()] * 18 + [anywhere()] * 2,
         out_specs=(in_vmem(),) * 7,
         scratch_shapes=[
             pltpu.VMEM((rows // POOL, channels // 128, cols, 128), f32),
@@ -1415,24 +1728,28 @@
         ]
         + sum_scratch(nt, ns, channels, 2 + gains.shape[0])
         + sum_scratch(nt, ns, channels)
-        + TileSum.scratch(nt, *wide.shape)
-        + TileSum.scratch(nt, *tall)
+        + TileSum.sems()
+        + TileSum.buffers(*tall)
+        + TileSum.sems()
+        + TileSum.sems()
         + FullSum.scratch(nt, ns, rows2, channels)
-        + FullSum.scratch(nt, ns, rows1, channels),
+        + (FullSum.scratch(nt, ns, cut, channels) if cut else [])
+        + FullSum.scratch(nt, ns, rows1 - cut, channels),
         cost_estimate=SHORT,
         compiler_params=params(cid, 62),
         name="outer_backward",
     )(
         cot, img, w2, w1, vec, stats, hidden, wide, tokens, gains, pooled, lifted, lift_weight,
-        attn_in, grad_q_t, grad_kv, grad_cq_w, grad_ck, grad_cv, act1, act2,
+        attn_in, grad_q_t, grad_kv, grad_ck, grad_cv, act1, act2,
     )
 
 
 def finish_kernel(text, up, down, *refs):
-    q, k, v, cq, ck, cv, o, co, second, first = refs[:10]
+    q, k, v, ck, cv, o, co, cq, second, first = refs[:10]
     lift, refs = refs[10:-13], refs[-13:]
-    for src, dst in zip((q, k, v, cq, o, co, second, first, up, down), refs[:10]):
+    for src, dst in zip((q, k, v, o, co, second, first, up, down), refs[:9]):
         dst[...] = src[...].astype(f32)
+    refs[9][...] = cq[...].T.astype(f32)
     turned = text[...].T
     refs[10][...] = dot(turned, ck[...])
     refs[11][...] = dot(turned, cv[...])
@@ -1442,15 +1759,16 @@
 def finish_grads(text, up, down, tall, wide, second, first, taps, text_rows):
     features, width = tall.shape[1], wide.shape[1]
     channels = first.shape[1]
-    steps = features // 16
+    steps = features // 32
     row = lambda size, lanes, skip=0: pl.BlockSpec((size, lanes), lambda i: (skip + i, 0))
     size = width // steps
-    tall_specs = [row(size, features, n * steps) for n in range(4)]
-    start = 4 * width // text_rows
+    tall_specs = [row(size, features, n * steps) for n in range(3)]
+    start = 3 * width // text_rows
     tall_specs += [
         pl.BlockSpec((text_rows, features), lambda i, n=n: (start + n, 0)) for n in range(2)
     ]
-    wide_specs = [row(16, width, n * steps) for n in range(2)]
+    wide_specs = [row(32, width, n * steps) for n in range(2)]
+    wide_specs.append(pl.BlockSpec((features, size), lambda i: (2, i)))
     size = taps // steps
     lift_size = channels // steps
     lift_specs = [
@@ -1464,22 +1782,23 @@
     return pl.pallas_call(
         finish_kernel,
         grid=(steps,),
-        out_shape=(shape(width, features),) * 4
+        out_shape=(shape(width, features),) * 3
         + (shape(features, width),) * 2
         + (shape(taps, channels),) * 2
-        + (shape(*up.shape), shape(*down.shape))
+        + (shape(*up.shape), shape(*down.shape), shape(width, features))
         + (shape(full, features), shape(full, features), shape(channels, width)),
         in_specs=in_specs,
-        out_specs=[row(width // steps, features)] * 4
-        + [row(16, width)] * 2
+        out_specs=[row(width // steps, features)] * 3
+        + [row(32, width)] * 2
         + [row(size, channels)] * 2
         + up_specs
+        + [row(width // steps, features)]
         + [row(full // steps, features)] * 2
         + [row(lift_size, width)],
         cost_estimate=SHORT,
         compiler_params=params(),
         name="finish_grads",
-    )(text, up, down, *[tall] * 6, *[wide] * 2, second, first, *[second] * len(lift_specs))
+    )(text, up, down, *[tall] * 5, *[wide] * 3, second, first, *[second] * len(lift_specs))
 
 
 def time_embed(time_steps, channels):
@@ -1491,35 +1810,8 @@
     return jnp.concatenate([jnp.sin(angles), jnp.cos(angles)], axis=1)
 
 
-def layer_stats(values, gain):
-    width = values.shape[1]
-    center = jnp.sum(values, axis=1, keepdims=True) / width
-    moved = values - center
-    inv_std = lax.rsqrt(jnp.sum(moved * moved, axis=1, keepdims=True) / width + EPSILON)
-    normed = moved * inv_std
-    return (normed * gain).astype(bf16), normed, inv_std
-
-
-def layer_back(grad_out, normed, inv_std, gain):
-    width = normed.shape[1]
-    scaled = grad_out * gain
-    mean_grad = jnp.sum(scaled, axis=1, keepdims=True) / width
-    mean_cross = jnp.sum(scaled * normed, axis=1, keepdims=True) / width
-    grad_in = inv_std * (scaled - mean_grad - normed * mean_cross)
-    return grad_in, jnp.sum(grad_out * normed, axis=0)
-
-
-def gelu_tanh(values):
-    return jax.nn.gelu(values, approximate=True)
-
-
 def weight_grad(inputs, grads):
     return lax.dot_general(inputs, grads, (((0,), (0,)), ((), ())), preferred_element_type=f32)
-
-
-def cross_scores(queries, keys, text_mask):
-    scores = jnp.einsum("sbqhd,bkhd->sbhqk", queries, keys, preferred_element_type=f32)
-    return jnp.where(text_mask[None, :, None, None, :], scores * HD ** (-0.5), -1000000000.0)
 
 
 def local(
@@ -1571,16 +1863,16 @@
         return full, mine
 
     _, inner_own = whole_tokens(inner_image)
-    cotan_full, cotan_own = whole_tokens(inner_cotan)
-    cotan_full = jnp.transpose(cotan_full, (2, 0, 1, 3, 4)).reshape(ns * own, width)
+    cotan_full, _ = whole_tokens(inner_cotan)
+    cotan_full = jnp.transpose(cotan_full, (2, 0, 1, 3, 4)).reshape(ns, own, width)
     own_gains = jnp.stack([attn_gain, cross_gain, mlp_gain])
 
     time_act = jax.nn.silu(time_embed(time_steps, channels))
     time_shift = jnp.dot(time_act, time_weight.astype(f32), precision=precise)
-    vectors = jnp.zeros((batch, 8, channels), f32)
-    for i, vector in enumerate([first_gain, first_bias, second_gain, second_bias]):
-        vectors = vectors.at[:, i].set(vector)
-    vectors = vectors.at[:, 4].set(time_shift)
+    fixed = jnp.stack([first_gain, first_bias, second_gain, second_bias])
+    fixed = jnp.broadcast_to(fixed[None], (batch, 4, channels))
+    empty = jnp.zeros((batch, 3, channels), f32)
+    vectors = jnp.concatenate([fixed, time_shift[:, None, :], empty], axis=1)
     as_rows = lambda w: w.reshape(9 * channels, channels)
     forward = [
         outer_forward(
@@ -1595,11 +1887,20 @@
     ]
     outer_out = jnp.stack([f[0] for f in forward])
     gains = jnp.transpose(forward[0][6], (1, 0, 2)).reshape(3, width)
-    pooled = jnp.stack([f[1] for f in forward]).astype(bf16).reshape(own, channels)
-
-    stream_in = inner_own.astype(f32) + dot(pooled, lift_weight).astype(bf16).astype(f32)
-    attn_low, attn_hat, attn_std = layer_stats(stream_in, gains[0])
-    attn_in = gather_sub(attn_low, 2).reshape(ns * own, width)
+    pooled = jnp.concatenate([f[1] for f in forward], axis=0)
+
+    flat = lambda v: v.reshape(-1, v.shape[-1])
+    block, rows_all = ((own, width), f32), ((ns, own, width), bf16)
+    stream_in, attn_in = chain_call(
+        enter_kernel,
+        "enter",
+        2,
+        (block, rows_all),
+        (inner_own, pooled, lift_weight, gains[0:1]),
+        (),
+        False,
+    )
+    attn_in = flat(attn_in)
 
     def per_sample(values, tokens_last):
         if tokens_last:
@@ -1623,99 +1924,123 @@
         query_weight, attn_in, (((0,), (1,)), ((), ())), preferred_element_type=f32
     ).astype(bf16)
     kv = dot(attn_in, kv_weight).astype(bf16)
-    head_q, head_kv = qkv_out(per_sample(query_t, True), per_sample(kv, False), 3)
-    head_mixed, head_mixed_f, head_lse = flash(head_q, head_kv)
-    mixed_t = all_samples(swap_heads(head_mixed, True, 4), True)
-    after_attn = stream_in + scatter_sub(weight_grad(mixed_t, out_weight), 5)
-
-    cross_low, cross_hat, cross_std = layer_stats(after_attn, gains[1])
-    cross_in = gather_sub(cross_low, 6).reshape(ns * own, width)
-    text_split = lambda w: jnp.einsum(
-        "bsw,we->bse", text_states, w, preferred_element_type=f32
-    ).astype(bf16).reshape(batch, -1, heads, HD)
-    cross_k, cross_v = text_split(cross_key), text_split(cross_value)
-    text_mask = jnp.arange(text_states.shape[1])[None, :] < text_lengths[:, None]
-    split = lambda v: v.reshape(ns, batch, lr * lc, heads, HD)
-    cross_q = split(dot(cross_in, cross_query).astype(bf16))
-    scores = cross_scores(cross_q, cross_k, text_mask)
-    cross_probs = jax.nn.softmax(scores, axis=-1)
-    cross_probs_low = cross_probs.astype(bf16)
-    cross_mixed = (
-        jnp.einsum("sbhqk,bkhd->sbqhd", cross_probs_low, cross_v, preferred_element_type=f32)
-        .astype(bf16)
-        .reshape(ns * own, features)
-    )
-    after_cross = after_attn + scatter_sub(dot(cross_mixed, cross_out), 7)
-
-    mlp_low, mlp_hat, mlp_std = layer_stats(after_cross, gains[2])
-    mlp_in = gather_sub(mlp_low, 8).reshape(ns * own, width)
-    lifted_up = dot(mlp_in, up_weight)
-    activated_f, gelu_pull = jax.vjp(gelu_tanh, lifted_up)
-    activated = activated_f.astype(bf16)
-
-    grad_act = dot_t(cotan_full, down_weight)
-    grad_lift_up = gelu_pull(grad_act)[0].astype(bf16)
-    grad_mlp_in = dot_t(grad_lift_up, up_weight).astype(bf16)
-    grad_down = weight_grad(activated, cotan_full).astype(bf16)
-    grad_up = weight_grad(mlp_in, grad_lift_up).astype(bf16)
-    grad_mlp_in, grad_down, grad_up = lax.optimization_barrier(
-        (grad_mlp_in, grad_down, grad_up)
+    mixed_t, head_q, head_kv, head_mixed_f, head_lse = self_attention(
+        per_sample(query_t, True), per_sample(kv, False), 3
+    )
+    mixed_t = all_samples(mixed_t, True)
+    after_attn, cross_in = chain_call(
+        attn_out_kernel,
+        "attn_out",
+        5,
+        (block, rows_all),
+        (mixed_t, out_weight, stream_in, gains[1:2]),
+        [pltpu.VMEM((ns * own, features), bf16)],
+        True,
+    )
+    text_rows = batch * text_states.shape[1]
+    text = text_states.reshape(text_rows, -1)
+    cross_k, cross_v = dot(text, cross_key).astype(bf16), dot(text, cross_value).astype(bf16)
+    sample_of = lambda count: jnp.arange(batch * count) // count
+    text_at = jnp.tile(jnp.arange(text_states.shape[1]), batch)
+    good = text_at < jnp.repeat(text_lengths, text_states.shape[1])
+    same = sample_of(lr * lc)[:, None] == sample_of(text_states.shape[1])[None, :]
+    mask = jnp.where(same & good[None, :], 1.0, 0.0).astype(f32)
+    head_rows = ((ns, own, features), bf16)
+    after_cross, mlp_in, cross_q, cross_mixed = chain_call(
+        cross_kernel,
+        "cross",
+        6,
+        (block, rows_all, head_rows, head_rows),
+        (cross_in, cross_query, cross_k, cross_v, mask, cross_out, after_attn, gains[2:3]),
+        (),
+        True,
+    )
+
+    units = up_weight.shape[1]
+    one_row = ((1, width), f32)
+    middle = pltpu.VMEM((ns * own, units), bf16)
+    grad_after_cross, grad_cross_full, grad_mlp_gain, down, grad_up, grad_down = chain_call(
+        mlp_kernel,
+        "mlp",
+        8,
+        (
+            block,
+            rows_all,
+            one_row,
+            ((ns * own, width), bf16),
+            ((width, units), bf16),
+            ((units, width), bf16),
+        ),
+        (mlp_in, cotan_full, up_weight, down_weight, after_cross, gains[2:3]),
+        [middle, middle],
+        True,
     )
     grad_down, grad_up = lax.psum((grad_down, grad_up), "tile")
-    grad_mid, grad_mlp_gain = layer_back(
-        scatter_sub(grad_mlp_in, 9), mlp_hat, mlp_std, gains[2]
-    )
-    grad_after_cross = cotan_own.astype(f32) + grad_mid
-    grad_cross_full = gather_sub(grad_after_cross.astype(bf16), 10).reshape(ns * own, width)
-    grad_cross_mixed = split(dot_t(grad_cross_full, cross_out).astype(bf16))
-    grad_cv = jnp.einsum(
-        "sbhqk,sbqhd->bkhd", cross_probs_low, grad_cross_mixed, preferred_element_type=f32
-    )
-    grad_probs = jnp.einsum(
-        "sbqhd,bkhd->sbhqk", grad_cross_mixed, cross_v, preferred_element_type=f32
-    )
-    grad_scores = (
-        cross_probs
-        * (grad_probs - jnp.sum(cross_probs * grad_probs, axis=-1, keepdims=True))
-    ).astype(bf16)
-    grad_cq = (
-        jnp.einsum("sbhqk,bkhd->sbqhd", grad_scores, cross_k, preferred_element_type=f32)
-        * HD ** (-0.5)
-    ).astype(bf16).reshape(ns * own, features)
-    grad_ck = jnp.einsum(
-        "sbhqk,sbqhd->bkhd", grad_scores, cross_q, preferred_element_type=f32
-    ) * HD ** (-0.5)
-    grad_mid, grad_cross_gain = layer_back(
-        scatter_sub(dot_t(grad_cq, cross_query), 11), cross_hat, cross_std, gains[1]
-    )
-    grad_after_attn = grad_after_cross + grad_mid
-    grad_attn_full = gather_sub(grad_after_attn.astype(bf16), 12).reshape(ns * own, width)
+    text_block = ((text_rows, features), bf16)
+    (
+        grad_after_attn,
+        grad_attn_full,
+        grad_cross_gain,
+        grad_ck,
+        grad_cv,
+        grad_early,
+    ) = chain_call(
+        cross_back_kernel,
+        "cross_back",
+        10,
+        (
+            block,
+            rows_all,
+            one_row,
+            text_block,
+            text_block,
+            ((2, features, width), bf16),
+        ),
+        (
+            grad_cross_full,
+            cross_out,
+            cross_q,
+            cross_k,
+            cross_v,
+            mask,
+            cross_query,
+            after_attn,
+            gains[1:2],
+            grad_after_cross,
+            cross_in,
+            cross_mixed,
+        ),
+        [pltpu.VMEM((text_rows, features), f32)] * 2
+        + [pltpu.VMEM((ns * own, features), bf16)],
+        True,
+    )
+    grad_attn_full = flat(grad_attn_full)
     grad_mixed_t = dot_t(out_weight, grad_attn_full).astype(bf16)
     head_d = swap_heads(per_sample(grad_mixed_t, True), False, 13)
-    head_dq, head_dkv = flash_back(head_q, head_d, head_mixed_f, head_lse, head_kv)
-    down = dot(activated, down_weight).astype(bf16)
-    grad_q_t, grad_kv, down_own, wide, grad_cq_w = dqkv_home(
-        head_dq,
-        head_dkv,
-        down,
+    head_dq, head_dkv, wide = flash_back(
+        head_q,
+        head_d,
+        head_mixed_f,
+        head_lse,
+        head_kv,
         mixed_t,
         grad_attn_full,
-        cross_mixed,
-        grad_cross_full,
-        cross_in,
-        grad_cq,
-        14,
-    )
+        grad_early.reshape(2 * features, width),
+        16,
+    )
+    grad_q_t, grad_kv, down_own = dqkv_home(head_dq, head_dkv, down, 14)
     grad_q_t, grad_kv = all_samples(grad_q_t, True), all_samples(grad_kv, False)
-    grad_attn_in = weight_grad(grad_q_t, query_weight.T) + dot_t(grad_kv, kv_weight)
-    grad_mid, grad_attn_gain = layer_back(
-        scatter_sub(grad_attn_in, 15), attn_hat, attn_std, gains[0]
-    )
-    inner_grad = grad_after_attn + grad_mid
-    grad_lifted = inner_grad.astype(bf16)
-
-    text_rows = grad_ck.shape[0] * grad_ck.shape[1]
-    grad_ck, grad_cv = (v.reshape(text_rows, features).astype(bf16) for v in (grad_ck, grad_cv))
+    grad_lifted, grad_attn_gain = chain_call(
+        attn_back_kernel,
+        "attn_back",
+        15,
+        (((own, width), bf16), one_row),
+        (grad_q_t, grad_kv, query_weight, kv_weight, stream_in, gains[0:1], grad_after_attn),
+        [pltpu.VMEM((ns * own, features), bf16), pltpu.VMEM((own, width), f32)],
+        True,
+        False,
+    )
+
     inner_sum = after_cross + down_own
     tokens = jnp.stack([inner_sum.astype(bf16), grad_lifted])
     tokens = tokens.reshape(2, own, ns, features).transpose(2, 0, 1, 3)
@@ -1743,7 +2068,6 @@
                 attn_in,
                 once(grad_q_t),
                 once(grad_kv),
-                once(grad_cq_w),
                 once(grad_ck),
                 once(grad_cv),
                 forward[b][2],
@@ -1763,7 +2087,7 @@
     else:
         sum2, sum1 = backward[0][4:6]
     ends = finish_grads(
-        text_states.reshape(text_rows, -1),
+        text,
         grad_up,
         grad_down,
         tall,
@@ -1773,9 +2097,9 @@
         9 * channels,
         text_rows,
     )
-    grad_q_w, grad_k_w, grad_v_w, grad_cq_w, grad_o_w, grad_co_w = ends[:6]
-    grad_conv_second, grad_conv_first = (v.reshape(conv_first.shape) for v in ends[6:8])
-    grad_up, grad_down = ends[8:10]
+    grad_q_w, grad_k_w, grad_v_w, grad_o_w, grad_co_w = ends[:5]
+    grad_conv_second, grad_conv_first = (v.reshape(conv_first.shape) for v in ends[5:7])
+    grad_up, grad_down, grad_cq_w = ends[7:10]
     grad_ck_w, grad_cv_w, grad_lift = ends[10:]
     stats = jnp.stack([f[5] for f in forward])
     back = jnp.stack([f[6] for f in backward])

time: 610 us -> 506 us (0.83)
  Pallas kernels: 483 us -> 450 us
  matrix products: 43.6 us -> 11.5 us
  other arithmetic: 31.8 us -> 8.51 us
  local copies, waits for them, and re-layouts: 23.4 us -> 14.7 us
    convert_element_type x7 -> x0, other arithmetic: 18.2 us -> none  [the longest x1 12.2 us: local(): grad_after_cross.astype(bf16)]
    dot_general x12 -> x0, matrix products: 17.2 us -> none  [the longest x4 9.35 us: weight_grad(): lax.dot_general(inputs, grads, (((0,), (0,)), ((), ())), preferred_elemen...]
    pallas_call x14 -> x9, Pallas kernels: 367 us -> 350 us  [the longest x1 133 us: outer_backward(): pl.pallas_call(functools.partial(outer_backward_kernel, nt, ns, cut), out...]
    dot_general x6 -> x1, matrix products: 11.5 us -> 2.41 us  [dot_t(): lax.dot_general(left, right, (((1,), (1,)), ((), ())), preferred_element_...]
    pallas_call x2 -> x1, Pallas kernels: 20 us -> 12.7 us  [swap_heads(): pl.pallas_call(functools.partial(swap_kernel, nt, u, home), out_shape=jax...]
    pallas_call x1, Pallas kernels: 36.4 us -> 29.5 us  [dqkv_home(): pl.pallas_call(functools.partial(dqkv_home_kernel, nt, ns, u), out_shape=...]
    dot_general x6 -> x3, matrix products: 12.7 us -> 6.5 us  [dot(): return jnp.dot(left, right, preferred_element_type=f32)]
  transfers between devices with their start and end apart: 3 -> 3, of which waited for: 0 -> 0; matrix products, arithmetic and copies ran while one was open for 5% -> 6% of each run, Pallas kernels for 51% -> 65%
where the time goes in v3:
time: 506 us; the launch traced here: 502 us
  Pallas kernels  450 us (89%)
  between operations  15.7 us (3%)
  local copies, waits for them, and re-layouts  14.7 us (3%)
  matrix products  11.5 us (2%)
  other arithmetic  8.51 us (2%)
    pallas_call x1, Pallas kernels, outer_backward(): pl.pallas_call(functools.partial(outer_backward_kernel, nt, ns, cut), out...  133 us
    pallas_call x6, Pallas kernels, chain_call(): pl.pallas_call(functools.partial(kernel, ns), out_shape=tuple((jax.ShapeD...  125 us
    pallas_call x1, Pallas kernels, flash_back(): pl.pallas_call(functools.partial(flash_back_kernel, nt), grid=(batch, nt)...  52.3 us
    pallas_call x1, Pallas kernels, outer_forward(): pl.pallas_call(functools.partial(outer_forward_kernel, nt, ns), out_shape...  43.3 us
    pallas_call x1, Pallas kernels, self_attention(): pl.pallas_call(functools.partial(self_attention_kernel, nt, u), out_shape...  40.6 us
    pallas_call x1, Pallas kernels, dqkv_home(): pl.pallas_call(functools.partial(dqkv_home_kernel, nt, ns, u), out_shape=...  29.5 us
    pallas_call x1, Pallas kernels, finish_grads(): pl.pallas_call(finish_kernel, grid=(steps,), out_shape=(shape(width, feat...  14.3 us
    pallas_call x1, Pallas kernels, swap_heads(): pl.pallas_call(functools.partial(swap_kernel, nt, u, home), out_shape=jax...  12.7 us
  transfers between devices with their start and end apart: 3, of which 0 were waited for; matrix products, arithmetic and copies ran while one was open for 6% of the time, Pallas kernels for 65%

profile of v3, /device:TPU:0, one launch (start us, length us, event | category | flops | bytes accessed | tf_op | source)
XLA Modules:
  0.0 501.8 jit_solution(13837724604798076073)
XLA Ops:
  7.3 0.7 all-gather.3.cloned.1.call-update
  8.0 0.7 all-gather.5.cloned.1.call-update
  9.8 0.7 maximum_bitcast_fusion.2
  10.5 0.7 maximum_bitcast_fusion.1.vec
  11.2 1.3 pad_maximum_fusion.2.gains
  12.5 43.3 %outer_forward.1 = (bf16[32,64,256]{2,1,0:T(8,128)(2,1)}, bf16[128,256]{1,0:T(8,128)(2,1)}, bf16[2912,768]{1,0:T(8,128)(2,1)}, bf16[2752,768]{1,0:T(8,128)(2,1)}...) custom-call(bf16[32,64,256]{2,1,0:T(8,128)(2,1)} %bitcast.112, bf16[2304,256]{1,0:T(8,128)(2,1)} %bitcast.105, ...), custom_call_target="tpu_custom_call" | custom-call | flops 1 | bytes 1 | tf_op jit(solution)/shard_map/outer_forward/pallas_call | solution.py:1403
  55.8 1.4 fusion.11
  57.9 0.2 copy.61
  58.2 0.2 copy.62
  58.5 0.7 and_select_fusion.mask
  59.2 2.7 convolution_convert_fusion.3.cv
  61.9 1.1 convolution_convert_fusion.4.ck
  62.9 1.7 constant_dynamic-slice_fusion.1
  64.6 12.8 %enter.1 = (f32[128,1024]{1,0:T(8,128)}, bf16[4,128,1024]{2,1,0:T(8,128)(2,1)}) custom-call(bf16[128,1024]{1,0:T(8,128)(2,1)} %bitcast.130, bf16[128,256]{1,0:T(8,128)(2,1)} %get-tuple-element.88.pooled, bf16[256,1024]{1,0:T(8,128)(2,1)} %lift_weight.1, f32[1,1024]{1,0:T(1,128)} %bitcast.140), custom_call_target="tpu_custom_call" | custom-call | flops 1 | bytes 1 | tf_op jit(solution)/shard_map/enter/pallas_call | solution.py:465
  77.4 2.4 fusion.1.q_ref
  79.8 2.8 fusion.kv_ref
  82.6 2.3 copy.64
  84.9 40.6 %self_attention.1 = (bf16[1,256,512]{2,1,0:T(8,128)(2,1)}, bf16[4,1,64,512]{3,2,1,0:T(8,128)(2,1)}, bf16[8,1,512,128]{3,2,1,0:T(8,128)(2,1)}, f32[4,1,64,512]{3,2,1,0:T(8,128)}, f32[4,1,1,512]{3,2,1,0:T(1,128)}) custom-call(bf16[1,256,512]{2,1,0:T(8,128)(2,1)} %fusion.1.q_ref, bf16[1,512,512]{2,1,0:T(8,128)(2,1)} %fusion.kv_ref), custom_call_target="tpu_custom_call" | custom-call | flops 1 | bytes 1 | tf_op jit(solution)/shard_map/self_attention/pallas_call | solution.py:826
  125.5 19.2 %attn_out.1 = (f32[128,1024]{1,0:T(8,128)}, bf16[4,128,1024]{2,1,0:T(8,128)(2,1)}) custom-call(bf16[256,512]{1,0:T(8,128)(2,1)} %bitcast.128, bf16[256,1024]{1,0:T(8,128)(2,1)} %weight.1, f32[128,1024]{1,0:T(8,128)} %get-tuple-element.93.before, f32[1,1024]{1,0:T(1,128)} %bitcast.144), custom_call_target="tpu_custom_call" | custom-call | flops 1 | bytes 1 | tf_op jit(solution)/shard_map/attn_out/pallas_call | solution.py:465
  144.7 24.1 %cross.1 = (f32[128,1024]{1,0:T(8,128)}, bf16[4,128,1024]{2,1,0:T(8,128)(2,1)}, bf16[4,128,256]{2,1,0:T(8,128)(2,1)}, bf16[4,128,256]{2,1,0:T(8,128)(2,1)}) custom-call(bf16[4,128,1024]{2,1,0:T(8,128)(2,1)} %get-tuple-element.94.cross_in, bf16[1024,256]{1,0:T(8,128)(2,1)} %wq.4, bf16[128,256]{1,0:T(8,128)(2,1)} %convolution_convert_fusion.4.ck, ...), custom_call_target="tpu_custom_call" | custom-call | flops 1 | bytes 1 | tf_op jit(solution)/shard_map/cross/pallas_call | solution.py:465
  168.8 27.4 %mlp.1 = (f32[128,1024]{1,0:T(8,128)}, bf16[4,128,1024]{2,1,0:T(8,128)(2,1)}, f32[1,1024]{1,0:T(1,128)}, bf16[512,1024]{1,0:T(8,128)(2,1)}, bf16[1024,1024]{1,0:T(8,128)(2,1)}, /*index=5*/bf16[1024,1024]{1,0:T(8,128)(2,1)}) custom-call(bf16[4,128,1024]{2,1,0:T(8,128)(2,1)} %get-tuple-element.96.mlp_in, bf16[4,128,1024]{2,1,0:T(8,128)(2,1)} %bitcast.116, ...), custom_call_target="tpu_custom_call" | custom-call | flops 1 | bytes 1 | tf_op jit(solution)/shard_map/mlp/pallas_call | solution.py:465
  196.2 1.3 copy.74.wkv
  197.5 0.8 fusion.3
  198.4 27.3 %cross_back.1 = (f32[128,1024]{1,0:T(8,128)}, bf16[4,128,1024]{2,1,0:T(8,128)(2,1)}, f32[1,1024]{1,0:T(1,128)}, bf16[128,256]{1,0:T(8,128)(2,1)}, bf16[128,256]{...) custom-call(bf16[4,128,1024]{2,1,0:T(8,128)(2,1)} %get-tuple-element.98.incoming, bf16[256,1024]{1,0:T(8,128)(2,1)} %wo.3, ...), custom_call_target="tpu_custom_call" | custom-call | flops 1 | bytes 1 | tf_op jit(solution)/shard_map/cross_back/pallas_call | solution.py:465
  225.7 2.4 fusion.2.x_ref
  228.1 12.7 %swap_heads.1.d_ref = bf16[4,1,64,512]{3,2,1,0:T(8,128)(2,1)} custom-call(bf16[1,256,512]{2,1,0:T(8,128)(2,1)} %fusion.2.x_ref), custom_call_target="tpu_custom_call" | custom-call | flops 1 | bytes 1 | tf_op jit(solution)/shard_map/swap_heads/pallas_call | solution.py:526
  240.8 52.3 %flash_back.1 = (bf16[4,1,64,512]{3,2,1,0:T(8,128)(2,1)}, bf16[8,1,512,128]{3,2,1,0:T(8,128)(2,1)}, bf16[768,1024]{1,0:T(8,128)(2,1)}) custom-call(bf16[4,1,64,512]{3,2,1,0:T(8,128)(2,1)} %get-tuple-element.91.q_ref, bf16[4,1,64,512]{3,2,1,0:T(8,128)(2,1)} %swap_heads.1.d_ref, f32[4,1,64,512]{3,2,1,0:T(8,128)} %get-tuple-element.103.of_ref, ...), custom_call_target="tpu_custom_call" | custom-call | flops 1 | bytes 1 | tf_op jit(solution)/shard_map/flash_back/pallas_call | solution.py:932
  293.0 29.5 %dqkv_home.1 = (bf16[1,256,512]{2,1,0:T(8,128)(2,1)}, bf16[1,512,512]{2,1,0:T(8,128)(2,1)}, f32[128,1024]{1,0:T(8,128)}) custom-call(bf16[4,1,64,512]{3,2,1,0:T(8,128)(2,1)} %get-tuple-element.108.dq_ref, bf16[8,1,512,128]{3,2,1,0:T(8,128)(2,1)} %get-tuple-element.109.dkv_ref, bf16[4,128,1024]{2,1,0:T(8,128)(2,1)} %bitcast.133), custom_call_target="tpu_custom_call" | custom-call | flops 1 | bytes 1 | tf_op jit(solution)/shard_map/dqkv_home/pallas_call | solution.py:585
  322.6 14.0 %attn_back.1 = (bf16[128,1024]{1,0:T(8,128)(2,1)}, f32[1,1024]{1,0:T(1,128)}) custom-call(bf16[256,512]{1,0:T(8,128)(2,1)} %bitcast.122, bf16[512,512]{1,0:T(8,128)(2,1)} %bitcast.118, bf16[1024,256]{1,0:T(8,128)(2,1)} %wq.5, bf16[1024,512]{1,0:T(8,128)(2,1)} %copy.74.wkv, f32[128,1024]{1,0:T(8,128)} %get-tuple-element.93.before, f32[1,1024]{1,0:T(1,128)} %bitcast.141, ...), custom_call_target="tpu_custom_call" | custom-call | flops 1 | bytes 1 | tf_op jit(solution)/shard_map/attn_back/pallas_call | solution.py:465
  336.6 0.7 pad_maximum_fusion.1
  337.4 0.6 reshape.268.gains
  338.0 0.2 copy.66
  338.2 0.1 copy.68
  338.4 0.2 copy.67
  338.6 0.1 copy.69
  338.7 0.8 maximum_bitcast_fusion.tokens
  339.6 132.6 %outer_backward.1 = (f32[32,64,256]{2,1,0:T(8,128)}, bf16[3328,256]{1,0:T(8,128)(2,1)}, bf16[768,1024]{1,0:T(8,128)(2,1)}, bf16[4,2,128,256]{3,2,1,0:T(8,128)(2,...) custom-call(bf16[32,64,256]{2,1,0:T(8,128)(2,1)} %bitcast.124, ...), custom_call_target="tpu_custom_call" | custom-call | flops 1 | bytes 1 | tf_op jit(solution)/shard_map/outer_backward/pallas_call | solution.py:1695
  472.1 1.1 slice_convert_fusion
  473.3 0.8 copy.71
  474.1 0.7 copy.70
  474.8 0.7 fusion.10
  475.5 0.6 fusion.9
  476.1 0.6 fusion.8
  476.6 0.8 broadcast_multiply_fusion
  477.5 14.3 %finish_grads.1 = (f32[1024,256]{1,0:T(8,128)}, f32[1024,256]{1,0:T(8,128)}, f32[1024,256]{1,0:T(8,128)}, f32[256,1024]{1,0:T(8,128)}, f32[256,1024]{1,0:T(8,128...) custom-call(bf16[128,4096]{1,0:T(8,128)(2,1)} %bitcast.104, ...), custom_call_target="tpu_custom_call" | custom-call | flops 1 | bytes 1 | tf_op jit(solution)/shard_map/finish_grads/pallas_call | solution.py:1782
  491.8 1.0 copy.82
  492.8 1.0 copy-done.5
  493.7 1.3 copy.83
  (52 shorter events, 0.7 us)
Async XLA Ops:
  7.2 2.3 copy-start
  7.2 50.7 %copy-start.9 = (bf16[1024,256]{1,0:T(8,128)(2,1)S(1)}, bf16[1024,256]{1,0:T(8,128)(2,1)}, u32[]{:S(2)}) copy-start(bf16[1024,256]{1,0:T(8,128)(2,1)} %param.43) | copy-start | bytes 1572868
  7.2 55.7 %all-gather.3.cloned.1.call-start = ((), (), s32[]{:S(2)}) async-start(), calls=%async_computation | async-start | bytes 1310720 | tf_op jit(solution)/shard_map/all_gather | solution.py:1860
  8.0 74.6 %all-gather.5.cloned.1.call-start = ((), (), s32[]{:S(2)}) async-start(), calls=%async_computation.1 | async-start | bytes 1310720 | tf_op jit(solution)/shard_map/all_gather | solution.py:1860
  8.7 468.7 %all-reduce.3.cloned.1.call-start = ((), (), s32[]{:S(2)}) async-start(), calls=%async_computation.2 | async-start | bytes 8388608 | tf_op jit(solution)/shard_map/psum | solution.py:1978
  12.5 45.7 %copy-start.10 = (bf16[1024,256]{1,0:T(8,128)(2,1)S(1)}, bf16[1024,256]{1,0:T(8,128)(2,1)}, u32[]{:S(2)}) copy-start(bf16[1024,256]{1,0:T(8,128)(2,1)} %param.44) | copy-start | bytes 1572868
  57.9 1.3 copy-start.2
  58.5 3.4 copy-start.4
  61.9 15.6 %copy-start.6 = (bf16[1024,256]{1,0:T(8,128)(2,1)S(1)}, bf16[1024,256]{1,0:T(8,128)(2,1)}, u32[]{:S(2)}) copy-start(bf16[1024,256]{1,0:T(8,128)(2,1)} %wq.5) | copy-start | bytes 1572868
  198.4 27.3 %copy-start.11 = (bf16[256,1024]{1,0:T(8,128)(2,1)S(1)}, bf16[256,1024]{1,0:T(8,128)(2,1)}, u32[]{:S(2)}) copy-start(bf16[256,1024]{1,0:T(8,128)(2,1)} %weight.1) | copy-start | bytes 1572868
  322.6 14.0 %copy-start.14 = (f32[1,1024]{1,0:T(1,128)S(1)}, f32[1,1024]{1,0:T(1,128)}, u32[]{:S(2)}) copy-start(f32[1,1024]{1,0:T(1,128)} %get-tuple-element.118) | copy-start | bytes 12292
  322.6 14.0 %copy-start.15 = (f32[1,1024]{1,0:T(1,128)S(1)}, f32[1,1024]{1,0:T(1,128)}, u32[]{:S(2)}) copy-start(f32[1,1024]{1,0:T(1,128)} %get-tuple-element.117) | copy-start | bytes 12292
  322.6 15.4 %copy-start.3 = (f32[128,1024]{1,0:T(8,128)S(1)}, f32[128,1024]{1,0:T(8,128)}, u32[]{:S(2)}) copy-start(f32[128,1024]{1,0:T(8,128)} %get-tuple-element.97.before) | copy-start | bytes 1572868
  322.6 15.4 %copy-start.12 = (f32[128,1024]{1,0:T(8,128)S(1)}, f32[128,1024]{1,0:T(8,128)}, u32[]{:S(2)}) copy-start(f32[128,1024]{1,0:T(8,128)} %get-tuple-element.111) | copy-start | bytes 1572868
  336.6 1.8 copy-start.7
  472.1 2.7 copy-start.13
  472.1 3.9 copy-start.16
  477.5 14.3 %copy-start.8 = (bf16[32,64,256]{2,1,0:T(8,128)(2,1)S(1)}, bf16[32,64,256]{2,1,0:T(8,128)(2,1)}, u32[]{:S(2)}) copy-start(bf16[32,64,256]{2,1,0:T(8,128)(2,1)} %get-tuple-element.85) | copy-start | bytes 3145732
  491.8 2.0 copy-start.5
  491.8 3.3 copy-start.1
Sparse Core Ops, SparseCore 0:
  9.6 21.8 all-gather.2
  33.1 16.1 all-gather.4
  196.3 184.8 all-reduce.2

commit v4 on v3

--- a/solution.py
+++ b/solution.py
@@ -27,6 +27,7 @@
 
 
 SHORT = pl.CostEstimate(flops=1, transcendentals=0, bytes_accessed=1)
+LONG = pl.CostEstimate(flops=20_000_000_000, transcendentals=0, bytes_accessed=60_000_000)
 
 
 def in_vmem():
@@ -245,16 +246,34 @@
     return grad_in, jnp.sum(grad_out * hat, axis=0, keepdims=True)
 
 
-def enter_kernel(ns, inner, pooled, lift, gain, stream, gathered, *sems):
+def tokens_of(ref, p):
+    return ref[:, p].reshape(-1, ref.shape[3]) if len(ref.shape) == 4 else ref[p]
+
+
+def by_head(first, second):
+    parts = []
+    for h in range(first.shape[1] // HD):
+        parts += [head_of(first, h), head_of(second, h)]
+    return side_by_side(parts)
+
+
+def enter_kernel(
+    ns, inner, pooled, lift, gain, wq, wk, wv, stream, gathered, q_out, kv_out, *sems
+):
     copies = Copies()
     gather = SubGather(ns, copies, gathered, sems)
-    value = inner[...].astype(f32) + dot(pooled[...], lift[...]).astype(bf16).astype(f32)
+    mine = tokens_of(inner, gather.s) if len(inner.shape) == 4 else inner[...]
+    value = mine.astype(f32) + dot(pooled[...], lift[...]).astype(bf16).astype(f32)
     stream[...] = value
-    gathered[gather.s] = (layer_hat(value)[0] * gain[...]).astype(bf16)
+    gathered[gather.s] = (layer_hat(value)[0] * gain[0:1, :]).astype(bf16)
     greet(sub_peers(ns))
     gather.start()
+    turned = wq[...].T
     gather.relay()
     gather.end()
+    rows = gathered[...].reshape(-1, gathered.shape[2])
+    q_out[...] = dot_t(turned, rows).astype(bf16)
+    kv_out[...] = by_head(dot(rows, wk[...]), dot(rows, wv[...])).astype(bf16)
     copies.finish()
 
 
@@ -274,7 +293,7 @@
     def normalize(j, part):
         value = before[part, :] + after[part, :]
         after[part, :] = value
-        gathered[gather.s, part] = (layer_hat(value)[0] * gain[...]).astype(bf16)
+        gathered[gather.s, part] = (layer_hat(value)[0] * gain[1:2, :]).astype(bf16)
         gather.start_one(j)
 
     scatter.run(make, after, None, normalize)
@@ -322,7 +341,7 @@
     def normalize(j, part):
         value = before[part, :] + after[part, :]
         after[part, :] = value
-        gathered[gather.s, part] = (layer_hat(value)[0] * gain[...]).astype(bf16)
+        gathered[gather.s, part] = (layer_hat(value)[0] * gain[2:3, :]).astype(bf16)
         gather.start_one(j)
 
     scatter.run(make, after, None, normalize)
@@ -333,9 +352,12 @@
 
 def mlp_kernel(
     ns, mlp_in, cotan, w_up, w_down, before, gain,
-    grad, gathered, gain_grad, down, up_grad, down_grad, activated, grad_up, *scratch
+    grad, gathered, gain_grad, down, up_grad, down_grad, activated, grad_up, cotans, *scratch
 ):
     copies = Copies()
+    for p in range(ns):
+        cotans[p] = tokens_of(cotan, p)
+    cotan = cotans
     scatter = SubScatter(ns, copies, *scratch[:4], scratch[4:8])
     gather = SubGather(ns, copies, gathered, scratch[8:])
     own = before.shape[0]
@@ -363,7 +385,7 @@
     gain_grad[...] = jnp.zeros_like(gain_grad)
 
     def normalize(j, part):
-        back, gains = layer_back(grad[part, :], before[part, :], gain[...])
+        back, gains = layer_back(grad[part, :], before[part, :], gain[2:3, :])
         gain_grad[...] += gains
         value = cotan[gather.s, part].astype(f32) + back
         grad[part, :] = value
@@ -418,7 +440,7 @@
     gain_grad[...] = jnp.zeros_like(gain_grad)
 
     def normalize(j, part):
-        back, gains = layer_back(grad[part, :], before[part, :], gain[...])
+        back, gains = layer_back(grad[part, :], before[part, :], gain[1:2, :])
         gain_grad[...] += gains
         value = residual[part, :] + back
         grad[part, :] = value
@@ -433,13 +455,14 @@
 
 
 def attn_back_kernel(
-    ns, dq_t, dkv, wq, wkv, before, gain, residual, out, gain_grad, turned, *scratch
+    ns, dq_t, dkv, wq, wk, wv, before, gain, residual, out, gain_grad, turned, wkv, *scratch
 ):
     copies = Copies()
     scatter = SubScatter(ns, copies, *scratch[1:5], scratch[5:9])
     total = scratch[0]
     own = before.shape[0]
     turned[...] = dq_t[...].T
+    wkv[...] = by_head(wk[...], wv[...])
 
     def make(p):
         rows = pl.ds(pl.multiple_of(p * own, 16), own)
@@ -448,13 +471,13 @@
 
     greet(sub_peers(ns))
     scatter.run(make, total)
-    back, gains = layer_back(total[...], before[...], gain[...])
+    back, gains = layer_back(total[...], before[...], gain[0:1, :])
     gain_grad[...] = gains
     out[...] = (residual[...] + back).astype(bf16)
     copies.finish()
 
 
-def chain_call(kernel, name, cid, outs, args, extra, scatter, gather=True):
+def chain_call(kernel, name, cid, outs, args, extra, scatter, gather=True, vmem=16, cost=SHORT):
     ns = lax.axis_size("sub")
     own, width = outs[0][0]
     scratch = list(extra)
@@ -468,8 +491,8 @@
         in_specs=[in_vmem()] * len(args),
         out_specs=(in_vmem(),) * len(outs),
         scratch_shapes=scratch,
-        cost_estimate=SHORT,
-        compiler_params=params(cid),
+        cost_estimate=cost,
+        compiler_params=params(cid, vmem),
         name=name,
     )(*args)
 
@@ -490,123 +513,6 @@
 
 def lanes_of(ref, i, size):
     return ref.at[:, :, pl.ds(pl.multiple_of(i * size, size), size)]
-
-
-def swap_kernel(nt, u, home, x_ref, o_ref, ss, rs, own):
-    t, s, nb, a, b, a_peer, b_peer, peers = deal(nt, u)
-    greet([a_peer(k) for k in range(1, u)])
-    taken = lambda i: x_ref.at[i] if home else rows_of(x_ref, i, HD)
-    placed = lambda i: rows_of(o_ref, i, HD) if home else o_ref.at[i]
-    local = pltpu.make_async_copy(taken(a), placed(a), own)
-    local.start()
-    copies = []
-    for k in range(1, u):
-        copies.append(
-            remote(taken(lax.rem(a + k, u)), placed(a), ss.at[k], rs.at[k], a_peer(k))
-        )
-        copies[-1].start()
-    for k in range(1, u):
-        arrived(placed(lax.rem(a + u - k, u)), ss.at[k], rs.at[k], (t, s))
-    for copy in copies:
-        copy.wait_send()
-    local.wait()
-
-
-def swap_heads(x, home, cid):
-    nt = lax.axis_size("tile")
-    if home:
-        u, batch, _, length = x.shape
-        shape = (batch, u * HD, length)
-    else:
-        batch, width, length = x.shape
-        u = width // HD
-        shape = (u, batch, HD, length)
-    if u == 1:
-        return x.reshape(shape)
-    return pl.pallas_call(
-        functools.partial(swap_kernel, nt, u, home),
-        out_shape=jax.ShapeDtypeStruct(shape, bf16),
-        in_specs=[anywhere()],
-        out_specs=anywhere(),
-        scratch_shapes=[dma(u), dma(u), pltpu.SemaphoreType.DMA],
-        cost_estimate=SHORT,
-        compiler_params=params(cid),
-        name="swap_heads",
-    )(x)
-
-
-def dqkv_home_kernel(
-    nt, ns, u, dq_ref, dkv_ref, beside_ref, qo, kvo, beside_out, got, stage, qs, qr, fs, fr, ks, kr, own, *scratch
-):
-    t, s, nb, a, b, a_peer, b_peer, peers = deal(nt, u)
-    me = (t, s)
-    copies = Copies()
-    beside = SubScatter(ns, copies, beside_ref, *scratch[:3], scratch[3:])
-    greet(peers + beside.peers())
-    order = list(range(1, u)) + [0]
-    for k in order:
-        for m in range(1, nb):
-            block = dkv_ref.at[lax.rem(a + k, u) * nb + lax.rem(b + m, nb)]
-            copies.send(block, got.at[m, k], fs.at[k, m], fr.at[k, m], b_peer(m))
-    beside.start()
-    for k in range(1, u):
-        block = dq_ref.at[lax.rem(a + k, u)]
-        copies.send(block, rows_of(qo, a, HD), qs.at[k], qr.at[k], a_peer(k))
-    local = [pltpu.make_async_copy(dq_ref.at[a], rows_of(qo, a, HD), own.at[0])]
-    local[0].start()
-    beside.cross()
-    for k in order:
-        total = dkv_ref[lax.rem(a + k, u) * nb + b].astype(f32)
-        for m in range(1, nb):
-            arrived(got.at[m, k], fs.at[k, m], fr.at[k, m], me)
-            total = total + got[m, k].astype(f32)
-        stage[k] = total.astype(bf16)
-        if k:
-            copies.send(stage.at[k], lanes_of(kvo, a, 2 * HD), ks.at[k], kr.at[k], a_peer(k))
-        else:
-            local.append(pltpu.make_async_copy(stage.at[0], lanes_of(kvo, a, 2 * HD), own.at[1]))
-            local[1].start()
-    beside.end(beside_out)
-    for k in range(1, u):
-        i = lax.rem(a + u - k, u)
-        arrived(rows_of(qo, i, HD), qs.at[k], qr.at[k], me)
-        arrived(lanes_of(kvo, i, 2 * HD), ks.at[k], kr.at[k], me)
-    copies.finish()
-    for copy in local:
-        copy.wait()
-
-
-def dqkv_home(dq, dkv, beside, cid):
-    nt, ns = lax.axis_size("tile"), lax.axis_size("sub")
-    u, batch, _, length = dq.shape
-    nb = nt // u
-    block = (batch, length, 2 * HD)
-    beside = beside.reshape(ns, -1, beside.shape[1])
-    return pl.pallas_call(
-        functools.partial(dqkv_home_kernel, nt, ns, u),
-        out_shape=(
-            jax.ShapeDtypeStruct((batch, u * HD, length), bf16),
-            jax.ShapeDtypeStruct((batch, length, u * 2 * HD), bf16),
-            jax.ShapeDtypeStruct(beside.shape[1:], f32),
-        ),
-        in_specs=[in_vmem()] * 3,
-        out_specs=(anywhere(), anywhere(), in_vmem()),
-        scratch_shapes=[
-            pltpu.VMEM((nb, u) + block, bf16),
-            pltpu.VMEM((u,) + block, bf16),
-            dma(u),
-            dma(u),
-            dma(u, nb),
-            dma(u, nb),
-            dma(u),
-            dma(u),
-            dma(2),
-        ]
-        + SubScatter.scratch(ns, *beside.shape[1:]),
-        cost_estimate=SHORT,
-        compiler_params=params(cid),
-        name="dqkv_home",
-    )(dq, dkv, beside)
 
 
 class TileSum:
@@ -779,8 +685,9 @@
     for k in range(1, u):
         arrived(qo.at[lax.rem(a + u - k, u)], qs.at[k], qr.at[k], me)
     local[0].wait()
-    order = [(0, 0)] + [(k, 0) for k in range(1, u)]
-    order += [(k, m) for k in range(u) for m in range(1, nb)]
+    near_first = sorted(range(1, u), key=lambda k: min(k, u - k))
+    order = [(0, m) for m in range(nb)] + [(k, 0) for k in near_first]
+    order += [(k, m) for k in near_first for m in range(1, nb)]
     for k, m in order[:-1]:
         tile = tile_of(k, m)
         if m:
@@ -844,121 +751,10 @@
         + [dma(u, nb) for _ in range(2)]
         + [dma(u) for _ in range(2)]
         + [dma(2)],
-        cost_estimate=SHORT,
-        compiler_params=params(cid),
+        cost_estimate=LONG,
+        compiler_params=params(cid, 24),
         name="self_attention",
     )(q, kv)
-
-
-def flash_back_kernel(
-    nt, q_ref, d_ref, of_ref, lse_ref, kv_ref, mixed_t, grad_attn, early_ref, dq_ref, dkv_ref, early,
-    qd, rows, delta, acc, mine, *scratch
-):
-    u, length = q_ref.shape[0], q_ref.shape[3]
-    j = pl.program_id(1)
-    last_j = pl.num_programs(1) - 1
-    at = lambda step: (pl.program_id(0) == 0) & (j == step)
-    sums = TileSum(nt, mine, early, scratch[:3], scratch[3:], None)
-    steps = list(sums.steps())
-
-    @pl.when(at(0))
-    def _():
-        features = mixed_t.shape[0]
-        mine[pl.ds(0, features), :] = dot(mixed_t[...], grad_attn[...]).astype(bf16)
-        mine[pl.ds(features, 2 * features), :] = early_ref[...]
-        spare = mine.shape[0] - 3 * features
-        if spare:
-            mine[pl.ds(3 * features, spare), :] = jnp.zeros((spare, mine.shape[1]), bf16)
-        clear(early)
-        a, b, s = sums.a, sums.b, sums.s
-        barrier = pltpu.get_barrier_semaphore()
-        up, down = a + 1 < nt // 2, a > 0
-        for there, peer in ((up, (a + 1) * 2 + b), (down, (a - 1) * 2 + b)):
-
-            @pl.when(there)
-            def _():
-                pl.semaphore_signal(barrier, inc=1, device_id=(peer, s), device_id_type=MESH)
-
-        pl.semaphore_signal(barrier, inc=1, device_id=sums.pair, device_id_type=MESH)
-        pl.semaphore_wait(barrier, 1 + jnp.where(up, 1, 0) + jnp.where(down, 1, 0))
-        sums.start()
-
-    @pl.when(j == 0)
-    def _():
-        for i in range(u):
-            q, d = q_ref[i, 0], d_ref[i, 0]
-            zero = jnp.zeros_like(q)
-            qd[i, 0] = jnp.concatenate([q * 0.125, zero], axis=0)
-            qd[i, 1] = jnp.concatenate([zero, d], axis=0)
-            rows[i, 0] = qd[i, 0].T
-            rows[i, 1] = qd[i, 1].T
-            delta[i] = jnp.sum(d.astype(f32) * of_ref[i, 0], axis=0, keepdims=True)
-            acc[i] = jnp.zeros_like(acc[i])
-
-    kv = kv_ref[0, 0]
-    kt = kv.T[:HD]
-    total = jnp.zeros(kv.shape, f32)
-    for i in range(u):
-        probs = jnp.exp(dot(kv, qd[i, 0]) - lse_ref[i, 0])
-        slope = dot(kv, qd[i, 1])
-        grads = (probs * (slope - delta[i])).astype(bf16)
-        total = total + dot(probs.astype(bf16), rows[i, 1]) + dot(grads, rows[i, 0])
-        acc[i] += dot(kt, grads)
-    dkv_ref[0, 0] = total.astype(bf16)
-
-    for before in range(3, 0, -1):
-
-        @pl.when(at(last_j - before))
-        def _():
-            sums.add(steps[2 * (3 - before) : 2 * (4 - before)])
-
-    @pl.when(at(last_j))
-    def _():
-        sums.add(steps[6:])
-        sums.end_add()
-
-    @pl.when(j == last_j)
-    def _():
-        for i in range(u):
-            dq_ref[i, 0] = (acc[i] * 0.125).astype(bf16)
-
-
-def flash_back(q, d, of, lse, kv, mixed_t, grad_attn, early, cid):
-    u, batch, _, length = q.shape
-    nt = kv.shape[0]
-    whole = pl.BlockSpec((u, 1, HD, length), lambda b, j: (0, b, 0, 0))
-    part = pl.BlockSpec((1, 1, length, 2 * HD), lambda b, j: (j, b, 0, 0))
-    sums = (round_up(3 * u * HD, 16 * nt), grad_attn.shape[1])
-    return pl.pallas_call(
-        functools.partial(flash_back_kernel, nt),
-        grid=(batch, nt),
-        out_shape=(
-            jax.ShapeDtypeStruct(q.shape, bf16),
-            jax.ShapeDtypeStruct(kv.shape, bf16),
-            jax.ShapeDtypeStruct(sums, bf16),
-        ),
-        in_specs=[
-            whole,
-            whole,
-            whole,
-            pl.BlockSpec((u, 1, 1, length), lambda b, j: (0, b, 0, 0)),
-            part,
-        ]
-        + [in_vmem()] * 3,
-        out_specs=(whole, part, in_vmem()),
-        scratch_shapes=[
-            pltpu.VMEM((u, 2, 2 * HD, length), bf16),
-            pltpu.VMEM((u, 2, length, 2 * HD), bf16),
-            pltpu.VMEM((u, 1, length), f32),
-            pltpu.VMEM((u, HD, length), f32),
-            pltpu.VMEM(sums, bf16),
-        ]
-        + TileSum.buffers(*sums)
-        + TileSum.sems(),
-        cost_estimate=SHORT,
-        compiler_params=params(cid),
-        name="flash_back",
-    )(q, d, of, lse, kv, mixed_t, grad_attn, early)
 
 
 class Nothing:
@@ -1061,6 +857,162 @@
         for k in range(self.far):
             block = self.out.at[self.rows(self.other(self.far - k), 1 - self.c)]
             arrived(block, self.s6.at[k], self.r6.at[k], self.me)
+
+
+def attention_back_kernel(
+    nt, ns, u, d_ref, q_ref, of_ref, lse_ref, kv_ref, mixed_t, grad_attn, early_ref, beside_ref,
+    qo, kvo, early_out, beside_out,
+    dealt, qd, rows, delta, acc, low, sent, kept, got, stage, mine,
+    ds, dr, fs, fr, ks, kr, qs, qr, own, *scratch
+):
+    t, s, nb, a, b, a_peer, b_peer, peers = deal(nt, u)
+    me = (t, s)
+    batch, length = d_ref.shape[0], d_ref.shape[2]
+    copies = Copies()
+    early = TileSum(nt, mine, early_out, scratch[:3], scratch[3:7], None)
+    beside = SubScatter(ns, copies, beside_ref, *scratch[7:10], scratch[10:])
+    steps = list(early.steps())
+    clear(early_out)
+    greet_all(nt, ns)
+    dealt[a] = d_ref[:, pl.ds(pl.multiple_of(a * HD, HD), HD), :]
+    for k in range(1, u):
+        block = rows_of(d_ref, lax.rem(a + k, u), HD)
+        copies.send(block, dealt.at[a], ds.at[k], dr.at[k], a_peer(k))
+    features = mixed_t.shape[0]
+    mine[pl.ds(0, features), :] = dot(mixed_t[...], grad_attn[...]).astype(bf16)
+    mine[pl.ds(features, 2 * features), :] = early_ref[...]
+    spare = mine.shape[0] - 3 * features
+    if spare:
+        mine[pl.ds(3 * features, spare), :] = jnp.zeros((spare, mine.shape[1]), bf16)
+    early.start()
+    beside.start()
+
+    def prepare(i):
+        for n in range(batch):
+            q, d = q_ref[i, n], dealt[i, n]
+            zero = jnp.zeros_like(q)
+            qd[i, n, 0] = jnp.concatenate([q * 0.125, zero], axis=0)
+            qd[i, n, 1] = jnp.concatenate([zero, d], axis=0)
+            rows[i, n, 0] = qd[i, n, 0].T
+            rows[i, n, 1] = qd[i, n, 1].T
+            delta[i, n] = jnp.sum(d.astype(f32) * of_ref[i, n], axis=0, keepdims=True)
+
+    clear(acc)
+    for k in range(u):
+        i = lax.rem(a + u - k, u)
+        if k:
+            arrived(dealt.at[i], ds.at[k], dr.at[k], me)
+        prepare(i)
+
+    def work(tile, n):
+        kv = kv_ref[tile, n]
+        kt = kv.T[:HD]
+        total = jnp.zeros(kv.shape, f32)
+        for i in range(u):
+            probs = jnp.exp(dot(kv, qd[i, n, 0]) - lse_ref[i, n])
+            slope = dot(kv, qd[i, n, 1])
+            grads = (probs * (slope - delta[i, n])).astype(bf16)
+            total = total + dot(probs.astype(bf16), rows[i, n, 1]) + dot(grads, rows[i, n, 0])
+            acc[i, n] += dot(kt, grads)
+        return total
+
+    def settle(k):
+        for n in range(batch):
+            total = kept[k, n]
+            for m in range(1, nb):
+                if n == 0:
+                    arrived(got.at[m, k], fs.at[k, m], fr.at[k, m], me)
+                total = total + got[m, k, n].astype(f32)
+            stage[k, n] = total.astype(bf16)
+        if k:
+            copies.send(stage.at[k], lanes_of(kvo, a, 2 * HD), ks.at[k], kr.at[k], a_peer(k))
+
+    order = list(range(1, u)) + [0]
+    done = 0
+    for at, k in enumerate(order):
+        for m in range(1, nb):
+            tile = lax.rem(a + k, u) * nb + lax.rem(b + m, nb)
+            for n in range(batch):
+                sent[m, k, n] = work(tile, n).astype(bf16)
+            copies.send(sent.at[m, k], got.at[m, k], fs.at[k, m], fr.at[k, m], b_peer(m))
+        if at == min(1, u - 1):
+            beside.cross()
+        for n in range(batch):
+            kept[k, n] = work(lax.rem(a + k, u) * nb + b, n)
+        if at:
+            settle(order[at - 1])
+            early.add(steps[done : done + 2])
+            done += 2
+    for k in list(range(1, u)) + [0]:
+        i = lax.rem(a + k, u)
+        for n in range(batch):
+            low[i, n] = (acc[i, n] * 0.125).astype(bf16)
+        if k:
+            copies.send(low.at[i], rows_of(qo, a, HD), qs.at[k], qr.at[k], a_peer(k))
+    local = [pltpu.make_async_copy(low.at[a], rows_of(qo, a, HD), own.at[0])]
+    local[0].start()
+    beside.end(beside_out)
+    settle(order[-1])
+    local.append(pltpu.make_async_copy(stage.at[0], lanes_of(kvo, a, 2 * HD), own.at[1]))
+    local[1].start()
+    early.add(steps[done:])
+    early.end_add()
+    for k in range(1, u):
+        i = lax.rem(a + u - k, u)
+        arrived(rows_of(qo, i, HD), qs.at[k], qr.at[k], me)
+        arrived(lanes_of(kvo, i, 2 * HD), ks.at[k], kr.at[k], me)
+    for copy in local:
+        copy.wait()
+    copies.finish()
+
+
+def attention_back(d, q, of, lse, kv, mixed_t, grad_attn, early, beside, cid):
+    nt, ns = lax.axis_size("tile"), lax.axis_size("sub")
+    u, batch, _, length = q.shape
+    nb = nt // u
+    block = (batch, length, 2 * HD)
+    sums = (round_up(3 * u * HD, 16 * nt), grad_attn.shape[1])
+    beside = beside.reshape(ns, -1, beside.shape[1])
+    shape = jax.ShapeDtypeStruct
+    return pl.pallas_call(
+        functools.partial(attention_back_kernel, nt, ns, u),
+        out_shape=(
+            shape(d.shape, bf16),
+            shape((batch, length, u * 2 * HD), bf16),
+            shape(sums, bf16),
+            shape(beside.shape[1:], f32),
+        ),
+        in_specs=[in_vmem()] * 9,
+        out_specs=(in_vmem(),) * 4,
+        scratch_shapes=[
+            pltpu.VMEM(q.shape, bf16),
+            pltpu.VMEM((u, batch, 2, 2 * HD, length), bf16),
+            pltpu.VMEM((u, batch, 2, length, 2 * HD), bf16),
+            pltpu.VMEM((u, batch, 1, length), f32),
+            pltpu.VMEM(q.shape, f32),
+            pltpu.VMEM(q.shape, bf16),
+            pltpu.VMEM((nb, u) + block, bf16),
+            pltpu.VMEM((u,) + block, f32),
+            pltpu.VMEM((nb, u) + block, bf16),
+            pltpu.VMEM((u,) + block, bf16),
+            pltpu.VMEM(sums, bf16),
+            dma(u),
+            dma(u),
+            dma(u, nb),
+            dma(u, nb),
+            dma(u),
+            dma(u),
+            dma(u),
+            dma(u),
+            dma(2),
+        ]
+        + TileSum.buffers(*sums)
+        + TileSum.sems()
+        + SubScatter.scratch(ns, *beside.shape[1:]),
+        cost_estimate=SHORT,
+        compiler_params=params(cid, 40),
+        name="attention_back",
+    )(d, q, of, lse, kv, mixed_t, grad_attn, early, beside)
 
 
 AROUND = [(-1, 0), (1, 0), (0, -1), (0, 1), (-1, -1), (-1, 1), (1, -1), (1, 1)]
@@ -1279,14 +1231,18 @@
 
 
 def outer_forward_kernel(
-    nt, ns, img, w1, w2, vec, gains, out, pooled, act1_out, act2_out, hidden, stats, gains_out,
-    body, left, right, flat, act1, act2, rowsum, border_ss, border_rs, keep, gain_ss, gain_rs, *sums
+    nt, ns, img, w1, w2, vec, gain1, gain2, gain3, text_in, wk_in, wv_in,
+    out, pooled, act1_out, act2_out, hidden, stats, gains_out, keys, values,
+    body, left, right, flat, act1, act2, rowsum, gains, text, wk, wv,
+    border_ss, border_rs, keep, gain_ss, gain_rs, *sums
 ):
     rows, cols, channels = img.shape
     pitch = cols + 16
     t, s = lax.axis_index("tile"), lax.axis_index("sub")
     sums1, sums2 = sums[:6], sums[6:]
     count = float(nt * ns * rows * cols * (channels // G))
+    pairs = ((text_in, text), (wk_in, wk), (wv_in, wv))
+    loads = [pltpu.make_async_copy(*pair, keep.at[2 + i]) for i, pair in enumerate(pairs)]
     clear(body, left, right)
     greet_all(nt, ns)
     top, bottom = body.at[pl.ds(0, 2)], body.at[pl.ds(rows + 2, 2)]
@@ -1296,9 +1252,11 @@
     local1 = row_sums(rows, channels, lambda i: (pixel(i), pixel(i) * pixel(i)))
     copies = sum_near(nt, ns, local1, sums1[0], sums1[2], sums1[3])
     copies += sum_far(nt, ns, sums1[0], sums1[1], *sums1[2:])
-    gains_out[s] = gains[...]
+    for copy in loads:
+        copy.start()
+    gains[s] = jnp.concatenate([gain1[...], gain2[...], gain3[...]], axis=0)
     for k in range(1, ns):
-        block, peer = gains_out.at[s], (t, lax.rem(s + k, ns))
+        block, peer = gains.at[s], (t, lax.rem(s + k, ns))
         copies.append(remote(block, block, gain_ss.at[k], gain_rs.at[s], peer))
         copies[-1].start()
 
@@ -1346,6 +1304,10 @@
     local2 = row_sums(rows, channels, lambda i: (hidden_row(i), hidden_row(i) * hidden_row(i)))
     copies += sum_near(nt, ns, local2, sums2[0], sums2[2], sums2[3])
     copies += sum_far(nt, ns, sums2[0], sums2[1], *sums2[2:])
+    for copy in loads:
+        copy.wait()
+    keys[...] = dot(text[...], wk[...]).astype(bf16)
+    values[...] = dot(text[...], wv[...]).astype(bf16)
     total2 = sum_end(nt, sums2[1], sums2[4], sums2[5])
     center2, std2 = moments(total2)
     scale2 = std2 * vec[2:3]
@@ -1387,14 +1349,15 @@
             pooled[place, :] = jnp.concatenate(means, axis=1).astype(bf16)
     for k in range(1, ns):
         p = lax.rem(s + k, ns)
-        arrived(gains_out.at[p], gain_ss.at[k], gain_rs.at[p], (t, s))
+        arrived(gains.at[p], gain_ss.at[k], gain_rs.at[p], (t, s))
+    gains_out[...] = side_by_side([gains[i] for i in range(ns)])
     for copy in copies:
         copy.wait_send()
     for copy in saved:
         copy.wait()
 
 
-def outer_forward(img, w1, w2, vec, gains, cid):
+def outer_forward(img, w1, w2, vec, gains, text, wk, wv, cid):
     nt, ns = lax.axis_size("tile"), lax.axis_size("sub")
     rows, cols, channels = img.shape
     pitch = cols + 16
@@ -1409,10 +1372,12 @@
             shape((long2, 3 * channels), bf16),
             shape((long2, channels), f32),
             shape((8, channels), f32),
-            shape((ns,) + gains.shape, f32),
+            shape((3, ns * wk.shape[1]), f32),
+            shape((text.shape[0], wk.shape[1]), bf16),
+            shape((text.shape[0], wk.shape[1]), bf16),
         ),
-        in_specs=[in_vmem()] * 5,
-        out_specs=(in_vmem(),) * 2 + (anywhere(),) * 2 + (in_vmem(),) * 3,
+        in_specs=[in_vmem()] * 7 + [anywhere()] * 3,
+        out_specs=(in_vmem(),) * 2 + (anywhere(),) * 2 + (in_vmem(),) * 5,
         scratch_shapes=[
             pltpu.VMEM((rows + 4, cols, channels), bf16),
             pltpu.VMEM((rows + 5, 16, channels), bf16),
@@ -1421,17 +1386,21 @@
             pltpu.VMEM((long1, 3 * channels), bf16),
             pltpu.VMEM((long2, 3 * channels), bf16),
             pltpu.VMEM((channels // 128, cols, 128), f32),
+            pltpu.VMEM((ns, 3, wk.shape[1]), f32),
+            pltpu.VMEM(text.shape, bf16),
+            pltpu.VMEM(wk.shape, bf16),
+            pltpu.VMEM(wv.shape, bf16),
             dma(8),
             dma(8),
-            dma(2),
+            dma(5),
             dma(ns),
             dma(ns),
         ]
         + sum_scratch(nt, ns, channels) * 2,
-        cost_estimate=SHORT,
+        cost_estimate=LONG,
         compiler_params=params(cid),
         name="outer_forward",
-    )(img, w1, w2, vec, gains)
+    )(img, w1, w2, vec, *gains, text, wk, wv)
 
 
 def kernel_grads(triple, grads_t, start, size, pitch, out, between=()):
@@ -1858,14 +1827,16 @@
 
     def whole_tokens(values):
         full = lax.all_gather(values, "sub", axis=2, tiled=True)
-        full = full.reshape(batch, lr, ns, lc, width)
-        mine = lax.dynamic_index_in_dim(full, s, 2, keepdims=False).reshape(own, width)
-        return full, mine
-
-    _, inner_own = whole_tokens(inner_image)
-    cotan_full, _ = whole_tokens(inner_cotan)
-    cotan_full = jnp.transpose(cotan_full, (2, 0, 1, 3, 4)).reshape(ns, own, width)
-    own_gains = jnp.stack([attn_gain, cross_gain, mlp_gain])
+        return full.reshape(batch, lr, ns, lc, width)
+
+    inner_own, cotan_full = whole_tokens(inner_image), whole_tokens(inner_cotan)
+    if batch == 1 and lc % 16 == 0:
+        inner_own, cotan_full = inner_own[0], cotan_full[0]
+    else:
+        inner_own = lax.dynamic_index_in_dim(inner_own, s, 2, keepdims=False)
+        inner_own = inner_own.reshape(own, width)
+        cotan_full = jnp.transpose(cotan_full, (2, 0, 1, 3, 4)).reshape(ns, own, width)
+    own_gains = [v.reshape(1, features) for v in (attn_gain, cross_gain, mlp_gain)]
 
     time_act = jax.nn.silu(time_embed(time_steps, channels))
     time_shift = jnp.dot(time_act, time_weight.astype(f32), precision=precise)
@@ -1874,6 +1845,8 @@
     empty = jnp.zeros((batch, 3, channels), f32)
     vectors = jnp.concatenate([fixed, time_shift[:, None, :], empty], axis=1)
     as_rows = lambda w: w.reshape(9 * channels, channels)
+    text_rows = batch * text_states.shape[1]
+    text = text_states.reshape(text_rows, -1)
     forward = [
         outer_forward(
             outer_image[b],
@@ -1881,24 +1854,34 @@
             as_rows(conv_second),
             vectors[b],
             own_gains,
+            text,
+            cross_key,
+            cross_value,
             20 + b,
         )
         for b in range(batch)
     ]
     outer_out = jnp.stack([f[0] for f in forward])
-    gains = jnp.transpose(forward[0][6], (1, 0, 2)).reshape(3, width)
+    gains, cross_k, cross_v = forward[0][6:]
     pooled = jnp.concatenate([f[1] for f in forward], axis=0)
 
     flat = lambda v: v.reshape(-1, v.shape[-1])
     block, rows_all = ((own, width), f32), ((ns, own, width), bf16)
-    stream_in, attn_in = chain_call(
+    stream_in, attn_in, query_t, kv = chain_call(
         enter_kernel,
         "enter",
         2,
-        (block, rows_all),
-        (inner_own, pooled, lift_weight, gains[0:1]),
+        (
+            block,
+            rows_all,
+            ((features, ns * own), bf16),
+            ((ns * own, 2 * features), bf16),
+        ),
+        (inner_own, pooled, lift_weight, gains, query_weight, key_weight, value_weight),
         (),
         False,
+        vmem=24,
+        cost=LONG,
     )
     attn_in = flat(attn_in)
 
@@ -1916,14 +1899,6 @@
         values = values.reshape(batch, ns, lr * lc, -1)
         return jnp.transpose(values, (1, 0, 2, 3)).reshape(ns * own, -1)
 
-    pair = lambda k, v: jnp.concatenate(
-        [k.reshape(-1, heads, HD), v.reshape(-1, heads, HD)], axis=2
-    ).reshape(-1, heads * 2 * HD)
-    kv_weight = pair(key_weight, value_weight)
-    query_t = lax.dot_general(
-        query_weight, attn_in, (((0,), (1,)), ((), ())), preferred_element_type=f32
-    ).astype(bf16)
-    kv = dot(attn_in, kv_weight).astype(bf16)
     mixed_t, head_q, head_kv, head_mixed_f, head_lse = self_attention(
         per_sample(query_t, True), per_sample(kv, False), 3
     )
@@ -1933,13 +1908,11 @@
         "attn_out",
         5,
         (block, rows_all),
-        (mixed_t, out_weight, stream_in, gains[1:2]),
+        (mixed_t, out_weight, stream_in, gains),
         [pltpu.VMEM((ns * own, features), bf16)],
         True,
-    )
-    text_rows = batch * text_states.shape[1]
-    text = text_states.reshape(text_rows, -1)
-    cross_k, cross_v = dot(text, cross_key).astype(bf16), dot(text, cross_value).astype(bf16)
+        cost=LONG,
+    )
     sample_of = lambda count: jnp.arange(batch * count) // count
     text_at = jnp.tile(jnp.arange(text_states.shape[1]), batch)
     good = text_at < jnp.repeat(text_lengths, text_states.shape[1])
@@ -1951,9 +1924,10 @@
         "cross",
         6,
         (block, rows_all, head_rows, head_rows),
-        (cross_in, cross_query, cross_k, cross_v, mask, cross_out, after_attn, gains[2:3]),
+        (cross_in, cross_query, cross_k, cross_v, mask, cross_out, after_attn, gains),
         (),
         True,
+        cost=LONG,
     )
 
     units = up_weight.shape[1]
@@ -1971,9 +1945,10 @@
             ((width, units), bf16),
             ((units, width), bf16),
         ),
-        (mlp_in, cotan_full, up_weight, down_weight, after_cross, gains[2:3]),
-        [middle, middle],
+        (mlp_in, cotan_full, up_weight, down_weight, after_cross, gains),
+        [middle, middle, pltpu.VMEM((ns, own, width), bf16)],
         True,
+        vmem=56,
     )
     grad_down, grad_up = lax.psum((grad_down, grad_up), "tile")
     text_block = ((text_rows, features), bf16)
@@ -2005,7 +1980,7 @@
             mask,
             cross_query,
             after_attn,
-            gains[1:2],
+            gains,
             grad_after_cross,
             cross_in,
             cross_mixed,
@@ -2013,30 +1988,43 @@
         [pltpu.VMEM((text_rows, features), f32)] * 2
         + [pltpu.VMEM((ns * own, features), bf16)],
         True,
+        vmem=56,
     )
     grad_attn_full = flat(grad_attn_full)
     grad_mixed_t = dot_t(out_weight, grad_attn_full).astype(bf16)
-    head_d = swap_heads(per_sample(grad_mixed_t, True), False, 13)
-    head_dq, head_dkv, wide = flash_back(
+    grad_q_t, grad_kv, wide, down_own = attention_back(
+        per_sample(grad_mixed_t, True),
         head_q,
-        head_d,
         head_mixed_f,
         head_lse,
         head_kv,
         mixed_t,
         grad_attn_full,
         grad_early.reshape(2 * features, width),
-        16,
-    )
-    grad_q_t, grad_kv, down_own = dqkv_home(head_dq, head_dkv, down, 14)
+        down,
+        13,
+    )
     grad_q_t, grad_kv = all_samples(grad_q_t, True), all_samples(grad_kv, False)
     grad_lifted, grad_attn_gain = chain_call(
         attn_back_kernel,
         "attn_back",
         15,
         (((own, width), bf16), one_row),
-        (grad_q_t, grad_kv, query_weight, kv_weight, stream_in, gains[0:1], grad_after_attn),
-        [pltpu.VMEM((ns * own, features), bf16), pltpu.VMEM((own, width), f32)],
+        (
+            grad_q_t,
+            grad_kv,
+            query_weight,
+            key_weight,
+            value_weight,
+            stream_in,
+            gains,
+            grad_after_attn,
+        ),
+        [
+            pltpu.VMEM((ns * own, features), bf16),
+            pltpu.VMEM((width, 2 * features), bf16),
+            pltpu.VMEM((own, width), f32),
+        ],
         True,
         False,
     )

time: 506 us -> 478 us (0.945)
  Pallas kernels: 450 us -> 430 us
  matrix products: 11.5 us -> 1.94 us
    pallas_call x6, Pallas kernels: 125 us -> 114 us  [chain_call(): pl.pallas_call(functools.partial(kernel, ns), out_shape=tuple((jax.ShapeD...]
    unnamed x38 -> x108, local copies, waits for them, and re-layouts: 3.75 us -> 13.2 us
    dot_general x4 -> x0, matrix products: 8.92 us -> none  [the longest x3 6.5 us: dot(): return jnp.dot(left, right, preferred_element_type=f32)]
    pallas_call x3 -> x1, Pallas kernels: 94.5 us -> 89.9 us  [attention_back(): pl.pallas_call(functools.partial(attention_back_kernel, nt, ns, u), out_s...]
  transfers between devices with their start and end apart: 3 -> 3, of which waited for: 0 -> 0; matrix products, arithmetic and copies ran while one was open for 6% -> 3% of each run, Pallas kernels for 65% -> 82%
where the time goes in v4:
time: 478 us; the launch traced here: 473 us
  Pallas kernels  430 us (90%)
  local copies, waits for them, and re-layouts  17.4 us (4%)
  between operations  16.1 us (3%)
  other arithmetic  5.79 us (1%)
    pallas_call x1, Pallas kernels, outer_backward(): pl.pallas_call(functools.partial(outer_backward_kernel, nt, ns, cut), out...  132 us
    pallas_call x6, Pallas kernels, chain_call(): pl.pallas_call(functools.partial(kernel, ns), out_shape=tuple((jax.ShapeD...  114 us
    pallas_call x1, Pallas kernels, attention_back(): pl.pallas_call(functools.partial(attention_back_kernel, nt, ns, u), out_s...  89.9 us
    pallas_call x1, Pallas kernels, outer_forward(): pl.pallas_call(functools.partial(outer_forward_kernel, nt, ns), out_shape...  43.8 us
    pallas_call x1, Pallas kernels, self_attention(): pl.pallas_call(functools.partial(self_attention_kernel, nt, u), out_shape...  36.3 us
    pallas_call x1, Pallas kernels, finish_grads(): pl.pallas_call(finish_kernel, grid=(steps,), out_shape=(shape(width, feat...  14.3 us
    unnamed x108, local copies, waits for them, and re-layouts  13.2 us
  transfers between devices with their start and end apart: 3, of which 0 were waited for; matrix products, arithmetic and copies ran while one was open for 3% of the time, Pallas kernels for 82%

profile of v4, /device:TPU:0, one launch (start us, length us, event | category | flops | bytes accessed | tf_op | source)
XLA Modules:
  0.0 473.1 jit_solution(393226932077897527)
XLA Ops:
  7.3 0.7 all-gather.3.cloned.1.call-update
  8.0 0.7 all-gather.5.cloned.1.call-update
  10.2 0.1 convolution_bitcast_fusion
  10.3 0.1 pad.7.clone
  10.4 0.1 and_select_fusion.mask
  10.5 0.2 copy-done.48
  10.7 0.7 maximum_bitcast_fusion.2
  11.5 0.7 maximum_bitcast_fusion.1.vec
  12.1 43.8 %outer_forward.1 = (bf16[32,64,256]{2,1,0:T(8,128)(2,1)}, bf16[128,256]{1,0:T(8,128)(2,1)}, bf16[2912,768]{1,0:T(8,128)(2,1)}, bf16[2752,768]{1,0:T(8,128)(2,1)}...) custom-call(bf16[32,64,256]{2,1,0:T(8,128)(2,1)} %bitcast.99, ...), custom_call_target="tpu_custom_call" | custom-call | flops 20000000000 | bytes 60000000 | tf_op jit(solution)/shard_map/outer_forward/pallas_call | solution.py:1366
  56.0 0.7 copy-done.34
  56.8 0.8 copy-done.37
  57.6 1.2 copy-done.42
  58.8 11.2 %enter.1 = (f32[128,1024]{1,0:T(8,128)S(1)}, bf16[4,128,1024]{2,1,0:T(8,128)(2,1)S(1)}, bf16[256,512]{1,0:T(8,128)(2,1)S(1)}, bf16[512,512]{1,0:T(8,128)(2,1)S(1)}) custom-call(bf16[8,4,16,1024]{3,2,1,0:T(8,128)(2,1)S(1)} %bitcast.89, bf16[128,256]{1,0:T(8,128)(2,1)S(1)} %copy-done.37, bf16[256,1024]{1,0:T(8,128)(2,1)S(1)} %copy-done.18, ...), custom_call_target="tpu_custom_call" | custom-call | flops 20000000000 | bytes 60000000 | tf_op jit(solution)/shard_map/enter/pallas_call | solution.py:488
  70.1 36.3 %self_attention.1 = (bf16[1,256,512]{2,1,0:T(8,128)(2,1)S(1)}, bf16[4,1,64,512]{3,2,1,0:T(8,128)(2,1)S(1)}, bf16[8,1,512,128]{3,2,1,0:T(8,128)(2,1)S(1)}, f32[4,...) custom-call(bf16[1,256,512]{2,1,0:T(8,128)(2,1)S(1)} %bitcast.91, bf16[1,512,512]{2,1,0:T(8,128)(2,1)S(1)} %bitcast.90), custom_call_target="tpu_custom_call" | custom-call | flops 20000000000 | bytes 60000000 | tf_op jit(solution)/shard_map/self_attention/pallas_call | solution.py:733
  106.6 16.8 %attn_out.1 = (f32[128,1024]{1,0:T(8,128)S(1)}, bf16[4,128,1024]{2,1,0:T(8,128)(2,1)S(1)}) custom-call(bf16[256,512]{1,0:T(8,128)(2,1)S(1)} %bitcast.86, bf16[256,1024]{1,0:T(8,128)(2,1)S(1)} %copy-done.43, f32[128,1024]{1,0:T(8,128)S(1)} %get-tuple-element.95.before, f32[3,1024]{1,0:T(4,128)S(1)} %copy-done.35), custom_call_target="tpu_custom_call" | custom-call | flops 20000000000 | bytes 60000000 | tf_op jit(solution)/shard_map/attn_out/pallas_call | solution.py:488
  123.5 20.9 %cross.1 = (f32[128,1024]{1,0:T(8,128)S(1)}, bf16[4,128,1024]{2,1,0:T(8,128)(2,1)S(1)}, bf16[4,128,256]{2,1,0:T(8,128)(2,1)S(1)}, bf16[4,128,256]{2,1,0:T(8,128)(2,1)S(1)}) custom-call(bf16[4,128,1024]{2,1,0:T(8,128)(2,1)S(1)} %get-tuple-element.96.cross_in, bf16[1024,256]{1,0:T(8,128)(2,1)S(1)} %copy-done.16, bf16[128,256]{1,0:T(8,128)(2,1)S(1)} %copy-done.38, ...), custom_call_target="tpu_custom_call" | custom-call | flops 20000000000 | bytes 60000000 | tf_op jit(solution)/shard_map/cross/pallas_call | solution.py:488
  144.4 0.8 copy-done.3
  145.2 1.0 copy-done.15
  146.2 0.7 copy-done.30
  146.9 0.7 copy-done.31
  147.6 27.3 %mlp.1 = (f32[128,1024]{1,0:T(8,128)}, bf16[4,128,1024]{2,1,0:T(8,128)(2,1)}, f32[1,1024]{1,0:T(1,128)}, bf16[512,1024]{1,0:T(8,128)(2,1)}, bf16[1024,1024]{1,0:T(8,128)(2,1)}, /*index=5*/bf16[1024,1024]{1,0:T(8,128)(2,1)}) custom-call(bf16[4,128,1024]{2,1,0:T(8,128)(2,1)} %copy-done.15, bf16[8,4,16,1024]{3,2,1,0:T(8,128)(2,1)} %bitcast.105, ...), custom_call_target="tpu_custom_call" | custom-call | flops 1 | bytes 1 | tf_op jit(solution)/shard_map/mlp/pallas_call | solution.py:488
  174.9 0.8 fusion.1
  175.7 26.8 %cross_back.1 = (f32[128,1024]{1,0:T(8,128)}, bf16[4,128,1024]{2,1,0:T(8,128)(2,1)}, f32[1,1024]{1,0:T(1,128)}, bf16[128,256]{1,0:T(8,128)(2,1)}, bf16[128,256]{...) custom-call(bf16[4,128,1024]{2,1,0:T(8,128)(2,1)} %get-tuple-element.102.incoming, bf16[256,1024]{1,0:T(8,128)(2,1)} %wo.3, ...), custom_call_target="tpu_custom_call" | custom-call | flops 1 | bytes 1 | tf_op jit(solution)/shard_map/cross_back/pallas_call | solution.py:488
  202.5 1.8 fusion.d_ref
  204.4 1.2 copy-done.13
  205.6 1.2 copy-done.14
  206.9 89.9 %attention_back.1 = (bf16[1,256,512]{2,1,0:T(8,128)(2,1)S(1)}, bf16[1,512,512]{2,1,0:T(8,128)(2,1)S(1)}, bf16[768,1024]{1,0:T(8,128)(2,1)S(1)}, f32[128,1024]{1,0:T(8,128)S(1)}) custom-call(bf16[1,256,512]{2,1,0:T(8,128)(2,1)S(1)} %fusion.d_ref, bf16[4,1,64,512]{3,2,1,0:T(8,128)(2,1)S(1)} %copy-done.33, f32[4,1,64,512]{3,2,1,0:T(8,128)S(1)} %get-tuple-element.108.of_ref, ...), custom_call_target="tpu_custom_call" | custom-call | flops 1 | bytes 1 | tf_op jit(solution)/shard_map/attention_back/pallas_call | solution.py:977
  296.9 1.1 copy-done.5
  298.1 11.5 %attn_back.1 = (bf16[128,1024]{1,0:T(8,128)(2,1)S(1)}, f32[1,1024]{1,0:T(1,128)S(1)}) custom-call(bf16[256,512]{1,0:T(8,128)(2,1)S(1)} %bitcast.79, bf16[512,512]{1,0:T(8,128)(2,1)S(1)} %bitcast.77, bf16[1024,256]{1,0:T(8,128)(2,1)S(1)} %copy-done.21, bf16[1024,256]{1,0:T(8,128)(2,1)S(1)} %copy-done.23, bf16[1024,256]{1,0:T(8,128)(2,1)S(1)} %copy-done.25, ...), custom_call_target="tpu_custom_call" | custom-call | flops 1 | bytes 1 | tf_op jit(solution)/shard_map/attn_back/pallas_call | solution.py:488
  309.7 0.6 reshape.246.gains
  310.3 0.1 add_convert_fusion
  310.4 0.2 copy.57
  310.6 0.1 copy.59
  310.7 0.2 copy.58
  310.9 0.1 copy.60
  311.0 0.8 maximum_bitcast_fusion.tokens
  311.9 131.5 %outer_backward.1 = (f32[32,64,256]{2,1,0:T(8,128)}, bf16[3328,256]{1,0:T(8,128)(2,1)}, bf16[768,1024]{1,0:T(8,128)(2,1)}, bf16[4,2,128,256]{3,2,1,0:T(8,128)(2,...) custom-call(bf16[32,64,256]{2,1,0:T(8,128)(2,1)} %bitcast.101, ...), custom_call_target="tpu_custom_call" | custom-call | flops 1 | bytes 1 | tf_op jit(solution)/shard_map/outer_backward/pallas_call | solution.py:1664
  443.4 1.1 slice_convert_fusion
  444.6 0.8 copy.62
  445.4 0.7 copy.61
  446.1 0.7 fusion.6
  446.8 0.6 fusion.5
  447.4 0.6 fusion.4
  447.9 0.8 broadcast_multiply_fusion
  448.8 14.3 %finish_grads.1 = (f32[1024,256]{1,0:T(8,128)}, f32[1024,256]{1,0:T(8,128)}, f32[1024,256]{1,0:T(8,128)}, f32[256,1024]{1,0:T(8,128)}, f32[256,1024]{1,0:T(8,128...) custom-call(bf16[128,4096]{1,0:T(8,128)(2,1)} %bitcast.98, ...), custom_call_target="tpu_custom_call" | custom-call | flops 1 | bytes 1 | tf_op jit(solution)/shard_map/finish_grads/pallas_call | solution.py:1751
  463.1 1.0 copy.70
  464.1 1.0 copy-done.45
  465.0 1.3 copy.71
  (110 shorter events, 0.5 us)
Async XLA Ops:
  7.2 3.0 copy-start
  7.2 48.8 %all-gather.3.cloned.1.call-start = ((), (), s32[]{:S(2)}) async-start(), calls=%async_computation | async-start | bytes 1310720 | tf_op jit(solution)/shard_map/all_gather | solution.py:1829
  8.0 139.7 %all-gather.5.cloned.1.call-start = ((), (), s32[]{:S(2)}) async-start(), calls=%async_computation.1 | async-start | bytes 1310720 | tf_op jit(solution)/shard_map/all_gather | solution.py:1829
  8.7 440.1 %all-reduce.3.cloned.1.call-start = ((), (), s32[]{:S(2)}) async-start(), calls=%async_computation.2 | async-start | bytes 8388608 | tf_op jit(solution)/shard_map/psum | solution.py:1953
  10.5 112.9 %copy-start.29 = (f32[128,128]{1,0:T(8,128)}, f32[128,128]{1,0:T(8,128)S(1)}, u32[]{:S(2)}) copy-start(f32[128,128]{1,0:T(8,128)S(1)} %and_select_fusion.mask) | copy-start | bytes 196612
  12.1 43.9 %copy-start.18 = (bf16[256,1024]{1,0:T(8,128)(2,1)S(1)}, bf16[256,1024]{1,0:T(8,128)(2,1)}, u32[]{:S(2)}) copy-start(bf16[256,1024]{1,0:T(8,128)(2,1)} %lift_weight.1) | copy-start | bytes 1572868
  12.1 43.9 %copy-start.20 = (bf16[1024,256]{1,0:T(8,128)(2,1)S(1)}, bf16[1024,256]{1,0:T(8,128)(2,1)}, u32[]{:S(2)}) copy-start(bf16[1024,256]{1,0:T(8,128)(2,1)} %wq.7) | copy-start | bytes 1572868
  12.1 43.9 %copy-start.22 = (bf16[1024,256]{1,0:T(8,128)(2,1)S(1)}, bf16[1024,256]{1,0:T(8,128)(2,1)}, u32[]{:S(2)}) copy-start(bf16[1024,256]{1,0:T(8,128)(2,1)} %wk.3) | copy-start | bytes 1572868
  12.1 43.9 %copy-start.24 = (bf16[1024,256]{1,0:T(8,128)(2,1)S(1)}, bf16[1024,256]{1,0:T(8,128)(2,1)}, u32[]{:S(2)}) copy-start(bf16[1024,256]{1,0:T(8,128)(2,1)} %wv.3) | copy-start | bytes 1572868
  57.6 1.2 copy-start.42
  70.1 36.4 %copy-start.8 = (bf16[4,128,1024]{2,1,0:T(8,128)(2,1)}, bf16[4,128,1024]{2,1,0:T(8,128)(2,1)S(1)}, u32[]{:S(2)}) copy-start(bf16[4,128,1024]{2,1,0:T(8,128)(2,1)S(1)} %get-tuple-element.122) | copy-start | bytes 3145732
  70.1 36.4 %copy-start.26 = (f32[128,1024]{1,0:T(8,128)}, f32[128,1024]{1,0:T(8,128)S(1)}, u32[]{:S(2)}) copy-start(f32[128,1024]{1,0:T(8,128)S(1)} %get-tuple-element.95.before) | copy-start | bytes 1572868
  70.1 36.4 %copy-start.35 = (f32[3,1024]{1,0:T(4,128)S(1)}, f32[3,1024]{1,0:T(4,128)}, u32[]{:S(2)}) copy-start(f32[3,1024]{1,0:T(4,128)} %get-tuple-element.91.gain) | copy-start | bytes 36868
  70.1 36.4 %copy-start.43 = (bf16[256,1024]{1,0:T(8,128)(2,1)S(1)}, bf16[256,1024]{1,0:T(8,128)(2,1)}, u32[]{:S(2)}) copy-start(bf16[256,1024]{1,0:T(8,128)(2,1)} %weight.1) | copy-start | bytes 1572868
  106.5 16.9 %copy-start.10 = (bf16[8,1,512,128]{3,2,1,0:T(8,128)(2,1)}, bf16[8,1,512,128]{3,2,1,0:T(8,128)(2,1)S(1)}, u32[]{:S(2)}) copy-start(bf16[8,1,512,128]{3,2,1,0:T(8,128)(2,1)S(1)} %get-tuple-element.110.kv_ref) | copy-start | bytes 3145732
  106.5 16.9 %copy-start.32 = (bf16[4,1,64,512]{3,2,1,0:T(8,128)(2,1)}, bf16[4,1,64,512]{3,2,1,0:T(8,128)(2,1)S(1)}, u32[]{:S(2)}) copy-start(bf16[4,1,64,512]{3,2,1,0:T(8,128)(2,1)S(1)} %get-tuple-element.107.q_ref) | copy-start | bytes 786436
  106.5 16.9 %copy-start.40 = (f32[4,1,1,512]{3,2,1,0:T(1,128)}, f32[4,1,1,512]{3,2,1,0:T(1,128)S(1)}, u32[]{:S(2)}) copy-start(f32[4,1,1,512]{3,2,1,0:T(1,128)S(1)} %get-tuple-element.109.lse_ref) | copy-start | bytes 24580
  106.6 16.9 %copy-start.16 = (bf16[1024,256]{1,0:T(8,128)(2,1)S(1)}, bf16[1024,256]{1,0:T(8,128)(2,1)}, u32[]{:S(2)}) copy-start(bf16[1024,256]{1,0:T(8,128)(2,1)} %wq.6) | copy-start | bytes 1572868
  106.6 16.9 %copy-start.17 = (bf16[256,1024]{1,0:T(8,128)(2,1)S(1)}, bf16[256,1024]{1,0:T(8,128)(2,1)}, u32[]{:S(2)}) copy-start(bf16[256,1024]{1,0:T(8,128)(2,1)} %wo.3) | copy-start | bytes 1572868
  106.6 16.9 %copy-start.38 = (bf16[128,256]{1,0:T(8,128)(2,1)S(1)}, bf16[128,256]{1,0:T(8,128)(2,1)}, u32[]{:S(2)}) copy-start(bf16[128,256]{1,0:T(8,128)(2,1)} %get-tuple-element.97.ck) | copy-start | bytes 196612
  106.6 16.9 %copy-start.39 = (bf16[128,256]{1,0:T(8,128)(2,1)S(1)}, bf16[128,256]{1,0:T(8,128)(2,1)}, u32[]{:S(2)}) copy-start(bf16[128,256]{1,0:T(8,128)(2,1)} %get-tuple-element.98.cv) | copy-start | bytes 196612
  123.4 21.0 %copy-start.9 = (bf16[4,128,1024]{2,1,0:T(8,128)(2,1)}, bf16[4,128,1024]{2,1,0:T(8,128)(2,1)S(1)}, u32[]{:S(2)}) copy-start(bf16[4,128,1024]{2,1,0:T(8,128)(2,1)S(1)} %get-tuple-element.96.cross_in) | copy-start | bytes 3145732
  123.4 21.0 %copy-start.19 = (f32[128,1024]{1,0:T(8,128)}, f32[128,1024]{1,0:T(8,128)S(1)}, u32[]{:S(2)}) copy-start(f32[128,1024]{1,0:T(8,128)S(1)} %get-tuple-element.99.before) | copy-start | bytes 1572868
  175.7 26.8 %copy-start.44 = (bf16[256,1024]{1,0:T(8,128)(2,1)S(1)}, bf16[256,1024]{1,0:T(8,128)(2,1)}, u32[]{:S(2)}) copy-start(bf16[256,1024]{1,0:T(8,128)(2,1)} %weight.1) | copy-start | bytes 1572868
  175.7 28.6 %copy-start.12 = (bf16[512,1024]{1,0:T(8,128)(2,1)S(1)}, bf16[512,1024]{1,0:T(8,128)(2,1)}, u32[]{:S(2)}) copy-start(bf16[512,1024]{1,0:T(8,128)(2,1)} %get-tuple-element.112) | copy-start | bytes 3145732
  175.7 28.6 %copy-start.33 = (bf16[4,1,64,512]{3,2,1,0:T(8,128)(2,1)S(1)}, bf16[4,1,64,512]{3,2,1,0:T(8,128)(2,1)}, u32[]{:S(2)}) copy-start(bf16[4,1,64,512]{3,2,1,0:T(8,128)(2,1)} %copy-done.32) | copy-start | bytes 786436
  175.7 28.6 %copy-start.41 = (f32[4,1,1,512]{3,2,1,0:T(1,128)S(1)}, f32[4,1,1,512]{3,2,1,0:T(1,128)}, u32[]{:S(2)}) copy-start(f32[4,1,1,512]{3,2,1,0:T(1,128)} %copy-done.40) | copy-start | bytes 24580
  202.5 1.9 copy-start.11
  204.4 1.2 copy-start.13
  205.6 1.2 copy-start.14
  206.9 91.2 %copy-start.21 = (bf16[1024,256]{1,0:T(8,128)(2,1)S(1)}, bf16[1024,256]{1,0:T(8,128)(2,1)}, u32[]{:S(2)}) copy-start(bf16[1024,256]{1,0:T(8,128)(2,1)} %wq.7) | copy-start | bytes 1572868
  206.9 91.2 %copy-start.23 = (bf16[1024,256]{1,0:T(8,128)(2,1)S(1)}, bf16[1024,256]{1,0:T(8,128)(2,1)}, u32[]{:S(2)}) copy-start(bf16[1024,256]{1,0:T(8,128)(2,1)} %wk.3) | copy-start | bytes 1572868
  206.9 91.2 %copy-start.25 = (bf16[1024,256]{1,0:T(8,128)(2,1)S(1)}, bf16[1024,256]{1,0:T(8,128)(2,1)}, u32[]{:S(2)}) copy-start(bf16[1024,256]{1,0:T(8,128)(2,1)} %wv.3) | copy-start | bytes 1572868
  206.9 91.2 %copy-start.27 = (f32[128,1024]{1,0:T(8,128)S(1)}, f32[128,1024]{1,0:T(8,128)}, u32[]{:S(2)}) copy-start(f32[128,1024]{1,0:T(8,128)} %copy-done.26) | copy-start | bytes 1572868
  206.9 91.2 %copy-start.28 = (f32[128,1024]{1,0:T(8,128)S(1)}, f32[128,1024]{1,0:T(8,128)}, u32[]{:S(2)}) copy-start(f32[128,1024]{1,0:T(8,128)} %get-tuple-element.117.residual) | copy-start | bytes 1572868
  206.9 91.2 %copy-start.36 = (f32[3,1024]{1,0:T(4,128)S(1)}, f32[3,1024]{1,0:T(4,128)}, u32[]{:S(2)}) copy-start(f32[3,1024]{1,0:T(4,128)} %get-tuple-element.91.gain) | copy-start | bytes 36868
  298.0 12.4 %copy-start.2 = (bf16[1,512,512]{2,1,0:T(8,128)(2,1)}, bf16[1,512,512]{2,1,0:T(8,128)(2,1)S(1)}, u32[]{:S(2)}) copy-start(bf16[1,512,512]{2,1,0:T(8,128)(2,1)S(1)} %get-tuple-element.116) | copy-start | bytes 1572868
  298.0 12.4 %copy-start.7 = (bf16[1,256,512]{2,1,0:T(8,128)(2,1)}, bf16[1,256,512]{2,1,0:T(8,128)(2,1)S(1)}, u32[]{:S(2)}) copy-start(bf16[1,256,512]{2,1,0:T(8,128)(2,1)S(1)} %get-tuple-element.115) | copy-start | bytes 786436
  298.0 11.6 %copy-start.50 = (f32[1,1024]{1,0:T(1,128)S(1)}, f32[1,1024]{1,0:T(1,128)}, u32[]{:S(2)}) copy-start(f32[1,1024]{1,0:T(1,128)} %get-tuple-element.121) | copy-start | bytes 12292
  298.0 11.6 %copy-start.51 = (f32[1,1024]{1,0:T(1,128)S(1)}, f32[1,1024]{1,0:T(1,128)}, u32[]{:S(2)}) copy-start(f32[1,1024]{1,0:T(1,128)} %get-tuple-element.120) | copy-start | bytes 12292
  298.0 12.3 %copy-start.4 = (f32[128,1024]{1,0:T(8,128)S(1)}, f32[128,1024]{1,0:T(8,128)}, u32[]{:S(2)}) copy-start(f32[128,1024]{1,0:T(8,128)} %copy-done.3) | copy-start | bytes 1572868
  309.6 2.3 copy-start.6
  443.4 2.7 copy-start.47
  443.4 3.9 copy-start.52
  443.4 4.5 copy-start.49
  448.8 14.3 %copy-start.46 = (bf16[32,64,256]{2,1,0:T(8,128)(2,1)S(1)}, bf16[32,64,256]{2,1,0:T(8,128)(2,1)}, u32[]{:S(2)}) copy-start(bf16[32,64,256]{2,1,0:T(8,128)(2,1)} %get-tuple-element.87) | copy-start | bytes 3145732
  463.1 2.0 copy-start.45
  463.1 3.3 copy-start.1
  (8 other events, 6.4 us)
Sparse Core Ops, SparseCore 0:
  9.6 22.0 all-gather.2
  33.2 15.8 all-gather.4
  175.0 176.8 all-reduce.2

commit v5 on v4

--- a/solution.py
+++ b/solution.py
@@ -518,26 +518,36 @@
 class TileSum:
     PARTS = 4
 
-    def __init__(self, nt, x, out, buffers, add_sems, share_sems):
+    def __init__(self, nt, x, out, pair, line, share_sems):
         t, s = lax.axis_index("tile"), lax.axis_index("sub")
         self.na, self.x, self.out = nt // 2, x, out
         self.a, self.b, self.s = t // 2, lax.rem(t, 2), s
         self.me, self.pair = (t, s), (self.a * 2 + 1 - self.b, s)
-        self.half = out.shape[0] // 2
+        self.half = (out.shape[0] if x is None else x.shape[0]) // 2
         self.piece = self.half // 2 // self.PARTS
-        if add_sems:
-            self.got1, self.stage, self.got2 = buffers
-            self.s1, self.r1, self.s2, self.r2 = add_sems
+        self.folded = None
+        if pair:
+            self.got1, self.s1, self.r1 = pair
+        if line:
+            self.stage, self.got2, self.s2, self.r2 = line
         if share_sems:
             self.s3, self.r3, self.s4, self.r4 = share_sems
 
     @staticmethod
     def buffers(rows, width):
-        return [pltpu.VMEM((rows // 2, width), bf16) for _ in range(3)]
+        return pltpu.VMEM((rows // 2, width), bf16)
 
     @staticmethod
     def sems():
-        return [dma(2, TileSum.PARTS) for _ in range(4)]
+        return [dma(2, TileSum.PARTS) for _ in range(2)]
+
+    @staticmethod
+    def pair_scratch(rows, width):
+        return [TileSum.buffers(rows, width)] + TileSum.sems()
+
+    @staticmethod
+    def line_scratch(rows, width):
+        return [TileSum.buffers(rows, width)] * 2 + TileSum.sems()
 
     def rows(self, b, e, j):
         start = b * self.half + (j * 2 + e) * self.piece
@@ -568,11 +578,23 @@
             for e in range(2):
                 self.step_of(self.along(e)[2], step, functools.partial(self.add_one, e))
 
+    def with_pair(self, e, j):
+        here, mine = self.rows(0, e, j), self.rows(self.b, e, j)
+        arrived(self.got1.at[here], self.s1.at[e, j], self.r1.at[e, j], self.me)
+        return self.x[mine].astype(f32) + self.got1[here].astype(f32)
+
+    def fold(self, half):
+        for j in range(self.PARTS):
+            for e in range(2):
+                half[self.rows(0, e, j)] = self.with_pair(e, j).astype(bf16)
+        for j in range(self.PARTS):
+            for e in range(2):
+                self.to_pair(e, j).wait_send()
+
     def add_one(self, e, j):
         _, after, way = self.along(e)
         here, mine = self.rows(0, e, j), self.rows(self.b, e, j)
-        arrived(self.got1.at[here], self.s1.at[e, j], self.r1.at[e, j], self.me)
-        both = self.x[mine].astype(f32) + self.got1[here].astype(f32)
+        both = self.with_pair(e, j) if self.folded is None else self.folded[here].astype(f32)
 
         @pl.when(way == 0)
         def _():
@@ -616,7 +638,8 @@
         for j in range(self.PARTS):
             for e in range(2):
                 _, after, way = self.along(e)
-                self.to_pair(e, j).wait_send()
+                if self.folded is None:
+                    self.to_pair(e, j).wait_send()
                 stage = self.stage.at[self.rows(0, e, j)]
                 sent = remote(stage, stage, self.s2.at[e, j], self.r2.at[e, j], after)
                 pl.when(way < self.na - 1)(sent.wait_send)
@@ -869,10 +892,8 @@
     me = (t, s)
     batch, length = d_ref.shape[0], d_ref.shape[2]
     copies = Copies()
-    early = TileSum(nt, mine, early_out, scratch[:3], scratch[3:7], None)
-    beside = SubScatter(ns, copies, beside_ref, *scratch[7:10], scratch[10:])
-    steps = list(early.steps())
-    clear(early_out)
+    early = TileSum(nt, mine, None, scratch[:3], None, None)
+    beside = SubScatter(ns, copies, beside_ref, *scratch[3:6], scratch[6:])
     greet_all(nt, ns)
     dealt[a] = d_ref[:, pl.ds(pl.multiple_of(a * HD, HD), HD), :]
     for k in range(1, u):
@@ -928,7 +949,6 @@
             copies.send(stage.at[k], lanes_of(kvo, a, 2 * HD), ks.at[k], kr.at[k], a_peer(k))
 
     order = list(range(1, u)) + [0]
-    done = 0
     for at, k in enumerate(order):
         for m in range(1, nb):
             tile = lax.rem(a + k, u) * nb + lax.rem(b + m, nb)
@@ -941,8 +961,6 @@
             kept[k, n] = work(lax.rem(a + k, u) * nb + b, n)
         if at:
             settle(order[at - 1])
-            early.add(steps[done : done + 2])
-            done += 2
     for k in list(range(1, u)) + [0]:
         i = lax.rem(a + k, u)
         for n in range(batch):
@@ -955,8 +973,7 @@
     settle(order[-1])
     local.append(pltpu.make_async_copy(stage.at[0], lanes_of(kvo, a, 2 * HD), own.at[1]))
     local[1].start()
-    early.add(steps[done:])
-    early.end_add()
+    early.fold(early_out)
     for k in range(1, u):
         i = lax.rem(a + u - k, u)
         arrived(rows_of(qo, i, HD), qs.at[k], qr.at[k], me)
@@ -979,7 +996,7 @@
         out_shape=(
             shape(d.shape, bf16),
             shape((batch, length, u * 2 * HD), bf16),
-            shape(sums, bf16),
+            shape((sums[0] // 2, sums[1]), bf16),
             shape(beside.shape[1:], f32),
         ),
         in_specs=[in_vmem()] * 9,
@@ -1006,8 +1023,7 @@
             dma(u),
             dma(2),
         ]
-        + TileSum.buffers(*sums)
-        + TileSum.sems()
+        + TileSum.pair_scratch(*sums)
         + SubScatter.scratch(ns, *beside.shape[1:]),
         cost_estimate=SHORT,
         compiler_params=params(cid, 40),
@@ -1424,10 +1440,10 @@
     t, s = lax.axis_index("tile"), lax.axis_index("sub")
     sums2, sums1, scratch = scratch[:6], scratch[6:12], scratch[12:]
     copies = Copies()
-    early = TileSum(nt, None, wide_out, None, None, scratch[:4])
-    late = TileSum(nt, tall, tall_out, scratch[4:7], scratch[7:11], scratch[11:15])
-    scratch = scratch[15:]
-    wide_out[...] = wide[...]
+    early = TileSum(nt, None, wide_out, None, scratch[:4], scratch[4:8])
+    early.folded = wide
+    late = TileSum(nt, tall, tall_out, scratch[8:11], scratch[11:15], scratch[15:19])
+    scratch = scratch[19:]
     second = FullSum(nt, ns, copies, own2, sum2_out, *scratch[:5], scratch[5:17])
     scratch = scratch[17:]
     first, rest = Nothing(), []
@@ -1498,7 +1514,7 @@
         )
     late.start()
     steps = list(early.steps())
-    early.share(steps[:1])
+    early.add(steps[:1])
     total = rows * pitch
 
     def turned(row):
@@ -1517,7 +1533,7 @@
     taps = 9 * channels
     turned(lambda i: grad2[i])
     held[0].wait()
-    between = [lambda k=k: early.share(steps[k : k + 1]) for k in (1, 2, 3)]
+    between = [lambda k=k: early.add(steps[k : k + 1]) for k in (1, 2, 3)]
     kernel_grads(act2, inner_t, 16, total, pitch, own2, between)
     lift_grad = dot(pooled[...].T, lifted[...]).astype(bf16)
     for n in range(width // channels):
@@ -1526,7 +1542,7 @@
         ]
     pad_below(own2, taps + width)
     second.start()
-    early.share(steps[4:5])
+    early.add(steps[4:5])
     finish(border)
     ok = lambda lift_by: (
         lambda i: (t * rows + i - lift_by >= 0) & (t * rows + i - lift_by < nt * rows)
@@ -1550,8 +1566,8 @@
             triple, w2t, start, size, pitch, dot_t
         ) * silu_slope(hat * gain2 + bias2)
         if start == size:
-            early.share(steps[5:6])
-    early.share(steps[6:])
+            early.add(steps[5:6])
+    early.add(steps[6:])
 
     at = lambda i: pl.multiple_of(16 + i * pitch, 16)
 
@@ -1564,6 +1580,7 @@
     plain = sum_near(nt, ns, local2, sums2[0], sums2[2], sums2[3])
     plain += sum_far(nt, ns, sums2[0], sums2[1], *sums2[2:])
     second.spread()
+    early.share(steps[:2])
     late.add(steps[:2])
     back2 = sum_end(nt, sums2[1], sums2[4], sums2[5])
     back2, gains_total = back2[:2], back2[2:]
@@ -1580,13 +1597,16 @@
         lambda i: grad_hidden(at(i) + cols, 16),
         lambda: grad_hidden(0, 16),
     )
+    early.share(steps[2:3])
     late.add(steps[2:3])
     turned(lambda i: flat[pl.ds(24 + (i + 1) * pitch, cols), :].astype(bf16))
     held[1].wait()
     between = [lambda: late.add(steps[3:4]), lambda: first.start(), lambda: late.add(steps[4:5])]
+    between[0] = lambda: (early.share(steps[3:4]), late.add(steps[3:4]))
     kernel_grads(act1, inner_t, 16 + pitch, total, pitch, own1, between)
     pad_below(own1, taps)
     rest.start()
+    early.share(steps[4:5])
     second.settle()
     first.cross()
     put_left_to_right(flat, triple.at[pl.ds(0, length)])
@@ -1600,8 +1620,10 @@
         hat = (img[pl.ds(start, step)].astype(f32) - center1) * std1
         outer_grad[pl.ds(start, step)] = value * silu_slope(hat * gain1 + bias1)
         if start == step:
+            early.share(steps[5:6])
             late.add(steps[5:6])
     first.spread()
+    early.share(steps[6:])
     late.add(steps[6:])
     late.share(steps[:1])
     local1 = row_sums(rows, channels, lambda i: (outer_grad[i], outer_grad[i] * hat1(i)))
@@ -1635,6 +1657,7 @@
         block = tokens_out.at[lax.rem(s + ns - k, ns)]
         arrived(block, token_ss.at[k], token_rs.at[k], (t, s))
     rest.relay()
+    early.end_add()
     early.end_share()
     second.end()
     first.end()
@@ -1666,7 +1689,7 @@
         out_shape=(
             shape(img.shape, f32),
             shape(tall, bf16),
-            shape(wide.shape, bf16),
+            shape((2 * wide.shape[0], wide.shape[1]), bf16),
             shape(tokens.shape, bf16),
             shape((rows2, channels), bf16),
             shape((rows1, channels), bf16),
@@ -1697,8 +1720,11 @@
         ]
         + sum_scratch(nt, ns, channels, 2 + gains.shape[0])
         + sum_scratch(nt, ns, channels)
+        + TileSum.line_scratch(2 * wide.shape[0], wide.shape[1])
         + TileSum.sems()
-        + TileSum.buffers(*tall)
+        + TileSum.sems()
+        + TileSum.pair_scratch(*tall)
+        + TileSum.line_scratch(*tall)
         + TileSum.sems()
         + TileSum.sems()
         + FullSum.scratch(nt, ns, rows2, channels)

time: 478 us -> 474 us (level)
    pallas_call x1, Pallas kernels: 89.9 us -> 62.1 us  [attention_back(): pl.pallas_call(functools.partial(attention_back_kernel, nt, ns, u), out_s...]
    pallas_call x1, Pallas kernels: 132 us -> 156 us  [outer_backward(): pl.pallas_call(functools.partial(outer_backward_kernel, nt, ns, cut), out...]
where the time goes in v5:
time: 474 us; the launch traced here: 470 us
  Pallas kernels  427 us (90%)
  local copies, waits for them, and re-layouts  17.1 us (4%)
  between operations  16.1 us (3%)
  other arithmetic  5.79 us (1%)
    pallas_call x1, Pallas kernels, outer_backward(): pl.pallas_call(functools.partial(outer_backward_kernel, nt, ns, cut), out...  156 us
    pallas_call x6, Pallas kernels, chain_call(): pl.pallas_call(functools.partial(kernel, ns), out_shape=tuple((jax.ShapeD...  114 us
    pallas_call x1, Pallas kernels, attention_back(): pl.pallas_call(functools.partial(attention_back_kernel, nt, ns, u), out_s...  62.1 us
    pallas_call x1, Pallas kernels, outer_forward(): pl.pallas_call(functools.partial(outer_forward_kernel, nt, ns), out_shape...  43.8 us
    pallas_call x1, Pallas kernels, self_attention(): pl.pallas_call(functools.partial(self_attention_kernel, nt, u), out_shape...  36.4 us
    pallas_call x1, Pallas kernels, finish_grads(): pl.pallas_call(finish_kernel, grid=(steps,), out_shape=(shape(width, feat...  14.3 us
    unnamed x108, local copies, waits for them, and re-layouts  12.9 us
  transfers between devices with their start and end apart: 3, of which 0 were waited for; matrix products, arithmetic and copies ran while one was open for 3% of the time, Pallas kernels for 82%

profile of v5, /device:TPU:0, one launch (start us, length us, event | category | flops | bytes accessed | tf_op | source)
XLA Modules:
  0.0 469.5 jit_solution(5987449513152797474)
XLA Ops:
  7.3 0.7 all-gather.3.cloned.1.call-update
  8.0 0.7 all-gather.5.cloned.1.call-update
  10.2 0.1 convolution_bitcast_fusion
  10.3 0.1 pad.7.clone
  10.4 0.1 and_select_fusion.mask
  10.5 0.2 copy-done.48
  10.7 0.7 maximum_bitcast_fusion.2
  11.5 0.7 maximum_bitcast_fusion.1.vec
  12.1 43.8 %outer_forward.1 = (bf16[32,64,256]{2,1,0:T(8,128)(2,1)}, bf16[128,256]{1,0:T(8,128)(2,1)}, bf16[2912,768]{1,0:T(8,128)(2,1)}, bf16[2752,768]{1,0:T(8,128)(2,1)}...) custom-call(bf16[32,64,256]{2,1,0:T(8,128)(2,1)} %bitcast.99, ...), custom_call_target="tpu_custom_call" | custom-call | flops 20000000000 | bytes 60000000 | tf_op jit(solution)/shard_map/outer_forward/pallas_call | solution.py:1382
  56.0 0.7 copy-done.34
  56.8 0.8 copy-done.37
  57.6 1.2 copy-done.42
  58.8 11.2 %enter.1 = (f32[128,1024]{1,0:T(8,128)S(1)}, bf16[4,128,1024]{2,1,0:T(8,128)(2,1)S(1)}, bf16[256,512]{1,0:T(8,128)(2,1)S(1)}, bf16[512,512]{1,0:T(8,128)(2,1)S(1)}) custom-call(bf16[8,4,16,1024]{3,2,1,0:T(8,128)(2,1)S(1)} %bitcast.89, bf16[128,256]{1,0:T(8,128)(2,1)S(1)} %copy-done.37, bf16[256,1024]{1,0:T(8,128)(2,1)S(1)} %copy-done.18, ...), custom_call_target="tpu_custom_call" | custom-call | flops 20000000000 | bytes 60000000 | tf_op jit(solution)/shard_map/enter/pallas_call | solution.py:488
  70.1 36.4 %self_attention.1 = (bf16[1,256,512]{2,1,0:T(8,128)(2,1)S(1)}, bf16[4,1,64,512]{3,2,1,0:T(8,128)(2,1)S(1)}, bf16[8,1,512,128]{3,2,1,0:T(8,128)(2,1)S(1)}, f32[4,...) custom-call(bf16[1,256,512]{2,1,0:T(8,128)(2,1)S(1)} %bitcast.91, bf16[1,512,512]{2,1,0:T(8,128)(2,1)S(1)} %bitcast.90), custom_call_target="tpu_custom_call" | custom-call | flops 20000000000 | bytes 60000000 | tf_op jit(solution)/shard_map/self_attention/pallas_call | solution.py:756
  106.6 16.8 %attn_out.1 = (f32[128,1024]{1,0:T(8,128)S(1)}, bf16[4,128,1024]{2,1,0:T(8,128)(2,1)S(1)}) custom-call(bf16[256,512]{1,0:T(8,128)(2,1)S(1)} %bitcast.86, bf16[256,1024]{1,0:T(8,128)(2,1)S(1)} %copy-done.43, f32[128,1024]{1,0:T(8,128)S(1)} %get-tuple-element.95.before, f32[3,1024]{1,0:T(4,128)S(1)} %copy-done.35), custom_call_target="tpu_custom_call" | custom-call | flops 20000000000 | bytes 60000000 | tf_op jit(solution)/shard_map/attn_out/pallas_call | solution.py:488
  123.5 20.9 %cross.1 = (f32[128,1024]{1,0:T(8,128)S(1)}, bf16[4,128,1024]{2,1,0:T(8,128)(2,1)S(1)}, bf16[4,128,256]{2,1,0:T(8,128)(2,1)S(1)}, bf16[4,128,256]{2,1,0:T(8,128)(2,1)S(1)}) custom-call(bf16[4,128,1024]{2,1,0:T(8,128)(2,1)S(1)} %get-tuple-element.96.cross_in, bf16[1024,256]{1,0:T(8,128)(2,1)S(1)} %copy-done.16, bf16[128,256]{1,0:T(8,128)(2,1)S(1)} %copy-done.38, ...), custom_call_target="tpu_custom_call" | custom-call | flops 20000000000 | bytes 60000000 | tf_op jit(solution)/shard_map/cross/pallas_call | solution.py:488
  144.5 0.8 copy-done.3
  145.2 1.0 copy-done.14
  146.2 0.7 copy-done.30
  146.9 0.7 copy-done.31
  147.6 27.3 %mlp.1 = (f32[128,1024]{1,0:T(8,128)}, bf16[4,128,1024]{2,1,0:T(8,128)(2,1)}, f32[1,1024]{1,0:T(1,128)}, bf16[512,1024]{1,0:T(8,128)(2,1)}, bf16[1024,1024]{1,0:T(8,128)(2,1)}, /*index=5*/bf16[1024,1024]{1,0:T(8,128)(2,1)}) custom-call(bf16[4,128,1024]{2,1,0:T(8,128)(2,1)} %copy-done.14, bf16[8,4,16,1024]{3,2,1,0:T(8,128)(2,1)} %bitcast.105, ...), custom_call_target="tpu_custom_call" | custom-call | flops 1 | bytes 1 | tf_op jit(solution)/shard_map/mlp/pallas_call | solution.py:488
  174.9 0.8 fusion.1
  175.8 26.8 %cross_back.1 = (f32[128,1024]{1,0:T(8,128)}, bf16[4,128,1024]{2,1,0:T(8,128)(2,1)}, f32[1,1024]{1,0:T(1,128)}, bf16[128,256]{1,0:T(8,128)(2,1)}, bf16[128,256]{...) custom-call(bf16[4,128,1024]{2,1,0:T(8,128)(2,1)} %get-tuple-element.102.incoming, bf16[256,1024]{1,0:T(8,128)(2,1)} %wo.3, ...), custom_call_target="tpu_custom_call" | custom-call | flops 1 | bytes 1 | tf_op jit(solution)/shard_map/cross_back/pallas_call | solution.py:488
  202.5 1.8 fusion.d_ref
  204.4 1.2 copy-done.12
  205.6 1.2 copy-done.13
  206.9 62.1 %attention_back.1 = (bf16[1,256,512]{2,1,0:T(8,128)(2,1)S(1)}, bf16[1,512,512]{2,1,0:T(8,128)(2,1)S(1)}, bf16[384,1024]{1,0:T(8,128)(2,1)S(1)}, f32[128,1024]{1,0:T(8,128)S(1)}) custom-call(bf16[1,256,512]{2,1,0:T(8,128)(2,1)S(1)} %fusion.d_ref, bf16[4,1,64,512]{3,2,1,0:T(8,128)(2,1)S(1)} %copy-done.33, f32[4,1,64,512]{3,2,1,0:T(8,128)S(1)} %get-tuple-element.108.of_ref, ...), custom_call_target="tpu_custom_call" | custom-call | flops 1 | bytes 1 | tf_op jit(solution)/shard_map/attention_back/pallas_call | solution.py:994
  269.1 0.9 copy-done.15
  270.0 11.5 %attn_back.1 = (bf16[128,1024]{1,0:T(8,128)(2,1)S(1)}, f32[1,1024]{1,0:T(1,128)S(1)}) custom-call(bf16[256,512]{1,0:T(8,128)(2,1)S(1)} %bitcast.79, bf16[512,512]{1,0:T(8,128)(2,1)S(1)} %bitcast.77, bf16[1024,256]{1,0:T(8,128)(2,1)S(1)} %copy-done.21, bf16[1024,256]{1,0:T(8,128)(2,1)S(1)} %copy-done.23, bf16[1024,256]{1,0:T(8,128)(2,1)S(1)} %copy-done.25, ...), custom_call_target="tpu_custom_call" | custom-call | flops 1 | bytes 1 | tf_op jit(solution)/shard_map/attn_back/pallas_call | solution.py:488
  281.6 0.6 reshape.246.gains
  282.2 0.1 add_convert_fusion
  282.3 0.2 copy.57
  282.5 0.1 copy.59
  282.7 0.2 copy.58
  282.8 0.1 copy.60
  283.0 0.8 maximum_bitcast_fusion.tokens
  283.8 155.9 %outer_backward.1 = (f32[32,64,256]{2,1,0:T(8,128)}, bf16[3328,256]{1,0:T(8,128)(2,1)}, bf16[768,1024]{1,0:T(8,128)(2,1)}, bf16[4,2,128,256]{3,2,1,0:T(8,128)(2,...) custom-call(bf16[32,64,256]{2,1,0:T(8,128)(2,1)} %bitcast.101, ...), custom_call_target="tpu_custom_call" | custom-call | flops 1 | bytes 1 | tf_op jit(solution)/shard_map/outer_backward/pallas_call | solution.py:1687
  439.8 1.1 slice_convert_fusion
  440.9 0.8 copy.62
  441.8 0.7 copy.61
  442.5 0.7 fusion.6
  443.2 0.6 fusion.5
  443.7 0.6 fusion.4
  444.3 0.8 broadcast_multiply_fusion
  445.1 14.3 %finish_grads.1 = (f32[1024,256]{1,0:T(8,128)}, f32[1024,256]{1,0:T(8,128)}, f32[1024,256]{1,0:T(8,128)}, f32[256,1024]{1,0:T(8,128)}, f32[256,1024]{1,0:T(8,128...) custom-call(bf16[128,4096]{1,0:T(8,128)(2,1)} %bitcast.98, ...), custom_call_target="tpu_custom_call" | custom-call | flops 1 | bytes 1 | tf_op jit(solution)/shard_map/finish_grads/pallas_call | solution.py:1777
  459.5 1.0 copy.70
  460.4 1.0 copy-done.45
  461.4 1.3 copy.71
  (110 shorter events, 0.5 us)
Async XLA Ops:
  7.2 3.0 copy-start
  7.2 48.8 %all-gather.3.cloned.1.call-start = ((), (), s32[]{:S(2)}) async-start(), calls=%async_computation | async-start | bytes 1310720 | tf_op jit(solution)/shard_map/all_gather | solution.py:1855
  8.0 139.7 %all-gather.5.cloned.1.call-start = ((), (), s32[]{:S(2)}) async-start(), calls=%async_computation.1 | async-start | bytes 1310720 | tf_op jit(solution)/shard_map/all_gather | solution.py:1855
  8.7 436.4 %all-reduce.3.cloned.1.call-start = ((), (), s32[]{:S(2)}) async-start(), calls=%async_computation.2 | async-start | bytes 8388608 | tf_op jit(solution)/shard_map/psum | solution.py:1979
  10.5 112.9 %copy-start.29 = (f32[128,128]{1,0:T(8,128)}, f32[128,128]{1,0:T(8,128)S(1)}, u32[]{:S(2)}) copy-start(f32[128,128]{1,0:T(8,128)S(1)} %and_select_fusion.mask) | copy-start | bytes 196612
  12.1 43.9 %copy-start.18 = (bf16[256,1024]{1,0:T(8,128)(2,1)S(1)}, bf16[256,1024]{1,0:T(8,128)(2,1)}, u32[]{:S(2)}) copy-start(bf16[256,1024]{1,0:T(8,128)(2,1)} %lift_weight.1) | copy-start | bytes 1572868
  12.1 43.9 %copy-start.20 = (bf16[1024,256]{1,0:T(8,128)(2,1)S(1)}, bf16[1024,256]{1,0:T(8,128)(2,1)}, u32[]{:S(2)}) copy-start(bf16[1024,256]{1,0:T(8,128)(2,1)} %wq.7) | copy-start | bytes 1572868
  12.1 43.9 %copy-start.22 = (bf16[1024,256]{1,0:T(8,128)(2,1)S(1)}, bf16[1024,256]{1,0:T(8,128)(2,1)}, u32[]{:S(2)}) copy-start(bf16[1024,256]{1,0:T(8,128)(2,1)} %wk.3) | copy-start | bytes 1572868
  12.1 43.9 %copy-start.24 = (bf16[1024,256]{1,0:T(8,128)(2,1)S(1)}, bf16[1024,256]{1,0:T(8,128)(2,1)}, u32[]{:S(2)}) copy-start(bf16[1024,256]{1,0:T(8,128)(2,1)} %wv.3) | copy-start | bytes 1572868
  57.6 1.2 copy-start.42
  70.1 36.4 %copy-start.7 = (bf16[4,128,1024]{2,1,0:T(8,128)(2,1)}, bf16[4,128,1024]{2,1,0:T(8,128)(2,1)S(1)}, u32[]{:S(2)}) copy-start(bf16[4,128,1024]{2,1,0:T(8,128)(2,1)S(1)} %get-tuple-element.122) | copy-start | bytes 3145732
  70.1 36.5 %copy-start.26 = (f32[128,1024]{1,0:T(8,128)}, f32[128,1024]{1,0:T(8,128)S(1)}, u32[]{:S(2)}) copy-start(f32[128,1024]{1,0:T(8,128)S(1)} %get-tuple-element.95.before) | copy-start | bytes 1572868
  70.1 36.5 %copy-start.35 = (f32[3,1024]{1,0:T(4,128)S(1)}, f32[3,1024]{1,0:T(4,128)}, u32[]{:S(2)}) copy-start(f32[3,1024]{1,0:T(4,128)} %get-tuple-element.91.gain) | copy-start | bytes 36868
  70.1 36.5 %copy-start.43 = (bf16[256,1024]{1,0:T(8,128)(2,1)S(1)}, bf16[256,1024]{1,0:T(8,128)(2,1)}, u32[]{:S(2)}) copy-start(bf16[256,1024]{1,0:T(8,128)(2,1)} %weight.1) | copy-start | bytes 1572868
  106.5 16.9 %copy-start.9 = (bf16[8,1,512,128]{3,2,1,0:T(8,128)(2,1)}, bf16[8,1,512,128]{3,2,1,0:T(8,128)(2,1)S(1)}, u32[]{:S(2)}) copy-start(bf16[8,1,512,128]{3,2,1,0:T(8,128)(2,1)S(1)} %get-tuple-element.110.kv_ref) | copy-start | bytes 3145732
  106.5 16.9 %copy-start.32 = (bf16[4,1,64,512]{3,2,1,0:T(8,128)(2,1)}, bf16[4,1,64,512]{3,2,1,0:T(8,128)(2,1)S(1)}, u32[]{:S(2)}) copy-start(bf16[4,1,64,512]{3,2,1,0:T(8,128)(2,1)S(1)} %get-tuple-element.107.q_ref) | copy-start | bytes 786436
  106.5 16.9 %copy-start.40 = (f32[4,1,1,512]{3,2,1,0:T(1,128)}, f32[4,1,1,512]{3,2,1,0:T(1,128)S(1)}, u32[]{:S(2)}) copy-start(f32[4,1,1,512]{3,2,1,0:T(1,128)S(1)} %get-tuple-element.109.lse_ref) | copy-start | bytes 24580
  106.6 16.9 %copy-start.16 = (bf16[1024,256]{1,0:T(8,128)(2,1)S(1)}, bf16[1024,256]{1,0:T(8,128)(2,1)}, u32[]{:S(2)}) copy-start(bf16[1024,256]{1,0:T(8,128)(2,1)} %wq.6) | copy-start | bytes 1572868
  106.6 16.9 %copy-start.17 = (bf16[256,1024]{1,0:T(8,128)(2,1)S(1)}, bf16[256,1024]{1,0:T(8,128)(2,1)}, u32[]{:S(2)}) copy-start(bf16[256,1024]{1,0:T(8,128)(2,1)} %wo.3) | copy-start | bytes 1572868
  106.6 16.9 %copy-start.38 = (bf16[128,256]{1,0:T(8,128)(2,1)S(1)}, bf16[128,256]{1,0:T(8,128)(2,1)}, u32[]{:S(2)}) copy-start(bf16[128,256]{1,0:T(8,128)(2,1)} %get-tuple-element.97.ck) | copy-start | bytes 196612
  106.6 16.9 %copy-start.39 = (bf16[128,256]{1,0:T(8,128)(2,1)S(1)}, bf16[128,256]{1,0:T(8,128)(2,1)}, u32[]{:S(2)}) copy-start(bf16[128,256]{1,0:T(8,128)(2,1)} %get-tuple-element.98.cv) | copy-start | bytes 196612
  123.4 21.0 %copy-start.8 = (bf16[4,128,1024]{2,1,0:T(8,128)(2,1)}, bf16[4,128,1024]{2,1,0:T(8,128)(2,1)S(1)}, u32[]{:S(2)}) copy-start(bf16[4,128,1024]{2,1,0:T(8,128)(2,1)S(1)} %get-tuple-element.96.cross_in) | copy-start | bytes 3145732
  123.4 21.0 %copy-start.19 = (f32[128,1024]{1,0:T(8,128)}, f32[128,1024]{1,0:T(8,128)S(1)}, u32[]{:S(2)}) copy-start(f32[128,1024]{1,0:T(8,128)S(1)} %get-tuple-element.99.before) | copy-start | bytes 1572868
  175.7 26.8 %copy-start.44 = (bf16[256,1024]{1,0:T(8,128)(2,1)S(1)}, bf16[256,1024]{1,0:T(8,128)(2,1)}, u32[]{:S(2)}) copy-start(bf16[256,1024]{1,0:T(8,128)(2,1)} %weight.1) | copy-start | bytes 1572868
  175.7 28.6 %copy-start.11 = (bf16[512,1024]{1,0:T(8,128)(2,1)S(1)}, bf16[512,1024]{1,0:T(8,128)(2,1)}, u32[]{:S(2)}) copy-start(bf16[512,1024]{1,0:T(8,128)(2,1)} %get-tuple-element.112) | copy-start | bytes 3145732
  175.7 28.6 %copy-start.33 = (bf16[4,1,64,512]{3,2,1,0:T(8,128)(2,1)S(1)}, bf16[4,1,64,512]{3,2,1,0:T(8,128)(2,1)}, u32[]{:S(2)}) copy-start(bf16[4,1,64,512]{3,2,1,0:T(8,128)(2,1)} %copy-done.32) | copy-start | bytes 786436
  175.8 28.6 %copy-start.41 = (f32[4,1,1,512]{3,2,1,0:T(1,128)S(1)}, f32[4,1,1,512]{3,2,1,0:T(1,128)}, u32[]{:S(2)}) copy-start(f32[4,1,1,512]{3,2,1,0:T(1,128)} %copy-done.40) | copy-start | bytes 24580
  202.5 1.9 copy-start.10
  204.4 1.2 copy-start.12
  205.6 1.3 copy-start.13
  206.9 63.1 %copy-start.21 = (bf16[1024,256]{1,0:T(8,128)(2,1)S(1)}, bf16[1024,256]{1,0:T(8,128)(2,1)}, u32[]{:S(2)}) copy-start(bf16[1024,256]{1,0:T(8,128)(2,1)} %wq.7) | copy-start | bytes 1572868
  206.9 63.1 %copy-start.23 = (bf16[1024,256]{1,0:T(8,128)(2,1)S(1)}, bf16[1024,256]{1,0:T(8,128)(2,1)}, u32[]{:S(2)}) copy-start(bf16[1024,256]{1,0:T(8,128)(2,1)} %wk.3) | copy-start | bytes 1572868
  206.9 63.1 %copy-start.25 = (bf16[1024,256]{1,0:T(8,128)(2,1)S(1)}, bf16[1024,256]{1,0:T(8,128)(2,1)}, u32[]{:S(2)}) copy-start(bf16[1024,256]{1,0:T(8,128)(2,1)} %wv.3) | copy-start | bytes 1572868
  206.9 63.1 %copy-start.27 = (f32[128,1024]{1,0:T(8,128)S(1)}, f32[128,1024]{1,0:T(8,128)}, u32[]{:S(2)}) copy-start(f32[128,1024]{1,0:T(8,128)} %copy-done.26) | copy-start | bytes 1572868
  206.9 63.1 %copy-start.28 = (f32[128,1024]{1,0:T(8,128)S(1)}, f32[128,1024]{1,0:T(8,128)}, u32[]{:S(2)}) copy-start(f32[128,1024]{1,0:T(8,128)} %get-tuple-element.117.residual) | copy-start | bytes 1572868
  206.9 63.1 %copy-start.36 = (f32[3,1024]{1,0:T(4,128)S(1)}, f32[3,1024]{1,0:T(4,128)}, u32[]{:S(2)}) copy-start(f32[3,1024]{1,0:T(4,128)} %get-tuple-element.91.gain) | copy-start | bytes 36868
  269.9 12.4 %copy-start.2 = (bf16[1,512,512]{2,1,0:T(8,128)(2,1)}, bf16[1,512,512]{2,1,0:T(8,128)(2,1)S(1)}, u32[]{:S(2)}) copy-start(bf16[1,512,512]{2,1,0:T(8,128)(2,1)S(1)} %get-tuple-element.116) | copy-start | bytes 1572868
  269.9 12.4 %copy-start.6 = (bf16[1,256,512]{2,1,0:T(8,128)(2,1)}, bf16[1,256,512]{2,1,0:T(8,128)(2,1)S(1)}, u32[]{:S(2)}) copy-start(bf16[1,256,512]{2,1,0:T(8,128)(2,1)S(1)} %get-tuple-element.115) | copy-start | bytes 786436
  269.9 11.6 %copy-start.50 = (f32[1,1024]{1,0:T(1,128)S(1)}, f32[1,1024]{1,0:T(1,128)}, u32[]{:S(2)}) copy-start(f32[1,1024]{1,0:T(1,128)} %get-tuple-element.121) | copy-start | bytes 12292
  269.9 11.6 %copy-start.51 = (f32[1,1024]{1,0:T(1,128)S(1)}, f32[1,1024]{1,0:T(1,128)}, u32[]{:S(2)}) copy-start(f32[1,1024]{1,0:T(1,128)} %get-tuple-element.120) | copy-start | bytes 12292
  269.9 12.3 %copy-start.4 = (f32[128,1024]{1,0:T(8,128)S(1)}, f32[128,1024]{1,0:T(8,128)}, u32[]{:S(2)}) copy-start(f32[128,1024]{1,0:T(8,128)} %copy-done.3) | copy-start | bytes 1572868
  281.5 2.3 copy-start.5
  439.8 2.7 copy-start.47
  439.8 3.9 copy-start.52
  439.8 4.5 copy-start.49
  445.1 14.3 %copy-start.46 = (bf16[32,64,256]{2,1,0:T(8,128)(2,1)S(1)}, bf16[32,64,256]{2,1,0:T(8,128)(2,1)}, u32[]{:S(2)}) copy-start(bf16[32,64,256]{2,1,0:T(8,128)(2,1)} %get-tuple-element.87) | copy-start | bytes 3145732
  459.4 2.0 copy-start.45
  459.5 3.3 copy-start.1
  (8 other events, 6.2 us)
Sparse Core Ops, SparseCore 0:
  9.6 22.0 all-gather.2
  33.2 15.8 all-gather.4
  175.0 190.5 all-reduce.2

commit v6 on v5

--- a/solution.py
+++ b/solution.py
@@ -1286,7 +1286,7 @@
     def moments(total):
         grouped = in_groups(total) / count
         center = grouped[0:1]
-        return center, lax.rsqrt(grouped[1:2] - center * center + EPSILON)
+        return center, lax.rsqrt(jnp.maximum(grouped[1:2] - center * center, 0.0) + EPSILON)
 
     center1, std1 = moments(total1)
     scale1 = std1 * vec[0:1]

time: 474 us -> 474 us (level)
  no operation moved by 1% of the time
where the time goes in v6:
time: 474 us; the launch traced here: 470 us
  Pallas kernels  427 us (90%)
  local copies, waits for them, and re-layouts  17.1 us (4%)
  between operations  16.1 us (3%)
  other arithmetic  5.79 us (1%)
    pallas_call x1, Pallas kernels, outer_backward(): pl.pallas_call(functools.partial(outer_backward_kernel, nt, ns, cut), out...  156 us
    pallas_call x6, Pallas kernels, chain_call(): pl.pallas_call(functools.partial(kernel, ns), out_shape=tuple((jax.ShapeD...  114 us
    pallas_call x1, Pallas kernels, attention_back(): pl.pallas_call(functools.partial(attention_back_kernel, nt, ns, u), out_s...  62.1 us
    pallas_call x1, Pallas kernels, outer_forward(): pl.pallas_call(functools.partial(outer_forward_kernel, nt, ns), out_shape...  43.8 us
    pallas_call x1, Pallas kernels, self_attention(): pl.pallas_call(functools.partial(self_attention_kernel, nt, u), out_shape...  36.4 us
    pallas_call x1, Pallas kernels, finish_grads(): pl.pallas_call(finish_kernel, grid=(steps,), out_shape=(shape(width, feat...  14.3 us
    unnamed x108, local copies, waits for them, and re-layouts  12.9 us
  transfers between devices with their start and end apart: 3, of which 0 were waited for; matrix products, arithmetic and copies ran while one was open for 3% of the time, Pallas kernels for 82%

profile of v6, /device:TPU:0, one launch (start us, length us, event | category | flops | bytes accessed | tf_op | source)
XLA Modules:
  0.0 469.5 jit_solution(11057389814620117190)
XLA Ops:
  7.3 0.7 all-gather.3.cloned.1.call-update
  8.0 0.7 all-gather.5.cloned.1.call-update
  10.2 0.1 convolution_bitcast_fusion
  10.3 0.1 pad.7.clone
  10.4 0.1 and_select_fusion.mask
  10.5 0.2 copy-done.48
  10.7 0.7 maximum_bitcast_fusion.2
  11.5 0.7 maximum_bitcast_fusion.1.vec
  12.1 43.8 %outer_forward.1 = (bf16[32,64,256]{2,1,0:T(8,128)(2,1)}, bf16[128,256]{1,0:T(8,128)(2,1)}, bf16[2912,768]{1,0:T(8,128)(2,1)}, bf16[2752,768]{1,0:T(8,128)(2,1)}...) custom-call(bf16[32,64,256]{2,1,0:T(8,128)(2,1)} %bitcast.99, ...), custom_call_target="tpu_custom_call" | custom-call | flops 20000000000 | bytes 60000000 | tf_op jit(solution)/shard_map/outer_forward/pallas_call | solution.py:1382
  56.1 0.7 copy-done.34
  56.8 0.8 copy-done.37
  57.6 1.2 copy-done.42
  58.8 11.2 %enter.1 = (f32[128,1024]{1,0:T(8,128)S(1)}, bf16[4,128,1024]{2,1,0:T(8,128)(2,1)S(1)}, bf16[256,512]{1,0:T(8,128)(2,1)S(1)}, bf16[512,512]{1,0:T(8,128)(2,1)S(1)}) custom-call(bf16[8,4,16,1024]{3,2,1,0:T(8,128)(2,1)S(1)} %bitcast.89, bf16[128,256]{1,0:T(8,128)(2,1)S(1)} %copy-done.37, bf16[256,1024]{1,0:T(8,128)(2,1)S(1)} %copy-done.18, ...), custom_call_target="tpu_custom_call" | custom-call | flops 20000000000 | bytes 60000000 | tf_op jit(solution)/shard_map/enter/pallas_call | solution.py:488
  70.1 36.4 %self_attention.1 = (bf16[1,256,512]{2,1,0:T(8,128)(2,1)S(1)}, bf16[4,1,64,512]{3,2,1,0:T(8,128)(2,1)S(1)}, bf16[8,1,512,128]{3,2,1,0:T(8,128)(2,1)S(1)}, f32[4,...) custom-call(bf16[1,256,512]{2,1,0:T(8,128)(2,1)S(1)} %bitcast.91, bf16[1,512,512]{2,1,0:T(8,128)(2,1)S(1)} %bitcast.90), custom_call_target="tpu_custom_call" | custom-call | flops 20000000000 | bytes 60000000 | tf_op jit(solution)/shard_map/self_attention/pallas_call | solution.py:756
  106.6 16.8 %attn_out.1 = (f32[128,1024]{1,0:T(8,128)S(1)}, bf16[4,128,1024]{2,1,0:T(8,128)(2,1)S(1)}) custom-call(bf16[256,512]{1,0:T(8,128)(2,1)S(1)} %bitcast.86, bf16[256,1024]{1,0:T(8,128)(2,1)S(1)} %copy-done.43, f32[128,1024]{1,0:T(8,128)S(1)} %get-tuple-element.95.before, f32[3,1024]{1,0:T(4,128)S(1)} %copy-done.35), custom_call_target="tpu_custom_call" | custom-call | flops 20000000000 | bytes 60000000 | tf_op jit(solution)/shard_map/attn_out/pallas_call | solution.py:488
  123.5 20.9 %cross.1 = (f32[128,1024]{1,0:T(8,128)S(1)}, bf16[4,128,1024]{2,1,0:T(8,128)(2,1)S(1)}, bf16[4,128,256]{2,1,0:T(8,128)(2,1)S(1)}, bf16[4,128,256]{2,1,0:T(8,128)(2,1)S(1)}) custom-call(bf16[4,128,1024]{2,1,0:T(8,128)(2,1)S(1)} %get-tuple-element.96.cross_in, bf16[1024,256]{1,0:T(8,128)(2,1)S(1)} %copy-done.16, bf16[128,256]{1,0:T(8,128)(2,1)S(1)} %copy-done.38, ...), custom_call_target="tpu_custom_call" | custom-call | flops 20000000000 | bytes 60000000 | tf_op jit(solution)/shard_map/cross/pallas_call | solution.py:488
  144.5 0.8 copy-done.3
  145.3 1.0 copy-done.14
  146.2 0.7 copy-done.30
  147.0 0.7 copy-done.31
  147.7 27.3 %mlp.1 = (f32[128,1024]{1,0:T(8,128)}, bf16[4,128,1024]{2,1,0:T(8,128)(2,1)}, f32[1,1024]{1,0:T(1,128)}, bf16[512,1024]{1,0:T(8,128)(2,1)}, bf16[1024,1024]{1,0:T(8,128)(2,1)}, /*index=5*/bf16[1024,1024]{1,0:T(8,128)(2,1)}) custom-call(bf16[4,128,1024]{2,1,0:T(8,128)(2,1)} %copy-done.14, bf16[8,4,16,1024]{3,2,1,0:T(8,128)(2,1)} %bitcast.105, ...), custom_call_target="tpu_custom_call" | custom-call | flops 1 | bytes 1 | tf_op jit(solution)/shard_map/mlp/pallas_call | solution.py:488
  175.0 0.8 fusion.1
  175.8 26.8 %cross_back.1 = (f32[128,1024]{1,0:T(8,128)}, bf16[4,128,1024]{2,1,0:T(8,128)(2,1)}, f32[1,1024]{1,0:T(1,128)}, bf16[128,256]{1,0:T(8,128)(2,1)}, bf16[128,256]{...) custom-call(bf16[4,128,1024]{2,1,0:T(8,128)(2,1)} %get-tuple-element.102.incoming, bf16[256,1024]{1,0:T(8,128)(2,1)} %wo.3, ...), custom_call_target="tpu_custom_call" | custom-call | flops 1 | bytes 1 | tf_op jit(solution)/shard_map/cross_back/pallas_call | solution.py:488
  202.6 1.8 fusion.d_ref
  204.5 1.2 copy-done.12
  205.7 1.3 copy-done.13
  207.0 62.1 %attention_back.1 = (bf16[1,256,512]{2,1,0:T(8,128)(2,1)S(1)}, bf16[1,512,512]{2,1,0:T(8,128)(2,1)S(1)}, bf16[384,1024]{1,0:T(8,128)(2,1)S(1)}, f32[128,1024]{1,0:T(8,128)S(1)}) custom-call(bf16[1,256,512]{2,1,0:T(8,128)(2,1)S(1)} %fusion.d_ref, bf16[4,1,64,512]{3,2,1,0:T(8,128)(2,1)S(1)} %copy-done.33, f32[4,1,64,512]{3,2,1,0:T(8,128)S(1)} %get-tuple-element.108.of_ref, ...), custom_call_target="tpu_custom_call" | custom-call | flops 1 | bytes 1 | tf_op jit(solution)/shard_map/attention_back/pallas_call | solution.py:994
  269.1 0.9 copy-done.15
  270.0 11.5 %attn_back.1 = (bf16[128,1024]{1,0:T(8,128)(2,1)S(1)}, f32[1,1024]{1,0:T(1,128)S(1)}) custom-call(bf16[256,512]{1,0:T(8,128)(2,1)S(1)} %bitcast.79, bf16[512,512]{1,0:T(8,128)(2,1)S(1)} %bitcast.77, bf16[1024,256]{1,0:T(8,128)(2,1)S(1)} %copy-done.21, bf16[1024,256]{1,0:T(8,128)(2,1)S(1)} %copy-done.23, bf16[1024,256]{1,0:T(8,128)(2,1)S(1)} %copy-done.25, ...), custom_call_target="tpu_custom_call" | custom-call | flops 1 | bytes 1 | tf_op jit(solution)/shard_map/attn_back/pallas_call | solution.py:488
  281.6 0.6 reshape.246.gains
  282.2 0.1 add_convert_fusion
  282.3 0.2 copy.57
  282.5 0.1 copy.59
  282.6 0.2 copy.58
  282.8 0.1 copy.60
  283.0 0.8 maximum_bitcast_fusion.tokens
  283.8 156.0 %outer_backward.1 = (f32[32,64,256]{2,1,0:T(8,128)}, bf16[3328,256]{1,0:T(8,128)(2,1)}, bf16[768,1024]{1,0:T(8,128)(2,1)}, bf16[4,2,128,256]{3,2,1,0:T(8,128)(2,...) custom-call(bf16[32,64,256]{2,1,0:T(8,128)(2,1)} %bitcast.101, ...), custom_call_target="tpu_custom_call" | custom-call | flops 1 | bytes 1 | tf_op jit(solution)/shard_map/outer_backward/pallas_call | solution.py:1687
  439.8 1.1 slice_convert_fusion
  440.9 0.8 copy.62
  441.8 0.7 copy.61
  442.5 0.7 fusion.6
  443.2 0.6 fusion.5
  443.7 0.6 fusion.4
  444.3 0.8 broadcast_multiply_fusion
  445.1 14.3 %finish_grads.1 = (f32[1024,256]{1,0:T(8,128)}, f32[1024,256]{1,0:T(8,128)}, f32[1024,256]{1,0:T(8,128)}, f32[256,1024]{1,0:T(8,128)}, f32[256,1024]{1,0:T(8,128...) custom-call(bf16[128,4096]{1,0:T(8,128)(2,1)} %bitcast.98, ...), custom_call_target="tpu_custom_call" | custom-call | flops 1 | bytes 1 | tf_op jit(solution)/shard_map/finish_grads/pallas_call | solution.py:1777
  459.5 1.0 copy.70
  460.4 1.0 copy-done.45
  461.4 1.3 copy.71
  (110 shorter events, 0.5 us)
Async XLA Ops:
  7.2 3.0 copy-start
  7.2 48.8 %all-gather.3.cloned.1.call-start = ((), (), s32[]{:S(2)}) async-start(), calls=%async_computation | async-start | bytes 1310720 | tf_op jit(solution)/shard_map/all_gather | solution.py:1855
  8.0 139.7 %all-gather.5.cloned.1.call-start = ((), (), s32[]{:S(2)}) async-start(), calls=%async_computation.1 | async-start | bytes 1310720 | tf_op jit(solution)/shard_map/all_gather | solution.py:1855
  8.7 436.4 %all-reduce.3.cloned.1.call-start = ((), (), s32[]{:S(2)}) async-start(), calls=%async_computation.2 | async-start | bytes 8388608 | tf_op jit(solution)/shard_map/psum | solution.py:1979
  10.5 112.9 %copy-start.29 = (f32[128,128]{1,0:T(8,128)}, f32[128,128]{1,0:T(8,128)S(1)}, u32[]{:S(2)}) copy-start(f32[128,128]{1,0:T(8,128)S(1)} %and_select_fusion.mask) | copy-start | bytes 196612
  12.1 43.9 %copy-start.18 = (bf16[256,1024]{1,0:T(8,128)(2,1)S(1)}, bf16[256,1024]{1,0:T(8,128)(2,1)}, u32[]{:S(2)}) copy-start(bf16[256,1024]{1,0:T(8,128)(2,1)} %lift_weight.1) | copy-start | bytes 1572868
  12.1 43.9 %copy-start.20 = (bf16[1024,256]{1,0:T(8,128)(2,1)S(1)}, bf16[1024,256]{1,0:T(8,128)(2,1)}, u32[]{:S(2)}) copy-start(bf16[1024,256]{1,0:T(8,128)(2,1)} %wq.7) | copy-start | bytes 1572868
  12.1 43.9 %copy-start.22 = (bf16[1024,256]{1,0:T(8,128)(2,1)S(1)}, bf16[1024,256]{1,0:T(8,128)(2,1)}, u32[]{:S(2)}) copy-start(bf16[1024,256]{1,0:T(8,128)(2,1)} %wk.3) | copy-start | bytes 1572868
  12.1 43.9 %copy-start.24 = (bf16[1024,256]{1,0:T(8,128)(2,1)S(1)}, bf16[1024,256]{1,0:T(8,128)(2,1)}, u32[]{:S(2)}) copy-start(bf16[1024,256]{1,0:T(8,128)(2,1)} %wv.3) | copy-start | bytes 1572868
  57.6 1.2 copy-start.42
  70.1 36.5 %copy-start.7 = (bf16[4,128,1024]{2,1,0:T(8,128)(2,1)}, bf16[4,128,1024]{2,1,0:T(8,128)(2,1)S(1)}, u32[]{:S(2)}) copy-start(bf16[4,128,1024]{2,1,0:T(8,128)(2,1)S(1)} %get-tuple-element.122) | copy-start | bytes 3145732
  70.1 36.5 %copy-start.26 = (f32[128,1024]{1,0:T(8,128)}, f32[128,1024]{1,0:T(8,128)S(1)}, u32[]{:S(2)}) copy-start(f32[128,1024]{1,0:T(8,128)S(1)} %get-tuple-element.95.before) | copy-start | bytes 1572868
  70.1 36.5 %copy-start.35 = (f32[3,1024]{1,0:T(4,128)S(1)}, f32[3,1024]{1,0:T(4,128)}, u32[]{:S(2)}) copy-start(f32[3,1024]{1,0:T(4,128)} %get-tuple-element.91.gain) | copy-start | bytes 36868
  70.1 36.5 %copy-start.43 = (bf16[256,1024]{1,0:T(8,128)(2,1)S(1)}, bf16[256,1024]{1,0:T(8,128)(2,1)}, u32[]{:S(2)}) copy-start(bf16[256,1024]{1,0:T(8,128)(2,1)} %weight.1) | copy-start | bytes 1572868
  106.5 16.9 %copy-start.9 = (bf16[8,1,512,128]{3,2,1,0:T(8,128)(2,1)}, bf16[8,1,512,128]{3,2,1,0:T(8,128)(2,1)S(1)}, u32[]{:S(2)}) copy-start(bf16[8,1,512,128]{3,2,1,0:T(8,128)(2,1)S(1)} %get-tuple-element.110.kv_ref) | copy-start | bytes 3145732
  106.5 16.9 %copy-start.32 = (bf16[4,1,64,512]{3,2,1,0:T(8,128)(2,1)}, bf16[4,1,64,512]{3,2,1,0:T(8,128)(2,1)S(1)}, u32[]{:S(2)}) copy-start(bf16[4,1,64,512]{3,2,1,0:T(8,128)(2,1)S(1)} %get-tuple-element.107.q_ref) | copy-start | bytes 786436
  106.5 16.9 %copy-start.40 = (f32[4,1,1,512]{3,2,1,0:T(1,128)}, f32[4,1,1,512]{3,2,1,0:T(1,128)S(1)}, u32[]{:S(2)}) copy-start(f32[4,1,1,512]{3,2,1,0:T(1,128)S(1)} %get-tuple-element.109.lse_ref) | copy-start | bytes 24580
  106.6 16.9 %copy-start.16 = (bf16[1024,256]{1,0:T(8,128)(2,1)S(1)}, bf16[1024,256]{1,0:T(8,128)(2,1)}, u32[]{:S(2)}) copy-start(bf16[1024,256]{1,0:T(8,128)(2,1)} %wq.6) | copy-start | bytes 1572868
  106.6 16.9 %copy-start.17 = (bf16[256,1024]{1,0:T(8,128)(2,1)S(1)}, bf16[256,1024]{1,0:T(8,128)(2,1)}, u32[]{:S(2)}) copy-start(bf16[256,1024]{1,0:T(8,128)(2,1)} %wo.3) | copy-start | bytes 1572868
  106.6 16.9 %copy-start.38 = (bf16[128,256]{1,0:T(8,128)(2,1)S(1)}, bf16[128,256]{1,0:T(8,128)(2,1)}, u32[]{:S(2)}) copy-start(bf16[128,256]{1,0:T(8,128)(2,1)} %get-tuple-element.97.ck) | copy-start | bytes 196612
  106.6 16.9 %copy-start.39 = (bf16[128,256]{1,0:T(8,128)(2,1)S(1)}, bf16[128,256]{1,0:T(8,128)(2,1)}, u32[]{:S(2)}) copy-start(bf16[128,256]{1,0:T(8,128)(2,1)} %get-tuple-element.98.cv) | copy-start | bytes 196612
  123.4 21.0 %copy-start.8 = (bf16[4,128,1024]{2,1,0:T(8,128)(2,1)}, bf16[4,128,1024]{2,1,0:T(8,128)(2,1)S(1)}, u32[]{:S(2)}) copy-start(bf16[4,128,1024]{2,1,0:T(8,128)(2,1)S(1)} %get-tuple-element.96.cross_in) | copy-start | bytes 3145732
  123.5 21.0 %copy-start.19 = (f32[128,1024]{1,0:T(8,128)}, f32[128,1024]{1,0:T(8,128)S(1)}, u32[]{:S(2)}) copy-start(f32[128,1024]{1,0:T(8,128)S(1)} %get-tuple-element.99.before) | copy-start | bytes 1572868
  175.8 26.8 %copy-start.44 = (bf16[256,1024]{1,0:T(8,128)(2,1)S(1)}, bf16[256,1024]{1,0:T(8,128)(2,1)}, u32[]{:S(2)}) copy-start(bf16[256,1024]{1,0:T(8,128)(2,1)} %weight.1) | copy-start | bytes 1572868
  175.8 28.6 %copy-start.11 = (bf16[512,1024]{1,0:T(8,128)(2,1)S(1)}, bf16[512,1024]{1,0:T(8,128)(2,1)}, u32[]{:S(2)}) copy-start(bf16[512,1024]{1,0:T(8,128)(2,1)} %get-tuple-element.112) | copy-start | bytes 3145732
  175.8 28.6 %copy-start.33 = (bf16[4,1,64,512]{3,2,1,0:T(8,128)(2,1)S(1)}, bf16[4,1,64,512]{3,2,1,0:T(8,128)(2,1)}, u32[]{:S(2)}) copy-start(bf16[4,1,64,512]{3,2,1,0:T(8,128)(2,1)} %copy-done.32) | copy-start | bytes 786436
  175.8 28.6 %copy-start.41 = (f32[4,1,1,512]{3,2,1,0:T(1,128)S(1)}, f32[4,1,1,512]{3,2,1,0:T(1,128)}, u32[]{:S(2)}) copy-start(f32[4,1,1,512]{3,2,1,0:T(1,128)} %copy-done.40) | copy-start | bytes 24580
  202.6 1.9 copy-start.10
  204.4 1.2 copy-start.12
  205.7 1.3 copy-start.13
  206.9 63.0 %copy-start.21 = (bf16[1024,256]{1,0:T(8,128)(2,1)S(1)}, bf16[1024,256]{1,0:T(8,128)(2,1)}, u32[]{:S(2)}) copy-start(bf16[1024,256]{1,0:T(8,128)(2,1)} %wq.7) | copy-start | bytes 1572868
  206.9 63.0 %copy-start.23 = (bf16[1024,256]{1,0:T(8,128)(2,1)S(1)}, bf16[1024,256]{1,0:T(8,128)(2,1)}, u32[]{:S(2)}) copy-start(bf16[1024,256]{1,0:T(8,128)(2,1)} %wk.3) | copy-start | bytes 1572868
  206.9 63.0 %copy-start.25 = (bf16[1024,256]{1,0:T(8,128)(2,1)S(1)}, bf16[1024,256]{1,0:T(8,128)(2,1)}, u32[]{:S(2)}) copy-start(bf16[1024,256]{1,0:T(8,128)(2,1)} %wv.3) | copy-start | bytes 1572868
  206.9 63.1 %copy-start.27 = (f32[128,1024]{1,0:T(8,128)S(1)}, f32[128,1024]{1,0:T(8,128)}, u32[]{:S(2)}) copy-start(f32[128,1024]{1,0:T(8,128)} %copy-done.26) | copy-start | bytes 1572868
  206.9 63.1 %copy-start.28 = (f32[128,1024]{1,0:T(8,128)S(1)}, f32[128,1024]{1,0:T(8,128)}, u32[]{:S(2)}) copy-start(f32[128,1024]{1,0:T(8,128)} %get-tuple-element.117.residual) | copy-start | bytes 1572868
  206.9 63.1 %copy-start.36 = (f32[3,1024]{1,0:T(4,128)S(1)}, f32[3,1024]{1,0:T(4,128)}, u32[]{:S(2)}) copy-start(f32[3,1024]{1,0:T(4,128)} %get-tuple-element.91.gain) | copy-start | bytes 36868
  269.9 12.4 %copy-start.2 = (bf16[1,512,512]{2,1,0:T(8,128)(2,1)}, bf16[1,512,512]{2,1,0:T(8,128)(2,1)S(1)}, u32[]{:S(2)}) copy-start(bf16[1,512,512]{2,1,0:T(8,128)(2,1)S(1)} %get-tuple-element.116) | copy-start | bytes 1572868
  269.9 12.4 %copy-start.6 = (bf16[1,256,512]{2,1,0:T(8,128)(2,1)}, bf16[1,256,512]{2,1,0:T(8,128)(2,1)S(1)}, u32[]{:S(2)}) copy-start(bf16[1,256,512]{2,1,0:T(8,128)(2,1)S(1)} %get-tuple-element.115) | copy-start | bytes 786436
  269.9 11.6 %copy-start.50 = (f32[1,1024]{1,0:T(1,128)S(1)}, f32[1,1024]{1,0:T(1,128)}, u32[]{:S(2)}) copy-start(f32[1,1024]{1,0:T(1,128)} %get-tuple-element.121) | copy-start | bytes 12292
  269.9 11.6 %copy-start.51 = (f32[1,1024]{1,0:T(1,128)S(1)}, f32[1,1024]{1,0:T(1,128)}, u32[]{:S(2)}) copy-start(f32[1,1024]{1,0:T(1,128)} %get-tuple-element.120) | copy-start | bytes 12292
  269.9 12.3 %copy-start.4 = (f32[128,1024]{1,0:T(8,128)S(1)}, f32[128,1024]{1,0:T(8,128)}, u32[]{:S(2)}) copy-start(f32[128,1024]{1,0:T(8,128)} %copy-done.3) | copy-start | bytes 1572868
  281.5 2.3 copy-start.5
  439.8 2.7 copy-start.47
  439.8 3.9 copy-start.52
  439.8 4.5 copy-start.49
  445.1 14.3 %copy-start.46 = (bf16[32,64,256]{2,1,0:T(8,128)(2,1)S(1)}, bf16[32,64,256]{2,1,0:T(8,128)(2,1)}, u32[]{:S(2)}) copy-start(bf16[32,64,256]{2,1,0:T(8,128)(2,1)} %get-tuple-element.87) | copy-start | bytes 3145732
  459.4 2.0 copy-start.45
  459.5 3.3 copy-start.1
  (8 other events, 6.2 us)
Sparse Core Ops, SparseCore 0:
  9.6 22.0 all-gather.2
  33.2 15.8 all-gather.4
  175.1 190.5 all-reduce.2
